TPU v7x, 512 devices: a whole 4x8x8 slice. The times are simulated.
512 devices in a mesh: gx: 16 (over z, core), gy: 4 (over y_hi), gz: 8 (over y_lo, x).
Axes of the slice: x: 4, y: 8 (y_hi: 4, y_lo: 2; y = y_hi * 2 + y_lo), z: 8, core: 2. Of those that a mesh axis runs over, the one named last changes fastest.
Arguments:
- tokens: bfloat16 [128, 32, 64, 384], P('gx', 'gy', 'gz'), may hold values from -60 to 60
- frozen: int32 [128, 32, 64], P('gx', 'gy', 'gz'), may hold values 0 or 1
- cotangent: bfloat16 [128, 32, 64, 384], P('gx', 'gy', 'gz'), may hold values from -6 to 6
- w_qkv: bfloat16 [384, 1152], replicated, may hold values from -0.3125 to 0.3125
- w_proj: bfloat16 [384, 384], replicated, may hold values from -0.3125 to 0.3125
- norm_gain: float32 [384], replicated, may hold values from 0.5 to 8
Outputs:
- block_out: bfloat16 [128, 32, 64, 384], P('gx', 'gy', 'gz')
- tokens_grad: bfloat16 [128, 32, 64, 384], P('gx', 'gy', 'gz')
- qkv_grad: float32 [384, 1152], replicated
- proj_grad: float32 [384, 384], replicated
- gain_grad: float32 [384], replicated
All inputs are finite; a program needn't handle non-finite values. No bound on the sum of `frozen` on one device may be relied on, other than what follows from the above.
Results may differ from a plain program's by a relative error of at most 0.015.
The roundings to bfloat16 on the way count: a program that leaves them out, or rounds other values in their place, can miss the bound.
Values may be sent and summed in bfloat16 or wider, within the bound.
No kernel may reach another device: no remote copies, remote signals or barrier semaphores. Data moves between devices by JAX's collectives and lax.ppermute only.
A program may use at most 64 MiB of HBM per device.

v0:
```python
import jax
import jax.numpy as jnp
from jax import lax
from jax.sharding import PartitionSpec as P

D = 384
HEADS = 12
HDIM = 32
WIN = 8


EPSILON = 1e-05


def shifted_2(block, axis, distance):
    devices = range(lax.axis_size(axis))
    route = [((i - distance) % len(devices), i) for i in devices]
    return lax.ppermute(block, axis, route)


def group_pass(queries, key_rows, values, d_mixed):
    score_scale = HDIM ** (-0.5)
    scores = (
        jnp.einsum("qhd,khd->hqk", queries, key_rows, preferred_element_type=jnp.float32)
        * score_scale
    )
    top_score = jnp.max(scores, axis=-1, keepdims=True)
    exp_terms = jnp.exp(scores - top_score)
    attn_probs = exp_terms / jnp.sum(exp_terms, axis=-1, keepdims=True)
    probs_low = attn_probs.astype(jnp.bfloat16)
    mixed_group = jnp.einsum(
        "hqk,khd->qhd", probs_low, values, preferred_element_type=jnp.float32
    ).astype(jnp.bfloat16)
    d_values = jnp.einsum(
        "hqk,qhd->khd", probs_low, d_mixed, preferred_element_type=jnp.float32
    ).astype(jnp.bfloat16)
    d_probs = jnp.einsum("qhd,khd->hqk", d_mixed, values, preferred_element_type=jnp.float32)
    d_scores = (
        attn_probs * (d_probs - jnp.sum(attn_probs * d_probs, axis=-1, keepdims=True)) * score_scale
    ).astype(jnp.bfloat16)
    d_queries = jnp.einsum(
        "hqk,khd->qhd", d_scores, key_rows, preferred_element_type=jnp.float32
    ).astype(jnp.bfloat16)
    d_keys = jnp.einsum(
        "hqk,qhd->khd", d_scores, queries, preferred_element_type=jnp.float32
    ).astype(jnp.bfloat16)
    return (mixed_group, d_queries, d_keys, d_values)


def window_pass(window_rows, window_cot, w_qkv, w_proj, norm_gain):
    row_count = window_rows.shape[0]
    groups = 2
    per_group = HEADS // groups
    widened = window_rows.astype(jnp.float32)
    row_mean = jnp.mean(widened, axis=-1, keepdims=True)
    centred = widened - row_mean
    inv_std = lax.rsqrt(jnp.mean(centred * centred, axis=-1, keepdims=True) + EPSILON)
    unit_rows = centred * inv_std
    normed = (unit_rows * norm_gain).astype(jnp.bfloat16)
    qkv_rows = jnp.dot(normed, w_qkv, preferred_element_type=jnp.float32).astype(jnp.bfloat16)
    d_mixed = jnp.dot(window_cot, w_proj.T, preferred_element_type=jnp.float32).astype(jnp.bfloat16)

    def grouped(rows):
        return rows.reshape(row_count, groups, per_group, HDIM).transpose(1, 0, 2, 3)

    def ungrouped(parts):
        return parts.transpose(1, 0, 2, 3).reshape(row_count, D)

    outputs = lax.map(
        lambda packed: group_pass(*packed),
        (
            grouped(qkv_rows[:, :D]),
            grouped(qkv_rows[:, D : 2 * D]),
            grouped(qkv_rows[:, 2 * D :]),
            grouped(d_mixed),
        ),
    )
    mixed_rows = ungrouped(outputs[0])
    branch = jnp.dot(mixed_rows, w_proj, preferred_element_type=jnp.float32).astype(jnp.bfloat16)
    d_qkv = jnp.concatenate(
        [ungrouped(outputs[1]), ungrouped(outputs[2]), ungrouped(outputs[3])], axis=1
    )
    proj_term = jnp.dot(mixed_rows.T, window_cot, preferred_element_type=jnp.float32)
    qkv_term = jnp.dot(normed.T, d_qkv, preferred_element_type=jnp.float32)
    d_normed = jnp.dot(d_qkv, w_qkv.T, preferred_element_type=jnp.float32)
    gain_term = jnp.sum(d_normed * unit_rows, axis=0)
    scaled_grad = d_normed * norm_gain
    d_rows = (
        inv_std
        * (
            scaled_grad
            - jnp.mean(scaled_grad, axis=-1, keepdims=True)
            - unit_rows * jnp.mean(scaled_grad * unit_rows, axis=-1, keepdims=True)
        )
    ).astype(jnp.bfloat16)
    return (branch, d_rows, qkv_term, proj_term, gain_term)


def partition(block):
    first, second, third, width = block.shape
    grid = block.reshape(first // WIN, WIN, second // WIN, WIN, third // WIN, WIN, width)
    return grid.transpose(0, 2, 4, 1, 3, 5, 6).reshape(-1, WIN**3, width)


def assemble(windows, first, second, third):
    grid = windows.reshape(
        first // WIN, second // WIN, third // WIN, WIN, WIN, WIN, windows.shape[-1]
    )
    return grid.transpose(0, 3, 1, 4, 2, 5, 6).reshape(first, second, third, windows.shape[-1])


def border(stacked, axis_pos, direction):
    half_width = WIN // 2
    extent = stacked.shape[axis_pos]
    if direction < 0:
        return lax.slice_in_dim(stacked, 0, half_width, axis=axis_pos)
    return lax.slice_in_dim(stacked, extent - half_width, extent, axis=axis_pos)


def attach(stacked, arrived, axis_pos, direction):
    half_width = WIN // 2
    extent = stacked.shape[axis_pos]
    if direction < 0:
        return jnp.concatenate(
            [lax.slice_in_dim(stacked, half_width, extent, axis=axis_pos), arrived], axis=axis_pos
        )
    return jnp.concatenate(
        [arrived, lax.slice_in_dim(stacked, 0, extent - half_width, axis=axis_pos)], axis=axis_pos
    )


def roll_half(stacked, direction):
    stacked = attach(
        stacked, shifted_2(border(stacked, 1, direction), "gx", direction), 1, direction
    )
    stacked = attach(
        stacked, shifted_2(border(stacked, 2, direction), "gy", direction), 2, direction
    )
    stacked = attach(
        stacked, shifted_2(border(stacked, 3, direction), "gz", direction), 3, direction
    )
    return stacked


def local(tokens, frozen, cotangent, w_qkv, w_proj, norm_gain):
    kept = jnp.where(frozen[..., None] == 1, tokens, jnp.zeros_like(tokens))
    shifted = roll_half(jnp.stack([kept, cotangent]), -1)
    zeros_init = (
        jnp.zeros((D, 3 * D), jnp.float32),
        jnp.zeros((D, D), jnp.float32),
        jnp.zeros((D,), jnp.float32),
    )

    def window_step(totals, window_pair):
        results = window_pass(window_pair[0], window_pair[1], w_qkv, w_proj, norm_gain)
        return (
            (totals[0] + results[2], totals[1] + results[3], totals[2] + results[4]),
            (results[0], results[1]),
        )

    totals, blocks = lax.scan(
        window_step, zeros_init, (partition(shifted[0]), partition(shifted[1]))
    )
    first, second, third = (tokens.shape[0], tokens.shape[1], tokens.shape[2])
    returned = jnp.stack(
        [assemble(blocks[0], first, second, third), assemble(blocks[1], first, second, third)]
    )
    restored = roll_half(returned, 1)
    summed = lax.psum((totals[0], totals[1], totals[2]), ("gx", "gy", "gz"))
    block_out = (kept.astype(jnp.float32) + restored[0].astype(jnp.float32)).astype(jnp.bfloat16)
    tokens_grad = jnp.where(
        frozen[..., None] == 1,
        cotangent.astype(jnp.float32) + restored[1].astype(jnp.float32),
        jnp.zeros((), jnp.float32),
    ).astype(jnp.bfloat16)
    everyone = (
        first * second * third * lax.axis_size("gx") * lax.axis_size("gy") * lax.axis_size("gz")
    )
    grad_scale = everyone ** (-0.5)
    return (
        block_out,
        tokens_grad,
        summed[0] * grad_scale,
        summed[1] * grad_scale,
        summed[2] * grad_scale,
    )


def solution(mesh):
    placed = (
        P("gx", "gy", "gz", None),
        P("gx", "gy", "gz"),
        P("gx", "gy", "gz", None),
        P(),
        P(),
        P(),
    )
    return jax.shard_map(
        local,
        mesh=mesh,
        in_specs=placed,
        out_specs=(P("gx", "gy", "gz", None), P("gx", "gy", "gz", None), P(), P(), P()),
        check_vma=False,
    )
```

profile of v0, /device:TPU:1, one launch (start us, length us, event | category | flops | bytes accessed | tf_op | source)
XLA Modules:
  0.0 447.3 jit_solution(671043157918539408)
XLA Ops:
  10.3 6.9 %collective-permute-start = (bf16[2,4,8,8,384]{4,3,2,1,0:T(8,128)(2,1)S(1)}, bf16[2,4,8,8,384]{4,3,2,1,0:T(8,128)(2,1)S(1)}, u32[]{:S(2)}, u32[]{:S(2)}) collective-permute-start(bf16[2,4,8,8,384]{4,3,2,1,0:T(8,128)(2,1)S(1)} %get-tuple-element.131), channel_id=1, source_target_pairs={{32,0},{64,32},{96,64},{128,96},{160,128},{192,160},{224,192},{256... | collective-permute-start | bytes 1179656 | tf_op jit(solution)/shard_map/ppermute | solution.py:18
  19.4 5.9 %collective-permute-start.1 = (bf16[2,8,4,8,384]{4,3,2,1,0:T(8,128)(2,1)S(1)}, bf16[2,8,4,8,384]{4,3,2,1,0:T(8,128)(2,1)S(1)}, u32[]{:S(2)}, u32[]{:S(2)}) collective-permute-start(bf16[2,8,4,8,384]{4,3,2,1,0:T(8,128)(2,1)S(1)} %get-tuple-element.129), channel_id=1, source_target_pairs={{8,0},{16,8},{24,16},{0,24},{9,1},{17,9},{25,17},{1,25},{10,2},{18... | collective-permute-start | bytes 1179656 | tf_op jit(solution)/shard_map/ppermute | solution.py:18
  25.3 11.0 %collective-permute-done.1 = bf16[2,8,4,8,384]{4,3,2,1,0:T(8,128)(2,1)S(1)} collective-permute-done((bf16[2,8,4,8,384]{4,3,2,1,0:T(8,128)(2,1)S(1)}, bf16[2,8,4,8,384]{4,3,2,1,0:T(8,128)(2,1)S(1)}, u32[]{:S(2)}, u32[]{:S(2)}) %collective-permute-start.1) | collective-permute-done | bytes 393248 | tf_op jit(solution)/shard_map/ppermute | solution.py:18
  38.5 6.6 %collective-permute-done.2 = bf16[2,8,8,4,384]{4,3,2,1,0:T(4,128)(2,1)S(1)} collective-permute-done((bf16[2,8,8,4,384]{4,3,2,1,0:T(4,128)(2,1)S(1)}, bf16[2,8,8,4,384]{4,3,2,1,0:T(4,128)(2,1)S(1)}, u32[]{:S(2)}, u32[]{:S(2)}) %collective-permute-start.2) | collective-permute-done | bytes 393248 | tf_op jit(solution)/shard_map/ppermute | solution.py:18
  50.4 76.5 %while.30 = (s32[]{:T(128)}, bf16[2,512,6,32]{1,3,2,0:T(8,128)(2,1)}, bf16[2,512,6,32]{1,3,2,0:T(8,128)(2,1)}, bf16[2,512,6,32]{1,3,2,0:T(8,128)(2,1)}, bf16[2,5...) while((s32[]{:T(128)}, ...), condition=%wide.region_6.7_spmd, body=%wide.region_2.6_spmd.sunk | while | flops 637410816 | bytes 84265168 | solution.py:69
  50.6 4.8 %fusion.173 = (f32[6,512]{1,0:T(8,128)S(1)}, f32[6,512,512]{1,2,0:T(8,128)}) fusion(bf16[2,512,6,32]{1,3,2,0:T(8,128)(2,1)S(1)} %get-tuple-element.221, s32[]{:T(128)} %get-tuple-element.204, bf16[2,512,6,32]{1,3,2,0:T(8,128)(2,1)S(1)} %get-tuple-element.220), kind=kOutput, calls=%fused_computation.123.clone.1 | convolution fusion | flops 105382400 | bytes 6697984 | tf_op jit(solution)/shard_map/while/body/eval_jaxpr/while/body/eval_jaxpr/sub | solution.py:28
  55.4 3.7 fusion.175
  59.1 9.3 %fusion.177 = bf16[2,512,6,32]{1,3,2,0:T(8,128)(2,1)S(1)} fusion(bf16[2,512,6,32]{1,3,2,0:T(8,128)(2,1)S(1)} %copy-done.23, s32[]{:T(128)} %get-tuple-element.204, f32[6,512,512]{1,2,0:T(8,128)} %fusion.175, bf16[2,512,6,32]{1,3,2,0:T(8,128)(2,1)S(1)} %get-tuple-element.220, f32[6,512,512]{1,2,0:T(8,128)} %get-tuple-element.192, ...), kind=kOutput, calls=%fused_computation.25.clone.1 | convolution fusion | flops 111775232 | bytes 25592832 | tf_op jit(solution)/shard_map/while/body/eval_jaxpr/while/body/eval_jaxpr/hqk,qhd->khd/dot_general | solution.py:44
  68.4 11.6 %fusion.176 = bf16[2,512,6,32]{1,3,2,0:T(8,128)(2,1)} fusion(bf16[2,512,6,32]{1,3,2,0:T(8,128)(2,1)} %get-tuple-element.206, s32[]{:T(128)} %get-tuple-element.204, f32[6,512,512]{1,2,0:T(8,128)} %fusion.175, bf16[2,512,6,32]{1,3,2,0:T(8,128)(2,1)S(1)} %get-tuple-element.221, f32[6,512,512]{1,2,0:T(8,128)} %get-tuple-element.192, ...), kind=kOutput, calls=%fused_computation.27.clone.1 | convolution fusion | flops 111775232 | bytes 25592832 | tf_op jit(solution)/shard_map/while/body/eval_jaxpr/while/body/eval_jaxpr/hqk,khd->qhd/dot_general | solution.py:41
  80.0 4.6 %fusion.178 = bf16[2,512,6,32]{1,3,2,0:T(8,128)(2,1)} fusion(bf16[2,512,6,32]{1,3,2,0:T(8,128)(2,1)} %get-tuple-element.208, s32[]{:T(128)} %get-tuple-element.204, bf16[2,512,6,32]{1,3,2,0:T(8,128)(2,1)S(1)} %get-tuple-element.222, f32[6,512,512]{1,2,0:T(8,128)} %get-tuple-element.192, f32[6,512]{1,0:T(8,128)S(1)} %get-tuple-element.193), kind=kOutput, calls=%fused_computation.21.clone.1 | convolution fusion | flops 103907328 | bytes 6702080 | tf_op jit(solution)/shard_map/while/body/eval_jaxpr/while/body/eval_jaxpr/hqk,qhd->khd/dot_general | solution.py:34
  84.6 3.4 fusion.174
  88.8 4.8 %fusion.173 = (f32[6,512]{1,0:T(8,128)S(1)}, f32[6,512,512]{1,2,0:T(8,128)}) fusion(bf16[2,512,6,32]{1,3,2,0:T(8,128)(2,1)S(1)} %get-tuple-element.221, s32[]{:T(128)} %get-tuple-element.204, bf16[2,512,6,32]{1,3,2,0:T(8,128)(2,1)S(1)} %get-tuple-element.220), kind=kOutput, calls=%fused_computation.123.clone.1 | convolution fusion | flops 105382400 | bytes 6697984 | tf_op jit(solution)/shard_map/while/body/eval_jaxpr/while/body/eval_jaxpr/sub | solution.py:28
  93.5 3.7 fusion.175
  97.2 9.3 %fusion.177 = bf16[2,512,6,32]{1,3,2,0:T(8,128)(2,1)S(1)} fusion(bf16[2,512,6,32]{1,3,2,0:T(8,128)(2,1)S(1)} %copy-done.23, s32[]{:T(128)} %get-tuple-element.204, f32[6,512,512]{1,2,0:T(8,128)} %fusion.175, bf16[2,512,6,32]{1,3,2,0:T(8,128)(2,1)S(1)} %get-tuple-element.220, f32[6,512,512]{1,2,0:T(8,128)} %get-tuple-element.192, ...), kind=kOutput, calls=%fused_computation.25.clone.1 | convolution fusion | flops 111775232 | bytes 25592832 | tf_op jit(solution)/shard_map/while/body/eval_jaxpr/while/body/eval_jaxpr/hqk,qhd->khd/dot_general | solution.py:44
  106.5 11.6 %fusion.176 = bf16[2,512,6,32]{1,3,2,0:T(8,128)(2,1)} fusion(bf16[2,512,6,32]{1,3,2,0:T(8,128)(2,1)} %get-tuple-element.206, s32[]{:T(128)} %get-tuple-element.204, f32[6,512,512]{1,2,0:T(8,128)} %fusion.175, bf16[2,512,6,32]{1,3,2,0:T(8,128)(2,1)S(1)} %get-tuple-element.221, f32[6,512,512]{1,2,0:T(8,128)} %get-tuple-element.192, ...), kind=kOutput, calls=%fused_computation.27.clone.1 | convolution fusion | flops 111775232 | bytes 25592832 | tf_op jit(solution)/shard_map/while/body/eval_jaxpr/while/body/eval_jaxpr/hqk,khd->qhd/dot_general | solution.py:41
  118.1 4.6 %fusion.178 = bf16[2,512,6,32]{1,3,2,0:T(8,128)(2,1)} fusion(bf16[2,512,6,32]{1,3,2,0:T(8,128)(2,1)} %get-tuple-element.208, s32[]{:T(128)} %get-tuple-element.204, bf16[2,512,6,32]{1,3,2,0:T(8,128)(2,1)S(1)} %get-tuple-element.222, f32[6,512,512]{1,2,0:T(8,128)} %get-tuple-element.192, f32[6,512]{1,0:T(8,128)S(1)} %get-tuple-element.193), kind=kOutput, calls=%fused_computation.21.clone.1 | convolution fusion | flops 103907328 | bytes 6702080 | tf_op jit(solution)/shard_map/while/body/eval_jaxpr/while/body/eval_jaxpr/hqk,qhd->khd/dot_general | solution.py:34
  122.7 3.4 fusion.174
  126.9 3.2 fusion.109
  133.6 11.5 %collective-permute-start.3 = (bf16[2,4,8,8,384]{4,3,2,1,0:T(8,128)(2,1)S(1)}, bf16[2,4,8,8,384]{4,3,2,1,0:T(8,128)(2,1)S(1)}, u32[]{:S(2)}, u32[]{:S(2)}) collective-permute-start(bf16[2,4,8,8,384]{4,3,2,1,0:T(8,128)(2,1)S(1)} %fusion.112), channel_id=1, source_target_pairs={{480,0},{0,32},{32,64},{64,96},{96,128},{128,160},{160,192},{192,2... | collective-permute-start | bytes 1179656 | tf_op jit(solution)/shard_map/ppermute | solution.py:18
  146.4 3.5 collective-permute-done.3
  150.1 4.2 collective-permute-start.4
  154.3 113.1 %psum.23 = f32[384]{0:T(512)S(1)} all-reduce(f32[384]{0:T(512)S(1)} %get-tuple-element.92), channel_id=1, replica_groups=mesh['gx'=16,'gy'=4,'gz'=8] {'gx','gy','gz'}, use_global_device_ids=true, to_apply=%region_12.13 | all-reduce | flops 384 | bytes 3072 | tf_op jit(solution)/shard_map/psum | solution.py:169
  268.3 3.7 collective-permute-start.5
  272.0 162.1 %all-reduce.3.cloned.1.call-done = (f32[384,1152]{1,0:T(8,128)}, f32[384,384]{1,0:T(8,128)}) async-done(((f32[384,1152]{1,0:T(8,128)}, f32[384,384]{1,0:T(8,128)}), (f32[384,1152]{1,0:T(8,128)}, f32[384,384]{1,0:T(8,128)})) %all-reduce.3.cloned.1.call-update) | async-done | bytes 2359312 | tf_op jit(solution)/shard_map/psum | solution.py:169
  (101 shorter events, 26.1 us)
Async XLA Ops:
  7.2 39.4 %copy-start = (bf16[384,1152]{1,0:T(8,128)(2,1)S(1)}, bf16[384,1152]{1,0:T(8,128)(2,1)}, u32[]{:S(2)}) copy-start(bf16[384,1152]{1,0:T(8,128)(2,1)} %param.11) | copy-start | bytes 2654212
  7.2 38.7 %copy-start.21 = (f32[384]{0:T(512)S(1)}, f32[384]{0:T(512)}, u32[]{:S(2)}) copy-start(f32[384]{0:T(512)} %param.13) | copy-start | bytes 4612
  7.2 426.9 %all-reduce.3.cloned.1.call-start = ((), (), s32[]{:S(2)}) async-start(), calls=%async_computation | async-start | bytes 4718592 | tf_op jit(solution)/shard_map/psum | solution.py:169
  10.3 9.0 %collective-permute-start = (bf16[2,4,8,8,384]{4,3,2,1,0:T(8,128)(2,1)S(1)}, bf16[2,4,8,8,384]{4,3,2,1,0:T(8,128)(2,1)S(1)}, u32[]{:S(2)}, u32[]{:S(2)}) collective-permute-start(bf16[2,4,8,8,384]{4,3,2,1,0:T(8,128)(2,1)S(1)} %get-tuple-element.131), channel_id=1, source_target_pairs={{32,0},{64,32},{96,64},{128,96},{160,128},{192,160},{224,192},{256... | collective-permute-start | bytes 1179656 | tf_op jit(solution)/shard_map/ppermute | solution.py:18
  19.4 16.9 %collective-permute-start.1 = (bf16[2,8,4,8,384]{4,3,2,1,0:T(8,128)(2,1)S(1)}, bf16[2,8,4,8,384]{4,3,2,1,0:T(8,128)(2,1)S(1)}, u32[]{:S(2)}, u32[]{:S(2)}) collective-permute-start(bf16[2,8,4,8,384]{4,3,2,1,0:T(8,128)(2,1)S(1)} %get-tuple-element.129), channel_id=1, source_target_pairs={{8,0},{16,8},{24,16},{0,24},{9,1},{17,9},{25,17},{1,25},{10,2},{18... | collective-permute-start | bytes 1179656 | tf_op jit(solution)/shard_map/ppermute | solution.py:18
  36.3 13.7 %copy-start.13 = (bf16[384,384]{1,0:T(8,128)(2,1)S(1)}, bf16[384,384]{1,0:T(8,128)(2,1)}, u32[]{:S(2)}) copy-start(bf16[384,384]{1,0:T(8,128)(2,1)} %param.12) | copy-start | bytes 884740
  36.6 8.5 %collective-permute-start.2 = (bf16[2,8,8,4,384]{4,3,2,1,0:T(4,128)(2,1)S(1)}, bf16[2,8,8,4,384]{4,3,2,1,0:T(4,128)(2,1)S(1)}, u32[]{:S(2)}, u32[]{:S(2)}) collective-permute-start(bf16[2,8,8,4,384]{4,3,2,1,0:T(4,128)(2,1)S(1)} %get-tuple-element.127), channel_id=1, source_target_pairs={{1,0},{2,1},{3,2},{4,3},{5,4},{6,5},{7,6},{0,7},{9,8},{10,9},{11,1... | collective-permute-start | bytes 1179656 | tf_op jit(solution)/shard_map/ppermute | solution.py:18
  45.4 5.0 %copy-start.1 = (bf16[1,8,8,8,384]{4,3,2,1,0:T(8,128)(2,1)}, bf16[1,8,8,8,384]{4,3,2,1,0:T(8,128)(2,1)S(1)}, u32[]{:S(2)}) copy-start(bf16[1,8,8,8,384]{4,3,2,1,0:T(8,128)(2,1)S(1)} %get-tuple-element.116) | copy-start | bytes 1179652
  50.4 76.5 %copy-start.8 = (bf16[512,384]{1,0:T(8,128)(2,1)S(1)}, bf16[512,384]{1,0:T(8,128)(2,1)}, u32[]{:S(2)}) copy-start(bf16[512,384]{1,0:T(8,128)(2,1)} %copy-done.7) | copy-start | bytes 1179652
  50.4 79.8 %copy-start.18 = (f32[512]{0:T(512)S(1)}, f32[512]{0:T(512)}, u32[]{:S(2)}) copy-start(f32[512]{0:T(512)} %copy-done.17) | copy-start | bytes 6148
  50.4 79.8 %copy-start.20 = (f32[512]{0:T(512)S(1)}, f32[512]{0:T(512)}, u32[]{:S(2)}) copy-start(f32[512]{0:T(512)} %copy-done.19) | copy-start | bytes 6148
  50.4 79.8 %copy-start.22 = (f32[384]{0:T(512)S(1)}, f32[384]{0:T(512)}, u32[]{:S(2)}) copy-start(f32[384]{0:T(512)} %param.13) | copy-start | bytes 4612
  68.4 11.6 %copy-start.24 = (bf16[2,512,6,32]{1,3,2,0:T(8,128)(2,1)}, bf16[2,512,6,32]{1,3,2,0:T(8,128)(2,1)S(1)}, u32[]{:S(2)}) copy-start(bf16[2,512,6,32]{1,3,2,0:T(8,128)(2,1)S(1)} %fusion.177) | copy-start | bytes 1179652 | tf_op jit(solution)/shard_map/while/body/eval_jaxpr/while
  106.5 11.6 %copy-start.24 = (bf16[2,512,6,32]{1,3,2,0:T(8,128)(2,1)}, bf16[2,512,6,32]{1,3,2,0:T(8,128)(2,1)S(1)}, u32[]{:S(2)}) copy-start(bf16[2,512,6,32]{1,3,2,0:T(8,128)(2,1)S(1)} %fusion.177) | copy-start | bytes 1179652 | tf_op jit(solution)/shard_map/while/body/eval_jaxpr/while
  126.9 5.8 %copy-start.11 = (bf16[2,512,6,32]{1,3,2,0:T(8,128)(2,1)S(1)}, bf16[2,512,6,32]{1,3,2,0:T(8,128)(2,1)}, u32[]{:S(2)}) copy-start(bf16[2,512,6,32]{1,3,2,0:T(8,128)(2,1)} %get-tuple-element.88) | copy-start | bytes 1179652
  126.9 5.8 %copy-start.14 = (bf16[384,384]{1,0:T(8,128)(2,1)S(1)}, bf16[384,384]{1,0:T(8,128)(2,1)}, u32[]{:S(2)}) copy-start(bf16[384,384]{1,0:T(8,128)(2,1)} %param.12) | copy-start | bytes 884740
  126.9 6.3 %copy-start.2 = (bf16[1,8,8,8,384]{4,3,2,1,0:T(8,128)(2,1)S(1)}, bf16[1,8,8,8,384]{4,3,2,1,0:T(8,128)(2,1)}, u32[]{:S(2)}) copy-start(bf16[1,8,8,8,384]{4,3,2,1,0:T(8,128)(2,1)} %copy-done.1) | copy-start | bytes 1179652
  130.2 15.0 %copy-start.4 = (bf16[1,8,8,8,384]{4,3,2,1,0:T(8,128)(2,1)S(1)}, bf16[1,8,8,8,384]{4,3,2,1,0:T(8,128)(2,1)}, u32[]{:S(2)}) copy-start(bf16[1,8,8,8,384]{4,3,2,1,0:T(8,128)(2,1)} %copy-done.3) | copy-start | bytes 1179652
  133.6 16.3 %collective-permute-start.3 = (bf16[2,4,8,8,384]{4,3,2,1,0:T(8,128)(2,1)S(1)}, bf16[2,4,8,8,384]{4,3,2,1,0:T(8,128)(2,1)S(1)}, u32[]{:S(2)}, u32[]{:S(2)}) collective-permute-start(bf16[2,4,8,8,384]{4,3,2,1,0:T(8,128)(2,1)S(1)} %fusion.112), channel_id=1, source_target_pairs={{480,0},{0,32},{32,64},{64,96},{96,128},{128,160},{160,192},{192,2... | collective-permute-start | bytes 1179656 | tf_op jit(solution)/shard_map/ppermute | solution.py:18
  146.4 292.8 %copy-start.5 = (bf16[8,8,8,384]{3,2,1,0:T(8,128)(2,1)S(1)}, bf16[8,8,8,384]{3,2,1,0:T(8,128)(2,1)}, u32[]{:S(2)}) copy-start(bf16[8,8,8,384]{3,2,1,0:T(8,128)(2,1)} %param.10) | copy-start | bytes 1179652
  146.4 292.8 %copy-start.6 = (bf16[8,8,8,384]{3,2,1,0:T(8,128)(2,1)S(1)}, bf16[8,8,8,384]{3,2,1,0:T(8,128)(2,1)}, u32[]{:S(2)}) copy-start(bf16[8,8,8,384]{3,2,1,0:T(8,128)(2,1)} %param.8) | copy-start | bytes 1179652
  146.4 292.8 %copy-start.16 = (pred[8,8,8]{2,1,0:T(8,128)(4,1)S(1)}, pred[8,8,8]{2,1,0:T(8,128)(4,1)}, u32[]{:S(2)}) copy-start(pred[8,8,8]{2,1,0:T(8,128)(4,1)} %copy-done.15) | copy-start | bytes 1540
  150.1 117.9 %collective-permute-start.4 = (bf16[2,8,4,8,384]{4,3,2,1,0:T(8,128)(2,1)S(1)}, bf16[2,8,4,8,384]{4,3,2,1,0:T(8,128)(2,1)S(1)}, u32[]{:S(2)}, u32[]{:S(2)}) collective-permute-start(bf16[2,8,4,8,384]{4,3,2,1,0:T(8,128)(2,1)S(1)} %get-tuple-element.124), channel_id=1, source_target_pairs={{24,0},{0,8},{8,16},{16,24},{25,1},{1,9},{9,17},{17,25},{26,2},{2,... | collective-permute-start | bytes 1179656 | tf_op jit(solution)/shard_map/ppermute | solution.py:18
  268.3 170.6 %collective-permute-start.5 = (bf16[2,8,8,4,384]{4,3,2,1,0:T(4,128)(2,1)S(1)}, bf16[2,8,8,4,384]{4,3,2,1,0:T(4,128)(2,1)S(1)}, u32[]{:S(2)}, u32[]{:S(2)}) collective-permute-start(bf16[2,8,8,4,384]{4,3,2,1,0:T(4,128)(2,1)S(1)} %fusion.111), channel_id=1, source_target_pairs={{7,0},{0,1},{1,2},{2,3},{3,4},{4,5},{5,6},{6,7},{15,8},{8,9},{9,10... | collective-permute-start | bytes 1179656 | tf_op jit(solution)/shard_map/ppermute | solution.py:18
  (12 other events, 24.5 us)
Sparse Core Ops, SparseCore 0:
  146.5 287.5 all-reduce.2
where the time goes:
time: 448 us; the launch traced here: 447 us
  waiting for transfers between devices  185 us (41%)
  blocking collectives  113 us (25%)
  matrix products  83.3 us (19%)
  starting transfers between devices  34.2 us (8%)
  between operations  14.5 us (3%)
  other arithmetic  13 us (3%)
    psum x1, waiting for transfers between devices, local(): summed = lax.psum((totals[0], totals[1], totals[2]), ('gx', 'gy', 'gz'))  162 us
    psum x1, blocking collectives, local(): summed = lax.psum((totals[0], totals[1], totals[2]), ('gx', 'gy', 'gz'))  113 us
    ppermute x6, starting transfers between devices, shifted_2(): return lax.ppermute(block, axis, route)  34.1 us
    dot_general x2, matrix products, group_pass(): jnp.einsum('hqk,khd->qhd', d_scores, key_rows, preferred_element_type=jnp...  23.2 us
    ppermute x6, waiting for transfers between devices, shifted_2(): return lax.ppermute(block, axis, route)  23.1 us
    dot_general x2, matrix products, group_pass(): jnp.einsum('hqk,qhd->khd', d_scores, queries, preferred_element_type=jnp....  18.5 us
    sub x2, matrix products, group_pass(): exp_terms = jnp.exp(scores - top_score)  9.57 us
    dot_general x2, matrix products, group_pass(): jnp.einsum('hqk,qhd->khd', probs_low, d_mixed, preferred_element_type=jnp...  9.15 us
  transfers between devices with their start and end apart: 7, of which 5 were waited for; matrix products, arithmetic and copies ran while one was open for 2% of the time, Pallas kernels for 0%

commit v1 on v0

v1 whole, which is shorter than its diff:
```python
import jax
import jax.numpy as jnp
import numpy as np
from jax import lax
from jax.experimental import pallas as pl
from jax.experimental.pallas import tpu as pltpu
from jax.sharding import Mesh, PartitionSpec as P

D = 384
HEADS = 12
HDIM = 32
WIN = 8
HALF = WIN // 2
ROWS = WIN**3
PIECE = HALF**3
EPSILON = 1e-05
BF = jnp.bfloat16
F32 = jnp.float32
LANES = 128
PER = LANES // HDIM
CHUNK = 256
SCALE = HDIM ** (-0.5)
LOG2E = 1.4426950408889634
GRAD_ROWS = 5120


def dot(left, right):
    return jnp.dot(left, right, preferred_element_type=F32)


def dot_t(left, right):
    return lax.dot_general(left, right, (((1,), (1,)), ((), ())), preferred_element_type=F32)


def window_kernel(
    tok, cot, w_qkv, w_proj, gain, branch, d_rows, grads,
    qkv, d_mixed, keys_t, values_t, mixed_t, d_queries_t, d_qkv, unit, inv_std, normed,
):
    step = 128
    for start in range(0, ROWS, step):
        part = pl.ds(start, step)
        rows = tok[part, :].astype(F32)
        centred = rows - jnp.mean(rows, axis=-1, keepdims=True)
        inverse = lax.rsqrt(jnp.mean(centred * centred, axis=-1, keepdims=True) + EPSILON)
        unit_rows = centred * inverse
        unit[part, :] = unit_rows
        inv_std[part, :] = jnp.broadcast_to(inverse, (step, LANES))
        normed[part, :] = (unit_rows * gain[...]).astype(BF)
    qkv[...] = dot(normed[...], w_qkv[...]).astype(BF)
    d_mixed[...] = dot_t(cot[...], w_proj[...]).astype(BF)
    keys_t[...] = qkv[:, D : 2 * D].T
    values_t[...] = qkv[:, 2 * D :].T
    lane = lax.broadcasted_iota(jnp.int32, (1, LANES), 1)

    def head_block(index, carry):
        offset = pl.multiple_of(index * LANES, LANES)
        q_block = qkv[:, pl.ds(offset, LANES)]
        k_block = qkv[:, pl.ds(offset + D, LANES)]
        v_block = qkv[:, pl.ds(offset + 2 * D, LANES)]
        m_block = d_mixed[:, pl.ds(offset, LANES)]
        d_keys = jnp.zeros((ROWS, LANES), F32)
        d_values = jnp.zeros((ROWS, LANES), F32)
        for head in range(PER):
            mine = (lane // HDIM) == head
            q_head = jnp.where(mine, q_block, jnp.zeros_like(q_block))
            m_head = jnp.where(mine, m_block, jnp.zeros_like(m_block))
            rows = pl.ds(offset + head * HDIM, HDIM)
            k_head_t = keys_t[rows, :]
            v_head_t = values_t[rows, :]
            for start in range(0, ROWS, CHUNK):
                q_part = q_head[start : start + CHUNK]
                m_part = m_head[start : start + CHUNK]
                scores = dot_t(k_block, q_part)
                top = jnp.max(scores, axis=0, keepdims=True)
                terms = jnp.exp2(scores * (SCALE * LOG2E) - top * (SCALE * LOG2E))
                inverse = 1.0 / jnp.sum(terms, axis=0, keepdims=True)
                probs_low = (terms * inverse).astype(BF)
                d_probs = dot_t(v_block, m_part)
                mixed_t[rows, pl.ds(start, CHUNK)] = dot(v_head_t, probs_low).astype(BF)
                d_values = d_values + dot(probs_low, m_part)
                scaled = inverse * SCALE
                shift = jnp.sum(terms * d_probs, axis=0, keepdims=True) * (inverse * scaled)
                d_scores = (terms * (d_probs * scaled - shift)).astype(BF)
                d_queries_t[rows, pl.ds(start, CHUNK)] = dot(k_head_t, d_scores).astype(BF)
                d_keys = d_keys + dot(d_scores, q_part)
        d_qkv[:, pl.ds(offset + D, LANES)] = d_keys.astype(BF)
        d_qkv[:, pl.ds(offset + 2 * D, LANES)] = d_values.astype(BF)
        return carry

    lax.fori_loop(0, D // LANES, head_block, 0)
    d_qkv[:, pl.ds(0, D)] = d_queries_t[...].T
    branch[...] = dot(mixed_t[...].T, w_proj[...]).astype(BF)
    normed_t = normed[...].T
    for block in range(9):
        term = dot(normed_t, d_qkv[:, block * LANES : (block + 1) * LANES])
        grads[pl.ds(block * D, D), :] = term.astype(BF)
    for block in range(3):
        term = dot(mixed_t[...], cot[:, block * LANES : (block + 1) * LANES])
        grads[pl.ds((9 + block) * D, D), :] = term.astype(BF)
    total = jnp.zeros((1, D), F32)
    for start in range(0, ROWS, step):
        part = pl.ds(start, step)
        d_normed = dot_t(d_qkv[part, :], w_qkv[...])
        unit_rows = unit[part, :]
        total = total + jnp.sum(d_normed * unit_rows, axis=0, keepdims=True)
        scaled = d_normed * gain[...]
        mean_1 = jnp.mean(scaled, axis=-1, keepdims=True)
        mean_2 = jnp.mean(scaled * unit_rows, axis=-1, keepdims=True)
        d_rows[part, :] = (inv_std[part, 0:1] * (scaled - mean_1 - unit_rows * mean_2)).astype(BF)
    tail = jnp.concatenate(
        [total[:, block * LANES : (block + 1) * LANES] for block in range(3)]
        + [jnp.zeros((13, LANES), F32)],
        axis=0,
    )
    grads[pl.ds(12 * D, 16), :] = tail.astype(BF)
    rest = GRAD_ROWS - 12 * D - 16
    grads[pl.ds(12 * D + 16, rest), :] = jnp.zeros((rest, LANES), BF)


def window_pass(tok, cot, w_qkv, w_proj, norm_gain):
    def buffer(shape, kind):
        return pltpu.VMEM(shape, kind)

    return pl.pallas_call(
        window_kernel,
        out_shape=(
            jax.ShapeDtypeStruct((ROWS, D), BF),
            jax.ShapeDtypeStruct((ROWS, D), BF),
            jax.ShapeDtypeStruct((GRAD_ROWS, LANES), BF),
        ),
        scratch_shapes=[
            buffer((ROWS, 3 * D), BF),
            buffer((ROWS, D), BF),
            buffer((D, ROWS), BF),
            buffer((D, ROWS), BF),
            buffer((D, ROWS), BF),
            buffer((D, ROWS), BF),
            buffer((ROWS, 3 * D), BF),
            buffer((ROWS, D), F32),
            buffer((ROWS, LANES), F32),
            buffer((ROWS, D), BF),
        ],
        compiler_params=pltpu.CompilerParams(vmem_limit_bytes=40 * 1024 * 1024),
        cost_estimate=pl.CostEstimate(
            flops=16_000_000_000, bytes_accessed=5_000_000, transcendentals=3_200_000
        ),
    )(tok, cot, w_qkv, w_proj, norm_gain.reshape(1, D))


LATTICE = ("z", "core", "y_hi", "y_lo", "x")
FIRST = ("z", "core")
SECOND = ("y_hi",)
THIRD = ("y_lo", "x")
SIZES = {"z": 8, "core": 2, "y_hi": 4, "y_lo": 2, "x": 4}


def extent(axes):
    return int(np.prod([SIZES[axis] for axis in axes]))


def scatter_sum(rows, axes):
    count = extent(axes)
    parts = rows.reshape(count, rows.shape[0] // count, LANES)
    arrived = lax.all_to_all(parts, axes, 0, 0)
    return jnp.sum(arrived.astype(F32), axis=0).astype(BF)


def everywhere(rows, axes):
    count = extent(axes)
    return lax.all_to_all(jnp.broadcast_to(rows[None], (count,) + rows.shape), axes, 0, 0)


def sum_over_devices(rows):
    rows = scatter_sum(rows, ("core",))
    rows = scatter_sum(rows, ("x",))
    rows = scatter_sum(rows, ("y_hi", "y_lo"))
    rows = jnp.sum(everywhere(rows, ("z",)).astype(F32), axis=0).astype(BF)
    for axes in (("y_hi", "y_lo"), ("x",), ("core",)):
        rows = everywhere(rows, axes).reshape(-1, LANES)
    return rows


def device_at(first, second, third):
    return ((first % 16) * 4 + second % 4) * 8 + third % 8


def route(kind, back):
    pairs = []
    for first in range(16):
        for second in range(4):
            for third in range(8):
                sign = 1 if first % 2 else -1
                move = {
                    "first": (first - 1, second, third),
                    "second": (first, second + sign, third),
                    "third": (first, second, third + sign),
                }[kind]
                pair = (device_at(first, second, third), device_at(*move))
                pairs.append(pair[::-1] if back else pair)
    return pairs


def send(block, kind, back=False):
    return lax.ppermute(block, LATTICE, route(kind, back))


def octants(block):
    grid = block.reshape(2, HALF, 2, HALF, 2, HALF, D)
    return grid.transpose(0, 2, 4, 1, 3, 5, 6).reshape(2, 2, 2, PIECE, D)


def whole(pieces):
    grid = pieces.reshape(2, 2, 2, HALF, HALF, HALF, D)
    return grid.transpose(0, 3, 1, 4, 2, 5, 6).reshape(WIN, WIN, WIN, D)


def slots(pieces, odd):
    even_order = jnp.stack([pieces[0], pieces[1, ::-1, ::-1]])
    odd_order = jnp.stack([pieces[0, ::-1, ::-1], pieces[1]])
    return jnp.where(odd, odd_order, even_order)


def gather_window(tok, cot):
    both = jnp.stack([tok, cot], axis=3)
    both = jnp.stack([both[1], send(both[0], "first")])
    both = jnp.stack([both[:, 0], send(both[:, 1], "second")])
    both = jnp.stack([both[:, :, 0], send(both[:, :, 1], "third")])
    windows = both.transpose(3, 0, 1, 2, 4, 5).reshape(2, ROWS, D)
    return windows[0], windows[1]


def return_window(branch, d_rows):
    both = jnp.stack([branch, d_rows]).reshape(2, 2, 2, 2, PIECE, D).transpose(1, 2, 3, 0, 4, 5)
    both = jnp.stack([both[0], send(both[1], "third", True)], axis=2)
    both = jnp.stack([both[0], send(both[1], "second", True)], axis=1)
    both = jnp.stack([send(both[1], "first", True), both[0]])
    return both[:, :, :, 0], both[:, :, :, 1]


def local(tokens, frozen, cotangent, w_qkv, w_proj, norm_gain):
    odd = lax.axis_index("core") == 1
    keep = frozen[..., None] == 1
    kept = jnp.where(keep, tokens, jnp.zeros_like(tokens))
    tok, cot = gather_window(slots(octants(kept), odd), slots(octants(cotangent), odd))
    branch, d_rows, grads = window_pass(tok, cot, w_qkv, w_proj, norm_gain)
    total = sum_over_devices(grads)
    branch, d_rows = return_window(branch, d_rows)
    branch = whole(slots(branch, odd))
    d_rows = whole(slots(d_rows, odd))
    block_out = (kept.astype(F32) + branch.astype(F32)).astype(BF)
    tokens_grad = jnp.where(keep, cotangent.astype(F32) + d_rows.astype(F32), 0.0).astype(BF)
    grad_scale = (ROWS * 512) ** (-0.5)
    blocks = total[: 12 * D].reshape(12, D, LANES).astype(F32) * grad_scale
    qkv_grad = blocks[:9].transpose(1, 0, 2).reshape(D, 3 * D)
    proj_grad = blocks[9:].transpose(1, 0, 2).reshape(D, D)
    gain_grad = total[12 * D : 12 * D + 3].reshape(D).astype(F32) * grad_scale
    return block_out, tokens_grad, qkv_grad, proj_grad, gain_grad


def solution(mesh):
    inner = Mesh(mesh.devices.reshape([SIZES[axis] for axis in LATTICE]), LATTICE)
    lattice = P(FIRST, SECOND, THIRD)
    wide = P(FIRST, SECOND, THIRD, None)
    return jax.shard_map(
        local,
        mesh=inner,
        in_specs=(wide, lattice, wide, P(), P(), P()),
        out_specs=(wide, wide, P(), P(), P()),
        check_vma=False,
    )
```

time: 448 us -> 166 us (0.37)
  waiting for transfers between devices: 185 us -> 53.2 us
  blocking collectives: 113 us -> 20.8 us
  matrix products: 83.3 us -> 0 us
  Pallas kernels: 0 us -> 21.2 us
  between operations: 14.5 us -> 1.13 us
  starting transfers between devices: 34.2 us -> 45.2 us
  local copies, waits for them, and re-layouts: 3.69 us -> 14.4 us
    psum x1 -> x0, waiting for transfers between devices: 162 us -> none  [local(): summed = lax.psum((totals[0], totals[1], totals[2]), ('gx', 'gy', 'gz'))]
    psum x1 -> x0, blocking collectives: 113 us -> none  [local(): summed = lax.psum((totals[0], totals[1], totals[2]), ('gx', 'gy', 'gz'))]
    dot_general x16 -> x0, matrix products: 73.8 us -> none  [the longest x2 23.2 us: group_pass(): jnp.einsum('hqk,khd->qhd', d_scores, key_rows, preferred_element_type=jnp...]
    all_to_all x0 -> x5, waiting for transfers between devices: none -> 31 us  [the longest x3 18.8 us: everywhere(): lax.all_to_all(jnp.broadcast_to(rows[None], (count,) + rows.shape), axes,...]
    all_to_all x0 -> x5, starting transfers between devices: none -> 22.7 us  [the longest x2 11.8 us: scatter_sum(): arrived = lax.all_to_all(parts, axes, 0, 0)]
    pallas_call x0 -> x1, Pallas kernels: none -> 21.2 us  [window_pass(): pl.pallas_call(window_kernel, out_shape=(jax.ShapeDtypeStruct((ROWS, D),...]
    all_to_all x0 -> x2, blocking collectives: none -> 20.8 us  [the longest x1 10.8 us: everywhere(): lax.all_to_all(jnp.broadcast_to(rows[None], (count,) + rows.shape), axes,...]
    ppermute x6, starting transfers between devices: 34.1 us -> 22.5 us  [send(): return lax.ppermute(block, LATTICE, route(kind, back))]
  transfers between devices with their start and end apart: 7 -> 11, of which waited for: 5 -> 8; matrix products, arithmetic and copies ran while one was open for 2% -> 5% of each run, Pallas kernels for 0% -> 0%
where the time goes in v1:
time: 166 us; the launch traced here: 165 us
  waiting for transfers between devices  53.2 us (32%)
  starting transfers between devices  45.2 us (27%)
  Pallas kernels  21.2 us (13%)
  blocking collectives  20.8 us (13%)
  local copies, waits for them, and re-layouts  14.4 us (9%)
  other arithmetic  8.83 us (5%)
    ppermute x6, starting transfers between devices, send(): return lax.ppermute(block, LATTICE, route(kind, back))  22.5 us
    ppermute x6, waiting for transfers between devices, send(): return lax.ppermute(block, LATTICE, route(kind, back))  22.3 us
    pallas_call x1, Pallas kernels, window_pass(): pl.pallas_call(window_kernel, out_shape=(jax.ShapeDtypeStruct((ROWS, D),...  21.2 us
    all_to_all x3, waiting for transfers between devices, everywhere(): lax.all_to_all(jnp.broadcast_to(rows[None], (count,) + rows.shape), axes,...  18.8 us
    all_to_all x2, waiting for transfers between devices, scatter_sum(): arrived = lax.all_to_all(parts, axes, 0, 0)  12.2 us
    all_to_all x2, starting transfers between devices, scatter_sum(): arrived = lax.all_to_all(parts, axes, 0, 0)  11.8 us
    all_to_all x3, starting transfers between devices, everywhere(): lax.all_to_all(jnp.broadcast_to(rows[None], (count,) + rows.shape), axes,...  10.9 us
    all_to_all x1, blocking collectives, everywhere(): lax.all_to_all(jnp.broadcast_to(rows[None], (count,) + rows.shape), axes,...  10.8 us
  transfers between devices with their start and end apart: 11, of which 8 were waited for; matrix products, arithmetic and copies ran while one was open for 5% of the time, Pallas kernels for 0%

profile of v1, /device:TPU:1, one launch (start us, length us, event | category | flops | bytes accessed | tf_op | source)
XLA Modules:
  0.0 164.9 jit_solution(14669570316511025739)
XLA Ops:
  4.7 6.9 %collective-permute-start = (bf16[2,2,2,64,384]{4,3,2,1,0:T(8,128)(2,1)S(1)}, bf16[2,2,2,64,384]{4,3,2,1,0:T(8,128)(2,1)S(1)}, u32[]{:S(2)}, u32[]{:S(2)}) collective-permute-start(bf16[2,2,2,64,384]{4,3,2,1,0:T(8,128)(2,1)S(1)} %get-tuple-element.34), channel_id=1, source_target_pairs={{0,480},{1,481},{2,482},{3,483},{4,484},{5,485},{6,486},{7,487},{8... | collective-permute-start | bytes 1179656 | tf_op jit(solution)/shard_map/ppermute | solution.py:204
  11.5 2.1 %collective-permute-done = bf16[2,2,2,64,384]{4,3,2,1,0:T(8,128)(2,1)S(1)} collective-permute-done((bf16[2,2,2,64,384]{4,3,2,1,0:T(8,128)(2,1)S(1)}, bf16[2,2,2,64,384]{4,3,2,1,0:T(8,128)(2,1)S(1)}, u32[]{:S(2)}, u32[]{:S(2)}) %collective-permute-start) | collective-permute-done | bytes 393248 | tf_op jit(solution)/shard_map/ppermute | solution.py:204
  13.7 4.2 %collective-permute-start.1 = (bf16[2,2,2,64,384]{4,3,0,2,1:T(8,128)(2,1)S(1)}, bf16[2,2,2,64,384]{4,3,0,2,1:T(8,128)(2,1)S(1)}, u32[]{:S(2)}, u32[]{:S(2)}) collective-permute-start(bf16[2,2,2,64,384]{4,3,0,2,1:T(8,128)(2,1)S(1)} %get-tuple-element.32), channel_id=1, source_target_pairs={{0,24},{1,25},{2,26},{3,27},{4,28},{5,29},{6,30},{7,31},{8,0},{9,1... | collective-permute-start | bytes 1179656 | tf_op jit(solution)/shard_map/ppermute | solution.py:204
  17.9 8.9 %collective-permute-done.1 = bf16[2,2,2,64,384]{4,3,0,2,1:T(8,128)(2,1)S(1)} collective-permute-done((bf16[2,2,2,64,384]{4,3,0,2,1:T(8,128)(2,1)S(1)}, bf16[2,2,2,64,384]{4,3,0,2,1:T(8,128)(2,1)S(1)}, u32[]{:S(2)}, u32[]{:S(2)}) %collective-permute-start.1) | collective-permute-done | bytes 393248 | tf_op jit(solution)/shard_map/ppermute | solution.py:204
  27.0 3.3 %collective-permute-start.2 = (bf16[2,2,2,64,384]{4,3,1,0,2:T(8,128)(2,1)S(1)}, bf16[2,2,2,64,384]{4,3,1,0,2:T(8,128)(2,1)S(1)}, u32[]{:S(2)}, u32[]{:S(2)}) collective-permute-start(bf16[2,2,2,64,384]{4,3,1,0,2:T(8,128)(2,1)S(1)} %get-tuple-element.30), channel_id=1, source_target_pairs={{0,7},{1,0},{2,1},{3,2},{4,3},{5,4},{6,5},{7,6},{8,15},{9,8},{10,9... | collective-permute-start | bytes 1179656 | tf_op jit(solution)/shard_map/ppermute | solution.py:204
  30.2 11.3 %collective-permute-done.2 = bf16[2,2,2,64,384]{4,3,1,0,2:T(8,128)(2,1)S(1)} collective-permute-done((bf16[2,2,2,64,384]{4,3,1,0,2:T(8,128)(2,1)S(1)}, bf16[2,2,2,64,384]{4,3,1,0,2:T(8,128)(2,1)S(1)}, u32[]{:S(2)}, u32[]{:S(2)}) %collective-permute-start.2) | collective-permute-done | bytes 393248 | tf_op jit(solution)/shard_map/ppermute | solution.py:204
  41.7 21.2 %shard_map.101 = (bf16[512,384]{1,0:T(8,128)(2,1)S(1)}, bf16[512,384]{1,0:T(8,128)(2,1)S(1)}, bf16[5120,128]{1,0:T(8,128)(2,1)S(1)}) custom-call(bf16[512,384]{1,0:T(8,128)(2,1)S(1)} %bitcast.106, bf16[512,384]{1,0:T(8,128)(2,1)S(1)} %bitcast.105, bf16[384,1152]{1,0:T(8,128)(2,1)S(1)} %copy-done, bf16[384,384]{1,0:T(8,128)(2,1)S(1)} %copy-done.1, ...), custom_call_target="tpu_custom_call" | custom-call | flops 16000000000 | bytes 5000000 | tf_op jit(solution)/shard_map/pallas_call | solution.py:124
  63.2 1.9 %collective-permute-start.3 = (bf16[2,2,2,64,384]{4,3,1,0,2:T(8,128)(2,1)S(1)}, bf16[2,2,2,64,384]{4,3,1,0,2:T(8,128)(2,1)S(1)}, u32[]{:S(2)}, u32[]{:S(2)}) collective-permute-start(bf16[2,2,2,64,384]{4,3,1,0,2:T(8,128)(2,1)S(1)} %get-tuple-element.25), channel_id=1, source_target_pairs={{7,0},{0,1},{1,2},{2,3},{3,4},{4,5},{5,6},{6,7},{15,8},{8,9},{9,10... | collective-permute-start | bytes 1179656 | tf_op jit(solution)/shard_map/ppermute | solution.py:204
  65.1 10.0 %all_to_all.35 = bf16[2,2560,128]{2,1,0:T(8,128)(2,1)S(1)} all-to-all(bf16[2,2560,128]{2,1,0:T(8,128)(2,1)S(1)} %bitcast.104), channel_id=1, replica_groups=mesh['z'=8,'core'=2,'y_hi'=4,'y_lo'=2,'x'=4] {'core'}, dimensions={0} | all-to-all | bytes 2621440 | tf_op jit(solution)/shard_map/all_to_all | solution.py:164
  76.4 5.8 %all-to-all-start.1 = ((bf16[4,640,128]{2,1,0:T(8,128)(2,1)}), bf16[4,640,128]{2,1,0:T(8,128)(2,1)S(1)}, u32[]{:S(2)}, u32[]{:S(2)}) async-start(bf16[4,640,128]{2,1,0:T(8,128)(2,1)} %bitcast.38), calls=%async_computation.1 | async-start | bytes 1310720 | tf_op jit(solution)/shard_map/all_to_all | solution.py:164
  82.3 6.2 %collective-permute-start.4 = (bf16[2,2,2,64,384]{4,3,0,2,1:T(8,128)(2,1)S(1)}, bf16[2,2,2,64,384]{4,3,0,2,1:T(8,128)(2,1)S(1)}, u32[]{:S(2)}, u32[]{:S(2)}) collective-permute-start(bf16[2,2,2,64,384]{4,3,0,2,1:T(8,128)(2,1)S(1)} %get-tuple-element.23), channel_id=1, source_target_pairs={{24,0},{25,1},{26,2},{27,3},{28,4},{29,5},{30,6},{31,7},{0,8},{1,9... | collective-permute-start | bytes 1179656 | tf_op jit(solution)/shard_map/ppermute | solution.py:204
  88.5 4.0 %all-to-all-done.1 = bf16[4,640,128]{2,1,0:T(8,128)(2,1)S(1)} async-done(((bf16[4,640,128]{2,1,0:T(8,128)(2,1)}), bf16[4,640,128]{2,1,0:T(8,128)(2,1)S(1)}, u32[]{:S(2)}, u32[]{:S(2)}) %all-to-all-start.1) | async-done | bytes 655392 | tf_op jit(solution)/shard_map/all_to_all | solution.py:164
  93.3 6.1 %all-to-all-start.2 = ((bf16[8,80,128]{2,1,0:T(8,128)(2,1)}), bf16[8,80,128]{2,1,0:T(8,128)(2,1)S(1)}, u32[]{:S(2)}, u32[]{:S(2)}) async-start(bf16[8,80,128]{2,1,0:T(8,128)(2,1)} %bitcast.39), calls=%async_computation.2 | async-start | bytes 327680 | tf_op jit(solution)/shard_map/all_to_all | solution.py:164
  99.4 8.2 %all-to-all-done.2 = bf16[8,80,128]{2,1,0:T(8,128)(2,1)S(1)} async-done(((bf16[8,80,128]{2,1,0:T(8,128)(2,1)}), bf16[8,80,128]{2,1,0:T(8,128)(2,1)S(1)}, u32[]{:S(2)}, u32[]{:S(2)}) %all-to-all-start.2) | async-done | bytes 163872 | tf_op jit(solution)/shard_map/all_to_all | solution.py:164
  108.4 3.4 %all-to-all-start.3 = ((bf16[8,80,128]{2,1,0:T(8,128)(2,1)}), bf16[8,80,128]{2,1,0:T(8,128)(2,1)S(1)}, u32[]{:S(2)}, u32[]{:S(2)}) async-start(bf16[8,80,128]{2,1,0:T(8,128)(2,1)} %broadcast_in_dim.51), calls=%async_computation.3 | async-start | bytes 327680 | tf_op jit(solution)/shard_map/all_to_all | solution.py:170
  112.1 7.9 %all-to-all-done.3 = bf16[8,80,128]{2,1,0:T(8,128)(2,1)S(1)} async-done(((bf16[8,80,128]{2,1,0:T(8,128)(2,1)}), bf16[8,80,128]{2,1,0:T(8,128)(2,1)S(1)}, u32[]{:S(2)}, u32[]{:S(2)}) %all-to-all-start.3) | async-done | bytes 163872 | tf_op jit(solution)/shard_map/all_to_all | solution.py:170
  120.7 4.0 %all-to-all-start.4 = ((bf16[8,80,128]{2,1,0:T(8,128)(2,1)}), bf16[8,80,128]{2,1,0:T(8,128)(2,1)}, u32[]{:S(2)}, u32[]{:S(2)}) async-start(bf16[8,80,128]{2,1,0:T(8,128)(2,1)} %broadcast_in_dim.52), calls=%async_computation.4 | async-start | bytes 327680 | tf_op jit(solution)/shard_map/all_to_all | solution.py:170
  127.8 5.1 %all-to-all-done.4 = bf16[8,80,128]{2,1,0:T(8,128)(2,1)} async-done(((bf16[8,80,128]{2,1,0:T(8,128)(2,1)}), bf16[8,80,128]{2,1,0:T(8,128)(2,1)}, u32[]{:S(2)}, u32[]{:S(2)}) %all-to-all-start.4) | async-done | bytes 163872 | tf_op jit(solution)/shard_map/all_to_all | solution.py:170
  133.0 1.9 %broadcast_in_dim.54 = bf16[4,640,128]{2,1,0:T(8,128)(2,1)} broadcast(bf16[640,128]{1,0:T(8,128)(2,1)} %bitcast.40), dimensions={1,2} | broadcast | bytes 819200 | tf_op jit(solution)/shard_map/broadcast_in_dim | solution.py:170
  134.8 3.5 %all-to-all-start.5 = ((bf16[4,640,128]{2,1,0:T(8,128)(2,1)}), bf16[4,640,128]{2,1,0:T(8,128)(2,1)S(1)}, u32[]{:S(2)}, u32[]{:S(2)}) async-start(bf16[4,640,128]{2,1,0:T(8,128)(2,1)} %broadcast_in_dim.54), calls=%async_computation.5 | async-start | bytes 1310720 | tf_op jit(solution)/shard_map/all_to_all | solution.py:170
  140.2 5.8 %all-to-all-done.5 = bf16[4,640,128]{2,1,0:T(8,128)(2,1)S(1)} async-done(((bf16[4,640,128]{2,1,0:T(8,128)(2,1)}), bf16[4,640,128]{2,1,0:T(8,128)(2,1)S(1)}, u32[]{:S(2)}, u32[]{:S(2)}) %all-to-all-start.5) | async-done | bytes 655392 | tf_op jit(solution)/shard_map/all_to_all | solution.py:170
  146.0 10.8 %all_to_all.36 = bf16[2,2560,128]{2,1,0:T(8,128)(2,1)S(1)} all-to-all(bf16[2,2560,128]{2,1,0:T(8,128)(2,1)S(1)} %broadcast_in_dim.56), channel_id=1, replica_groups=mesh['z'=8,'core'=2,'y_hi'=4,'y_lo'=2,'x'=4] {'core'}, dimensions={0} | all-to-all | bytes 2621440 | tf_op jit(solution)/shard_map/all_to_all | solution.py:170
  159.5 2.2 %copy.78 = f32[384,9,128]{0,2,1:T(8,128)S(1)} copy(f32[384,9,128]{2,0,1:T(8,128)} %bitcast.110) | data formatting | bytes 3538944 | tf_op jit(solution)/shard_map/transpose | solution.py:254
  161.7 1.9 %copy.80 = f32[384,1152]{1,0:T(8,128)} copy(f32[384,1152]{0,1:T(8,128)S(1)} %bitcast.111) | data formatting | bytes 3538944
  (83 shorter events, 17.3 us)
Async XLA Ops:
  2.6 1.0 copy-start.3
  4.6 25.6 %copy-start.5 = (f32[384]{0:T(512)S(1)}, f32[384]{0:T(512)}, u32[]{:S(2)}) copy-start(f32[384]{0:T(512)} %param.11) | copy-start | bytes 4612
  4.7 9.0 %collective-permute-start = (bf16[2,2,2,64,384]{4,3,2,1,0:T(8,128)(2,1)S(1)}, bf16[2,2,2,64,384]{4,3,2,1,0:T(8,128)(2,1)S(1)}, u32[]{:S(2)}, u32[]{:S(2)}) collective-permute-start(bf16[2,2,2,64,384]{4,3,2,1,0:T(8,128)(2,1)S(1)} %get-tuple-element.34), channel_id=1, source_target_pairs={{0,480},{1,481},{2,482},{3,483},{4,484},{5,485},{6,486},{7,487},{8... | collective-permute-start | bytes 1179656 | tf_op jit(solution)/shard_map/ppermute | solution.py:204
  13.7 13.1 %collective-permute-start.1 = (bf16[2,2,2,64,384]{4,3,0,2,1:T(8,128)(2,1)S(1)}, bf16[2,2,2,64,384]{4,3,0,2,1:T(8,128)(2,1)S(1)}, u32[]{:S(2)}, u32[]{:S(2)}) collective-permute-start(bf16[2,2,2,64,384]{4,3,0,2,1:T(8,128)(2,1)S(1)} %get-tuple-element.32), channel_id=1, source_target_pairs={{0,24},{1,25},{2,26},{3,27},{4,28},{5,29},{6,30},{7,31},{8,0},{9,1... | collective-permute-start | bytes 1179656 | tf_op jit(solution)/shard_map/ppermute | solution.py:204
  26.9 14.8 %copy-start = (bf16[384,1152]{1,0:T(8,128)(2,1)S(1)}, bf16[384,1152]{1,0:T(8,128)(2,1)}, u32[]{:S(2)}) copy-start(bf16[384,1152]{1,0:T(8,128)(2,1)} %w_qkv.1) | copy-start | bytes 2654212
  27.0 14.8 %copy-start.1 = (bf16[384,384]{1,0:T(8,128)(2,1)S(1)}, bf16[384,384]{1,0:T(8,128)(2,1)}, u32[]{:S(2)}) copy-start(bf16[384,384]{1,0:T(8,128)(2,1)} %w_proj.1) | copy-start | bytes 884740
  27.0 14.6 %collective-permute-start.2 = (bf16[2,2,2,64,384]{4,3,1,0,2:T(8,128)(2,1)S(1)}, bf16[2,2,2,64,384]{4,3,1,0,2:T(8,128)(2,1)S(1)}, u32[]{:S(2)}, u32[]{:S(2)}) collective-permute-start(bf16[2,2,2,64,384]{4,3,1,0,2:T(8,128)(2,1)S(1)} %get-tuple-element.30), channel_id=1, source_target_pairs={{0,7},{1,0},{2,1},{3,2},{4,3},{5,4},{6,5},{7,6},{8,15},{9,8},{10,9... | collective-permute-start | bytes 1179656 | tf_op jit(solution)/shard_map/ppermute | solution.py:204
  63.2 19.0 %collective-permute-start.3 = (bf16[2,2,2,64,384]{4,3,1,0,2:T(8,128)(2,1)S(1)}, bf16[2,2,2,64,384]{4,3,1,0,2:T(8,128)(2,1)S(1)}, u32[]{:S(2)}, u32[]{:S(2)}) collective-permute-start(bf16[2,2,2,64,384]{4,3,1,0,2:T(8,128)(2,1)S(1)} %get-tuple-element.25), channel_id=1, source_target_pairs={{7,0},{0,1},{1,2},{2,3},{3,4},{4,5},{5,6},{6,7},{15,8},{8,9},{9,10... | collective-permute-start | bytes 1179656 | tf_op jit(solution)/shard_map/ppermute | solution.py:204
  76.4 16.1 %all-to-all-start.1 = ((bf16[4,640,128]{2,1,0:T(8,128)(2,1)}), bf16[4,640,128]{2,1,0:T(8,128)(2,1)S(1)}, u32[]{:S(2)}, u32[]{:S(2)}) async-start(bf16[4,640,128]{2,1,0:T(8,128)(2,1)} %bitcast.38), calls=%async_computation.1 | async-start | bytes 1310720 | tf_op jit(solution)/shard_map/all_to_all | solution.py:164
  82.3 17.0 %collective-permute-start.4 = (bf16[2,2,2,64,384]{4,3,0,2,1:T(8,128)(2,1)S(1)}, bf16[2,2,2,64,384]{4,3,0,2,1:T(8,128)(2,1)S(1)}, u32[]{:S(2)}, u32[]{:S(2)}) collective-permute-start(bf16[2,2,2,64,384]{4,3,0,2,1:T(8,128)(2,1)S(1)} %get-tuple-element.23), channel_id=1, source_target_pairs={{24,0},{25,1},{26,2},{27,3},{28,4},{29,5},{30,6},{31,7},{0,8},{1,9... | collective-permute-start | bytes 1179656 | tf_op jit(solution)/shard_map/ppermute | solution.py:204
  93.3 14.4 %all-to-all-start.2 = ((bf16[8,80,128]{2,1,0:T(8,128)(2,1)}), bf16[8,80,128]{2,1,0:T(8,128)(2,1)S(1)}, u32[]{:S(2)}, u32[]{:S(2)}) async-start(bf16[8,80,128]{2,1,0:T(8,128)(2,1)} %bitcast.39), calls=%async_computation.2 | async-start | bytes 327680 | tf_op jit(solution)/shard_map/all_to_all | solution.py:164
  99.4 25.3 %collective-permute-start.5 = (bf16[2,2,2,64,384]{4,3,2,1,0:T(8,128)(2,1)S(1)}, bf16[2,2,2,64,384]{4,3,2,1,0:T(8,128)(2,1)S(1)}, u32[]{:S(2)}, u32[]{:S(2)}) collective-permute-start(bf16[2,2,2,64,384]{4,3,2,1,0:T(8,128)(2,1)S(1)} %fusion.9), channel_id=1, source_target_pairs={{480,0},{481,1},{482,2},{483,3},{484,4},{485,5},{486,6},{487,7},{4... | collective-permute-start | bytes 1179656 | tf_op jit(solution)/shard_map/ppermute | solution.py:204
  108.4 11.6 %all-to-all-start.3 = ((bf16[8,80,128]{2,1,0:T(8,128)(2,1)}), bf16[8,80,128]{2,1,0:T(8,128)(2,1)S(1)}, u32[]{:S(2)}, u32[]{:S(2)}) async-start(bf16[8,80,128]{2,1,0:T(8,128)(2,1)} %broadcast_in_dim.51), calls=%async_computation.3 | async-start | bytes 327680 | tf_op jit(solution)/shard_map/all_to_all | solution.py:170
  120.7 12.3 %all-to-all-start.4 = ((bf16[8,80,128]{2,1,0:T(8,128)(2,1)}), bf16[8,80,128]{2,1,0:T(8,128)(2,1)}, u32[]{:S(2)}, u32[]{:S(2)}) async-start(bf16[8,80,128]{2,1,0:T(8,128)(2,1)} %broadcast_in_dim.52), calls=%async_computation.4 | async-start | bytes 327680 | tf_op jit(solution)/shard_map/all_to_all | solution.py:170
  133.0 6.3 %copy-start.4 = (bf16[8,8,8,384]{3,2,1,0:T(8,128)(2,1)S(1)}, bf16[8,8,8,384]{3,2,1,0:T(8,128)(2,1)}, u32[]{:S(2)}) copy-start(bf16[8,8,8,384]{3,2,1,0:T(8,128)(2,1)} %param.6) | copy-start | bytes 1179652
  134.8 11.1 %all-to-all-start.5 = ((bf16[4,640,128]{2,1,0:T(8,128)(2,1)}), bf16[4,640,128]{2,1,0:T(8,128)(2,1)S(1)}, u32[]{:S(2)}, u32[]{:S(2)}) async-start(bf16[4,640,128]{2,1,0:T(8,128)(2,1)} %broadcast_in_dim.54), calls=%async_computation.5 | async-start | bytes 1310720 | tf_op jit(solution)/shard_map/all_to_all | solution.py:170
  157.5 2.0 %copy-start.2 = (f32[4608,128]{1,0:T(8,128)}, f32[4608,128]{1,0:T(8,128)S(1)}, u32[]{:S(2)}) copy-start(f32[4608,128]{1,0:T(8,128)S(1)} %convert_multiply_fusion) | copy-start | bytes 7077892
  161.7 1.9 %slice-start = ((f32[4608,128]{1,0:T(8,128)}), f32[1152,128]{1,0:T(8,128)S(1)}, s32[]{:S(2)}) async-start(f32[4608,128]{1,0:T(8,128)} %copy-done.2), calls=%async_computation.7 | async-start | bytes 1179648 | tf_op jit(solution)/shard_map/slice | solution.py:255

commit v2 on v1

v2 whole, which is shorter than its diff:
```python
import jax
import jax.numpy as jnp
import numpy as np
from jax import lax
from jax.experimental import pallas as pl
from jax.experimental.pallas import tpu as pltpu
from jax.sharding import Mesh, PartitionSpec as P

D = 384
HEADS = 12
HDIM = 32
WIN = 8
HALF = WIN // 2
ROWS = WIN**3
PIECE = HALF**3
EPSILON = 1e-05
BF = jnp.bfloat16
F32 = jnp.float32
LANES = 128
PER = LANES // HDIM
CHUNK = 256
SCALE = HDIM ** (-0.5)
LOG2E = 1.4426950408889634
GRAD_ROWS = 5120


def dot(left, right):
    return jnp.dot(left, right, preferred_element_type=F32)


def dot_t(left, right):
    return lax.dot_general(left, right, (((1,), (1,)), ((), ())), preferred_element_type=F32)


def window_kernel(
    own, behind, side_1, side_2, side_3, w_qkv, w_proj, gain, back_0, back_1, back_2, back_3, grads,
    cot, qkv, d_mixed, keys_t, values_t, mixed_t, d_queries_t, d_qkv, unit, inv_std, normed,
):
    step = 2 * PIECE
    gain_row = gain[...]

    def arrived(group, array):
        if group == 0:
            return own[0, array], behind[0, array]
        side = (side_1, side_2, side_3)[group - 1]
        return side[0, array], side[1, array]

    for group in range(4):
        part = pl.ds(group * step, step)
        cot[part, :] = jnp.concatenate(arrived(group, 1), axis=0)
        rows = jnp.concatenate(arrived(group, 0), axis=0).astype(F32)
        centred = rows - jnp.mean(rows, axis=-1, keepdims=True)
        inverse = lax.rsqrt(jnp.mean(centred * centred, axis=-1, keepdims=True) + EPSILON)
        unit_rows = centred * inverse
        unit[part, :] = unit_rows
        inv_std[part, :] = jnp.broadcast_to(inverse, (step, LANES))
        normed[part, :] = (unit_rows * gain_row).astype(BF)
    qkv[...] = dot(normed[...], w_qkv[...]).astype(BF)
    d_mixed[...] = dot_t(cot[...], w_proj[...]).astype(BF)
    keys_t[...] = qkv[:, D : 2 * D].T
    values_t[...] = qkv[:, 2 * D :].T
    lane = lax.broadcasted_iota(jnp.int32, (1, LANES), 1)

    def head_block(index, carry):
        offset = pl.multiple_of(index * LANES, LANES)
        q_block = qkv[:, pl.ds(offset, LANES)]
        k_block = qkv[:, pl.ds(offset + D, LANES)]
        v_block = qkv[:, pl.ds(offset + 2 * D, LANES)]
        m_block = d_mixed[:, pl.ds(offset, LANES)]
        d_keys = jnp.zeros((ROWS, LANES), F32)
        d_values = jnp.zeros((ROWS, LANES), F32)
        for head in range(PER):
            mine = (lane // HDIM) == head
            q_head = jnp.where(mine, q_block, jnp.zeros_like(q_block))
            m_head = jnp.where(mine, m_block, jnp.zeros_like(m_block))
            rows = pl.ds(offset + head * HDIM, HDIM)
            k_head_t = keys_t[rows, :]
            v_head_t = values_t[rows, :]
            for start in range(0, ROWS, CHUNK):
                q_part = q_head[start : start + CHUNK]
                m_part = m_head[start : start + CHUNK]
                scores = dot_t(k_block, q_part)
                top = jnp.max(scores, axis=0, keepdims=True)
                terms = jnp.exp2(scores * (SCALE * LOG2E) - top * (SCALE * LOG2E))
                inverse = 1.0 / jnp.sum(terms, axis=0, keepdims=True)
                probs_low = (terms * inverse).astype(BF)
                d_probs = dot_t(v_block, m_part)
                mixed_t[rows, pl.ds(start, CHUNK)] = dot(v_head_t, probs_low).astype(BF)
                d_values = d_values + dot(probs_low, m_part)
                scaled = inverse * SCALE
                shift = jnp.sum(terms * d_probs, axis=0, keepdims=True) * (inverse * scaled)
                d_scores = (terms * (d_probs * scaled - shift)).astype(BF)
                d_queries_t[rows, pl.ds(start, CHUNK)] = dot(k_head_t, d_scores).astype(BF)
                d_keys = d_keys + dot(d_scores, q_part)
        d_qkv[:, pl.ds(offset + D, LANES)] = d_keys.astype(BF)
        d_qkv[:, pl.ds(offset + 2 * D, LANES)] = d_values.astype(BF)
        return carry

    lax.fori_loop(0, D // LANES, head_block, 0)
    d_qkv[:, pl.ds(0, D)] = d_queries_t[...].T
    branch = dot(mixed_t[...].T, w_proj[...]).astype(BF)
    backs = (back_0, back_1, back_2, back_3)
    for group in range(4):
        for place in range(2):
            start = (2 * group + place) * PIECE
            backs[group][place, 0] = branch[start : start + PIECE]
    normed_t = normed[...].T
    for block in range(9):
        term = dot(normed_t, d_qkv[:, block * LANES : (block + 1) * LANES])
        grads[pl.ds(block * D, D), :] = term.astype(BF)
    for block in range(3):
        term = dot(mixed_t[...], cot[:, block * LANES : (block + 1) * LANES])
        grads[pl.ds((9 + block) * D, D), :] = term.astype(BF)
    total = jnp.zeros((1, D), F32)
    for group in range(4):
        part = pl.ds(group * step, step)
        d_normed = dot_t(d_qkv[part, :], w_qkv[...])
        unit_rows = unit[part, :]
        total = total + jnp.sum(d_normed * unit_rows, axis=0, keepdims=True)
        scaled = d_normed * gain_row
        mean_1 = jnp.mean(scaled, axis=-1, keepdims=True)
        mean_2 = jnp.mean(scaled * unit_rows, axis=-1, keepdims=True)
        d_rows = (inv_std[part, 0:1] * (scaled - mean_1 - unit_rows * mean_2)).astype(BF)
        backs[group][0, 1] = d_rows[:PIECE]
        backs[group][1, 1] = d_rows[PIECE:]
    tail = jnp.concatenate(
        [total[:, block * LANES : (block + 1) * LANES] for block in range(3)]
        + [jnp.zeros((13, LANES), F32)],
        axis=0,
    )
    grads[pl.ds(12 * D, 16), :] = tail.astype(BF)
    rest = GRAD_ROWS - 12 * D - 16
    grads[pl.ds(12 * D + 16, rest), :] = jnp.zeros((rest, LANES), BF)


def order(odd, upper, inverse):
    flip = odd if upper == 0 else 1 - odd
    shape = (WIN * WIN, WIN * WIN)
    row = lax.broadcasted_iota(jnp.int32, shape, 1 if inverse else 0)
    token = lax.broadcasted_iota(jnp.int32, shape, 0 if inverse else 1)
    along_y = ((row >> 5) ^ flip) * HALF + ((row >> 2) & 3)
    along_z = (((row >> 4) & 1) ^ flip) * HALF + (row & 3)
    return token == along_y * WIN + along_z


def ones_where(chosen):
    return jnp.where(chosen, 1.0, 0.0)


def cut_kernel(odd, tokens, frozen, cotangent, own, ahead):
    for upper, target in ((0, ahead), (1, own)):
        matrix = ones_where(order(odd[0], upper, False))
        for plane in range(HALF):
            index = upper * HALF + plane
            part = pl.ds(index * WIN * WIN, WIN * WIN)
            keep = ones_where(frozen[index : index + 1, :] == 1)
            kept = dot((matrix * keep).astype(BF), tokens[part, :]).astype(BF)
            cot = dot(matrix.astype(BF), cotangent[part, :]).astype(BF)
            for group in range(4):
                rows = slice(group * 16, group * 16 + 16)
                target[group, 0, pl.ds(plane * 16, 16), :] = kept[rows]
                target[group, 1, pl.ds(plane * 16, 16), :] = cot[rows]


def join_kernel(odd, tokens, frozen, cotangent, home_0, home_1, home_2, home_3, ahead, block_out, tokens_grad):
    homes = (home_0, home_1, home_2, home_3)
    shape = (WIN * WIN, WIN * WIN)
    diagonal = ones_where(lax.broadcasted_iota(jnp.int32, shape, 0) == lax.broadcasted_iota(jnp.int32, shape, 1))
    for upper in range(2):
        matrix = ones_where(order(odd[0], upper, True)).astype(BF)
        for plane in range(HALF):
            index = upper * HALF + plane
            part = pl.ds(index * WIN * WIN, WIN * WIN)
            keep = (diagonal * ones_where(frozen[index : index + 1, :] == 1)).astype(BF)
            rows = pl.ds(plane * 16, 16)

            def pieces(array):
                if upper:
                    found = [homes[group][0, array, rows, :] for group in range(4)]
                else:
                    found = [ahead[group, array, rows, :] for group in range(4)]
                return dot(matrix, jnp.concatenate(found, axis=0))

            block_out[part, :] = (dot(keep, tokens[part, :]) + pieces(0)).astype(BF)
            grown = (cotangent[part, :].astype(F32) + pieces(1)).astype(BF)
            tokens_grad[part, :] = dot(keep, grown).astype(BF)


def total_kernel(copies, parts, out):
    total = parts[0].astype(F32)
    for index in range(1, parts.shape[0]):
        total = total + parts[index].astype(F32)
    total = total.astype(BF)
    for index in range(copies):
        out[index] = total


def total_of(parts, copies):
    return pl.pallas_call(
        lambda *refs: total_kernel(copies, *refs),
        out_shape=jax.ShapeDtypeStruct((copies,) + parts.shape[1:], BF),
    )(parts)


def grads_kernel(core, mine, other, qkv_grad, proj_grad, gain_grad):
    grad_scale = (ROWS * 512) ** (-0.5)
    half = GRAD_ROWS // 2
    first = core[0] == 0

    def rows(start, stop):
        found = []
        if start < half:
            part = pl.ds(start, min(stop, half) - start)
            found.append(jnp.where(first, mine[part, :].astype(F32), other[part, :].astype(F32)))
        if stop > half:
            low = max(start, half)
            part = pl.ds(low - half, stop - low)
            found.append(jnp.where(first, other[part, :].astype(F32), mine[part, :].astype(F32)))
        return (found[0] if len(found) == 1 else jnp.concatenate(found, axis=0)) * grad_scale

    for block in range(12):
        target, column = (qkv_grad, block) if block < 9 else (proj_grad, block - 9)
        target[:, column * LANES : (column + 1) * LANES] = rows(block * D, (block + 1) * D)
    tail = rows(12 * D, 12 * D + 16)
    for block in range(3):
        gain_grad[:, block * LANES : (block + 1) * LANES] = tail[block : block + 1]


SCALAR = pl.BlockSpec(memory_space=pltpu.SMEM)
WHOLE = pl.BlockSpec(memory_space=pltpu.VMEM)


def window_pass(own, behind, sides, w_qkv, w_proj, norm_gain):
    def buffer(shape, kind):
        return pltpu.VMEM(shape, kind)

    return pl.pallas_call(
        window_kernel,
        out_shape=(jax.ShapeDtypeStruct((2, 2, PIECE, D), BF),) * 4
        + (jax.ShapeDtypeStruct((GRAD_ROWS, LANES), BF),),
        scratch_shapes=[
            buffer((ROWS, D), BF),
            buffer((ROWS, 3 * D), BF),
            buffer((ROWS, D), BF),
            buffer((D, ROWS), BF),
            buffer((D, ROWS), BF),
            buffer((D, ROWS), BF),
            buffer((D, ROWS), BF),
            buffer((ROWS, 3 * D), BF),
            buffer((ROWS, D), F32),
            buffer((ROWS, LANES), F32),
            buffer((ROWS, D), BF),
        ],
        compiler_params=pltpu.CompilerParams(vmem_limit_bytes=40 * 1024 * 1024),
        cost_estimate=pl.CostEstimate(
            flops=16_000_000_000, bytes_accessed=5_000_000, transcendentals=3_200_000
        ),
    )(own, behind, *sides, w_qkv, w_proj, norm_gain.reshape(1, D))


LATTICE = ("z_hi", "z_lo", "core", "y_hi", "y_lo", "x")
FIRST = ("z_hi", "z_lo", "core")
SECOND = ("y_hi",)
THIRD = ("y_lo", "x")
SIZES = {"z_hi": 4, "z_lo": 2, "core": 2, "y_hi": 4, "y_lo": 2, "x": 4}
NEAR = ("x", "y_lo", "z_lo")
FAR = ("y_hi", "z_hi")
GROUP = 16


def sum_over_devices(rows):
    halves = lax.all_to_all(rows.reshape(2, GRAD_ROWS // 2, LANES), "core", 0, 0)
    parts = total_of(halves, 1).reshape(GROUP, GRAD_ROWS // 2 // GROUP, LANES)
    parts = lax.all_to_all(parts, NEAR, 0, 0)
    parts = lax.all_to_all(total_of(parts, GROUP), FAR, 0, 0)
    parts = lax.all_to_all(total_of(parts, GROUP), NEAR, 0, 0)
    mine = parts.reshape(GRAD_ROWS // 2, LANES)
    return mine, lax.ppermute(mine, "core", [(0, 1), (1, 0)])


def device_at(first, second, third):
    return ((first % 16) * 4 + second % 4) * 8 + third % 8


def route(kind, back):
    pairs = []
    for first in range(16):
        for second in range(4):
            for third in range(8):
                sign = 1 if first % 2 else -1
                if kind == 0:
                    move = (first - 1, second, third)
                else:
                    move = (first, second + sign * (kind >> 1), third + sign * (kind & 1))
                pair = (device_at(first, second, third), device_at(*move))
                pairs.append(pair[::-1] if back else pair)
    return pairs


def send(block, kind, back=False):
    return lax.ppermute(block, LATTICE, route(kind, back))


def local(tokens, frozen, cotangent, w_qkv, w_proj, norm_gain):
    core = lax.axis_index("core").reshape(1)
    token_rows, cot_rows = tokens.reshape(ROWS, D), cotangent.reshape(ROWS, D)
    frozen_rows = frozen.reshape(WIN, WIN * WIN)
    own, ahead = pl.pallas_call(
        cut_kernel,
        out_shape=(jax.ShapeDtypeStruct((4, 2, PIECE, D), BF),) * 2,
        in_specs=[SCALAR, WHOLE, WHOLE, WHOLE],
    )(core, token_rows, frozen_rows, cot_rows)
    behind = send(ahead, 0)
    sides = [None] * 4
    for kind in (3, 2, 1):
        sides[kind] = send(jnp.stack([own[kind], behind[kind]]), kind)
    *backs, grads = window_pass(own, behind, sides[1:], w_qkv, w_proj, norm_gain)
    mine, other = sum_over_devices(grads)
    for kind in (3, 2, 1):
        backs[kind] = send(backs[kind], kind, True)
    ahead = send(jnp.stack([back[1] for back in backs]), 0, True)
    block_out, tokens_grad = pl.pallas_call(
        join_kernel,
        out_shape=(jax.ShapeDtypeStruct((ROWS, D), BF),) * 2,
        in_specs=[SCALAR] + [WHOLE] * 8,
    )(core, token_rows, frozen_rows, cot_rows, *backs, ahead)
    qkv_grad, proj_grad, gain_grad = pl.pallas_call(
        grads_kernel,
        out_shape=(
            jax.ShapeDtypeStruct((D, 3 * D), F32),
            jax.ShapeDtypeStruct((D, D), F32),
            jax.ShapeDtypeStruct((1, D), F32),
        ),
        in_specs=[SCALAR, WHOLE, WHOLE],
    )(core, mine, other)
    shape = (WIN, WIN, WIN, D)
    return block_out.reshape(shape), tokens_grad.reshape(shape), qkv_grad, proj_grad, gain_grad.reshape(D)


def solution(mesh):
    inner = Mesh(mesh.devices.reshape([SIZES[axis] for axis in LATTICE]), LATTICE)
    lattice = P(FIRST, SECOND, THIRD)
    wide = P(FIRST, SECOND, THIRD, None)
    return jax.shard_map(
        local,
        mesh=inner,
        in_specs=(wide, lattice, wide, P(), P(), P()),
        out_specs=(wide, wide, P(), P(), P()),
        check_vma=False,
    )
```

time: 166 us -> 165 us (level); the launches traced: 165 us -> 162 us
  waiting for transfers between devices: 53.2 us -> 12.1 us
  blocking collectives: 20.8 us -> 57.2 us
  Pallas kernels: 21.2 us -> 36.5 us
  local copies, waits for them, and re-layouts: 14.4 us -> 4.15 us
  other arithmetic: 8.83 us -> 1.42 us
  starting transfers between devices: 45.2 us -> 49.6 us
    all_to_all x2 -> x3, blocking collectives: 20.8 us -> 57.2 us  [the longest x1 26.2 us: sum_over_devices(): parts = lax.all_to_all(total_of(parts, GROUP), FAR, 0, 0)]
    all_to_all x5 -> x1, waiting for transfers between devices: 31 us -> 0.01 us  [sum_over_devices(): parts = lax.all_to_all(total_of(parts, GROUP), NEAR, 0, 0)]
    all_to_all x5 -> x1, starting transfers between devices: 22.7 us -> 5.15 us  [sum_over_devices(): parts = lax.all_to_all(total_of(parts, GROUP), NEAR, 0, 0)]
    pallas_call x1 -> x7, Pallas kernels: 21.2 us -> 36.5 us  [the longest x1 21.2 us: window_pass(): pl.pallas_call(window_kernel, out_shape=(jax.ShapeDtypeStruct((2, 2, PIEC...]
    ppermute x6 -> x8, starting transfers between devices: 22.5 us -> 36.1 us  [send(): return lax.ppermute(block, LATTICE, route(kind, back))]
    ppermute x6 -> x8, waiting for transfers between devices: 22.3 us -> 12.1 us  [send(): return lax.ppermute(block, LATTICE, route(kind, back))]
    ppermute x0 -> x1, starting transfers between devices: none -> 8.28 us  [sum_over_devices(): return (mine, lax.ppermute(mine, 'core', [(0, 1), (1, 0)]))]
    broadcast_in_dim x4 -> x0, local copies, waits for them, and re-layouts: 3.35 us -> none  [everywhere(): jnp.broadcast_to(rows[None], (count,) + rows.shape)]
  transfers between devices with their start and end apart: 11 -> 10, of which waited for: 8 -> 4; matrix products, arithmetic and copies ran while one was open for 5% -> 1% of each run, Pallas kernels for 0% -> 2%
where the time goes in v2:
time: 165 us; the launch traced here: 162 us
  blocking collectives  57.2 us (35%)
  starting transfers between devices  49.6 us (30%)
  Pallas kernels  36.5 us (22%)
  waiting for transfers between devices  12.1 us (7%)
  local copies, waits for them, and re-layouts  4.15 us (3%)
    ppermute x8, starting transfers between devices, send(): return lax.ppermute(block, LATTICE, route(kind, back))  36.1 us
    all_to_all x1, blocking collectives, sum_over_devices(): parts = lax.all_to_all(total_of(parts, GROUP), FAR, 0, 0)  26.2 us
    pallas_call x1, Pallas kernels, window_pass(): pl.pallas_call(window_kernel, out_shape=(jax.ShapeDtypeStruct((2, 2, PIEC...  21.2 us
    all_to_all x1, blocking collectives, sum_over_devices(): parts = lax.all_to_all(parts, NEAR, 0, 0)  16.3 us
    all_to_all x1, blocking collectives, sum_over_devices(): lax.all_to_all(rows.reshape(2, GRAD_ROWS // 2, LANES), 'core', 0, 0)  14.7 us
    ppermute x8, waiting for transfers between devices, send(): return lax.ppermute(block, LATTICE, route(kind, back))  12.1 us
    ppermute x1, starting transfers between devices, sum_over_devices(): return (mine, lax.ppermute(mine, 'core', [(0, 1), (1, 0)]))  8.28 us
    pallas_call x3, Pallas kernels, total_of(): pl.pallas_call(lambda *refs: total_kernel(copies, *refs), out_shape=jax.S...  6.34 us
  transfers between devices with their start and end apart: 10, of which 4 were waited for; matrix products, arithmetic and copies ran while one was open for 1% of the time, Pallas kernels for 2%

profile of v2, /device:TPU:1, one launch (start us, length us, event | category | flops | bytes accessed | tf_op | source)
XLA Modules:
  0.0 161.8 jit_solution(1792644607199176342)
XLA Ops:
  0.6 1.4 reshape.45.frozen
  2.1 2.2 %shard_map.101 = (bf16[4,2,64,384]{3,2,1,0:T(8,128)(2,1)}, bf16[4,2,64,384]{3,2,1,0:T(8,128)(2,1)}) custom-call(s32[1]{0:T(128)} %bitcast.odd.core, bf16[512,384]{1,0:T(8,128)(2,1)} %bitcast.12, s32[8,64]{1,0:T(8,128)} %reshape.45.frozen, bf16[512,384]{1,0:T(8,128)(2,1)} %bitcast.14), custom_call_target="tpu_custom_call" | custom-call | tf_op jit(solution)/shard_map/pallas_call | solution.py:308
  4.3 6.9 %collective-permute-start = (bf16[4,2,64,384]{3,2,1,0:T(8,128)(2,1)}, bf16[4,2,64,384]{3,2,1,0:T(8,128)(2,1)S(1)}, u32[]{:S(2)}, u32[]{:S(2)}) collective-permute-start(bf16[4,2,64,384]{3,2,1,0:T(8,128)(2,1)} %get-tuple-element.18), channel_id=1, source_target_pairs={{0,480},{1,481},{2,482},{3,483},{4,484},{5,485},{6,486},{7,487},{8... | collective-permute-start | bytes 1179656 | tf_op jit(solution)/shard_map/ppermute | solution.py:301
  13.6 3.1 %collective-permute-start.1 = (bf16[2,2,64,384]{3,2,1,0:T(8,128)(2,1)S(1)}, bf16[2,2,64,384]{3,2,1,0:T(8,128)(2,1)S(1)}, u32[]{:S(2)}, u32[]{:S(2)}) collective-permute-start(bf16[2,2,64,384]{3,2,1,0:T(8,128)(2,1)S(1)} %pad_maximum_fusion.1), channel_id=1, source_target_pairs={{0,7},{1,0},{2,1},{3,2},{4,3},{5,4},{6,5},{7,6},{8,15},{9,8},{10,9... | collective-permute-start | bytes 589832 | tf_op jit(solution)/shard_map/ppermute | solution.py:301
  16.7 4.2 %collective-permute-start.2 = (bf16[2,2,64,384]{3,2,1,0:T(8,128)(2,1)S(1)}, bf16[2,2,64,384]{3,2,1,0:T(8,128)(2,1)S(1)}, u32[]{:S(2)}, u32[]{:S(2)}) collective-permute-start(bf16[2,2,64,384]{3,2,1,0:T(8,128)(2,1)S(1)} %pad_maximum_fusion.2), channel_id=1, source_target_pairs={{0,24},{1,25},{2,26},{3,27},{4,28},{5,29},{6,30},{7,31},{8,0},{9,1... | collective-permute-start | bytes 589832 | tf_op jit(solution)/shard_map/ppermute | solution.py:301
  21.0 6.4 %collective-permute-start.3 = (bf16[2,2,64,384]{3,2,1,0:T(8,128)(2,1)S(1)}, bf16[2,2,64,384]{3,2,1,0:T(8,128)(2,1)S(1)}, u32[]{:S(2)}, u32[]{:S(2)}) collective-permute-start(bf16[2,2,64,384]{3,2,1,0:T(8,128)(2,1)S(1)} %pad_maximum_fusion.3), channel_id=1, source_target_pairs={{0,31},{1,24},{2,25},{3,26},{4,27},{5,28},{6,29},{7,30},{8,7},{9,0... | collective-permute-start | bytes 589832 | tf_op jit(solution)/shard_map/ppermute | solution.py:301
  27.4 5.7 %collective-permute-done.3.side_3 = bf16[2,2,64,384]{3,2,1,0:T(8,128)(2,1)S(1)} collective-permute-done((bf16[2,2,64,384]{3,2,1,0:T(8,128)(2,1)S(1)}, bf16[2,2,64,384]{3,2,1,0:T(8,128)(2,1)S(1)}, u32[]{:S(2)}, u32[]{:S(2)}) %collective-permute-start.3) | collective-permute-done | bytes 196640 | tf_op jit(solution)/shard_map/ppermute | solution.py:301
  33.1 21.2 %shard_map.102 = (bf16[2,2,64,384]{3,2,1,0:T(8,128)(2,1)S(1)}, bf16[2,2,64,384]{3,2,1,0:T(8,128)(2,1)S(1)}, bf16[2,2,64,384]{3,2,1,0:T(8,128)(2,1)S(1)}, bf16[2,...) custom-call(bf16[4,2,64,384]{3,2,1,0:T(8,128)(2,1)S(1)} %copy-done.1, ...), custom_call_target="tpu_custom_call" | custom-call | flops 16000000000 | bytes 5000000 | tf_op jit(solution)/shard_map/pallas_call | solution.py:237
  54.3 14.7 %all_to_all.20.refs_0_ = bf16[2,2560,128]{2,1,0:T(8,128)(2,1)} all-to-all(bf16[2,2560,128]{2,1,0:T(8,128)(2,1)S(1)} %bitcast.8), channel_id=1, replica_groups=mesh['z_hi'=4,'z_lo'=2,'core'=2,'y_hi'=4,'y_lo'=2,'x'=4] {'core'}, dimensions={0} | all-to-all | bytes 2621440 | tf_op jit(solution)/shard_map/all_to_all | solution.py:272
  69.0 2.3 %shard_map.104 = bf16[1,2560,128]{2,1,0:T(8,128)(2,1)} custom-call(bf16[2,2560,128]{2,1,0:T(8,128)(2,1)} %all_to_all.20.refs_0_), custom_call_target="tpu_custom_call" | custom-call | tf_op jit(solution)/shard_map/pallas_call | solution.py:199
  71.3 16.3 %all_to_all.21.refs_0_ = bf16[16,160,128]{2,1,0:T(8,128)(2,1)} all-to-all(bf16[16,160,128]{2,1,0:T(8,128)(2,1)} %bitcast.11), channel_id=1, replica_groups=mesh['z_hi'=4,'z_lo'=2,'core'=2,'y_hi'=4,'y_lo'=2,'x'=4] {'x','y_lo','z_..., dimensions={0} | all-to-all | bytes 1310720 | tf_op jit(solution)/shard_map/all_to_all | solution.py:274
  87.6 2.0 %shard_map.105 = bf16[16,160,128]{2,1,0:T(8,128)(2,1)} custom-call(bf16[16,160,128]{2,1,0:T(8,128)(2,1)} %all_to_all.21.refs_0_), custom_call_target="tpu_custom_call" | custom-call | tf_op jit(solution)/shard_map/pallas_call | solution.py:199
  89.6 26.2 %all_to_all.22.refs_0_ = bf16[16,160,128]{2,1,0:T(8,128)(2,1)} all-to-all(bf16[16,160,128]{2,1,0:T(8,128)(2,1)} %shard_map.105), channel_id=1, replica_groups=mesh['z_hi'=4,'z_lo'=2,'core'=2,'y_hi'=4,'y_lo'=2,'x'=4] {'y_hi','z_hi'}, dimensions={0} | all-to-all | bytes 1310720 | tf_op jit(solution)/shard_map/all_to_all | solution.py:275
  115.8 2.0 %shard_map.106 = bf16[16,160,128]{2,1,0:T(8,128)(2,1)} custom-call(bf16[16,160,128]{2,1,0:T(8,128)(2,1)} %all_to_all.22.refs_0_), custom_call_target="tpu_custom_call" | custom-call | tf_op jit(solution)/shard_map/pallas_call | solution.py:199
  117.8 5.1 %all-to-all-start.3 = ((bf16[16,160,128]{2,1,0:T(8,128)(2,1)}), bf16[16,160,128]{2,1,0:T(8,128)(2,1)S(1)}, u32[]{:S(2)}, u32[]{:S(2)}) async-start(bf16[16,160,128]{2,1,0:T(8,128)(2,1)} %shard_map.106), calls=%async_computation.3 | async-start | bytes 1310720 | tf_op jit(solution)/shard_map/all_to_all | solution.py:276
  123.0 5.4 %collective-permute-start.4 = (bf16[2,2,64,384]{3,2,1,0:T(8,128)(2,1)S(1)}, bf16[2,2,64,384]{3,2,1,0:T(8,128)(2,1)S(1)}, u32[]{:S(2)}, u32[]{:S(2)}) collective-permute-start(bf16[2,2,64,384]{3,2,1,0:T(8,128)(2,1)S(1)} %get-tuple-element.20), channel_id=1, source_target_pairs={{7,0},{0,1},{1,2},{2,3},{3,4},{4,5},{5,6},{6,7},{15,8},{8,9},{9,10... | collective-permute-start | bytes 589832 | tf_op jit(solution)/shard_map/ppermute | solution.py:301
  128.4 4.3 %collective-permute-start.5 = (bf16[2,2,64,384]{3,2,1,0:T(8,128)(2,1)S(1)}, bf16[2,2,64,384]{3,2,1,0:T(8,128)(2,1)S(1)}, u32[]{:S(2)}, u32[]{:S(2)}) collective-permute-start(bf16[2,2,64,384]{3,2,1,0:T(8,128)(2,1)S(1)} %get-tuple-element.21), channel_id=1, source_target_pairs={{24,0},{25,1},{26,2},{27,3},{28,4},{29,5},{30,6},{31,7},{0,8},{1,9... | collective-permute-start | bytes 589832 | tf_op jit(solution)/shard_map/ppermute | solution.py:301
  132.7 1.9 %collective-permute-start.6 = (bf16[2,2,64,384]{3,2,1,0:T(8,128)(2,1)S(1)}, bf16[2,2,64,384]{3,2,1,0:T(8,128)(2,1)S(1)}, u32[]{:S(2)}, u32[]{:S(2)}) collective-permute-start(bf16[2,2,64,384]{3,2,1,0:T(8,128)(2,1)S(1)} %get-tuple-element.22), channel_id=1, source_target_pairs={{31,0},{24,1},{25,2},{26,3},{27,4},{28,5},{29,6},{30,7},{7,8},{0,9... | collective-permute-start | bytes 589832 | tf_op jit(solution)/shard_map/ppermute | solution.py:301
  134.7 8.3 %collective-permute-start.8 = (bf16[2560,128]{1,0:T(8,128)(2,1)S(1)}, bf16[2560,128]{1,0:T(8,128)(2,1)S(1)}, u32[]{:S(2)}, u32[]{:S(2)}) collective-permute-start(bf16[2560,128]{1,0:T(8,128)(2,1)S(1)} %bitcast.9), channel_id=1, source_target_pairs={{0,32},{32,0},{1,33},{33,1},{2,34},{34,2},{3,35},{35,3},{4,36},{36... | collective-permute-start | bytes 1966088 | tf_op jit(solution)/shard_map/ppermute | solution.py:278
  143.6 3.9 %collective-permute-start.7 = (bf16[4,2,64,384]{3,2,1,0:T(8,128)(2,1)S(1)}, bf16[4,2,64,384]{3,2,1,0:T(8,128)(2,1)S(1)}, u32[]{:S(2)}, u32[]{:S(2)}) collective-permute-start(bf16[4,2,64,384]{3,2,1,0:T(8,128)(2,1)S(1)} %pad_maximum_fusion), channel_id=1, source_target_pairs={{480,0},{481,1},{482,2},{483,3},{484,4},{485,5},{486,6},{487,7},{4... | collective-permute-start | bytes 1179656 | tf_op jit(solution)/shard_map/ppermute | solution.py:301
  147.5 4.7 %collective-permute-done.7.ahead = bf16[4,2,64,384]{3,2,1,0:T(8,128)(2,1)S(1)} collective-permute-done((bf16[4,2,64,384]{3,2,1,0:T(8,128)(2,1)S(1)}, bf16[4,2,64,384]{3,2,1,0:T(8,128)(2,1)S(1)}, u32[]{:S(2)}, u32[]{:S(2)}) %collective-permute-start.7) | collective-permute-done | bytes 393248 | tf_op jit(solution)/shard_map/ppermute | solution.py:301
  153.0 3.9 %shard_map.103 = (bf16[512,384]{1,0:T(8,128)(2,1)}, bf16[512,384]{1,0:T(8,128)(2,1)}) custom-call(s32[1]{0:T(128)} %bitcast.odd.core, bf16[512,384]{1,0:T(8,128)(2,1)} %bitcast.13, s32[8,64]{1,0:T(8,128)} %reshape.45.frozen, bf16[512,384]{1,0:T(8,128)(2,1)} %bitcast.15, bf16[2,2,64,384]{3,2,1,0:T(8,128)(2,1)} %copy-done, bf16[2,2,64,384]{3,2,1,0:T(8,128)(2,1)} %copy-done.6, ...), custom_call_target="tpu_custom_call" | custom-call | tf_op jit(solution)/shard_map/pallas_call | solution.py:322
  157.7 2.8 %shard_map.107 = (f32[384,1152]{1,0:T(8,128)}, f32[384,384]{1,0:T(8,128)}, f32[1,384]{1,0:T(1,128)}) custom-call(s32[1]{0:T(128)} %bitcast.odd.core, bf16[2560,128]{1,0:T(8,128)(2,1)} %bitcast.10, bf16[2560,128]{1,0:T(8,128)(2,1)} %copy-done.5), custom_call_target="tpu_custom_call" | custom-call | tf_op jit(solution)/shard_map/pallas_call | solution.py:327
  160.5 1.3 reduce
  (41 shorter events, 4.6 us)
Async XLA Ops:
  4.3 23.1 %copy-start.10 = (f32[384]{0:T(512)S(1)}, f32[384]{0:T(512)}, u32[]{:S(2)}) copy-start(f32[384]{0:T(512)} %param.11) | copy-start | bytes 4612
  4.3 28.8 %copy-start.1 = (bf16[4,2,64,384]{3,2,1,0:T(8,128)(2,1)S(1)}, bf16[4,2,64,384]{3,2,1,0:T(8,128)(2,1)}, u32[]{:S(2)}) copy-start(bf16[4,2,64,384]{3,2,1,0:T(8,128)(2,1)} %get-tuple-element.17.own) | copy-start | bytes 1179652
  4.3 28.8 %copy-start.2 = (bf16[384,1152]{1,0:T(8,128)(2,1)S(1)}, bf16[384,1152]{1,0:T(8,128)(2,1)}, u32[]{:S(2)}) copy-start(bf16[384,1152]{1,0:T(8,128)(2,1)} %w_qkv.1) | copy-start | bytes 2654212
  4.3 28.8 %copy-start.3 = (bf16[384,384]{1,0:T(8,128)(2,1)S(1)}, bf16[384,384]{1,0:T(8,128)(2,1)}, u32[]{:S(2)}) copy-start(bf16[384,384]{1,0:T(8,128)(2,1)} %w_proj.1) | copy-start | bytes 884740
  4.3 9.2 %collective-permute-start = (bf16[4,2,64,384]{3,2,1,0:T(8,128)(2,1)}, bf16[4,2,64,384]{3,2,1,0:T(8,128)(2,1)S(1)}, u32[]{:S(2)}, u32[]{:S(2)}) collective-permute-start(bf16[4,2,64,384]{3,2,1,0:T(8,128)(2,1)} %get-tuple-element.18), channel_id=1, source_target_pairs={{0,480},{1,481},{2,482},{3,483},{4,484},{5,485},{6,486},{7,487},{8... | collective-permute-start | bytes 1179656 | tf_op jit(solution)/shard_map/ppermute | solution.py:301
  13.6 13.8 %collective-permute-start.1 = (bf16[2,2,64,384]{3,2,1,0:T(8,128)(2,1)S(1)}, bf16[2,2,64,384]{3,2,1,0:T(8,128)(2,1)S(1)}, u32[]{:S(2)}, u32[]{:S(2)}) collective-permute-start(bf16[2,2,64,384]{3,2,1,0:T(8,128)(2,1)S(1)} %pad_maximum_fusion.1), channel_id=1, source_target_pairs={{0,7},{1,0},{2,1},{3,2},{4,3},{5,4},{6,5},{7,6},{8,15},{9,8},{10,9... | collective-permute-start | bytes 589832 | tf_op jit(solution)/shard_map/ppermute | solution.py:301
  16.7 10.7 %collective-permute-start.2 = (bf16[2,2,64,384]{3,2,1,0:T(8,128)(2,1)S(1)}, bf16[2,2,64,384]{3,2,1,0:T(8,128)(2,1)S(1)}, u32[]{:S(2)}, u32[]{:S(2)}) collective-permute-start(bf16[2,2,64,384]{3,2,1,0:T(8,128)(2,1)S(1)} %pad_maximum_fusion.2), channel_id=1, source_target_pairs={{0,24},{1,25},{2,26},{3,27},{4,28},{5,29},{6,30},{7,31},{8,0},{9,1... | collective-permute-start | bytes 589832 | tf_op jit(solution)/shard_map/ppermute | solution.py:301
  21.0 12.1 %collective-permute-start.3 = (bf16[2,2,64,384]{3,2,1,0:T(8,128)(2,1)S(1)}, bf16[2,2,64,384]{3,2,1,0:T(8,128)(2,1)S(1)}, u32[]{:S(2)}, u32[]{:S(2)}) collective-permute-start(bf16[2,2,64,384]{3,2,1,0:T(8,128)(2,1)S(1)} %pad_maximum_fusion.3), channel_id=1, source_target_pairs={{0,31},{1,24},{2,25},{3,26},{4,27},{5,28},{6,29},{7,30},{8,7},{9,0... | collective-permute-start | bytes 589832 | tf_op jit(solution)/shard_map/ppermute | solution.py:301
  54.3 88.7 %copy-start = (bf16[2,2,64,384]{3,2,1,0:T(8,128)(2,1)}, bf16[2,2,64,384]{3,2,1,0:T(8,128)(2,1)S(1)}, u32[]{:S(2)}) copy-start(bf16[2,2,64,384]{3,2,1,0:T(8,128)(2,1)S(1)} %get-tuple-element.19.home_0) | copy-start | bytes 589828
  117.8 16.8 %all-to-all-start.3 = ((bf16[16,160,128]{2,1,0:T(8,128)(2,1)}), bf16[16,160,128]{2,1,0:T(8,128)(2,1)S(1)}, u32[]{:S(2)}, u32[]{:S(2)}) async-start(bf16[16,160,128]{2,1,0:T(8,128)(2,1)} %shard_map.106), calls=%async_computation.3 | async-start | bytes 1310720 | tf_op jit(solution)/shard_map/all_to_all | solution.py:276
  123.0 20.0 %collective-permute-start.4 = (bf16[2,2,64,384]{3,2,1,0:T(8,128)(2,1)S(1)}, bf16[2,2,64,384]{3,2,1,0:T(8,128)(2,1)S(1)}, u32[]{:S(2)}, u32[]{:S(2)}) collective-permute-start(bf16[2,2,64,384]{3,2,1,0:T(8,128)(2,1)S(1)} %get-tuple-element.20), channel_id=1, source_target_pairs={{7,0},{0,1},{1,2},{2,3},{3,4},{4,5},{5,6},{6,7},{15,8},{8,9},{9,10... | collective-permute-start | bytes 589832 | tf_op jit(solution)/shard_map/ppermute | solution.py:301
  128.4 14.7 %collective-permute-start.5 = (bf16[2,2,64,384]{3,2,1,0:T(8,128)(2,1)S(1)}, bf16[2,2,64,384]{3,2,1,0:T(8,128)(2,1)S(1)}, u32[]{:S(2)}, u32[]{:S(2)}) collective-permute-start(bf16[2,2,64,384]{3,2,1,0:T(8,128)(2,1)S(1)} %get-tuple-element.21), channel_id=1, source_target_pairs={{24,0},{25,1},{26,2},{27,3},{28,4},{29,5},{30,6},{31,7},{0,8},{1,9... | collective-permute-start | bytes 589832 | tf_op jit(solution)/shard_map/ppermute | solution.py:301
  132.7 10.8 %collective-permute-start.6 = (bf16[2,2,64,384]{3,2,1,0:T(8,128)(2,1)S(1)}, bf16[2,2,64,384]{3,2,1,0:T(8,128)(2,1)S(1)}, u32[]{:S(2)}, u32[]{:S(2)}) collective-permute-start(bf16[2,2,64,384]{3,2,1,0:T(8,128)(2,1)S(1)} %get-tuple-element.22), channel_id=1, source_target_pairs={{31,0},{24,1},{25,2},{26,3},{27,4},{28,5},{29,6},{30,7},{7,8},{0,9... | collective-permute-start | bytes 589832 | tf_op jit(solution)/shard_map/ppermute | solution.py:301
  134.6 22.2 %copy-start.4 = (bf16[16,160,128]{2,1,0:T(8,128)(2,1)}, bf16[16,160,128]{2,1,0:T(8,128)(2,1)S(1)}, u32[]{:S(2)}) copy-start(bf16[16,160,128]{2,1,0:T(8,128)(2,1)S(1)} %all-to-all-done.3) | copy-start | bytes 1966084
  134.7 22.2 %collective-permute-start.8 = (bf16[2560,128]{1,0:T(8,128)(2,1)S(1)}, bf16[2560,128]{1,0:T(8,128)(2,1)S(1)}, u32[]{:S(2)}, u32[]{:S(2)}) collective-permute-start(bf16[2560,128]{1,0:T(8,128)(2,1)S(1)} %bitcast.9), channel_id=1, source_target_pairs={{0,32},{32,0},{1,33},{33,1},{2,34},{34,2},{3,35},{35,3},{4,36},{36... | collective-permute-start | bytes 1966088 | tf_op jit(solution)/shard_map/ppermute | solution.py:278
  143.0 9.2 %copy-start.6 = (bf16[2,2,64,384]{3,2,1,0:T(8,128)(2,1)}, bf16[2,2,64,384]{3,2,1,0:T(8,128)(2,1)S(1)}, u32[]{:S(2)}) copy-start(bf16[2,2,64,384]{3,2,1,0:T(8,128)(2,1)S(1)} %collective-permute-done.4.home_1) | copy-start | bytes 589828
  143.0 9.2 %copy-start.7 = (bf16[2,2,64,384]{3,2,1,0:T(8,128)(2,1)}, bf16[2,2,64,384]{3,2,1,0:T(8,128)(2,1)S(1)}, u32[]{:S(2)}) copy-start(bf16[2,2,64,384]{3,2,1,0:T(8,128)(2,1)S(1)} %collective-permute-done.5.home_2) | copy-start | bytes 589828
  143.5 8.7 %copy-start.8 = (bf16[2,2,64,384]{3,2,1,0:T(8,128)(2,1)}, bf16[2,2,64,384]{3,2,1,0:T(8,128)(2,1)S(1)}, u32[]{:S(2)}) copy-start(bf16[2,2,64,384]{3,2,1,0:T(8,128)(2,1)S(1)} %collective-permute-done.6.home_3) | copy-start | bytes 589828
  143.6 8.6 %collective-permute-start.7 = (bf16[4,2,64,384]{3,2,1,0:T(8,128)(2,1)S(1)}, bf16[4,2,64,384]{3,2,1,0:T(8,128)(2,1)S(1)}, u32[]{:S(2)}, u32[]{:S(2)}) collective-permute-start(bf16[4,2,64,384]{3,2,1,0:T(8,128)(2,1)S(1)} %pad_maximum_fusion), channel_id=1, source_target_pairs={{480,0},{481,1},{482,2},{483,3},{484,4},{485,5},{486,6},{487,7},{4... | collective-permute-start | bytes 1179656 | tf_op jit(solution)/shard_map/ppermute | solution.py:301
  152.2 0.7 copy-start.9
  156.8 0.9 copy-start.5

commit v3 on v2

--- a/solution.py
+++ b/solution.py
@@ -21,7 +21,7 @@
 CHUNK = 256
 SCALE = HDIM ** (-0.5)
 LOG2E = 1.4426950408889634
-GRAD_ROWS = 5120
+GRAD_ROWS = 12 * D
 
 
 def dot(left, right):
@@ -111,26 +111,16 @@
     for block in range(3):
         term = dot(mixed_t[...], cot[:, block * LANES : (block + 1) * LANES])
         grads[pl.ds((9 + block) * D, D), :] = term.astype(BF)
-    total = jnp.zeros((1, D), F32)
     for group in range(4):
         part = pl.ds(group * step, step)
         d_normed = dot_t(d_qkv[part, :], w_qkv[...])
         unit_rows = unit[part, :]
-        total = total + jnp.sum(d_normed * unit_rows, axis=0, keepdims=True)
         scaled = d_normed * gain_row
         mean_1 = jnp.mean(scaled, axis=-1, keepdims=True)
         mean_2 = jnp.mean(scaled * unit_rows, axis=-1, keepdims=True)
         d_rows = (inv_std[part, 0:1] * (scaled - mean_1 - unit_rows * mean_2)).astype(BF)
         backs[group][0, 1] = d_rows[:PIECE]
         backs[group][1, 1] = d_rows[PIECE:]
-    tail = jnp.concatenate(
-        [total[:, block * LANES : (block + 1) * LANES] for block in range(3)]
-        + [jnp.zeros((13, LANES), F32)],
-        axis=0,
-    )
-    grads[pl.ds(12 * D, 16), :] = tail.astype(BF)
-    rest = GRAD_ROWS - 12 * D - 16
-    grads[pl.ds(12 * D + 16, rest), :] = jnp.zeros((rest, LANES), BF)
 
 
 def order(odd, upper, inverse):
@@ -147,14 +137,26 @@
     return jnp.where(chosen, 1.0, 0.0)
 
 
+def keep_rows(frozen):
+    table = ones_where(frozen[...].reshape(WIN * WIN, WIN) == 1).astype(BF)
+    column = lax.broadcasted_iota(jnp.int32, (WIN, WIN * WIN), 1)
+    row = lax.broadcasted_iota(jnp.int32, (WIN, WIN * WIN), 0)
+    spread = dot(table, ones_where((column & 7) == row).astype(BF))
+    chosen = ones_where((column >> 3) == row)
+    return [
+        jnp.sum(spread[plane * WIN : (plane + 1) * WIN] * chosen, axis=0, keepdims=True)
+        for plane in range(WIN)
+    ]
+
+
 def cut_kernel(odd, tokens, frozen, cotangent, own, ahead):
+    keeps = keep_rows(frozen)
     for upper, target in ((0, ahead), (1, own)):
         matrix = ones_where(order(odd[0], upper, False))
         for plane in range(HALF):
             index = upper * HALF + plane
             part = pl.ds(index * WIN * WIN, WIN * WIN)
-            keep = ones_where(frozen[index : index + 1, :] == 1)
-            kept = dot((matrix * keep).astype(BF), tokens[part, :]).astype(BF)
+            kept = dot((matrix * keeps[index]).astype(BF), tokens[part, :]).astype(BF)
             cot = dot(matrix.astype(BF), cotangent[part, :]).astype(BF)
             for group in range(4):
                 rows = slice(group * 16, group * 16 + 16)
@@ -164,6 +166,7 @@
 
 def join_kernel(odd, tokens, frozen, cotangent, home_0, home_1, home_2, home_3, ahead, block_out, tokens_grad):
     homes = (home_0, home_1, home_2, home_3)
+    keeps = keep_rows(frozen)
     shape = (WIN * WIN, WIN * WIN)
     diagonal = ones_where(lax.broadcasted_iota(jnp.int32, shape, 0) == lax.broadcasted_iota(jnp.int32, shape, 1))
     for upper in range(2):
@@ -171,7 +174,7 @@
         for plane in range(HALF):
             index = upper * HALF + plane
             part = pl.ds(index * WIN * WIN, WIN * WIN)
-            keep = (diagonal * ones_where(frozen[index : index + 1, :] == 1)).astype(BF)
+            keep = (diagonal * keeps[index]).astype(BF)
             rows = pl.ds(plane * 16, 16)
 
             def pieces(array):
@@ -186,7 +189,13 @@
             tokens_grad[part, :] = dot(keep, grown).astype(BF)
 
 
-def total_kernel(copies, parts, out):
+SCALAR = pl.BlockSpec(memory_space=pltpu.SMEM)
+WHOLE = pl.BlockSpec(memory_space=pltpu.VMEM)
+SMALL = pltpu.CompilerParams(vmem_limit_bytes=12 * 1024 * 1024)
+
+
+def total_kernel(copies, parts, *rest):
+    out = rest[-1]
     total = parts[0].astype(F32)
     for index in range(1, parts.shape[0]):
         total = total + parts[index].astype(F32)
@@ -195,39 +204,35 @@
         out[index] = total
 
 
-def total_of(parts, copies):
+def total_of(parts, copies, after=()):
     return pl.pallas_call(
         lambda *refs: total_kernel(copies, *refs),
         out_shape=jax.ShapeDtypeStruct((copies,) + parts.shape[1:], BF),
-    )(parts)
-
-
-def grads_kernel(core, mine, other, qkv_grad, proj_grad, gain_grad):
+        in_specs=[WHOLE] + [pl.BlockSpec(memory_space=pl.ANY)] * len(after),
+        compiler_params=SMALL,
+    )(parts, *after)
+
+
+def grads_kernel(core, mine, other, w_qkv, gain, qkv_grad, proj_grad, gain_grad):
     grad_scale = (ROWS * 512) ** (-0.5)
     half = GRAD_ROWS // 2
     first = core[0] == 0
-
-    def rows(start, stop):
-        found = []
+    weighted = jnp.zeros((D, LANES), F32)
+    for block in range(12):
+        start = block * D
         if start < half:
-            part = pl.ds(start, min(stop, half) - start)
-            found.append(jnp.where(first, mine[part, :].astype(F32), other[part, :].astype(F32)))
-        if stop > half:
-            low = max(start, half)
-            part = pl.ds(low - half, stop - low)
-            found.append(jnp.where(first, other[part, :].astype(F32), mine[part, :].astype(F32)))
-        return (found[0] if len(found) == 1 else jnp.concatenate(found, axis=0)) * grad_scale
-
-    for block in range(12):
+            part = pl.ds(start, D)
+            found = jnp.where(first, mine[part, :].astype(F32), other[part, :].astype(F32))
+        else:
+            part = pl.ds(start - half, D)
+            found = jnp.where(first, other[part, :].astype(F32), mine[part, :].astype(F32))
+        found = found * grad_scale
         target, column = (qkv_grad, block) if block < 9 else (proj_grad, block - 9)
-        target[:, column * LANES : (column + 1) * LANES] = rows(block * D, (block + 1) * D)
-    tail = rows(12 * D, 12 * D + 16)
-    for block in range(3):
-        gain_grad[:, block * LANES : (block + 1) * LANES] = tail[block : block + 1]
-
-
-SCALAR = pl.BlockSpec(memory_space=pltpu.SMEM)
-WHOLE = pl.BlockSpec(memory_space=pltpu.VMEM)
+        columns = slice(column * LANES, (column + 1) * LANES)
+        target[:, columns] = found
+        if block < 9:
+            weighted = weighted + found * w_qkv[:, columns].astype(F32)
+    gain_grad[...] = jnp.sum(weighted.T, axis=0, keepdims=True) / gain[...]
 
 
 def window_pass(own, behind, sides, w_qkv, w_proj, norm_gain):
@@ -268,12 +273,19 @@
 GROUP = 16
 
 
-def sum_over_devices(rows):
+def near_sum(rows):
     halves = lax.all_to_all(rows.reshape(2, GRAD_ROWS // 2, LANES), "core", 0, 0)
     parts = total_of(halves, 1).reshape(GROUP, GRAD_ROWS // 2 // GROUP, LANES)
     parts = lax.all_to_all(parts, NEAR, 0, 0)
-    parts = lax.all_to_all(total_of(parts, GROUP), FAR, 0, 0)
-    parts = lax.all_to_all(total_of(parts, GROUP), NEAR, 0, 0)
+    return parts
+
+
+def far_sum(parts, after):
+    return lax.all_to_all(total_of(parts, GROUP, after), FAR, 0, 0)
+
+
+def spread_sum(parts, after):
+    parts = lax.all_to_all(total_of(parts, GROUP, after), NEAR, 0, 0)
     mine = parts.reshape(GRAD_ROWS // 2, LANES)
     return mine, lax.ppermute(mine, "core", [(0, 1), (1, 0)])
 
@@ -304,26 +316,29 @@
 def local(tokens, frozen, cotangent, w_qkv, w_proj, norm_gain):
     core = lax.axis_index("core").reshape(1)
     token_rows, cot_rows = tokens.reshape(ROWS, D), cotangent.reshape(ROWS, D)
-    frozen_rows = frozen.reshape(WIN, WIN * WIN)
     own, ahead = pl.pallas_call(
         cut_kernel,
         out_shape=(jax.ShapeDtypeStruct((4, 2, PIECE, D), BF),) * 2,
         in_specs=[SCALAR, WHOLE, WHOLE, WHOLE],
-    )(core, token_rows, frozen_rows, cot_rows)
+        compiler_params=SMALL,
+    )(core, token_rows, frozen, cot_rows)
     behind = send(ahead, 0)
     sides = [None] * 4
     for kind in (3, 2, 1):
         sides[kind] = send(jnp.stack([own[kind], behind[kind]]), kind)
     *backs, grads = window_pass(own, behind, sides[1:], w_qkv, w_proj, norm_gain)
-    mine, other = sum_over_devices(grads)
+    parts = near_sum(grads)
     for kind in (3, 2, 1):
         backs[kind] = send(backs[kind], kind, True)
+    parts = far_sum(parts, backs[1:])
     ahead = send(jnp.stack([back[1] for back in backs]), 0, True)
     block_out, tokens_grad = pl.pallas_call(
         join_kernel,
         out_shape=(jax.ShapeDtypeStruct((ROWS, D), BF),) * 2,
         in_specs=[SCALAR] + [WHOLE] * 8,
-    )(core, token_rows, frozen_rows, cot_rows, *backs, ahead)
+        compiler_params=SMALL,
+    )(core, token_rows, frozen, cot_rows, *backs, ahead)
+    mine, other = spread_sum(parts, (block_out, tokens_grad))
     qkv_grad, proj_grad, gain_grad = pl.pallas_call(
         grads_kernel,
         out_shape=(
@@ -331,8 +346,9 @@
             jax.ShapeDtypeStruct((D, D), F32),
             jax.ShapeDtypeStruct((1, D), F32),
         ),
-        in_specs=[SCALAR, WHOLE, WHOLE],
-    )(core, mine, other)
+        in_specs=[SCALAR] + [WHOLE] * 4,
+        compiler_params=SMALL,
+    )(core, mine, other, w_qkv, norm_gain.reshape(1, D))
     shape = (WIN, WIN, WIN, D)
     return block_out.reshape(shape), tokens_grad.reshape(shape), qkv_grad, proj_grad, gain_grad.reshape(D)
 

time: 165 us -> 148 us (0.90); the launches traced: 162 us -> 147 us
  blocking collectives: 57.2 us -> 28.7 us
  waiting for transfers between devices: 12.1 us -> 33.2 us
  Pallas kernels: 36.5 us -> 27.8 us
    all_to_all x3 -> x2, blocking collectives: 57.2 us -> 28.7 us  [the longest x1 15.1 us: spread_sum(): parts = lax.all_to_all(total_of(parts, GROUP, after), NEAR, 0, 0)]
    ppermute x8, waiting for transfers between devices: 12.1 us -> 31.6 us  [send(): return lax.ppermute(block, LATTICE, route(kind, back))]
    all_to_all x1 -> x2, starting transfers between devices: 5.15 us -> 9.63 us  [the longest x1 4.86 us: near_sum(): parts = lax.all_to_all(parts, NEAR, 0, 0)]
    pallas_call x3, Pallas kernels: 6.34 us -> 1.94 us  [total_of(): pl.pallas_call(lambda *refs: total_kernel(copies, *refs), out_shape=jax.S...]
    unnamed x22, local copies, waits for them, and re-layouts: 1.64 us -> 4.76 us
    ppermute x1, starting transfers between devices: 8.28 us -> 5.17 us  [spread_sum(): return (mine, lax.ppermute(mine, 'core', [(0, 1), (1, 0)]))]
    pallas_call x1, Pallas kernels: 2.25 us -> 0.47 us  [local(): pl.pallas_call(cut_kernel, out_shape=(jax.ShapeDtypeStruct((4, 2, PIECE,...]
  transfers between devices with their start and end apart: 10 -> 11, of which waited for: 4 -> 6; matrix products, arithmetic and copies ran while one was open for 1% -> 0% of each run, Pallas kernels for 2% -> 2%
where the time goes in v3:
time: 148 us; the launch traced here: 147 us
  starting transfers between devices  51.1 us (35%)
  waiting for transfers between devices  33.2 us (22%)
  blocking collectives  28.7 us (19%)
  Pallas kernels  27.8 us (19%)
  local copies, waits for them, and re-layouts  4.87 us (3%)
    ppermute x8, starting transfers between devices, send(): return lax.ppermute(block, LATTICE, route(kind, back))  36.3 us
    ppermute x8, waiting for transfers between devices, send(): return lax.ppermute(block, LATTICE, route(kind, back))  31.6 us
    pallas_call x1, Pallas kernels, window_pass(): pl.pallas_call(window_kernel, out_shape=(jax.ShapeDtypeStruct((2, 2, PIEC...  21.2 us
    all_to_all x1, blocking collectives, spread_sum(): parts = lax.all_to_all(total_of(parts, GROUP, after), NEAR, 0, 0)  15.1 us
    all_to_all x1, blocking collectives, near_sum(): lax.all_to_all(rows.reshape(2, GRAD_ROWS // 2, LANES), 'core', 0, 0)  13.7 us
    ppermute x1, starting transfers between devices, spread_sum(): return (mine, lax.ppermute(mine, 'core', [(0, 1), (1, 0)]))  5.17 us
    all_to_all x1, starting transfers between devices, near_sum(): parts = lax.all_to_all(parts, NEAR, 0, 0)  4.86 us
    all_to_all x1, starting transfers between devices, far_sum(): return lax.all_to_all(total_of(parts, GROUP, after), FAR, 0, 0)  4.76 us
  transfers between devices with their start and end apart: 11, of which 6 were waited for; matrix products, arithmetic and copies ran while one was open for 0% of the time, Pallas kernels for 2%

profile of v3, /device:TPU:1, one launch (start us, length us, event | category | flops | bytes accessed | tf_op | source)
XLA Modules:
  0.0 147.3 jit_solution(12816661524930184074)
XLA Ops:
  1.6 1.0 copy-done.2
  3.9 6.9 %collective-permute-start = (bf16[4,2,64,384]{3,2,1,0:T(8,128)(2,1)S(1)}, bf16[4,2,64,384]{3,2,1,0:T(8,128)(2,1)S(1)}, u32[]{:S(2)}, u32[]{:S(2)}) collective-permute-start(bf16[4,2,64,384]{3,2,1,0:T(8,128)(2,1)S(1)} %get-tuple-element.18), channel_id=1, source_target_pairs={{0,480},{1,481},{2,482},{3,483},{4,484},{5,485},{6,486},{7,487},{8... | collective-permute-start | bytes 1179656 | tf_op jit(solution)/shard_map/ppermute | solution.py:313
  10.8 2.0 %collective-permute-done.behind = bf16[4,2,64,384]{3,2,1,0:T(8,128)(2,1)S(1)} collective-permute-done((bf16[4,2,64,384]{3,2,1,0:T(8,128)(2,1)S(1)}, bf16[4,2,64,384]{3,2,1,0:T(8,128)(2,1)S(1)}, u32[]{:S(2)}, u32[]{:S(2)}) %collective-permute-start) | collective-permute-done | bytes 393248 | tf_op jit(solution)/shard_map/ppermute | solution.py:313
  12.9 3.1 %collective-permute-start.1 = (bf16[2,2,64,384]{3,2,1,0:T(8,128)(2,1)S(1)}, bf16[2,2,64,384]{3,2,1,0:T(8,128)(2,1)S(1)}, u32[]{:S(2)}, u32[]{:S(2)}) collective-permute-start(bf16[2,2,64,384]{3,2,1,0:T(8,128)(2,1)S(1)} %pad_maximum_fusion.1), channel_id=1, source_target_pairs={{0,7},{1,0},{2,1},{3,2},{4,3},{5,4},{6,5},{7,6},{8,15},{9,8},{10,9... | collective-permute-start | bytes 589832 | tf_op jit(solution)/shard_map/ppermute | solution.py:313
  16.1 4.2 %collective-permute-start.2 = (bf16[2,2,64,384]{3,2,1,0:T(8,128)(2,1)S(1)}, bf16[2,2,64,384]{3,2,1,0:T(8,128)(2,1)S(1)}, u32[]{:S(2)}, u32[]{:S(2)}) collective-permute-start(bf16[2,2,64,384]{3,2,1,0:T(8,128)(2,1)S(1)} %pad_maximum_fusion.2), channel_id=1, source_target_pairs={{0,24},{1,25},{2,26},{3,27},{4,28},{5,29},{6,30},{7,31},{8,0},{9,1... | collective-permute-start | bytes 589832 | tf_op jit(solution)/shard_map/ppermute | solution.py:313
  20.3 6.4 %collective-permute-start.3 = (bf16[2,2,64,384]{3,2,1,0:T(8,128)(2,1)S(1)}, bf16[2,2,64,384]{3,2,1,0:T(8,128)(2,1)S(1)}, u32[]{:S(2)}, u32[]{:S(2)}) collective-permute-start(bf16[2,2,64,384]{3,2,1,0:T(8,128)(2,1)S(1)} %pad_maximum_fusion.3), channel_id=1, source_target_pairs={{0,31},{1,24},{2,25},{3,26},{4,27},{5,28},{6,29},{7,30},{8,7},{9,0... | collective-permute-start | bytes 589832 | tf_op jit(solution)/shard_map/ppermute | solution.py:313
  26.7 5.7 %collective-permute-done.3.side_3 = bf16[2,2,64,384]{3,2,1,0:T(8,128)(2,1)S(1)} collective-permute-done((bf16[2,2,64,384]{3,2,1,0:T(8,128)(2,1)S(1)}, bf16[2,2,64,384]{3,2,1,0:T(8,128)(2,1)S(1)}, u32[]{:S(2)}, u32[]{:S(2)}) %collective-permute-start.3) | collective-permute-done | bytes 196640 | tf_op jit(solution)/shard_map/ppermute | solution.py:313
  32.4 21.2 %shard_map.102 = (bf16[2,2,64,384]{3,2,1,0:T(8,128)(2,1)S(1)}, bf16[2,2,64,384]{3,2,1,0:T(8,128)(2,1)S(1)}, bf16[2,2,64,384]{3,2,1,0:T(8,128)(2,1)S(1)}, bf16[2,...) custom-call(bf16[4,2,64,384]{3,2,1,0:T(8,128)(2,1)S(1)} %get-tuple-element.17.own, ...), custom_call_target="tpu_custom_call" | custom-call | flops 16000000000 | bytes 5000000 | tf_op jit(solution)/shard_map/pallas_call | solution.py:242
  53.6 13.7 %all_to_all.20.refs_0_ = bf16[2,2304,128]{2,1,0:T(8,128)(2,1)S(1)} all-to-all(bf16[2,2304,128]{2,1,0:T(8,128)(2,1)S(1)} %bitcast.14), channel_id=1, replica_groups=mesh['z_hi'=4,'z_lo'=2,'core'=2,'y_hi'=4,'y_lo'=2,'x'=4] {'core'}, dimensions={0} | all-to-all | bytes 2359296 | tf_op jit(solution)/shard_map/all_to_all | solution.py:277
  68.2 4.9 %all-to-all-start.1 = ((bf16[16,144,128]{2,1,0:T(8,128)(2,1)}), bf16[16,144,128]{2,1,0:T(8,128)(2,1)S(1)}, u32[]{:S(2)}, u32[]{:S(2)}) async-start(bf16[16,144,128]{2,1,0:T(8,128)(2,1)} %bitcast.6), calls=%async_computation.1 | async-start | bytes 1179648 | tf_op jit(solution)/shard_map/all_to_all | solution.py:279
  73.1 5.4 %collective-permute-start.4 = (bf16[2,2,64,384]{3,2,1,0:T(8,128)(2,1)S(1)}, bf16[2,2,64,384]{3,2,1,0:T(8,128)(2,1)S(1)}, u32[]{:S(2)}, u32[]{:S(2)}) collective-permute-start(bf16[2,2,64,384]{3,2,1,0:T(8,128)(2,1)S(1)} %get-tuple-element.20), channel_id=1, source_target_pairs={{7,0},{0,1},{1,2},{2,3},{3,4},{4,5},{5,6},{6,7},{15,8},{8,9},{9,10... | collective-permute-start | bytes 589832 | tf_op jit(solution)/shard_map/ppermute | solution.py:313
  78.5 3.8 %collective-permute-start.5 = (bf16[2,2,64,384]{3,2,1,0:T(8,128)(2,1)S(1)}, bf16[2,2,64,384]{3,2,1,0:T(8,128)(2,1)S(1)}, u32[]{:S(2)}, u32[]{:S(2)}) collective-permute-start(bf16[2,2,64,384]{3,2,1,0:T(8,128)(2,1)S(1)} %get-tuple-element.21), channel_id=1, source_target_pairs={{24,0},{25,1},{26,2},{27,3},{28,4},{29,5},{30,6},{31,7},{0,8},{1,9... | collective-permute-start | bytes 589832 | tf_op jit(solution)/shard_map/ppermute | solution.py:313
  82.2 2.1 %collective-permute-start.6 = (bf16[2,2,64,384]{3,2,1,0:T(8,128)(2,1)S(1)}, bf16[2,2,64,384]{3,2,1,0:T(8,128)(2,1)S(1)}, u32[]{:S(2)}, u32[]{:S(2)}) collective-permute-start(bf16[2,2,64,384]{3,2,1,0:T(8,128)(2,1)S(1)} %get-tuple-element.22), channel_id=1, source_target_pairs={{31,0},{24,1},{25,2},{26,3},{27,4},{28,5},{29,6},{30,7},{7,8},{0,9... | collective-permute-start | bytes 589832 | tf_op jit(solution)/shard_map/ppermute | solution.py:313
  84.4 2.7 %collective-permute-done.5.home_2.refs_2_ = bf16[2,2,64,384]{3,2,1,0:T(8,128)(2,1)S(1)} collective-permute-done((bf16[2,2,64,384]{3,2,1,0:T(8,128)(2,1)S(1)}, bf16[2,2,64,384]{3,2,1,0:T(8,128)(2,1)S(1)}, u32[]{:S(2)}, u32[]{:S(2)}) %collective-permute-start.5) | collective-permute-done | bytes 196640 | tf_op jit(solution)/shard_map/ppermute | solution.py:313
  87.1 5.8 %collective-permute-done.6.home_3.refs_3_ = bf16[2,2,64,384]{3,2,1,0:T(8,128)(2,1)S(1)} collective-permute-done((bf16[2,2,64,384]{3,2,1,0:T(8,128)(2,1)S(1)}, bf16[2,2,64,384]{3,2,1,0:T(8,128)(2,1)S(1)}, u32[]{:S(2)}, u32[]{:S(2)}) %collective-permute-start.6) | collective-permute-done | bytes 196640 | tf_op jit(solution)/shard_map/ppermute | solution.py:313
  93.8 4.8 %all-to-all-start.2 = ((bf16[16,144,128]{2,1,0:T(8,128)(2,1)}), bf16[16,144,128]{2,1,0:T(8,128)(2,1)S(1)}, u32[]{:S(2)}, u32[]{:S(2)}) async-start(bf16[16,144,128]{2,1,0:T(8,128)(2,1)} %shard_map.105), calls=%async_computation.2 | async-start | bytes 1179648 | tf_op jit(solution)/shard_map/all_to_all | solution.py:284
  98.7 4.5 %collective-permute-start.7 = (bf16[4,2,64,384]{3,2,1,0:T(8,128)(2,1)S(1)}, bf16[4,2,64,384]{3,2,1,0:T(8,128)(2,1)S(1)}, u32[]{:S(2)}, u32[]{:S(2)}) collective-permute-start(bf16[4,2,64,384]{3,2,1,0:T(8,128)(2,1)S(1)} %pad_maximum_fusion), channel_id=1, source_target_pairs={{480,0},{481,1},{482,2},{483,3},{484,4},{485,5},{486,6},{487,7},{4... | collective-permute-start | bytes 1179656 | tf_op jit(solution)/shard_map/ppermute | solution.py:313
  103.2 15.3 %collective-permute-done.7.ahead = bf16[4,2,64,384]{3,2,1,0:T(8,128)(2,1)S(1)} collective-permute-done((bf16[4,2,64,384]{3,2,1,0:T(8,128)(2,1)S(1)}, bf16[4,2,64,384]{3,2,1,0:T(8,128)(2,1)S(1)}, u32[]{:S(2)}, u32[]{:S(2)}) %collective-permute-start.7) | collective-permute-done | bytes 393248 | tf_op jit(solution)/shard_map/ppermute | solution.py:313
  118.5 2.4 %shard_map.103 = (bf16[512,384]{1,0:T(8,128)(2,1)}, bf16[512,384]{1,0:T(8,128)(2,1)}) custom-call(s32[1]{0:T(128)} %bitcast.odd.core, bf16[512,384]{1,0:T(8,128)(2,1)S(1)} %bitcast.11, s32[8,8,8]{2,1,0:T(8,128)S(1)} %copy-done.8, bf16[512,384]{1,0:T(8,128)(2,1)S(1)} %bitcast.13, bf16[2,2,64,384]{3,2,1,0:T(8,128)(2,1)S(1)} %get-tuple-element.19.home_0, ...), custom_call_target="tpu_custom_call" | custom-call | tf_op jit(solution)/shard_map/pallas_call | solution.py:335
  121.0 1.0 copy-done.5
  123.1 15.1 %all_to_all.21 = bf16[16,144,128]{2,1,0:T(8,128)(2,1)S(1)} all-to-all(bf16[16,144,128]{2,1,0:T(8,128)(2,1)S(1)} %shard_map.106), channel_id=1, replica_groups=mesh['z_hi'=4,'z_lo'=2,'core'=2,'y_hi'=4,'y_lo'=2,'x'=4] {'x','y_lo','z_..., dimensions={0} | all-to-all | bytes 1179648 | tf_op jit(solution)/shard_map/all_to_all | solution.py:288
  138.1 5.2 %collective-permute-start.8 = (bf16[2304,128]{1,0:T(8,128)(2,1)S(1)}, bf16[2304,128]{1,0:T(8,128)(2,1)S(1)}, u32[]{:S(2)}, u32[]{:S(2)}) collective-permute-start(bf16[2304,128]{1,0:T(8,128)(2,1)S(1)} %bitcast.8), channel_id=1, source_target_pairs={{0,32},{32,0},{1,33},{33,1},{2,34},{34,2},{3,35},{35,3},{4,36},{36... | collective-permute-start | bytes 1769480 | tf_op jit(solution)/shard_map/ppermute | solution.py:290
  143.3 1.6 %collective-permute-done.8.other = bf16[2304,128]{1,0:T(8,128)(2,1)S(1)} collective-permute-done((bf16[2304,128]{1,0:T(8,128)(2,1)S(1)}, bf16[2304,128]{1,0:T(8,128)(2,1)S(1)}, u32[]{:S(2)}, u32[]{:S(2)}) %collective-permute-start.8) | collective-permute-done | bytes 589856 | tf_op jit(solution)/shard_map/ppermute | solution.py:290
  144.9 1.8 %shard_map.107 = (f32[384,1152]{1,0:T(8,128)}, f32[384,384]{1,0:T(8,128)}, f32[1,384]{1,0:T(1,128)S(1)}) custom-call(s32[1]{0:T(128)} %bitcast.odd.core, bf16[2304,128]{1,0:T(8,128)(2,1)S(1)} %bitcast.9, bf16[2304,128]{1,0:T(8,128)(2,1)S(1)} %collective-permute-done.8.other, bf16[384,1152]{1,0:T(8,128)(2,1)S(1)} %copy-done.4, f32[1,384]{1,0:T(1,128)S(1)} %reshape.44.gain), custom_call_target="tpu_custom_call" | custom-call | tf_op jit(solution)/shard_map/pallas_call | solution.py:342
  (41 shorter events, 6.0 us)
Async XLA Ops:
  0.6 1.0 copy-start
  1.6 1.0 copy-start.2
  2.6 0.8 copy-start.7
  3.9 9.0 %collective-permute-start = (bf16[4,2,64,384]{3,2,1,0:T(8,128)(2,1)S(1)}, bf16[4,2,64,384]{3,2,1,0:T(8,128)(2,1)S(1)}, u32[]{:S(2)}, u32[]{:S(2)}) collective-permute-start(bf16[4,2,64,384]{3,2,1,0:T(8,128)(2,1)S(1)} %get-tuple-element.18), channel_id=1, source_target_pairs={{0,480},{1,481},{2,482},{3,483},{4,484},{5,485},{6,486},{7,487},{8... | collective-permute-start | bytes 1179656 | tf_op jit(solution)/shard_map/ppermute | solution.py:313
  10.8 15.9 %copy-start.10 = (f32[384]{0:T(512)S(1)}, f32[384]{0:T(512)}, u32[]{:S(2)}) copy-start(f32[384]{0:T(512)} %param.11) | copy-start | bytes 4612
  10.8 21.6 %copy-start.4 = (bf16[384,1152]{1,0:T(8,128)(2,1)S(1)}, bf16[384,1152]{1,0:T(8,128)(2,1)}, u32[]{:S(2)}) copy-start(bf16[384,1152]{1,0:T(8,128)(2,1)} %w_qkv.3) | copy-start | bytes 2654212
  10.8 21.6 %copy-start.9 = (bf16[384,384]{1,0:T(8,128)(2,1)S(1)}, bf16[384,384]{1,0:T(8,128)(2,1)}, u32[]{:S(2)}) copy-start(bf16[384,384]{1,0:T(8,128)(2,1)} %w_proj.1) | copy-start | bytes 884740
  12.9 13.8 %collective-permute-start.1 = (bf16[2,2,64,384]{3,2,1,0:T(8,128)(2,1)S(1)}, bf16[2,2,64,384]{3,2,1,0:T(8,128)(2,1)S(1)}, u32[]{:S(2)}, u32[]{:S(2)}) collective-permute-start(bf16[2,2,64,384]{3,2,1,0:T(8,128)(2,1)S(1)} %pad_maximum_fusion.1), channel_id=1, source_target_pairs={{0,7},{1,0},{2,1},{3,2},{4,3},{5,4},{6,5},{7,6},{8,15},{9,8},{10,9... | collective-permute-start | bytes 589832 | tf_op jit(solution)/shard_map/ppermute | solution.py:313
  16.1 10.7 %collective-permute-start.2 = (bf16[2,2,64,384]{3,2,1,0:T(8,128)(2,1)S(1)}, bf16[2,2,64,384]{3,2,1,0:T(8,128)(2,1)S(1)}, u32[]{:S(2)}, u32[]{:S(2)}) collective-permute-start(bf16[2,2,64,384]{3,2,1,0:T(8,128)(2,1)S(1)} %pad_maximum_fusion.2), channel_id=1, source_target_pairs={{0,24},{1,25},{2,26},{3,27},{4,28},{5,29},{6,30},{7,31},{8,0},{9,1... | collective-permute-start | bytes 589832 | tf_op jit(solution)/shard_map/ppermute | solution.py:313
  20.3 12.1 %collective-permute-start.3 = (bf16[2,2,64,384]{3,2,1,0:T(8,128)(2,1)S(1)}, bf16[2,2,64,384]{3,2,1,0:T(8,128)(2,1)S(1)}, u32[]{:S(2)}, u32[]{:S(2)}) collective-permute-start(bf16[2,2,64,384]{3,2,1,0:T(8,128)(2,1)S(1)} %pad_maximum_fusion.3), channel_id=1, source_target_pairs={{0,31},{1,24},{2,25},{3,26},{4,27},{5,28},{6,29},{7,30},{8,7},{9,0... | collective-permute-start | bytes 589832 | tf_op jit(solution)/shard_map/ppermute | solution.py:313
  68.2 24.6 %all-to-all-start.1 = ((bf16[16,144,128]{2,1,0:T(8,128)(2,1)}), bf16[16,144,128]{2,1,0:T(8,128)(2,1)S(1)}, u32[]{:S(2)}, u32[]{:S(2)}) async-start(bf16[16,144,128]{2,1,0:T(8,128)(2,1)} %bitcast.6), calls=%async_computation.1 | async-start | bytes 1179648 | tf_op jit(solution)/shard_map/all_to_all | solution.py:279
  73.1 11.3 %collective-permute-start.4 = (bf16[2,2,64,384]{3,2,1,0:T(8,128)(2,1)S(1)}, bf16[2,2,64,384]{3,2,1,0:T(8,128)(2,1)S(1)}, u32[]{:S(2)}, u32[]{:S(2)}) collective-permute-start(bf16[2,2,64,384]{3,2,1,0:T(8,128)(2,1)S(1)} %get-tuple-element.20), channel_id=1, source_target_pairs={{7,0},{0,1},{1,2},{2,3},{3,4},{4,5},{5,6},{6,7},{15,8},{8,9},{9,10... | collective-permute-start | bytes 589832 | tf_op jit(solution)/shard_map/ppermute | solution.py:313
  78.5 8.6 %collective-permute-start.5 = (bf16[2,2,64,384]{3,2,1,0:T(8,128)(2,1)S(1)}, bf16[2,2,64,384]{3,2,1,0:T(8,128)(2,1)S(1)}, u32[]{:S(2)}, u32[]{:S(2)}) collective-permute-start(bf16[2,2,64,384]{3,2,1,0:T(8,128)(2,1)S(1)} %get-tuple-element.21), channel_id=1, source_target_pairs={{24,0},{25,1},{26,2},{27,3},{28,4},{29,5},{30,6},{31,7},{0,8},{1,9... | collective-permute-start | bytes 589832 | tf_op jit(solution)/shard_map/ppermute | solution.py:313
  82.2 10.6 %collective-permute-start.6 = (bf16[2,2,64,384]{3,2,1,0:T(8,128)(2,1)S(1)}, bf16[2,2,64,384]{3,2,1,0:T(8,128)(2,1)S(1)}, u32[]{:S(2)}, u32[]{:S(2)}) collective-permute-start(bf16[2,2,64,384]{3,2,1,0:T(8,128)(2,1)S(1)} %get-tuple-element.22), channel_id=1, source_target_pairs={{31,0},{24,1},{25,2},{26,3},{27,4},{28,5},{29,6},{30,7},{7,8},{0,9... | collective-permute-start | bytes 589832 | tf_op jit(solution)/shard_map/ppermute | solution.py:313
  93.8 24.8 %copy-start.1 = (bf16[8,8,8,384]{3,2,1,0:T(8,128)(2,1)S(1)}, bf16[8,8,8,384]{3,2,1,0:T(8,128)(2,1)}, u32[]{:S(2)}) copy-start(bf16[8,8,8,384]{3,2,1,0:T(8,128)(2,1)} %param.6) | copy-start | bytes 1179652
  93.8 24.8 %copy-start.3 = (bf16[8,8,8,384]{3,2,1,0:T(8,128)(2,1)S(1)}, bf16[8,8,8,384]{3,2,1,0:T(8,128)(2,1)}, u32[]{:S(2)}) copy-start(bf16[8,8,8,384]{3,2,1,0:T(8,128)(2,1)} %param.8) | copy-start | bytes 1179652
  93.8 24.8 %copy-start.8 = (s32[8,8,8]{2,1,0:T(8,128)S(1)}, s32[8,8,8]{2,1,0:T(8,128)}, u32[]{:S(2)}) copy-start(s32[8,8,8]{2,1,0:T(8,128)} %frozen.3) | copy-start | bytes 6148
  93.8 27.2 %all-to-all-start.2 = ((bf16[16,144,128]{2,1,0:T(8,128)(2,1)}), bf16[16,144,128]{2,1,0:T(8,128)(2,1)S(1)}, u32[]{:S(2)}, u32[]{:S(2)}) async-start(bf16[16,144,128]{2,1,0:T(8,128)(2,1)} %shard_map.105), calls=%async_computation.2 | async-start | bytes 1179648 | tf_op jit(solution)/shard_map/all_to_all | solution.py:284
  98.7 19.8 %collective-permute-start.7 = (bf16[4,2,64,384]{3,2,1,0:T(8,128)(2,1)S(1)}, bf16[4,2,64,384]{3,2,1,0:T(8,128)(2,1)S(1)}, u32[]{:S(2)}, u32[]{:S(2)}) collective-permute-start(bf16[4,2,64,384]{3,2,1,0:T(8,128)(2,1)S(1)} %pad_maximum_fusion), channel_id=1, source_target_pairs={{480,0},{481,1},{482,2},{483,3},{484,4},{485,5},{486,6},{487,7},{4... | collective-permute-start | bytes 1179656 | tf_op jit(solution)/shard_map/ppermute | solution.py:313
  121.0 1.0 copy-start.5
  122.0 1.0 copy-start.6
  138.1 6.8 %collective-permute-start.8 = (bf16[2304,128]{1,0:T(8,128)(2,1)S(1)}, bf16[2304,128]{1,0:T(8,128)(2,1)S(1)}, u32[]{:S(2)}, u32[]{:S(2)}) collective-permute-start(bf16[2304,128]{1,0:T(8,128)(2,1)S(1)} %bitcast.8), channel_id=1, source_target_pairs={{0,32},{32,0},{1,33},{33,1},{2,34},{34,2},{3,35},{35,3},{4,36},{36... | collective-permute-start | bytes 1769480 | tf_op jit(solution)/shard_map/ppermute | solution.py:290

commit v4 on v3

--- a/solution.py
+++ b/solution.py
@@ -149,7 +149,17 @@
     ]
 
 
-def cut_kernel(odd, tokens, frozen, cotangent, own, ahead):
+def cut_kernel(odd, tokens_in, frozen_in, cotangent_in, own, ahead, tokens, frozen, cotangent, arrivals):
+    moves = [
+        pltpu.make_async_copy(source, target, arrivals.at[index])
+        for index, (source, target) in enumerate(
+            ((frozen_in, frozen), (tokens_in, tokens), (cotangent_in, cotangent))
+        )
+    ]
+    for move in moves:
+        move.start()
+    for move in moves:
+        move.wait()
     keeps = keep_rows(frozen)
     for upper, target in ((0, ahead), (1, own)):
         matrix = ones_where(order(odd[0], upper, False))
@@ -232,7 +242,7 @@
         target[:, columns] = found
         if block < 9:
             weighted = weighted + found * w_qkv[:, columns].astype(F32)
-    gain_grad[...] = jnp.sum(weighted.T, axis=0, keepdims=True) / gain[...]
+    gain_grad[...] = (jnp.sum(weighted.T, axis=0, keepdims=True) / gain[...]).reshape(D)
 
 
 def window_pass(own, behind, sides, w_qkv, w_proj, norm_gain):
@@ -269,8 +279,8 @@
 THIRD = ("y_lo", "x")
 SIZES = {"z_hi": 4, "z_lo": 2, "core": 2, "y_hi": 4, "y_lo": 2, "x": 4}
 NEAR = ("x", "y_lo", "z_lo")
-FAR = ("y_hi", "z_hi")
 GROUP = 16
+FAR = 4
 
 
 def near_sum(rows):
@@ -280,8 +290,8 @@
     return parts
 
 
-def far_sum(parts, after):
-    return lax.all_to_all(total_of(parts, GROUP, after), FAR, 0, 0)
+def far_sum(parts, axis, after=()):
+    return lax.all_to_all(total_of(parts, FAR, after), axis, 0, 0)
 
 
 def spread_sum(parts, after):
@@ -319,8 +329,14 @@
     own, ahead = pl.pallas_call(
         cut_kernel,
         out_shape=(jax.ShapeDtypeStruct((4, 2, PIECE, D), BF),) * 2,
-        in_specs=[SCALAR, WHOLE, WHOLE, WHOLE],
-        compiler_params=SMALL,
+        in_specs=[SCALAR] + [pl.BlockSpec(memory_space=pltpu.HBM)] * 3,
+        scratch_shapes=[
+            pltpu.VMEM((ROWS, D), BF),
+            pltpu.VMEM((WIN, WIN, WIN), jnp.int32),
+            pltpu.VMEM((ROWS, D), BF),
+            pltpu.SemaphoreType.DMA((3,)),
+        ],
+        compiler_params=pltpu.CompilerParams(vmem_limit_bytes=56 * 1024 * 1024),
     )(core, token_rows, frozen, cot_rows)
     behind = send(ahead, 0)
     sides = [None] * 4
@@ -330,7 +346,7 @@
     parts = near_sum(grads)
     for kind in (3, 2, 1):
         backs[kind] = send(backs[kind], kind, True)
-    parts = far_sum(parts, backs[1:])
+    parts = far_sum(far_sum(parts, "y_hi"), "z_hi", backs[1:])
     ahead = send(jnp.stack([back[1] for back in backs]), 0, True)
     block_out, tokens_grad = pl.pallas_call(
         join_kernel,
@@ -338,19 +354,19 @@
         in_specs=[SCALAR] + [WHOLE] * 8,
         compiler_params=SMALL,
     )(core, token_rows, frozen, cot_rows, *backs, ahead)
-    mine, other = spread_sum(parts, (block_out, tokens_grad))
+    mine, other = spread_sum(parts, (ahead,))
     qkv_grad, proj_grad, gain_grad = pl.pallas_call(
         grads_kernel,
         out_shape=(
             jax.ShapeDtypeStruct((D, 3 * D), F32),
             jax.ShapeDtypeStruct((D, D), F32),
-            jax.ShapeDtypeStruct((1, D), F32),
+            jax.ShapeDtypeStruct((D,), F32),
         ),
         in_specs=[SCALAR] + [WHOLE] * 4,
         compiler_params=SMALL,
     )(core, mine, other, w_qkv, norm_gain.reshape(1, D))
     shape = (WIN, WIN, WIN, D)
-    return block_out.reshape(shape), tokens_grad.reshape(shape), qkv_grad, proj_grad, gain_grad.reshape(D)
+    return block_out.reshape(shape), tokens_grad.reshape(shape), qkv_grad, proj_grad, gain_grad
 
 
 def solution(mesh):

time: 148 us -> 144 us (0.973)
  waiting for transfers between devices: 33.2 us -> 26.5 us
  blocking collectives: 28.7 us -> 33.3 us
  local copies, waits for them, and re-layouts: 4.87 us -> 1.25 us
  Pallas kernels: 27.8 us -> 30.2 us
    ppermute x8, waiting for transfers between devices: 31.6 us -> 15.3 us  [send(): return lax.ppermute(block, LATTICE, route(kind, back))]
    all_to_all x1 -> x2, waiting for transfers between devices: 0.01 us -> 11.3 us  [far_sum(): return lax.all_to_all(total_of(parts, FAR, after), axis, 0, 0)]
    unnamed x22 -> x14, local copies, waits for them, and re-layouts: 4.76 us -> 0.03 us
    all_to_all x1, blocking collectives: 15.1 us -> 19.5 us  [spread_sum(): parts = lax.all_to_all(total_of(parts, GROUP, after), NEAR, 0, 0)]
    all_to_all x1 -> x2, starting transfers between devices: 4.76 us -> 6.95 us  [far_sum(): return lax.all_to_all(total_of(parts, FAR, after), axis, 0, 0)]
    pallas_call x1, Pallas kernels: 0.47 us -> 2.41 us  [local(): pl.pallas_call(cut_kernel, out_shape=(jax.ShapeDtypeStruct((4, 2, PIECE,...]
    ppermute x1, waiting for transfers between devices: 1.61 us -> 0.01 us  [spread_sum(): return (mine, lax.ppermute(mine, 'core', [(0, 1), (1, 0)]))]
  transfers between devices with their start and end apart: 11 -> 12, of which waited for: 6 -> 6; matrix products, arithmetic and copies ran while one was open for 0% -> 1% of each run, Pallas kernels for 2% -> 2%
where the time goes in v4:
time: 144 us
  starting transfers between devices  51.2 us (36%)
  blocking collectives  33.3 us (23%)
  Pallas kernels  30.2 us (21%)
  waiting for transfers between devices  26.5 us (18%)
    ppermute x8, starting transfers between devices, send(): return lax.ppermute(block, LATTICE, route(kind, back))  35.4 us
    pallas_call x1, Pallas kernels, window_pass(): pl.pallas_call(window_kernel, out_shape=(jax.ShapeDtypeStruct((2, 2, PIEC...  21.2 us
    all_to_all x1, blocking collectives, spread_sum(): parts = lax.all_to_all(total_of(parts, GROUP, after), NEAR, 0, 0)  19.5 us
    ppermute x8, waiting for transfers between devices, send(): return lax.ppermute(block, LATTICE, route(kind, back))  15.3 us
    all_to_all x1, blocking collectives, near_sum(): lax.all_to_all(rows.reshape(2, GRAD_ROWS // 2, LANES), 'core', 0, 0)  13.8 us
    all_to_all x2, waiting for transfers between devices, far_sum(): return lax.all_to_all(total_of(parts, FAR, after), axis, 0, 0)  11.3 us
    all_to_all x2, starting transfers between devices, far_sum(): return lax.all_to_all(total_of(parts, FAR, after), axis, 0, 0)  6.95 us
    all_to_all x1, starting transfers between devices, near_sum(): parts = lax.all_to_all(parts, NEAR, 0, 0)  4.85 us
  transfers between devices with their start and end apart: 12, of which 6 were waited for; matrix products, arithmetic and copies ran while one was open for 1% of the time, Pallas kernels for 2%

profile of v4, /device:TPU:1, one launch (start us, length us, event | category | flops | bytes accessed | tf_op | source)
XLA Modules:
  0.0 143.5 jit_solution(18229589752375437067)
XLA Ops:
  0.6 2.4 %shard_map.101 = (bf16[4,2,64,384]{3,2,1,0:T(8,128)(2,1)}, bf16[4,2,64,384]{3,2,1,0:T(8,128)(2,1)}) custom-call(s32[1]{0:T(128)} %bitcast.odd.core, bf16[512,384]{1,0:T(8,128)(2,1)} %bitcast.10, s32[8,8,8]{2,1,0:T(8,128)} %frozen.1, bf16[512,384]{1,0:T(8,128)(2,1)} %bitcast.12), custom_call_target="tpu_custom_call" | custom-call | tf_op jit(solution)/shard_map/pallas_call | solution.py:329
  3.1 6.9 %collective-permute-start = (bf16[4,2,64,384]{3,2,1,0:T(8,128)(2,1)}, bf16[4,2,64,384]{3,2,1,0:T(8,128)(2,1)S(1)}, u32[]{:S(2)}, u32[]{:S(2)}) collective-permute-start(bf16[4,2,64,384]{3,2,1,0:T(8,128)(2,1)} %get-tuple-element.18), channel_id=1, source_target_pairs={{0,480},{1,481},{2,482},{3,483},{4,484},{5,485},{6,486},{7,487},{8... | collective-permute-start | bytes 1179656 | tf_op jit(solution)/shard_map/ppermute | solution.py:323
  10.0 1.1 fusion
  12.3 3.1 %collective-permute-start.1 = (bf16[2,2,64,384]{3,2,1,0:T(8,128)(2,1)S(1)}, bf16[2,2,64,384]{3,2,1,0:T(8,128)(2,1)S(1)}, u32[]{:S(2)}, u32[]{:S(2)}) collective-permute-start(bf16[2,2,64,384]{3,2,1,0:T(8,128)(2,1)S(1)} %pad_maximum_fusion.1), channel_id=1, source_target_pairs={{0,7},{1,0},{2,1},{3,2},{4,3},{5,4},{6,5},{7,6},{8,15},{9,8},{10,9... | collective-permute-start | bytes 589832 | tf_op jit(solution)/shard_map/ppermute | solution.py:323
  15.5 4.2 %collective-permute-start.2 = (bf16[2,2,64,384]{3,2,1,0:T(8,128)(2,1)S(1)}, bf16[2,2,64,384]{3,2,1,0:T(8,128)(2,1)S(1)}, u32[]{:S(2)}, u32[]{:S(2)}) collective-permute-start(bf16[2,2,64,384]{3,2,1,0:T(8,128)(2,1)S(1)} %pad_maximum_fusion.2), channel_id=1, source_target_pairs={{0,24},{1,25},{2,26},{3,27},{4,28},{5,29},{6,30},{7,31},{8,0},{9,1... | collective-permute-start | bytes 589832 | tf_op jit(solution)/shard_map/ppermute | solution.py:323
  19.7 6.4 %collective-permute-start.3 = (bf16[2,2,64,384]{3,2,1,0:T(8,128)(2,1)S(1)}, bf16[2,2,64,384]{3,2,1,0:T(8,128)(2,1)S(1)}, u32[]{:S(2)}, u32[]{:S(2)}) collective-permute-start(bf16[2,2,64,384]{3,2,1,0:T(8,128)(2,1)S(1)} %pad_maximum_fusion.3), channel_id=1, source_target_pairs={{0,31},{1,24},{2,25},{3,26},{4,27},{5,28},{6,29},{7,30},{8,7},{9,0... | collective-permute-start | bytes 589832 | tf_op jit(solution)/shard_map/ppermute | solution.py:323
  26.1 5.7 %collective-permute-done.3.side_3 = bf16[2,2,64,384]{3,2,1,0:T(8,128)(2,1)S(1)} collective-permute-done((bf16[2,2,64,384]{3,2,1,0:T(8,128)(2,1)S(1)}, bf16[2,2,64,384]{3,2,1,0:T(8,128)(2,1)S(1)}, u32[]{:S(2)}, u32[]{:S(2)}) %collective-permute-start.3) | collective-permute-done | bytes 196640 | tf_op jit(solution)/shard_map/ppermute | solution.py:323
  31.8 21.2 %shard_map.102 = (bf16[2,2,64,384]{3,2,1,0:T(8,128)(2,1)S(1)}, bf16[2,2,64,384]{3,2,1,0:T(8,128)(2,1)S(1)}, bf16[2,2,64,384]{3,2,1,0:T(8,128)(2,1)S(1)}, bf16[2,...) custom-call(bf16[4,2,64,384]{3,2,1,0:T(8,128)(2,1)S(1)} %copy-done.3, ...), custom_call_target="tpu_custom_call" | custom-call | flops 16000000000 | bytes 5000000 | tf_op jit(solution)/shard_map/pallas_call | solution.py:252
  53.0 13.8 %all_to_all.25.refs_0_ = bf16[2,2304,128]{2,1,0:T(8,128)(2,1)S(1)} all-to-all(bf16[2,2304,128]{2,1,0:T(8,128)(2,1)S(1)} %bitcast.14), channel_id=1, replica_groups=mesh['z_hi'=4,'z_lo'=2,'core'=2,'y_hi'=4,'y_lo'=2,'x'=4] {'core'}, dimensions={0} | all-to-all | bytes 2359296 | tf_op jit(solution)/shard_map/all_to_all | solution.py:287
  67.7 4.9 %all-to-all-start.1 = ((bf16[16,144,128]{2,1,0:T(8,128)(2,1)}), bf16[16,144,128]{2,1,0:T(8,128)(2,1)S(1)}, u32[]{:S(2)}, u32[]{:S(2)}) async-start(bf16[16,144,128]{2,1,0:T(8,128)(2,1)} %bitcast.6), calls=%async_computation.1 | async-start | bytes 1179648 | tf_op jit(solution)/shard_map/all_to_all | solution.py:289
  72.6 5.4 %collective-permute-start.4 = (bf16[2,2,64,384]{3,2,1,0:T(8,128)(2,1)S(1)}, bf16[2,2,64,384]{3,2,1,0:T(8,128)(2,1)S(1)}, u32[]{:S(2)}, u32[]{:S(2)}) collective-permute-start(bf16[2,2,64,384]{3,2,1,0:T(8,128)(2,1)S(1)} %get-tuple-element.20), channel_id=1, source_target_pairs={{7,0},{0,1},{1,2},{2,3},{3,4},{4,5},{5,6},{6,7},{15,8},{8,9},{9,10... | collective-permute-start | bytes 589832 | tf_op jit(solution)/shard_map/ppermute | solution.py:323
  78.0 3.8 %collective-permute-start.5 = (bf16[2,2,64,384]{3,2,1,0:T(8,128)(2,1)S(1)}, bf16[2,2,64,384]{3,2,1,0:T(8,128)(2,1)S(1)}, u32[]{:S(2)}, u32[]{:S(2)}) collective-permute-start(bf16[2,2,64,384]{3,2,1,0:T(8,128)(2,1)S(1)} %get-tuple-element.21), channel_id=1, source_target_pairs={{24,0},{25,1},{26,2},{27,3},{28,4},{29,5},{30,6},{31,7},{0,8},{1,9... | collective-permute-start | bytes 589832 | tf_op jit(solution)/shard_map/ppermute | solution.py:323
  81.8 2.1 %collective-permute-start.6 = (bf16[2,2,64,384]{3,2,1,0:T(8,128)(2,1)S(1)}, bf16[2,2,64,384]{3,2,1,0:T(8,128)(2,1)S(1)}, u32[]{:S(2)}, u32[]{:S(2)}) collective-permute-start(bf16[2,2,64,384]{3,2,1,0:T(8,128)(2,1)S(1)} %get-tuple-element.22), channel_id=1, source_target_pairs={{31,0},{24,1},{25,2},{26,3},{27,4},{28,5},{29,6},{30,7},{7,8},{0,9... | collective-permute-start | bytes 589832 | tf_op jit(solution)/shard_map/ppermute | solution.py:323
  83.9 2.7 %collective-permute-done.5.home_2.refs_2_ = bf16[2,2,64,384]{3,2,1,0:T(8,128)(2,1)S(1)} collective-permute-done((bf16[2,2,64,384]{3,2,1,0:T(8,128)(2,1)S(1)}, bf16[2,2,64,384]{3,2,1,0:T(8,128)(2,1)S(1)}, u32[]{:S(2)}, u32[]{:S(2)}) %collective-permute-start.5) | collective-permute-done | bytes 196640 | tf_op jit(solution)/shard_map/ppermute | solution.py:323
  86.6 5.8 %collective-permute-done.6.home_3.refs_3_ = bf16[2,2,64,384]{3,2,1,0:T(8,128)(2,1)S(1)} collective-permute-done((bf16[2,2,64,384]{3,2,1,0:T(8,128)(2,1)S(1)}, bf16[2,2,64,384]{3,2,1,0:T(8,128)(2,1)S(1)}, u32[]{:S(2)}, u32[]{:S(2)}) %collective-permute-start.6) | collective-permute-done | bytes 196640 | tf_op jit(solution)/shard_map/ppermute | solution.py:323
  93.1 3.6 %all-to-all-start.2 = ((bf16[4,144,128]{2,1,0:T(8,128)(2,1)}), bf16[4,144,128]{2,1,0:T(8,128)(2,1)S(1)}, u32[]{:S(2)}, u32[]{:S(2)}) async-start(bf16[4,144,128]{2,1,0:T(8,128)(2,1)} %shard_map.105), calls=%async_computation.2 | async-start | bytes 294912 | tf_op jit(solution)/shard_map/all_to_all | solution.py:294
  96.8 3.6 %collective-permute-start.7 = (bf16[4,2,64,384]{3,2,1,0:T(8,128)(2,1)S(1)}, bf16[4,2,64,384]{3,2,1,0:T(8,128)(2,1)S(1)}, u32[]{:S(2)}, u32[]{:S(2)}) collective-permute-start(bf16[4,2,64,384]{3,2,1,0:T(8,128)(2,1)S(1)} %pad_maximum_fusion), channel_id=1, source_target_pairs={{480,0},{481,1},{482,2},{483,3},{484,4},{485,5},{486,6},{487,7},{4... | collective-permute-start | bytes 1179656 | tf_op jit(solution)/shard_map/ppermute | solution.py:323
  100.4 3.6 %all-to-all-done.2.refs_0_ = bf16[4,144,128]{2,1,0:T(8,128)(2,1)S(1)} async-done(((bf16[4,144,128]{2,1,0:T(8,128)(2,1)}), bf16[4,144,128]{2,1,0:T(8,128)(2,1)S(1)}, u32[]{:S(2)}, u32[]{:S(2)}) %all-to-all-start.2) | async-done | bytes 147488 | tf_op jit(solution)/shard_map/all_to_all | solution.py:294
  104.8 3.3 %all-to-all-start.3 = ((bf16[4,144,128]{2,1,0:T(8,128)(2,1)}), bf16[4,144,128]{2,1,0:T(8,128)(2,1)S(1)}, u32[]{:S(2)}, u32[]{:S(2)}) async-start(bf16[4,144,128]{2,1,0:T(8,128)(2,1)} %shard_map.106), calls=%async_computation.3 | async-start | bytes 294912 | tf_op jit(solution)/shard_map/all_to_all | solution.py:294
  108.2 7.6 %all-to-all-done.3.refs_0_ = bf16[4,144,128]{2,1,0:T(8,128)(2,1)S(1)} async-done(((bf16[4,144,128]{2,1,0:T(8,128)(2,1)}), bf16[4,144,128]{2,1,0:T(8,128)(2,1)S(1)}, u32[]{:S(2)}, u32[]{:S(2)}) %all-to-all-start.3) | async-done | bytes 147488 | tf_op jit(solution)/shard_map/all_to_all | solution.py:294
  115.8 19.5 %all_to_all.26 = bf16[16,144,128]{2,1,0:T(8,128)(2,1)S(1)} all-to-all(bf16[16,144,128]{2,1,0:T(8,128)(2,1)S(1)} %shard_map.107), channel_id=1, replica_groups=mesh['z_hi'=4,'z_lo'=2,'core'=2,'y_hi'=4,'y_lo'=2,'x'=4] {'x','y_lo','z_..., dimensions={0} | all-to-all | bytes 1179648 | tf_op jit(solution)/shard_map/all_to_all | solution.py:298
  135.3 3.9 %collective-permute-start.8 = (bf16[2304,128]{1,0:T(8,128)(2,1)S(1)}, bf16[2304,128]{1,0:T(8,128)(2,1)S(1)}, u32[]{:S(2)}, u32[]{:S(2)}) collective-permute-start(bf16[2304,128]{1,0:T(8,128)(2,1)S(1)} %bitcast.8), channel_id=1, source_target_pairs={{0,32},{32,0},{1,33},{33,1},{2,34},{34,2},{3,35},{35,3},{4,36},{36... | collective-permute-start | bytes 1769480 | tf_op jit(solution)/shard_map/ppermute | solution.py:300
  139.3 2.4 %shard_map.103 = (bf16[512,384]{1,0:T(8,128)(2,1)}, bf16[512,384]{1,0:T(8,128)(2,1)}) custom-call(s32[1]{0:T(128)} %bitcast.odd.core, bf16[512,384]{1,0:T(8,128)(2,1)S(1)} %bitcast.11, s32[8,8,8]{2,1,0:T(8,128)S(1)} %copy-done.4, bf16[512,384]{1,0:T(8,128)(2,1)S(1)} %bitcast.13, bf16[2,2,64,384]{3,2,1,0:T(8,128)(2,1)S(1)} %get-tuple-element.19.home_0, ...), custom_call_target="tpu_custom_call" | custom-call | tf_op jit(solution)/shard_map/pallas_call | solution.py:351
  141.7 1.8 %shard_map.108 = (f32[384,1152]{1,0:T(8,128)}, f32[384,384]{1,0:T(8,128)}, f32[384]{0:T(512)}) custom-call(s32[1]{0:T(128)} %bitcast.odd.core, bf16[2304,128]{1,0:T(8,128)(2,1)S(1)} %bitcast.9, bf16[2304,128]{1,0:T(8,128)(2,1)S(1)} %collective-permute-done.8.other, bf16[384,1152]{1,0:T(8,128)(2,1)S(1)} %copy-done.2, f32[1,384]{1,0:T(1,128)S(1)} %reshape.41.gain), custom_call_target="tpu_custom_call" | custom-call | tf_op jit(solution)/shard_map/pallas_call | solution.py:358
  (35 shorter events, 3.8 us)
Async XLA Ops:
  3.1 9.2 %collective-permute-start = (bf16[4,2,64,384]{3,2,1,0:T(8,128)(2,1)}, bf16[4,2,64,384]{3,2,1,0:T(8,128)(2,1)S(1)}, u32[]{:S(2)}, u32[]{:S(2)}) collective-permute-start(bf16[4,2,64,384]{3,2,1,0:T(8,128)(2,1)} %get-tuple-element.18), channel_id=1, source_target_pairs={{0,480},{1,481},{2,482},{3,483},{4,484},{5,485},{6,486},{7,487},{8... | collective-permute-start | bytes 1179656 | tf_op jit(solution)/shard_map/ppermute | solution.py:323
  9.9 16.1 %copy-start.6 = (f32[384]{0:T(512)S(1)}, f32[384]{0:T(512)}, u32[]{:S(2)}) copy-start(f32[384]{0:T(512)} %param.11) | copy-start | bytes 4612
  9.9 21.9 %copy-start.2 = (bf16[384,1152]{1,0:T(8,128)(2,1)S(1)}, bf16[384,1152]{1,0:T(8,128)(2,1)}, u32[]{:S(2)}) copy-start(bf16[384,1152]{1,0:T(8,128)(2,1)} %w_qkv.3) | copy-start | bytes 2654212
  9.9 21.9 %copy-start.3 = (bf16[4,2,64,384]{3,2,1,0:T(8,128)(2,1)S(1)}, bf16[4,2,64,384]{3,2,1,0:T(8,128)(2,1)}, u32[]{:S(2)}) copy-start(bf16[4,2,64,384]{3,2,1,0:T(8,128)(2,1)} %get-tuple-element.17.own) | copy-start | bytes 1179652
  10.0 21.9 %copy-start.5 = (bf16[384,384]{1,0:T(8,128)(2,1)S(1)}, bf16[384,384]{1,0:T(8,128)(2,1)}, u32[]{:S(2)}) copy-start(bf16[384,384]{1,0:T(8,128)(2,1)} %w_proj.1) | copy-start | bytes 884740
  12.3 13.8 %collective-permute-start.1 = (bf16[2,2,64,384]{3,2,1,0:T(8,128)(2,1)S(1)}, bf16[2,2,64,384]{3,2,1,0:T(8,128)(2,1)S(1)}, u32[]{:S(2)}, u32[]{:S(2)}) collective-permute-start(bf16[2,2,64,384]{3,2,1,0:T(8,128)(2,1)S(1)} %pad_maximum_fusion.1), channel_id=1, source_target_pairs={{0,7},{1,0},{2,1},{3,2},{4,3},{5,4},{6,5},{7,6},{8,15},{9,8},{10,9... | collective-permute-start | bytes 589832 | tf_op jit(solution)/shard_map/ppermute | solution.py:323
  15.5 10.7 %collective-permute-start.2 = (bf16[2,2,64,384]{3,2,1,0:T(8,128)(2,1)S(1)}, bf16[2,2,64,384]{3,2,1,0:T(8,128)(2,1)S(1)}, u32[]{:S(2)}, u32[]{:S(2)}) collective-permute-start(bf16[2,2,64,384]{3,2,1,0:T(8,128)(2,1)S(1)} %pad_maximum_fusion.2), channel_id=1, source_target_pairs={{0,24},{1,25},{2,26},{3,27},{4,28},{5,29},{6,30},{7,31},{8,0},{9,1... | collective-permute-start | bytes 589832 | tf_op jit(solution)/shard_map/ppermute | solution.py:323
  19.7 12.1 %collective-permute-start.3 = (bf16[2,2,64,384]{3,2,1,0:T(8,128)(2,1)S(1)}, bf16[2,2,64,384]{3,2,1,0:T(8,128)(2,1)S(1)}, u32[]{:S(2)}, u32[]{:S(2)}) collective-permute-start(bf16[2,2,64,384]{3,2,1,0:T(8,128)(2,1)S(1)} %pad_maximum_fusion.3), channel_id=1, source_target_pairs={{0,31},{1,24},{2,25},{3,26},{4,27},{5,28},{6,29},{7,30},{8,7},{9,0... | collective-permute-start | bytes 589832 | tf_op jit(solution)/shard_map/ppermute | solution.py:323
  67.7 24.7 %all-to-all-start.1 = ((bf16[16,144,128]{2,1,0:T(8,128)(2,1)}), bf16[16,144,128]{2,1,0:T(8,128)(2,1)S(1)}, u32[]{:S(2)}, u32[]{:S(2)}) async-start(bf16[16,144,128]{2,1,0:T(8,128)(2,1)} %bitcast.6), calls=%async_computation.1 | async-start | bytes 1179648 | tf_op jit(solution)/shard_map/all_to_all | solution.py:289
  72.6 11.3 %collective-permute-start.4 = (bf16[2,2,64,384]{3,2,1,0:T(8,128)(2,1)S(1)}, bf16[2,2,64,384]{3,2,1,0:T(8,128)(2,1)S(1)}, u32[]{:S(2)}, u32[]{:S(2)}) collective-permute-start(bf16[2,2,64,384]{3,2,1,0:T(8,128)(2,1)S(1)} %get-tuple-element.20), channel_id=1, source_target_pairs={{7,0},{0,1},{1,2},{2,3},{3,4},{4,5},{5,6},{6,7},{15,8},{8,9},{9,10... | collective-permute-start | bytes 589832 | tf_op jit(solution)/shard_map/ppermute | solution.py:323
  78.0 8.6 %collective-permute-start.5 = (bf16[2,2,64,384]{3,2,1,0:T(8,128)(2,1)S(1)}, bf16[2,2,64,384]{3,2,1,0:T(8,128)(2,1)S(1)}, u32[]{:S(2)}, u32[]{:S(2)}) collective-permute-start(bf16[2,2,64,384]{3,2,1,0:T(8,128)(2,1)S(1)} %get-tuple-element.21), channel_id=1, source_target_pairs={{24,0},{25,1},{26,2},{27,3},{28,4},{29,5},{30,6},{31,7},{0,8},{1,9... | collective-permute-start | bytes 589832 | tf_op jit(solution)/shard_map/ppermute | solution.py:323
  81.8 10.6 %collective-permute-start.6 = (bf16[2,2,64,384]{3,2,1,0:T(8,128)(2,1)S(1)}, bf16[2,2,64,384]{3,2,1,0:T(8,128)(2,1)S(1)}, u32[]{:S(2)}, u32[]{:S(2)}) collective-permute-start(bf16[2,2,64,384]{3,2,1,0:T(8,128)(2,1)S(1)} %get-tuple-element.22), channel_id=1, source_target_pairs={{31,0},{24,1},{25,2},{26,3},{27,4},{28,5},{29,6},{30,7},{7,8},{0,9... | collective-permute-start | bytes 589832 | tf_op jit(solution)/shard_map/ppermute | solution.py:323
  93.1 10.9 %all-to-all-start.2 = ((bf16[4,144,128]{2,1,0:T(8,128)(2,1)}), bf16[4,144,128]{2,1,0:T(8,128)(2,1)S(1)}, u32[]{:S(2)}, u32[]{:S(2)}) async-start(bf16[4,144,128]{2,1,0:T(8,128)(2,1)} %shard_map.105), calls=%async_computation.2 | async-start | bytes 294912 | tf_op jit(solution)/shard_map/all_to_all | solution.py:294
  96.8 11.3 %collective-permute-start.7 = (bf16[4,2,64,384]{3,2,1,0:T(8,128)(2,1)S(1)}, bf16[4,2,64,384]{3,2,1,0:T(8,128)(2,1)S(1)}, u32[]{:S(2)}, u32[]{:S(2)}) collective-permute-start(bf16[4,2,64,384]{3,2,1,0:T(8,128)(2,1)S(1)} %pad_maximum_fusion), channel_id=1, source_target_pairs={{480,0},{481,1},{482,2},{483,3},{484,4},{485,5},{486,6},{487,7},{4... | collective-permute-start | bytes 1179656 | tf_op jit(solution)/shard_map/ppermute | solution.py:323
  104.8 11.0 %all-to-all-start.3 = ((bf16[4,144,128]{2,1,0:T(8,128)(2,1)}), bf16[4,144,128]{2,1,0:T(8,128)(2,1)S(1)}, u32[]{:S(2)}, u32[]{:S(2)}) async-start(bf16[4,144,128]{2,1,0:T(8,128)(2,1)} %shard_map.106), calls=%async_computation.3 | async-start | bytes 294912 | tf_op jit(solution)/shard_map/all_to_all | solution.py:294
  108.1 31.2 %copy-start = (bf16[8,8,8,384]{3,2,1,0:T(8,128)(2,1)S(1)}, bf16[8,8,8,384]{3,2,1,0:T(8,128)(2,1)}, u32[]{:S(2)}) copy-start(bf16[8,8,8,384]{3,2,1,0:T(8,128)(2,1)} %param.6) | copy-start | bytes 1179652
  108.1 31.2 %copy-start.1 = (bf16[8,8,8,384]{3,2,1,0:T(8,128)(2,1)S(1)}, bf16[8,8,8,384]{3,2,1,0:T(8,128)(2,1)}, u32[]{:S(2)}) copy-start(bf16[8,8,8,384]{3,2,1,0:T(8,128)(2,1)} %param.8) | copy-start | bytes 1179652
  108.1 31.2 %copy-start.4 = (s32[8,8,8]{2,1,0:T(8,128)S(1)}, s32[8,8,8]{2,1,0:T(8,128)}, u32[]{:S(2)}) copy-start(s32[8,8,8]{2,1,0:T(8,128)} %frozen.1) | copy-start | bytes 6148
  135.3 6.4 %collective-permute-start.8 = (bf16[2304,128]{1,0:T(8,128)(2,1)S(1)}, bf16[2304,128]{1,0:T(8,128)(2,1)S(1)}, u32[]{:S(2)}, u32[]{:S(2)}) collective-permute-start(bf16[2304,128]{1,0:T(8,128)(2,1)S(1)} %bitcast.8), channel_id=1, source_target_pairs={{0,32},{32,0},{1,33},{33,1},{2,34},{34,2},{3,35},{35,3},{4,36},{36... | collective-permute-start | bytes 1769480 | tf_op jit(solution)/shard_map/ppermute | solution.py:300

commit v5 on v4

--- a/solution.py
+++ b/solution.py
@@ -1,3 +1,5 @@
+import functools
+
 import jax
 import jax.numpy as jnp
 import numpy as np
@@ -33,7 +35,7 @@
 
 
 def window_kernel(
-    own, behind, side_1, side_2, side_3, w_qkv, w_proj, gain, back_0, back_1, back_2, back_3, grads,
+    own, behind, side_3, side_2, side_1, w_qkv, w_proj, gain, back_0, back_1, back_2, back_3, grads,
     cot, qkv, d_mixed, keys_t, values_t, mixed_t, d_queries_t, d_qkv, unit, inv_std, normed,
 ):
     step = 2 * PIECE
@@ -61,42 +63,43 @@
     values_t[...] = qkv[:, 2 * D :].T
     lane = lax.broadcasted_iota(jnp.int32, (1, LANES), 1)
 
-    def head_block(index, carry):
-        offset = pl.multiple_of(index * LANES, LANES)
-        q_block = qkv[:, pl.ds(offset, LANES)]
-        k_block = qkv[:, pl.ds(offset + D, LANES)]
-        v_block = qkv[:, pl.ds(offset + 2 * D, LANES)]
-        m_block = d_mixed[:, pl.ds(offset, LANES)]
-        d_keys = jnp.zeros((ROWS, LANES), F32)
-        d_values = jnp.zeros((ROWS, LANES), F32)
-        for head in range(PER):
-            mine = (lane // HDIM) == head
-            q_head = jnp.where(mine, q_block, jnp.zeros_like(q_block))
-            m_head = jnp.where(mine, m_block, jnp.zeros_like(m_block))
-            rows = pl.ds(offset + head * HDIM, HDIM)
-            k_head_t = keys_t[rows, :]
-            v_head_t = values_t[rows, :]
-            for start in range(0, ROWS, CHUNK):
-                q_part = q_head[start : start + CHUNK]
-                m_part = m_head[start : start + CHUNK]
-                scores = dot_t(k_block, q_part)
-                top = jnp.max(scores, axis=0, keepdims=True)
-                terms = jnp.exp2(scores * (SCALE * LOG2E) - top * (SCALE * LOG2E))
-                inverse = 1.0 / jnp.sum(terms, axis=0, keepdims=True)
-                probs_low = (terms * inverse).astype(BF)
-                d_probs = dot_t(v_block, m_part)
-                mixed_t[rows, pl.ds(start, CHUNK)] = dot(v_head_t, probs_low).astype(BF)
-                d_values = d_values + dot(probs_low, m_part)
-                scaled = inverse * SCALE
-                shift = jnp.sum(terms * d_probs, axis=0, keepdims=True) * (inverse * scaled)
-                d_scores = (terms * (d_probs * scaled - shift)).astype(BF)
-                d_queries_t[rows, pl.ds(start, CHUNK)] = dot(k_head_t, d_scores).astype(BF)
-                d_keys = d_keys + dot(d_scores, q_part)
-        d_qkv[:, pl.ds(offset + D, LANES)] = d_keys.astype(BF)
-        d_qkv[:, pl.ds(offset + 2 * D, LANES)] = d_values.astype(BF)
-        return carry
-
-    lax.fori_loop(0, D // LANES, head_block, 0)
+    def first_products(head, start):
+        block = slice(head // PER * LANES, (head // PER + 1) * LANES)
+        mine = (lane // HDIM) == head % PER
+        queries = pl.ds(start, CHUNK)
+        zeros = jnp.zeros((CHUNK, LANES), BF)
+        q_part = jnp.where(mine, qkv[queries, block], zeros)
+        m_part = jnp.where(mine, d_mixed[queries, block], zeros)
+        scores = dot_t(qkv[:, D + block.start : D + block.stop], q_part)
+        d_probs = dot_t(qkv[:, 2 * D + block.start : 2 * D + block.stop], m_part)
+        return q_part, m_part, scores, d_probs
+
+    steps = [(head, start) for head in range(HEADS) for start in range(0, ROWS, CHUNK)]
+    ready = first_products(*steps[0])
+    for index, (head, start) in enumerate(steps):
+        q_part, m_part, scores, d_probs = ready
+        if index + 1 < len(steps):
+            ready = first_products(*steps[index + 1])
+        if head % PER == 0 and start == 0:
+            d_keys = jnp.zeros((ROWS, LANES), F32)
+            d_values = jnp.zeros((ROWS, LANES), F32)
+        rows = pl.ds(head * HDIM, HDIM)
+        top = jnp.max(scores, axis=0, keepdims=True)
+        terms = jnp.exp2(scores * (SCALE * LOG2E) - top * (SCALE * LOG2E))
+        inverse = 1.0 / jnp.sum(terms, axis=0, keepdims=True)
+        probs_low = (terms * inverse).astype(BF)
+        mixed_t[rows, pl.ds(start, CHUNK)] = dot(values_t[rows, :], probs_low).astype(BF)
+        d_values = d_values + dot(probs_low, m_part)
+        scaled = inverse * SCALE
+        shift = jnp.sum(terms * d_probs, axis=0, keepdims=True) * (inverse * scaled)
+        d_scores = (terms * (d_probs * scaled - shift)).astype(BF)
+        d_queries_t[rows, pl.ds(start, CHUNK)] = dot(keys_t[rows, :], d_scores).astype(BF)
+        d_keys = d_keys + dot(d_scores, q_part)
+        if head % PER == PER - 1 and start + CHUNK == ROWS:
+            block = head // PER * LANES
+            d_qkv[:, D + block : D + block + LANES] = d_keys.astype(BF)
+            d_qkv[:, 2 * D + block : 2 * D + block + LANES] = d_values.astype(BF)
+
     d_qkv[:, pl.ds(0, D)] = d_queries_t[...].T
     branch = dot(mixed_t[...].T, w_proj[...]).astype(BF)
     backs = (back_0, back_1, back_2, back_3)
@@ -204,8 +207,8 @@
 SMALL = pltpu.CompilerParams(vmem_limit_bytes=12 * 1024 * 1024)
 
 
-def total_kernel(copies, parts, *rest):
-    out = rest[-1]
+def total_kernel(parts, *rest, copies, out_at):
+    out = rest[out_at]
     total = parts[0].astype(F32)
     for index in range(1, parts.shape[0]):
         total = total + parts[index].astype(F32)
@@ -214,13 +217,18 @@
         out[index] = total
 
 
-def total_of(parts, copies, after=()):
-    return pl.pallas_call(
-        lambda *refs: total_kernel(copies, *refs),
-        out_shape=jax.ShapeDtypeStruct((copies,) + parts.shape[1:], BF),
-        in_specs=[WHOLE] + [pl.BlockSpec(memory_space=pl.ANY)] * len(after),
+def total_of(parts, copies, after=(), through=()):
+    anywhere = pl.BlockSpec(memory_space=pl.ANY)
+    total, *passed = pl.pallas_call(
+        functools.partial(total_kernel, copies=copies, out_at=len(after) + len(through)),
+        out_shape=[jax.ShapeDtypeStruct((copies,) + parts.shape[1:], BF)]
+        + [jax.ShapeDtypeStruct(array.shape, array.dtype) for array in through],
+        in_specs=[WHOLE] + [anywhere] * (len(after) + len(through)),
+        out_specs=[WHOLE] + [anywhere] * len(through),
+        input_output_aliases={1 + len(after) + at: 1 + at for at in range(len(through))},
         compiler_params=SMALL,
-    )(parts, *after)
+    )(parts, *after, *through)
+    return (total, *passed) if through else total
 
 
 def grads_kernel(core, mine, other, w_qkv, gain, qkv_grad, proj_grad, gain_grad):
@@ -270,7 +278,7 @@
         cost_estimate=pl.CostEstimate(
             flops=16_000_000_000, bytes_accessed=5_000_000, transcendentals=3_200_000
         ),
-    )(own, behind, *sides, w_qkv, w_proj, norm_gain.reshape(1, D))
+    )(own, behind, *sides[::-1], w_qkv, w_proj, norm_gain.reshape(1, D))
 
 
 LATTICE = ("z_hi", "z_lo", "core", "y_hi", "y_lo", "x")
@@ -288,10 +296,6 @@
     parts = total_of(halves, 1).reshape(GROUP, GRAD_ROWS // 2 // GROUP, LANES)
     parts = lax.all_to_all(parts, NEAR, 0, 0)
     return parts
-
-
-def far_sum(parts, axis, after=()):
-    return lax.all_to_all(total_of(parts, FAR, after), axis, 0, 0)
 
 
 def spread_sum(parts, after):
@@ -340,14 +344,16 @@
     )(core, token_rows, frozen, cot_rows)
     behind = send(ahead, 0)
     sides = [None] * 4
-    for kind in (3, 2, 1):
+    for kind in (1, 2, 3):
         sides[kind] = send(jnp.stack([own[kind], behind[kind]]), kind)
     *backs, grads = window_pass(own, behind, sides[1:], w_qkv, w_proj, norm_gain)
     parts = near_sum(grads)
-    for kind in (3, 2, 1):
+    parts, *backs[1:] = total_of(parts, FAR, through=backs[1:])
+    for kind in (1, 2, 3):
         backs[kind] = send(backs[kind], kind, True)
-    parts = far_sum(far_sum(parts, "y_hi"), "z_hi", backs[1:])
     ahead = send(jnp.stack([back[1] for back in backs]), 0, True)
+    parts = total_of(lax.all_to_all(parts, "y_hi", 0, 0), FAR)
+    parts = lax.all_to_all(parts, "z_hi", 0, 0)
     block_out, tokens_grad = pl.pallas_call(
         join_kernel,
         out_shape=(jax.ShapeDtypeStruct((ROWS, D), BF),) * 2,

time: 144 us -> 135 us (0.938)
  blocking collectives: 33.3 us -> 51 us
  waiting for transfers between devices: 26.5 us -> 16.8 us
  starting transfers between devices: 51.2 us -> 42.2 us
  Pallas kernels: 30.2 us -> 22.1 us
    all_to_all x0 -> x2, blocking collectives: none -> 29.2 us  [the longest x1 15.6 us: near_sum(): parts = lax.all_to_all(parts, NEAR, 0, 0)]
    all_to_all x3 -> x1, waiting for transfers between devices: 11.3 us -> 0.37 us  [local(): parts = total_of(lax.all_to_all(parts, 'y_hi', 0, 0), FAR)]
    all_to_all x3 -> x1, starting transfers between devices: 11.8 us -> 3.35 us  [local(): parts = total_of(lax.all_to_all(parts, 'y_hi', 0, 0), FAR)]
    all_to_all x1, blocking collectives: 13.8 us -> 5.69 us  [near_sum(): lax.all_to_all(rows.reshape(2, GRAD_ROWS // 2, LANES), 'core', 0, 0)]
    pallas_call x1, Pallas kernels: 21.2 us -> 14.5 us  [window_pass(): pl.pallas_call(window_kernel, out_shape=(jax.ShapeDtypeStruct((2, 2, PIEC...]
    all_to_all x1, blocking collectives: 19.5 us -> 16.1 us  [spread_sum(): parts = lax.all_to_all(total_of(parts, GROUP, after), NEAR, 0, 0)]
    ppermute x8, starting transfers between devices: 35.4 us -> 33.8 us  [send(): return lax.ppermute(block, LATTICE, route(kind, back))]
    pallas_call x4, Pallas kernels: 2.42 us -> 0.95 us  [total_of(): pl.pallas_call(functools.partial(total_kernel, copies=copies, out_at=len(...]
  transfers between devices with their start and end apart: 12 -> 10, of which waited for: 6 -> 5; matrix products, arithmetic and copies ran while one was open for 1% -> 1% of each run, Pallas kernels for 2% -> 2%
where the time goes in v5:
time: 135 us; the launch traced here: 134 us
  blocking collectives  51 us (38%)
  starting transfers between devices  42.2 us (31%)
  Pallas kernels  22.1 us (16%)
  waiting for transfers between devices  16.8 us (12%)
    ppermute x8, starting transfers between devices, send(): return lax.ppermute(block, LATTICE, route(kind, back))  33.8 us
    ppermute x8, waiting for transfers between devices, send(): return lax.ppermute(block, LATTICE, route(kind, back))  16.5 us
    all_to_all x1, blocking collectives, spread_sum(): parts = lax.all_to_all(total_of(parts, GROUP, after), NEAR, 0, 0)  16.1 us
    all_to_all x1, blocking collectives, near_sum(): parts = lax.all_to_all(parts, NEAR, 0, 0)  15.6 us
    pallas_call x1, Pallas kernels, window_pass(): pl.pallas_call(window_kernel, out_shape=(jax.ShapeDtypeStruct((2, 2, PIEC...  14.5 us
    all_to_all x1, blocking collectives, local(): parts = lax.all_to_all(parts, 'z_hi', 0, 0)  13.6 us
    all_to_all x1, blocking collectives, near_sum(): lax.all_to_all(rows.reshape(2, GRAD_ROWS // 2, LANES), 'core', 0, 0)  5.69 us
    ppermute x1, starting transfers between devices, spread_sum(): return (mine, lax.ppermute(mine, 'core', [(0, 1), (1, 0)]))  5.14 us
  transfers between devices with their start and end apart: 10, of which 5 were waited for; matrix products, arithmetic and copies ran while one was open for 1% of the time, Pallas kernels for 2%

profile of v5, /device:TPU:1, one launch (start us, length us, event | category | flops | bytes accessed | tf_op | source)
XLA Modules:
  0.0 134.4 jit_solution(5245064808435940923)
XLA Ops:
  0.6 2.4 %shard_map.101 = (bf16[4,2,64,384]{3,2,1,0:T(8,128)(2,1)}, bf16[4,2,64,384]{3,2,1,0:T(8,128)(2,1)}) custom-call(s32[1]{0:T(128)} %bitcast.odd.core, bf16[512,384]{1,0:T(8,128)(2,1)} %bitcast.11, s32[8,8,8]{2,1,0:T(8,128)} %frozen.1, bf16[512,384]{1,0:T(8,128)(2,1)} %bitcast.13), custom_call_target="tpu_custom_call" | custom-call | tf_op jit(solution)/shard_map/pallas_call | solution.py:333
  3.1 6.9 %collective-permute-start = (bf16[4,2,64,384]{3,2,1,0:T(8,128)(2,1)}, bf16[4,2,64,384]{3,2,1,0:T(8,128)(2,1)S(1)}, u32[]{:S(2)}, u32[]{:S(2)}) collective-permute-start(bf16[4,2,64,384]{3,2,1,0:T(8,128)(2,1)} %get-tuple-element.22), channel_id=1, source_target_pairs={{0,480},{1,481},{2,482},{3,483},{4,484},{5,485},{6,486},{7,487},{8... | collective-permute-start | bytes 1179656 | tf_op jit(solution)/shard_map/ppermute | solution.py:327
  10.0 1.1 fusion
  11.1 1.1 collective-permute-done.behind
  12.3 5.1 %collective-permute-start.1 = (bf16[2,2,64,384]{3,2,1,0:T(8,128)(2,1)S(1)}, bf16[2,2,64,384]{3,2,1,0:T(8,128)(2,1)S(1)}, u32[]{:S(2)}, u32[]{:S(2)}) collective-permute-start(bf16[2,2,64,384]{3,2,1,0:T(8,128)(2,1)S(1)} %pad_maximum_fusion.1), channel_id=1, source_target_pairs={{0,31},{1,24},{2,25},{3,26},{4,27},{5,28},{6,29},{7,30},{8,7},{9,0... | collective-permute-start | bytes 589832 | tf_op jit(solution)/shard_map/ppermute | solution.py:327
  17.5 5.4 %collective-permute-start.2 = (bf16[2,2,64,384]{3,2,1,0:T(8,128)(2,1)S(1)}, bf16[2,2,64,384]{3,2,1,0:T(8,128)(2,1)S(1)}, u32[]{:S(2)}, u32[]{:S(2)}) collective-permute-start(bf16[2,2,64,384]{3,2,1,0:T(8,128)(2,1)S(1)} %pad_maximum_fusion.2), channel_id=1, source_target_pairs={{0,24},{1,25},{2,26},{3,27},{4,28},{5,29},{6,30},{7,31},{8,0},{9,1... | collective-permute-start | bytes 589832 | tf_op jit(solution)/shard_map/ppermute | solution.py:327
  23.0 3.1 %collective-permute-start.3 = (bf16[2,2,64,384]{3,2,1,0:T(8,128)(2,1)S(1)}, bf16[2,2,64,384]{3,2,1,0:T(8,128)(2,1)S(1)}, u32[]{:S(2)}, u32[]{:S(2)}) collective-permute-start(bf16[2,2,64,384]{3,2,1,0:T(8,128)(2,1)S(1)} %pad_maximum_fusion.3), channel_id=1, source_target_pairs={{0,7},{1,0},{2,1},{3,2},{4,3},{5,4},{6,5},{7,6},{8,15},{9,8},{10,9... | collective-permute-start | bytes 589832 | tf_op jit(solution)/shard_map/ppermute | solution.py:327
  26.1 3.4 %collective-permute-done.2.side_2 = bf16[2,2,64,384]{3,2,1,0:T(8,128)(2,1)S(1)} collective-permute-done((bf16[2,2,64,384]{3,2,1,0:T(8,128)(2,1)S(1)}, bf16[2,2,64,384]{3,2,1,0:T(8,128)(2,1)S(1)}, u32[]{:S(2)}, u32[]{:S(2)}) %collective-permute-start.2) | collective-permute-done | bytes 196640 | tf_op jit(solution)/shard_map/ppermute | solution.py:327
  29.5 7.1 %collective-permute-done.3.side_1 = bf16[2,2,64,384]{3,2,1,0:T(8,128)(2,1)S(1)} collective-permute-done((bf16[2,2,64,384]{3,2,1,0:T(8,128)(2,1)S(1)}, bf16[2,2,64,384]{3,2,1,0:T(8,128)(2,1)S(1)}, u32[]{:S(2)}, u32[]{:S(2)}) %collective-permute-start.3) | collective-permute-done | bytes 196640 | tf_op jit(solution)/shard_map/ppermute | solution.py:327
  36.6 14.5 %shard_map.102 = (bf16[2,2,64,384]{3,2,1,0:T(8,128)(2,1)S(1)}, bf16[2,2,64,384]{3,2,1,0:T(8,128)(2,1)S(1)}, bf16[2,2,64,384]{3,2,1,0:T(8,128)(2,1)S(1)}, bf16[2,...) custom-call(bf16[4,2,64,384]{3,2,1,0:T(8,128)(2,1)S(1)} %copy-done.3, ...), custom_call_target="tpu_custom_call" | custom-call | flops 16000000000 | bytes 5000000 | tf_op jit(solution)/shard_map/pallas_call | solution.py:260
  51.2 5.7 %all_to_all.25.parts = bf16[2,2304,128]{2,1,0:T(8,128)(2,1)S(1)} all-to-all(bf16[2,2304,128]{2,1,0:T(8,128)(2,1)S(1)} %bitcast.15), channel_id=1, replica_groups=mesh['z_hi'=4,'z_lo'=2,'core'=2,'y_hi'=4,'y_lo'=2,'x'=4] {'core'}, dimensions={0} | all-to-all | bytes 2359296 | tf_op jit(solution)/shard_map/all_to_all | solution.py:295
  57.0 15.6 %all_to_all.26.parts = bf16[16,144,128]{2,1,0:T(8,128)(2,1)S(1)} all-to-all(bf16[16,144,128]{2,1,0:T(8,128)(2,1)S(1)} %bitcast.10), channel_id=1, replica_groups=mesh['z_hi'=4,'z_lo'=2,'core'=2,'y_hi'=4,'y_lo'=2,'x'=4] {'x','y_lo','z_..., dimensions={0} | all-to-all | bytes 1179648 | tf_op jit(solution)/shard_map/all_to_all | solution.py:297
  72.6 0.7 shard_map.104
  73.3 3.1 %collective-permute-start.4 = (bf16[2,2,64,384]{3,2,1,0:T(8,128)(2,1)S(1)}, bf16[2,2,64,384]{3,2,1,0:T(8,128)(2,1)S(1)}, u32[]{:S(2)}, u32[]{:S(2)}) collective-permute-start(bf16[2,2,64,384]{3,2,1,0:T(8,128)(2,1)S(1)} %get-tuple-element.28), channel_id=1, source_target_pairs={{7,0},{0,1},{1,2},{2,3},{3,4},{4,5},{5,6},{6,7},{15,8},{8,9},{9,10... | collective-permute-start | bytes 589832 | tf_op jit(solution)/shard_map/ppermute | solution.py:327
  76.4 5.3 %collective-permute-start.5 = (bf16[2,2,64,384]{3,2,1,0:T(8,128)(2,1)S(1)}, bf16[2,2,64,384]{3,2,1,0:T(8,128)(2,1)S(1)}, u32[]{:S(2)}, u32[]{:S(2)}) collective-permute-start(bf16[2,2,64,384]{3,2,1,0:T(8,128)(2,1)S(1)} %get-tuple-element.29), channel_id=1, source_target_pairs={{24,0},{25,1},{26,2},{27,3},{28,4},{29,5},{30,6},{31,7},{0,8},{1,9... | collective-permute-start | bytes 589832 | tf_op jit(solution)/shard_map/ppermute | solution.py:327
  81.7 1.9 %collective-permute-start.6 = (bf16[2,2,64,384]{3,2,1,0:T(8,128)(2,1)S(1)}, bf16[2,2,64,384]{3,2,1,0:T(8,128)(2,1)S(1)}, u32[]{:S(2)}, u32[]{:S(2)}) collective-permute-start(bf16[2,2,64,384]{3,2,1,0:T(8,128)(2,1)S(1)} %get-tuple-element.30), channel_id=1, source_target_pairs={{31,0},{24,1},{25,2},{26,3},{27,4},{28,5},{29,6},{30,7},{7,8},{0,9... | collective-permute-start | bytes 589832 | tf_op jit(solution)/shard_map/ppermute | solution.py:327
  83.6 3.3 %all-to-all-start.2 = ((bf16[4,144,128]{2,1,0:T(8,128)(2,1)}), bf16[4,144,128]{2,1,0:T(8,128)(2,1)S(1)}, u32[]{:S(2)}, u32[]{:S(2)}) async-start(bf16[4,144,128]{2,1,0:T(8,128)(2,1)} %get-tuple-element.33), calls=%async_computation.2 | async-start | bytes 294912 | tf_op jit(solution)/shard_map/all_to_all | solution.py:355
  87.0 4.8 %collective-permute-done.6.home_3 = bf16[2,2,64,384]{3,2,1,0:T(8,128)(2,1)S(1)} collective-permute-done((bf16[2,2,64,384]{3,2,1,0:T(8,128)(2,1)S(1)}, bf16[2,2,64,384]{3,2,1,0:T(8,128)(2,1)S(1)}, u32[]{:S(2)}, u32[]{:S(2)}) %collective-permute-start.6) | collective-permute-done | bytes 196640 | tf_op jit(solution)/shard_map/ppermute | solution.py:327
  92.0 2.9 %collective-permute-start.7 = (bf16[4,2,64,384]{3,2,1,0:T(8,128)(2,1)S(1)}, bf16[4,2,64,384]{3,2,1,0:T(8,128)(2,1)S(1)}, u32[]{:S(2)}, u32[]{:S(2)}) collective-permute-start(bf16[4,2,64,384]{3,2,1,0:T(8,128)(2,1)S(1)} %pad_maximum_fusion), channel_id=1, source_target_pairs={{480,0},{481,1},{482,2},{483,3},{484,4},{485,5},{486,6},{487,7},{4... | collective-permute-start | bytes 1179656 | tf_op jit(solution)/shard_map/ppermute | solution.py:327
  95.2 13.6 %all_to_all.27.parts = bf16[4,144,128]{2,1,0:T(8,128)(2,1)S(1)} all-to-all(bf16[4,144,128]{2,1,0:T(8,128)(2,1)S(1)} %shard_map.106), channel_id=1, replica_groups=mesh['z_hi'=4,'z_lo'=2,'core'=2,'y_hi'=4,'y_lo'=2,'x'=4] {'z_hi'}, dimensions={0} | all-to-all | bytes 294912 | tf_op jit(solution)/shard_map/all_to_all | solution.py:356
  108.9 16.1 %all_to_all.28 = bf16[16,144,128]{2,1,0:T(8,128)(2,1)S(1)} all-to-all(bf16[16,144,128]{2,1,0:T(8,128)(2,1)S(1)} %shard_map.107), channel_id=1, replica_groups=mesh['z_hi'=4,'z_lo'=2,'core'=2,'y_hi'=4,'y_lo'=2,'x'=4] {'x','y_lo','z_..., dimensions={0} | all-to-all | bytes 1179648 | tf_op jit(solution)/shard_map/all_to_all | solution.py:302
  125.0 5.1 %collective-permute-start.8 = (bf16[2304,128]{1,0:T(8,128)(2,1)S(1)}, bf16[2304,128]{1,0:T(8,128)(2,1)S(1)}, u32[]{:S(2)}, u32[]{:S(2)}) collective-permute-start(bf16[2304,128]{1,0:T(8,128)(2,1)S(1)} %bitcast.8), channel_id=1, source_target_pairs={{0,32},{32,0},{1,33},{33,1},{2,34},{34,2},{3,35},{35,3},{4,36},{36... | collective-permute-start | bytes 1769480 | tf_op jit(solution)/shard_map/ppermute | solution.py:304
  130.2 2.4 %shard_map.105 = (bf16[512,384]{1,0:T(8,128)(2,1)}, bf16[512,384]{1,0:T(8,128)(2,1)}) custom-call(s32[1]{0:T(128)} %bitcast.odd.core, bf16[512,384]{1,0:T(8,128)(2,1)S(1)} %bitcast.12, s32[8,8,8]{2,1,0:T(8,128)S(1)} %copy-done.4, bf16[512,384]{1,0:T(8,128)(2,1)S(1)} %bitcast.14, bf16[2,2,64,384]{3,2,1,0:T(8,128)(2,1)S(1)} %get-tuple-element.23.home_0, ...), custom_call_target="tpu_custom_call" | custom-call | tf_op jit(solution)/shard_map/pallas_call | solution.py:357
  132.6 1.8 %shard_map.108 = (f32[384,1152]{1,0:T(8,128)}, f32[384,384]{1,0:T(8,128)}, f32[384]{0:T(512)}) custom-call(s32[1]{0:T(128)} %bitcast.odd.core, bf16[2304,128]{1,0:T(8,128)(2,1)S(1)} %bitcast.9, bf16[2304,128]{1,0:T(8,128)(2,1)S(1)} %collective-permute-done.8.other, bf16[384,1152]{1,0:T(8,128)(2,1)S(1)} %copy-done.2, f32[1,384]{1,0:T(1,128)S(1)} %reshape.41.gain), custom_call_target="tpu_custom_call" | custom-call | tf_op jit(solution)/shard_map/pallas_call | solution.py:364
  (33 shorter events, 0.8 us)
Async XLA Ops:
  3.1 9.2 %collective-permute-start = (bf16[4,2,64,384]{3,2,1,0:T(8,128)(2,1)}, bf16[4,2,64,384]{3,2,1,0:T(8,128)(2,1)S(1)}, u32[]{:S(2)}, u32[]{:S(2)}) collective-permute-start(bf16[4,2,64,384]{3,2,1,0:T(8,128)(2,1)} %get-tuple-element.22), channel_id=1, source_target_pairs={{0,480},{1,481},{2,482},{3,483},{4,484},{5,485},{6,486},{7,487},{8... | collective-permute-start | bytes 1179656 | tf_op jit(solution)/shard_map/ppermute | solution.py:327
  9.9 16.1 %copy-start.6 = (f32[384]{0:T(512)S(1)}, f32[384]{0:T(512)}, u32[]{:S(2)}) copy-start(f32[384]{0:T(512)} %param.11) | copy-start | bytes 4612
  9.9 26.7 %copy-start.2 = (bf16[384,1152]{1,0:T(8,128)(2,1)S(1)}, bf16[384,1152]{1,0:T(8,128)(2,1)}, u32[]{:S(2)}) copy-start(bf16[384,1152]{1,0:T(8,128)(2,1)} %w_qkv.3) | copy-start | bytes 2654212
  10.0 26.7 %copy-start.3 = (bf16[4,2,64,384]{3,2,1,0:T(8,128)(2,1)S(1)}, bf16[4,2,64,384]{3,2,1,0:T(8,128)(2,1)}, u32[]{:S(2)}) copy-start(bf16[4,2,64,384]{3,2,1,0:T(8,128)(2,1)} %get-tuple-element.21.own) | copy-start | bytes 1179652
  10.0 26.7 %copy-start.5 = (bf16[384,384]{1,0:T(8,128)(2,1)S(1)}, bf16[384,384]{1,0:T(8,128)(2,1)}, u32[]{:S(2)}) copy-start(bf16[384,384]{1,0:T(8,128)(2,1)} %w_proj.1) | copy-start | bytes 884740
  12.3 13.8 %collective-permute-start.1 = (bf16[2,2,64,384]{3,2,1,0:T(8,128)(2,1)S(1)}, bf16[2,2,64,384]{3,2,1,0:T(8,128)(2,1)S(1)}, u32[]{:S(2)}, u32[]{:S(2)}) collective-permute-start(bf16[2,2,64,384]{3,2,1,0:T(8,128)(2,1)S(1)} %pad_maximum_fusion.1), channel_id=1, source_target_pairs={{0,31},{1,24},{2,25},{3,26},{4,27},{5,28},{6,29},{7,30},{8,7},{9,0... | collective-permute-start | bytes 589832 | tf_op jit(solution)/shard_map/ppermute | solution.py:327
  17.5 12.0 %collective-permute-start.2 = (bf16[2,2,64,384]{3,2,1,0:T(8,128)(2,1)S(1)}, bf16[2,2,64,384]{3,2,1,0:T(8,128)(2,1)S(1)}, u32[]{:S(2)}, u32[]{:S(2)}) collective-permute-start(bf16[2,2,64,384]{3,2,1,0:T(8,128)(2,1)S(1)} %pad_maximum_fusion.2), channel_id=1, source_target_pairs={{0,24},{1,25},{2,26},{3,27},{4,28},{5,29},{6,30},{7,31},{8,0},{9,1... | collective-permute-start | bytes 589832 | tf_op jit(solution)/shard_map/ppermute | solution.py:327
  23.0 13.7 %collective-permute-start.3 = (bf16[2,2,64,384]{3,2,1,0:T(8,128)(2,1)S(1)}, bf16[2,2,64,384]{3,2,1,0:T(8,128)(2,1)S(1)}, u32[]{:S(2)}, u32[]{:S(2)}) collective-permute-start(bf16[2,2,64,384]{3,2,1,0:T(8,128)(2,1)S(1)} %pad_maximum_fusion.3), channel_id=1, source_target_pairs={{0,7},{1,0},{2,1},{3,2},{4,3},{5,4},{6,5},{7,6},{8,15},{9,8},{10,9... | collective-permute-start | bytes 589832 | tf_op jit(solution)/shard_map/ppermute | solution.py:327
  73.3 13.7 %collective-permute-start.4 = (bf16[2,2,64,384]{3,2,1,0:T(8,128)(2,1)S(1)}, bf16[2,2,64,384]{3,2,1,0:T(8,128)(2,1)S(1)}, u32[]{:S(2)}, u32[]{:S(2)}) collective-permute-start(bf16[2,2,64,384]{3,2,1,0:T(8,128)(2,1)S(1)} %get-tuple-element.28), channel_id=1, source_target_pairs={{7,0},{0,1},{1,2},{2,3},{3,4},{4,5},{5,6},{6,7},{15,8},{8,9},{9,10... | collective-permute-start | bytes 589832 | tf_op jit(solution)/shard_map/ppermute | solution.py:327
  76.4 10.6 %collective-permute-start.5 = (bf16[2,2,64,384]{3,2,1,0:T(8,128)(2,1)S(1)}, bf16[2,2,64,384]{3,2,1,0:T(8,128)(2,1)S(1)}, u32[]{:S(2)}, u32[]{:S(2)}) collective-permute-start(bf16[2,2,64,384]{3,2,1,0:T(8,128)(2,1)S(1)} %get-tuple-element.29), channel_id=1, source_target_pairs={{24,0},{25,1},{26,2},{27,3},{28,4},{29,5},{30,6},{31,7},{0,8},{1,9... | collective-permute-start | bytes 589832 | tf_op jit(solution)/shard_map/ppermute | solution.py:327
  81.7 10.2 %collective-permute-start.6 = (bf16[2,2,64,384]{3,2,1,0:T(8,128)(2,1)S(1)}, bf16[2,2,64,384]{3,2,1,0:T(8,128)(2,1)S(1)}, u32[]{:S(2)}, u32[]{:S(2)}) collective-permute-start(bf16[2,2,64,384]{3,2,1,0:T(8,128)(2,1)S(1)} %get-tuple-element.30), channel_id=1, source_target_pairs={{31,0},{24,1},{25,2},{26,3},{27,4},{28,5},{29,6},{30,7},{7,8},{0,9... | collective-permute-start | bytes 589832 | tf_op jit(solution)/shard_map/ppermute | solution.py:327
  83.6 11.6 %all-to-all-start.2 = ((bf16[4,144,128]{2,1,0:T(8,128)(2,1)}), bf16[4,144,128]{2,1,0:T(8,128)(2,1)S(1)}, u32[]{:S(2)}, u32[]{:S(2)}) async-start(bf16[4,144,128]{2,1,0:T(8,128)(2,1)} %get-tuple-element.33), calls=%async_computation.2 | async-start | bytes 294912 | tf_op jit(solution)/shard_map/all_to_all | solution.py:355
  92.0 16.9 %collective-permute-start.7 = (bf16[4,2,64,384]{3,2,1,0:T(8,128)(2,1)S(1)}, bf16[4,2,64,384]{3,2,1,0:T(8,128)(2,1)S(1)}, u32[]{:S(2)}, u32[]{:S(2)}) collective-permute-start(bf16[4,2,64,384]{3,2,1,0:T(8,128)(2,1)S(1)} %pad_maximum_fusion), channel_id=1, source_target_pairs={{480,0},{481,1},{482,2},{483,3},{484,4},{485,5},{486,6},{487,7},{4... | collective-permute-start | bytes 1179656 | tf_op jit(solution)/shard_map/ppermute | solution.py:327
  108.9 21.3 %copy-start = (bf16[8,8,8,384]{3,2,1,0:T(8,128)(2,1)S(1)}, bf16[8,8,8,384]{3,2,1,0:T(8,128)(2,1)}, u32[]{:S(2)}) copy-start(bf16[8,8,8,384]{3,2,1,0:T(8,128)(2,1)} %param.6) | copy-start | bytes 1179652
  108.9 21.3 %copy-start.1 = (bf16[8,8,8,384]{3,2,1,0:T(8,128)(2,1)S(1)}, bf16[8,8,8,384]{3,2,1,0:T(8,128)(2,1)}, u32[]{:S(2)}) copy-start(bf16[8,8,8,384]{3,2,1,0:T(8,128)(2,1)} %param.8) | copy-start | bytes 1179652
  108.9 21.3 %copy-start.4 = (s32[8,8,8]{2,1,0:T(8,128)S(1)}, s32[8,8,8]{2,1,0:T(8,128)}, u32[]{:S(2)}) copy-start(s32[8,8,8]{2,1,0:T(8,128)} %frozen.1) | copy-start | bytes 6148
  125.0 7.6 %collective-permute-start.8 = (bf16[2304,128]{1,0:T(8,128)(2,1)S(1)}, bf16[2304,128]{1,0:T(8,128)(2,1)S(1)}, u32[]{:S(2)}, u32[]{:S(2)}) collective-permute-start(bf16[2304,128]{1,0:T(8,128)(2,1)S(1)} %bitcast.8), channel_id=1, source_target_pairs={{0,32},{32,0},{1,33},{33,1},{2,34},{34,2},{3,35},{35,3},{4,36},{36... | collective-permute-start | bytes 1769480 | tf_op jit(solution)/shard_map/ppermute | solution.py:304

commit v6 on v5

--- a/solution.py
+++ b/solution.py
@@ -35,8 +35,8 @@
 
 
 def window_kernel(
-    own, behind, side_3, side_2, side_1, w_qkv, w_proj, gain, back_0, back_1, back_2, back_3, grads,
-    cot, qkv, d_mixed, keys_t, values_t, mixed_t, d_queries_t, d_qkv, unit, inv_std, normed,
+    own, behind, side_3, side_2, side_1, w_qkv, w_proj, gain, grads, mixed_t, d_qkv, unit, inv_std,
+    cot, qkv, d_mixed, keys_t, values_t, d_queries_t, normed,
 ):
     step = 2 * PIECE
     gain_row = gain[...]
@@ -101,12 +101,6 @@
             d_qkv[:, 2 * D + block : 2 * D + block + LANES] = d_values.astype(BF)
 
     d_qkv[:, pl.ds(0, D)] = d_queries_t[...].T
-    branch = dot(mixed_t[...].T, w_proj[...]).astype(BF)
-    backs = (back_0, back_1, back_2, back_3)
-    for group in range(4):
-        for place in range(2):
-            start = (2 * group + place) * PIECE
-            backs[group][place, 0] = branch[start : start + PIECE]
     normed_t = normed[...].T
     for block in range(9):
         term = dot(normed_t, d_qkv[:, block * LANES : (block + 1) * LANES])
@@ -114,16 +108,24 @@
     for block in range(3):
         term = dot(mixed_t[...], cot[:, block * LANES : (block + 1) * LANES])
         grads[pl.ds((9 + block) * D, D), :] = term.astype(BF)
+
+
+def rows_kernel(mixed_t, d_qkv, unit, inv_std, w_qkv, w_proj, gain, back_0, back_1, back_y):
+    step = 2 * PIECE
+    backs = (back_0, back_1, back_y.at[0], back_y.at[1])
+    branch = dot(mixed_t[...].T, w_proj[...]).astype(BF)
     for group in range(4):
         part = pl.ds(group * step, step)
         d_normed = dot_t(d_qkv[part, :], w_qkv[...])
         unit_rows = unit[part, :]
-        scaled = d_normed * gain_row
+        scaled = d_normed * gain[...]
         mean_1 = jnp.mean(scaled, axis=-1, keepdims=True)
         mean_2 = jnp.mean(scaled * unit_rows, axis=-1, keepdims=True)
         d_rows = (inv_std[part, 0:1] * (scaled - mean_1 - unit_rows * mean_2)).astype(BF)
-        backs[group][0, 1] = d_rows[:PIECE]
-        backs[group][1, 1] = d_rows[PIECE:]
+        for place in range(2):
+            start = (2 * group + place) * PIECE
+            backs[group][place, 0] = branch[start : start + PIECE]
+            backs[group][place, 1] = d_rows[place * PIECE : (place + 1) * PIECE]
 
 
 def order(odd, upper, inverse):
@@ -177,8 +179,9 @@
                 target[group, 1, pl.ds(plane * 16, 16), :] = cot[rows]
 
 
-def join_kernel(odd, tokens, frozen, cotangent, home_0, home_1, home_2, home_3, ahead, block_out, tokens_grad):
-    homes = (home_0, home_1, home_2, home_3)
+def join_kernel(odd, tokens, frozen, cotangent, home_0, home_x, home_2, ahead, block_out, tokens_grad, token):
+    homes = (home_0, home_x.at[0], home_2.at[0], home_x.at[1])
+    token[...] = jnp.zeros_like(token)
     keeps = keep_rows(frozen)
     shape = (WIN * WIN, WIN * WIN)
     diagonal = ones_where(lax.broadcasted_iota(jnp.int32, shape, 0) == lax.broadcasted_iota(jnp.int32, shape, 1))
@@ -229,6 +232,18 @@
         compiler_params=SMALL,
     )(parts, *after, *through)
     return (total, *passed) if through else total
+
+
+def hold(array, until):
+    anywhere = pl.BlockSpec(memory_space=pl.ANY)
+    return pl.pallas_call(
+        lambda *refs: None,
+        out_shape=jax.ShapeDtypeStruct(array.shape, array.dtype),
+        in_specs=[anywhere] * 2,
+        out_specs=anywhere,
+        input_output_aliases={0: 0},
+        compiler_params=SMALL,
+    )(array, until)
 
 
 def grads_kernel(core, mine, other, w_qkv, gain, qkv_grad, proj_grad, gain_grad):
@@ -257,10 +272,16 @@
     def buffer(shape, kind):
         return pltpu.VMEM(shape, kind)
 
-    return pl.pallas_call(
+    gain = norm_gain.reshape(1, D)
+    grads, *kept = pl.pallas_call(
         window_kernel,
-        out_shape=(jax.ShapeDtypeStruct((2, 2, PIECE, D), BF),) * 4
-        + (jax.ShapeDtypeStruct((GRAD_ROWS, LANES), BF),),
+        out_shape=(
+            jax.ShapeDtypeStruct((GRAD_ROWS, LANES), BF),
+            jax.ShapeDtypeStruct((D, ROWS), BF),
+            jax.ShapeDtypeStruct((ROWS, 3 * D), BF),
+            jax.ShapeDtypeStruct((ROWS, D), F32),
+            jax.ShapeDtypeStruct((ROWS, LANES), F32),
+        ),
         scratch_shapes=[
             buffer((ROWS, D), BF),
             buffer((ROWS, 3 * D), BF),
@@ -268,17 +289,21 @@
             buffer((D, ROWS), BF),
             buffer((D, ROWS), BF),
             buffer((D, ROWS), BF),
-            buffer((D, ROWS), BF),
-            buffer((ROWS, 3 * D), BF),
-            buffer((ROWS, D), F32),
-            buffer((ROWS, LANES), F32),
             buffer((ROWS, D), BF),
         ],
-        compiler_params=pltpu.CompilerParams(vmem_limit_bytes=40 * 1024 * 1024),
+        compiler_params=pltpu.CompilerParams(vmem_limit_bytes=32 * 1024 * 1024),
         cost_estimate=pl.CostEstimate(
-            flops=16_000_000_000, bytes_accessed=5_000_000, transcendentals=3_200_000
+            flops=12_000_000_000, bytes_accessed=5_000_000, transcendentals=3_200_000
         ),
-    )(own, behind, *sides[::-1], w_qkv, w_proj, norm_gain.reshape(1, D))
+    )(own, behind, *sides[::-1], w_qkv, w_proj, gain)
+    backs = pl.pallas_call(
+        rows_kernel,
+        out_shape=(jax.ShapeDtypeStruct((2, 2, PIECE, D), BF),) * 2
+        + (jax.ShapeDtypeStruct((2, 2, 2, PIECE, D), BF),),
+        compiler_params=pltpu.CompilerParams(vmem_limit_bytes=24 * 1024 * 1024),
+        cost_estimate=pl.CostEstimate(flops=2_000_000_000, bytes_accessed=4_000_000, transcendentals=0),
+    )(*kept, w_qkv, w_proj, gain)
+    return *backs, grads
 
 
 LATTICE = ("z_hi", "z_lo", "core", "y_hi", "y_lo", "x")
@@ -296,12 +321,6 @@
     parts = total_of(halves, 1).reshape(GROUP, GRAD_ROWS // 2 // GROUP, LANES)
     parts = lax.all_to_all(parts, NEAR, 0, 0)
     return parts
-
-
-def spread_sum(parts, after):
-    parts = lax.all_to_all(total_of(parts, GROUP, after), NEAR, 0, 0)
-    mine = parts.reshape(GRAD_ROWS // 2, LANES)
-    return mine, lax.ppermute(mine, "core", [(0, 1), (1, 0)])
 
 
 def device_at(first, second, third):
@@ -346,21 +365,24 @@
     sides = [None] * 4
     for kind in (1, 2, 3):
         sides[kind] = send(jnp.stack([own[kind], behind[kind]]), kind)
-    *backs, grads = window_pass(own, behind, sides[1:], w_qkv, w_proj, norm_gain)
+    back_0, back_1, back_y, grads = window_pass(own, behind, sides[1:], w_qkv, w_proj, norm_gain)
     parts = near_sum(grads)
-    parts, *backs[1:] = total_of(parts, FAR, through=backs[1:])
-    for kind in (1, 2, 3):
-        backs[kind] = send(backs[kind], kind, True)
-    ahead = send(jnp.stack([back[1] for back in backs]), 0, True)
+    parts, back_y = total_of(parts, FAR, through=(back_y,))
+    home_y = send(back_y, 2, True)
     parts = total_of(lax.all_to_all(parts, "y_hi", 0, 0), FAR)
-    parts = lax.all_to_all(parts, "z_hi", 0, 0)
-    block_out, tokens_grad = pl.pallas_call(
+    home_x = send(jnp.stack([back_1, home_y[1]]), 1, True)
+    parts = total_of(lax.all_to_all(parts, "z_hi", 0, 0), GROUP, after=(home_x,))
+    mine = lax.all_to_all(parts, NEAR, 0, 0).reshape(GRAD_ROWS // 2, LANES)
+    ahead = send(jnp.stack([back_0[1], home_x[0, 1], home_y[0, 1], home_x[1, 1]]), 0, True)
+    block_out, tokens_grad, token = pl.pallas_call(
         join_kernel,
-        out_shape=(jax.ShapeDtypeStruct((ROWS, D), BF),) * 2,
-        in_specs=[SCALAR] + [WHOLE] * 8,
+        out_shape=(jax.ShapeDtypeStruct((ROWS, D), BF),) * 2 + (jax.ShapeDtypeStruct((8, LANES), F32),),
+        in_specs=[SCALAR] + [WHOLE] * 7,
         compiler_params=SMALL,
-    )(core, token_rows, frozen, cot_rows, *backs, ahead)
-    mine, other = spread_sum(parts, (ahead,))
+        cost_estimate=pl.CostEstimate(flops=300_000_000, bytes_accessed=4_000_000, transcendentals=0),
+    )(core, token_rows, frozen, cot_rows, back_0, home_x, home_y, ahead)
+    mine = hold(mine, token)
+    other = lax.ppermute(mine, "core", [(0, 1), (1, 0)])
     qkv_grad, proj_grad, gain_grad = pl.pallas_call(
         grads_kernel,
         out_shape=(

time: 135 us -> 131 us (0.970)
  blocking collectives: 51 us -> 17 us
  waiting for transfers between devices: 16.8 us -> 33.6 us
  starting transfers between devices: 42.2 us -> 50.7 us
  local copies, waits for them, and re-layouts: 1.24 us -> 3.67 us
  Pallas kernels: 22.1 us -> 24.1 us
    all_to_all x3 -> x1, blocking collectives: 45.3 us -> 11.3 us  [local(): lax.all_to_all(parts, 'z_hi', 0, 0)]
    all_to_all x0 -> x2, starting transfers between devices: none -> 8.66 us  [the longest x1 4.94 us: near_sum(): parts = lax.all_to_all(parts, NEAR, 0, 0)]
    ppermute x8 -> x7, waiting for transfers between devices: 16.5 us -> 24.3 us  [send(): return lax.ppermute(block, LATTICE, route(kind, back))]
    all_to_all x0 -> x2, waiting for transfers between devices: none -> 6.14 us  [the longest x1 6.14 us: near_sum(): parts = lax.all_to_all(parts, NEAR, 0, 0)]
    ppermute x1, starting transfers between devices: 5.14 us -> 2.27 us  [local(): other = lax.ppermute(mine, 'core', [(0, 1), (1, 0)])]
    ppermute x8 -> x7, starting transfers between devices: 33.8 us -> 36.4 us  [send(): return lax.ppermute(block, LATTICE, route(kind, back))]
    unnamed x14 -> x22, local copies, waits for them, and re-layouts: 0.03 us -> 2.43 us
    pallas_call x4, Pallas kernels: 0.95 us -> 2.58 us  [total_of(): pl.pallas_call(functools.partial(total_kernel, copies=copies, out_at=len(...]
  transfers between devices with their start and end apart: 10 -> 11, of which waited for: 5 -> 8; matrix products, arithmetic and copies ran while one was open for 1% -> 1% of each run, Pallas kernels for 2% -> 3%
where the time goes in v6:
time: 131 us; the launch traced here: 130 us
  starting transfers between devices  50.7 us (39%)
  waiting for transfers between devices  33.6 us (26%)
  Pallas kernels  24.1 us (18%)
  blocking collectives  17 us (13%)
  local copies, waits for them, and re-layouts  3.67 us (3%)
    ppermute x7, starting transfers between devices, send(): return lax.ppermute(block, LATTICE, route(kind, back))  36.4 us
    ppermute x7, waiting for transfers between devices, send(): return lax.ppermute(block, LATTICE, route(kind, back))  24.3 us
    pallas_call x1, Pallas kernels, window_pass(): pl.pallas_call(window_kernel, out_shape=(jax.ShapeDtypeStruct((GRAD_ROWS,...  13.3 us
    all_to_all x1, blocking collectives, local(): lax.all_to_all(parts, 'z_hi', 0, 0)  11.3 us
    all_to_all x1, waiting for transfers between devices, near_sum(): parts = lax.all_to_all(parts, NEAR, 0, 0)  6.14 us
    all_to_all x1, blocking collectives, near_sum(): lax.all_to_all(rows.reshape(2, GRAD_ROWS // 2, LANES), 'core', 0, 0)  5.7 us
    all_to_all x1, starting transfers between devices, near_sum(): parts = lax.all_to_all(parts, NEAR, 0, 0)  4.94 us
    all_to_all x1, starting transfers between devices, local(): mine = lax.all_to_all(parts, NEAR, 0, 0).reshape(GRAD_ROWS // 2, LANES)  3.72 us
  transfers between devices with their start and end apart: 11, of which 8 were waited for; matrix products, arithmetic and copies ran while one was open for 1% of the time, Pallas kernels for 3%

profile of v6, /device:TPU:1, one launch (start us, length us, event | category | flops | bytes accessed | tf_op | source)
XLA Modules:
  0.0 130.2 jit_solution(13273837642334419361)
XLA Ops:
  0.6 2.4 %shard_map.101 = (bf16[4,2,64,384]{3,2,1,0:T(8,128)(2,1)}, bf16[4,2,64,384]{3,2,1,0:T(8,128)(2,1)}) custom-call(s32[1]{0:T(128)} %bitcast.odd.core, bf16[512,384]{1,0:T(8,128)(2,1)} %bitcast.16, s32[8,8,8]{2,1,0:T(8,128)} %frozen.1, bf16[512,384]{1,0:T(8,128)(2,1)} %bitcast.18), custom_call_target="tpu_custom_call" | custom-call | tf_op jit(solution)/shard_map/pallas_call | solution.py:352
  3.1 6.9 %collective-permute-start = (bf16[4,2,64,384]{3,2,1,0:T(8,128)(2,1)}, bf16[4,2,64,384]{3,2,1,0:T(8,128)(2,1)S(1)}, u32[]{:S(2)}, u32[]{:S(2)}) collective-permute-start(bf16[4,2,64,384]{3,2,1,0:T(8,128)(2,1)} %get-tuple-element.24), channel_id=1, source_target_pairs={{0,480},{1,481},{2,482},{3,483},{4,484},{5,485},{6,486},{7,487},{8... | collective-permute-start | bytes 1179656 | tf_op jit(solution)/shard_map/ppermute | solution.py:346
  12.3 5.1 %collective-permute-start.1 = (bf16[2,2,64,384]{3,2,1,0:T(8,128)(2,1)S(1)}, bf16[2,2,64,384]{3,2,1,0:T(8,128)(2,1)S(1)}, u32[]{:S(2)}, u32[]{:S(2)}) collective-permute-start(bf16[2,2,64,384]{3,2,1,0:T(8,128)(2,1)S(1)} %pad_maximum_fusion.2), channel_id=1, source_target_pairs={{0,31},{1,24},{2,25},{3,26},{4,27},{5,28},{6,29},{7,30},{8,7},{9,0... | collective-permute-start | bytes 589832 | tf_op jit(solution)/shard_map/ppermute | solution.py:346
  17.5 5.4 %collective-permute-start.2 = (bf16[2,2,64,384]{3,2,1,0:T(8,128)(2,1)S(1)}, bf16[2,2,64,384]{3,2,1,0:T(8,128)(2,1)S(1)}, u32[]{:S(2)}, u32[]{:S(2)}) collective-permute-start(bf16[2,2,64,384]{3,2,1,0:T(8,128)(2,1)S(1)} %pad_maximum_fusion.3), channel_id=1, source_target_pairs={{0,24},{1,25},{2,26},{3,27},{4,28},{5,29},{6,30},{7,31},{8,0},{9,1... | collective-permute-start | bytes 589832 | tf_op jit(solution)/shard_map/ppermute | solution.py:346
  22.9 3.1 %collective-permute-start.3 = (bf16[2,2,64,384]{3,2,1,0:T(8,128)(2,1)S(1)}, bf16[2,2,64,384]{3,2,1,0:T(8,128)(2,1)S(1)}, u32[]{:S(2)}, u32[]{:S(2)}) collective-permute-start(bf16[2,2,64,384]{3,2,1,0:T(8,128)(2,1)S(1)} %pad_maximum_fusion.4), channel_id=1, source_target_pairs={{0,7},{1,0},{2,1},{3,2},{4,3},{5,4},{6,5},{7,6},{8,15},{9,8},{10,9... | collective-permute-start | bytes 589832 | tf_op jit(solution)/shard_map/ppermute | solution.py:346
  26.1 3.4 %collective-permute-done.2.side_2 = bf16[2,2,64,384]{3,2,1,0:T(8,128)(2,1)S(1)} collective-permute-done((bf16[2,2,64,384]{3,2,1,0:T(8,128)(2,1)S(1)}, bf16[2,2,64,384]{3,2,1,0:T(8,128)(2,1)S(1)}, u32[]{:S(2)}, u32[]{:S(2)}) %collective-permute-start.2) | collective-permute-done | bytes 196640 | tf_op jit(solution)/shard_map/ppermute | solution.py:346
  29.5 7.1 %collective-permute-done.3.side_1 = bf16[2,2,64,384]{3,2,1,0:T(8,128)(2,1)S(1)} collective-permute-done((bf16[2,2,64,384]{3,2,1,0:T(8,128)(2,1)S(1)}, bf16[2,2,64,384]{3,2,1,0:T(8,128)(2,1)S(1)}, u32[]{:S(2)}, u32[]{:S(2)}) %collective-permute-start.3) | collective-permute-done | bytes 196640 | tf_op jit(solution)/shard_map/ppermute | solution.py:346
  36.6 13.3 %shard_map.102 = (bf16[4608,128]{1,0:T(8,128)(2,1)S(1)}, bf16[384,512]{1,0:T(8,128)(2,1)S(1)}, bf16[512,1152]{1,0:T(8,128)(2,1)S(1)}, f32[512,384]{1,0:T(8,128)S(1)}, f32[512,128]{1,0:T(8,128)S(1)}) custom-call(bf16[4,2,64,384]{3,2,1,0:T(8,128)(2,1)S(1)} %copy-done.3, bf16[4,2,64,384]{3,2,1,0:T(8,128)(2,1)S(1)} %collective-permute-done.behind, ...), custom_call_target="tpu_custom_call" | custom-call | flops 12000000000 | bytes 5000000 | tf_op jit(solution)/shard_map/pallas_call | solution.py:276
  50.0 5.7 %all_to_all.25.parts = bf16[2,2304,128]{2,1,0:T(8,128)(2,1)S(1)} all-to-all(bf16[2,2304,128]{2,1,0:T(8,128)(2,1)S(1)} %bitcast.20), channel_id=1, replica_groups=mesh['z_hi'=4,'z_lo'=2,'core'=2,'y_hi'=4,'y_lo'=2,'x'=4] {'core'}, dimensions={0} | all-to-all | bytes 2359296 | tf_op jit(solution)/shard_map/all_to_all | solution.py:320
  56.6 4.9 %all-to-all-start.1 = ((bf16[16,144,128]{2,1,0:T(8,128)(2,1)}), bf16[16,144,128]{2,1,0:T(8,128)(2,1)S(1)}, u32[]{:S(2)}, u32[]{:S(2)}) async-start(bf16[16,144,128]{2,1,0:T(8,128)(2,1)} %bitcast.5), calls=%async_computation.1 | async-start | bytes 1179648 | tf_op jit(solution)/shard_map/all_to_all | solution.py:322
  64.0 1.6 %shard_map.103 = (bf16[2,2,64,384]{3,2,1,0:T(8,128)(2,1)S(1)}, bf16[2,2,64,384]{3,2,1,0:T(8,128)(2,1)S(1)}, bf16[2,2,2,64,384]{4,3,2,1,0:T(8,128)(2,1)S(1)}) custom-call(bf16[384,512]{1,0:T(8,128)(2,1)S(1)} %get-tuple-element.25.mixed_t, bf16[512,1152]{1,0:T(8,128)(2,1)S(1)} %copy-done.7, f32[512,384]{1,0:T(8,128)S(1)} %copy-done.9, ...), custom_call_target="tpu_custom_call" | custom-call | flops 2000000000 | bytes 4000000 | tf_op jit(solution)/shard_map/pallas_call | solution.py:299
  65.6 6.1 %all-to-all-done.1.parts = bf16[16,144,128]{2,1,0:T(8,128)(2,1)S(1)} async-done(((bf16[16,144,128]{2,1,0:T(8,128)(2,1)}), bf16[16,144,128]{2,1,0:T(8,128)(2,1)S(1)}, u32[]{:S(2)}, u32[]{:S(2)}) %all-to-all-start.1) | async-done | bytes 589856 | tf_op jit(solution)/shard_map/all_to_all | solution.py:322
  72.5 5.2 %collective-permute-start.4 = (bf16[2,2,2,64,384]{4,3,2,1,0:T(8,128)(2,1)S(1)}, bf16[2,2,2,64,384]{4,3,2,1,0:T(8,128)(2,1)S(1)}, u32[]{:S(2)}, u32[]{:S(2)}) collective-permute-start(bf16[2,2,2,64,384]{4,3,2,1,0:T(8,128)(2,1)S(1)} %get-tuple-element.33), channel_id=1, source_target_pairs={{24,0},{25,1},{26,2},{27,3},{28,4},{29,5},{30,6},{31,7},{0,8},{1,9... | collective-permute-start | bytes 1179656 | tf_op jit(solution)/shard_map/ppermute | solution.py:346
  77.7 3.3 %all-to-all-start.2 = ((bf16[4,144,128]{2,1,0:T(8,128)(2,1)}), bf16[4,144,128]{2,1,0:T(8,128)(2,1)S(1)}, u32[]{:S(2)}, u32[]{:S(2)}) async-start(bf16[4,144,128]{2,1,0:T(8,128)(2,1)} %get-tuple-element.36), calls=%async_computation.2 | async-start | bytes 294912 | tf_op jit(solution)/shard_map/all_to_all | solution.py:372
  81.1 6.2 %collective-permute-done.4.home_2 = bf16[2,2,2,64,384]{4,3,2,1,0:T(8,128)(2,1)S(1)} collective-permute-done((bf16[2,2,2,64,384]{4,3,2,1,0:T(8,128)(2,1)S(1)}, bf16[2,2,2,64,384]{4,3,2,1,0:T(8,128)(2,1)S(1)}, u32[]{:S(2)}, u32[]{:S(2)}) %collective-permute-start.4) | collective-permute-done | bytes 393248 | tf_op jit(solution)/shard_map/ppermute | solution.py:346
  87.3 3.4 %collective-permute-start.5 = (bf16[2,2,2,64,384]{4,3,2,1,0:T(8,128)(2,1)S(1)}, bf16[2,2,2,64,384]{4,3,2,1,0:T(8,128)(2,1)S(1)}, u32[]{:S(2)}, u32[]{:S(2)}) collective-permute-start(bf16[2,2,2,64,384]{4,3,2,1,0:T(8,128)(2,1)S(1)} %pad_maximum_fusion), channel_id=1, source_target_pairs={{7,0},{0,1},{1,2},{2,3},{3,4},{4,5},{5,6},{6,7},{15,8},{8,9},{9,10... | collective-permute-start | bytes 1179656 | tf_op jit(solution)/shard_map/ppermute | solution.py:346
  92.2 11.3 %all_to_all.26.parts = bf16[4,144,128]{2,1,0:T(8,128)(2,1)S(1)} all-to-all(bf16[4,144,128]{2,1,0:T(8,128)(2,1)S(1)} %shard_map.107), channel_id=1, replica_groups=mesh['z_hi'=4,'z_lo'=2,'core'=2,'y_hi'=4,'y_lo'=2,'x'=4] {'z_hi'}, dimensions={0} | all-to-all | bytes 294912 | tf_op jit(solution)/shard_map/all_to_all | solution.py:374
  104.4 3.7 %all-to-all-start.4 = ((bf16[16,144,128]{2,1,0:T(8,128)(2,1)}), bf16[16,144,128]{2,1,0:T(8,128)(2,1)S(1)}, u32[]{:S(2)}, u32[]{:S(2)}) async-start(bf16[16,144,128]{2,1,0:T(8,128)(2,1)} %shard_map.108), calls=%async_computation.4 | async-start | bytes 1179648 | tf_op jit(solution)/shard_map/all_to_all | solution.py:375
  108.3 7.2 %collective-permute-start.6 = (bf16[4,2,64,384]{3,2,1,0:T(8,128)(2,1)S(1)}, bf16[4,2,64,384]{3,2,1,0:T(8,128)(2,1)S(1)}, u32[]{:S(2)}, u32[]{:S(2)}) collective-permute-start(bf16[4,2,64,384]{3,2,1,0:T(8,128)(2,1)S(1)} %pad_maximum_fusion.1), channel_id=1, source_target_pairs={{480,0},{481,1},{482,2},{483,3},{484,4},{485,5},{486,6},{487,7},{4... | collective-permute-start | bytes 1179656 | tf_op jit(solution)/shard_map/ppermute | solution.py:346
  115.5 6.5 %collective-permute-done.6.ahead = bf16[4,2,64,384]{3,2,1,0:T(8,128)(2,1)S(1)} collective-permute-done((bf16[4,2,64,384]{3,2,1,0:T(8,128)(2,1)S(1)}, bf16[4,2,64,384]{3,2,1,0:T(8,128)(2,1)S(1)}, u32[]{:S(2)}, u32[]{:S(2)}) %collective-permute-start.6) | collective-permute-done | bytes 393248 | tf_op jit(solution)/shard_map/ppermute | solution.py:346
  122.1 2.4 %shard_map.106 = (bf16[512,384]{1,0:T(8,128)(2,1)}, bf16[512,384]{1,0:T(8,128)(2,1)}, f32[8,128]{1,0:T(8,128)S(1)}) custom-call(s32[1]{0:T(128)} %bitcast.odd.core, bf16[512,384]{1,0:T(8,128)(2,1)S(1)} %bitcast.17, s32[8,8,8]{2,1,0:T(8,128)S(1)} %copy-done.4, bf16[512,384]{1,0:T(8,128)(2,1)S(1)} %bitcast.19, ...), custom_call_target="tpu_custom_call" | custom-call | flops 300000000 | bytes 4000000 | tf_op jit(solution)/shard_map/pallas_call | solution.py:377
  124.5 2.3 %collective-permute-start.7 = (bf16[2304,128]{1,0:T(8,128)(2,1)S(1)}, bf16[2304,128]{1,0:T(8,128)(2,1)S(1)}, u32[]{:S(2)}, u32[]{:S(2)}) collective-permute-start(bf16[2304,128]{1,0:T(8,128)(2,1)S(1)} %shard_map.109.mine), channel_id=1, source_target_pairs={{0,32},{32,0},{1,33},{33,1},{2,34},{34,2},{3,35},{35,3},{4,36},{36... | collective-permute-start | bytes 1769480 | tf_op jit(solution)/shard_map/ppermute | solution.py:385
  126.8 1.6 %collective-permute-done.7.other = bf16[2304,128]{1,0:T(8,128)(2,1)S(1)} collective-permute-done((bf16[2304,128]{1,0:T(8,128)(2,1)S(1)}, bf16[2304,128]{1,0:T(8,128)(2,1)S(1)}, u32[]{:S(2)}, u32[]{:S(2)}) %collective-permute-start.7) | collective-permute-done | bytes 589856 | tf_op jit(solution)/shard_map/ppermute | solution.py:385
  128.4 1.8 %shard_map.110 = (f32[384,1152]{1,0:T(8,128)}, f32[384,384]{1,0:T(8,128)}, f32[384]{0:T(512)}) custom-call(s32[1]{0:T(128)} %bitcast.odd.core, bf16[2304,128]{1,0:T(8,128)(2,1)S(1)} %shard_map.109.mine, bf16[2304,128]{1,0:T(8,128)(2,1)S(1)} %collective-permute-done.7.other, bf16[384,1152]{1,0:T(8,128)(2,1)S(1)} %copy-done.2, f32[1,384]{1,0:T(1,128)S(1)} %reshape.41.gain), custom_call_target="tpu_custom_call" | custom-call | tf_op jit(solution)/shard_map/pallas_call | solution.py:386
  (44 shorter events, 9.1 us)
Async XLA Ops:
  3.1 9.2 %collective-permute-start = (bf16[4,2,64,384]{3,2,1,0:T(8,128)(2,1)}, bf16[4,2,64,384]{3,2,1,0:T(8,128)(2,1)S(1)}, u32[]{:S(2)}, u32[]{:S(2)}) collective-permute-start(bf16[4,2,64,384]{3,2,1,0:T(8,128)(2,1)} %get-tuple-element.24), channel_id=1, source_target_pairs={{0,480},{1,481},{2,482},{3,483},{4,484},{5,485},{6,486},{7,487},{8... | collective-permute-start | bytes 1179656 | tf_op jit(solution)/shard_map/ppermute | solution.py:346
  9.9 16.1 %copy-start.10 = (f32[384]{0:T(512)S(1)}, f32[384]{0:T(512)}, u32[]{:S(2)}) copy-start(f32[384]{0:T(512)} %param.11) | copy-start | bytes 4612
  9.9 26.7 %copy-start.2 = (bf16[384,1152]{1,0:T(8,128)(2,1)S(1)}, bf16[384,1152]{1,0:T(8,128)(2,1)}, u32[]{:S(2)}) copy-start(bf16[384,1152]{1,0:T(8,128)(2,1)} %w_qkv.5) | copy-start | bytes 2654212
  10.0 26.7 %copy-start.3 = (bf16[4,2,64,384]{3,2,1,0:T(8,128)(2,1)S(1)}, bf16[4,2,64,384]{3,2,1,0:T(8,128)(2,1)}, u32[]{:S(2)}) copy-start(bf16[4,2,64,384]{3,2,1,0:T(8,128)(2,1)} %get-tuple-element.23.own) | copy-start | bytes 1179652
  10.0 26.7 %copy-start.5 = (bf16[384,384]{1,0:T(8,128)(2,1)S(1)}, bf16[384,384]{1,0:T(8,128)(2,1)}, u32[]{:S(2)}) copy-start(bf16[384,384]{1,0:T(8,128)(2,1)} %w_proj.3) | copy-start | bytes 884740
  12.3 13.8 %collective-permute-start.1 = (bf16[2,2,64,384]{3,2,1,0:T(8,128)(2,1)S(1)}, bf16[2,2,64,384]{3,2,1,0:T(8,128)(2,1)S(1)}, u32[]{:S(2)}, u32[]{:S(2)}) collective-permute-start(bf16[2,2,64,384]{3,2,1,0:T(8,128)(2,1)S(1)} %pad_maximum_fusion.2), channel_id=1, source_target_pairs={{0,31},{1,24},{2,25},{3,26},{4,27},{5,28},{6,29},{7,30},{8,7},{9,0... | collective-permute-start | bytes 589832 | tf_op jit(solution)/shard_map/ppermute | solution.py:346
  17.5 12.0 %collective-permute-start.2 = (bf16[2,2,64,384]{3,2,1,0:T(8,128)(2,1)S(1)}, bf16[2,2,64,384]{3,2,1,0:T(8,128)(2,1)S(1)}, u32[]{:S(2)}, u32[]{:S(2)}) collective-permute-start(bf16[2,2,64,384]{3,2,1,0:T(8,128)(2,1)S(1)} %pad_maximum_fusion.3), channel_id=1, source_target_pairs={{0,24},{1,25},{2,26},{3,27},{4,28},{5,29},{6,30},{7,31},{8,0},{9,1... | collective-permute-start | bytes 589832 | tf_op jit(solution)/shard_map/ppermute | solution.py:346
  22.9 13.7 %collective-permute-start.3 = (bf16[2,2,64,384]{3,2,1,0:T(8,128)(2,1)S(1)}, bf16[2,2,64,384]{3,2,1,0:T(8,128)(2,1)S(1)}, u32[]{:S(2)}, u32[]{:S(2)}) collective-permute-start(bf16[2,2,64,384]{3,2,1,0:T(8,128)(2,1)S(1)} %pad_maximum_fusion.4), channel_id=1, source_target_pairs={{0,7},{1,0},{2,1},{3,2},{4,3},{5,4},{6,5},{7,6},{8,15},{9,8},{10,9... | collective-permute-start | bytes 589832 | tf_op jit(solution)/shard_map/ppermute | solution.py:346
  50.0 5.7 %copy-start.6 = (bf16[512,1152]{1,0:T(8,128)(2,1)}, bf16[512,1152]{1,0:T(8,128)(2,1)S(1)}, u32[]{:S(2)}) copy-start(bf16[512,1152]{1,0:T(8,128)(2,1)S(1)} %get-tuple-element.26.d_qkv) | copy-start | bytes 3538948
  50.0 5.7 %copy-start.8 = (f32[512,384]{1,0:T(8,128)}, f32[512,384]{1,0:T(8,128)S(1)}, u32[]{:S(2)}) copy-start(f32[512,384]{1,0:T(8,128)S(1)} %get-tuple-element.27.unit) | copy-start | bytes 2359300
  56.6 15.1 %all-to-all-start.1 = ((bf16[16,144,128]{2,1,0:T(8,128)(2,1)}), bf16[16,144,128]{2,1,0:T(8,128)(2,1)S(1)}, u32[]{:S(2)}, u32[]{:S(2)}) async-start(bf16[16,144,128]{2,1,0:T(8,128)(2,1)} %bitcast.5), calls=%async_computation.1 | async-start | bytes 1179648 | tf_op jit(solution)/shard_map/all_to_all | solution.py:322
  61.6 1.3 copy-start.7
  62.9 1.1 copy-start.9
  72.5 14.8 %collective-permute-start.4 = (bf16[2,2,2,64,384]{4,3,2,1,0:T(8,128)(2,1)S(1)}, bf16[2,2,2,64,384]{4,3,2,1,0:T(8,128)(2,1)S(1)}, u32[]{:S(2)}, u32[]{:S(2)}) collective-permute-start(bf16[2,2,2,64,384]{4,3,2,1,0:T(8,128)(2,1)S(1)} %get-tuple-element.33), channel_id=1, source_target_pairs={{24,0},{25,1},{26,2},{27,3},{28,4},{29,5},{30,6},{31,7},{0,8},{1,9... | collective-permute-start | bytes 1179656 | tf_op jit(solution)/shard_map/ppermute | solution.py:346
  77.7 14.5 %all-to-all-start.2 = ((bf16[4,144,128]{2,1,0:T(8,128)(2,1)}), bf16[4,144,128]{2,1,0:T(8,128)(2,1)S(1)}, u32[]{:S(2)}, u32[]{:S(2)}) async-start(bf16[4,144,128]{2,1,0:T(8,128)(2,1)} %get-tuple-element.36), calls=%async_computation.2 | async-start | bytes 294912 | tf_op jit(solution)/shard_map/all_to_all | solution.py:372
  87.3 16.3 %collective-permute-start.5 = (bf16[2,2,2,64,384]{4,3,2,1,0:T(8,128)(2,1)S(1)}, bf16[2,2,2,64,384]{4,3,2,1,0:T(8,128)(2,1)S(1)}, u32[]{:S(2)}, u32[]{:S(2)}) collective-permute-start(bf16[2,2,2,64,384]{4,3,2,1,0:T(8,128)(2,1)S(1)} %pad_maximum_fusion), channel_id=1, source_target_pairs={{7,0},{0,1},{1,2},{2,3},{3,4},{4,5},{5,6},{6,7},{15,8},{8,9},{9,10... | collective-permute-start | bytes 1179656 | tf_op jit(solution)/shard_map/ppermute | solution.py:346
  104.4 17.6 %copy-start = (bf16[8,8,8,384]{3,2,1,0:T(8,128)(2,1)S(1)}, bf16[8,8,8,384]{3,2,1,0:T(8,128)(2,1)}, u32[]{:S(2)}) copy-start(bf16[8,8,8,384]{3,2,1,0:T(8,128)(2,1)} %param.6) | copy-start | bytes 1179652
  104.4 17.6 %copy-start.1 = (bf16[8,8,8,384]{3,2,1,0:T(8,128)(2,1)S(1)}, bf16[8,8,8,384]{3,2,1,0:T(8,128)(2,1)}, u32[]{:S(2)}) copy-start(bf16[8,8,8,384]{3,2,1,0:T(8,128)(2,1)} %param.8) | copy-start | bytes 1179652
  104.4 17.6 %copy-start.4 = (s32[8,8,8]{2,1,0:T(8,128)S(1)}, s32[8,8,8]{2,1,0:T(8,128)}, u32[]{:S(2)}) copy-start(s32[8,8,8]{2,1,0:T(8,128)} %frozen.1) | copy-start | bytes 6148
  104.4 20.1 %all-to-all-start.4 = ((bf16[16,144,128]{2,1,0:T(8,128)(2,1)}), bf16[16,144,128]{2,1,0:T(8,128)(2,1)S(1)}, u32[]{:S(2)}, u32[]{:S(2)}) async-start(bf16[16,144,128]{2,1,0:T(8,128)(2,1)} %shard_map.108), calls=%async_computation.4 | async-start | bytes 1179648 | tf_op jit(solution)/shard_map/all_to_all | solution.py:375
  108.3 13.8 %collective-permute-start.6 = (bf16[4,2,64,384]{3,2,1,0:T(8,128)(2,1)S(1)}, bf16[4,2,64,384]{3,2,1,0:T(8,128)(2,1)S(1)}, u32[]{:S(2)}, u32[]{:S(2)}) collective-permute-start(bf16[4,2,64,384]{3,2,1,0:T(8,128)(2,1)S(1)} %pad_maximum_fusion.1), channel_id=1, source_target_pairs={{480,0},{481,1},{482,2},{483,3},{484,4},{485,5},{486,6},{487,7},{4... | collective-permute-start | bytes 1179656 | tf_op jit(solution)/shard_map/ppermute | solution.py:346
  124.5 3.9 %collective-permute-start.7 = (bf16[2304,128]{1,0:T(8,128)(2,1)S(1)}, bf16[2304,128]{1,0:T(8,128)(2,1)S(1)}, u32[]{:S(2)}, u32[]{:S(2)}) collective-permute-start(bf16[2304,128]{1,0:T(8,128)(2,1)S(1)} %shard_map.109.mine), channel_id=1, source_target_pairs={{0,32},{32,0},{1,33},{33,1},{2,34},{34,2},{3,35},{35,3},{4,36},{36... | collective-permute-start | bytes 1769480 | tf_op jit(solution)/shard_map/ppermute | solution.py:385

commit v7 on v5

--- a/solution.py
+++ b/solution.py
@@ -35,7 +35,7 @@
 
 
 def window_kernel(
-    own, behind, side_3, side_2, side_1, w_qkv, w_proj, gain, back_0, back_1, back_2, back_3, grads,
+    own, behind, side_3, side_2, side_1, w_qkv, w_proj, gain, back_0, back_2, back_x, grads,
     cot, qkv, d_mixed, keys_t, values_t, mixed_t, d_queries_t, d_qkv, unit, inv_std, normed,
 ):
     step = 2 * PIECE
@@ -102,7 +102,7 @@
 
     d_qkv[:, pl.ds(0, D)] = d_queries_t[...].T
     branch = dot(mixed_t[...].T, w_proj[...]).astype(BF)
-    backs = (back_0, back_1, back_2, back_3)
+    backs = (back_0, back_x.at[0], back_2, back_x.at[1])
     for group in range(4):
         for place in range(2):
             start = (2 * group + place) * PIECE
@@ -177,8 +177,9 @@
                 target[group, 1, pl.ds(plane * 16, 16), :] = cot[rows]
 
 
-def join_kernel(odd, tokens, frozen, cotangent, home_0, home_1, home_2, home_3, ahead, block_out, tokens_grad):
-    homes = (home_0, home_1, home_2, home_3)
+def join_kernel(odd, tokens, frozen, cotangent, home_0, home_x, home_y, ahead, block_out, tokens_grad, token):
+    homes = (home_0, home_x.at[0], home_y.at[0], home_y.at[1])
+    token[...] = jnp.zeros_like(token)
     keeps = keep_rows(frozen)
     shape = (WIN * WIN, WIN * WIN)
     diagonal = ones_where(lax.broadcasted_iota(jnp.int32, shape, 0) == lax.broadcasted_iota(jnp.int32, shape, 1))
@@ -229,6 +230,18 @@
         compiler_params=SMALL,
     )(parts, *after, *through)
     return (total, *passed) if through else total
+
+
+def hold(array, until):
+    anywhere = pl.BlockSpec(memory_space=pl.ANY)
+    return pl.pallas_call(
+        lambda *refs: None,
+        out_shape=jax.ShapeDtypeStruct(array.shape, array.dtype),
+        in_specs=[anywhere] * 2,
+        out_specs=anywhere,
+        input_output_aliases={0: 0},
+        compiler_params=SMALL,
+    )(array, until)
 
 
 def grads_kernel(core, mine, other, w_qkv, gain, qkv_grad, proj_grad, gain_grad):
@@ -259,8 +272,8 @@
 
     return pl.pallas_call(
         window_kernel,
-        out_shape=(jax.ShapeDtypeStruct((2, 2, PIECE, D), BF),) * 4
-        + (jax.ShapeDtypeStruct((GRAD_ROWS, LANES), BF),),
+        out_shape=(jax.ShapeDtypeStruct((2, 2, PIECE, D), BF),) * 2
+        + (jax.ShapeDtypeStruct((2, 2, 2, PIECE, D), BF), jax.ShapeDtypeStruct((GRAD_ROWS, LANES), BF)),
         scratch_shapes=[
             buffer((ROWS, D), BF),
             buffer((ROWS, 3 * D), BF),
@@ -296,12 +309,6 @@
     parts = total_of(halves, 1).reshape(GROUP, GRAD_ROWS // 2 // GROUP, LANES)
     parts = lax.all_to_all(parts, NEAR, 0, 0)
     return parts
-
-
-def spread_sum(parts, after):
-    parts = lax.all_to_all(total_of(parts, GROUP, after), NEAR, 0, 0)
-    mine = parts.reshape(GRAD_ROWS // 2, LANES)
-    return mine, lax.ppermute(mine, "core", [(0, 1), (1, 0)])
 
 
 def device_at(first, second, third):
@@ -346,21 +353,24 @@
     sides = [None] * 4
     for kind in (1, 2, 3):
         sides[kind] = send(jnp.stack([own[kind], behind[kind]]), kind)
-    *backs, grads = window_pass(own, behind, sides[1:], w_qkv, w_proj, norm_gain)
+    back_0, back_2, back_x, grads = window_pass(own, behind, sides[1:], w_qkv, w_proj, norm_gain)
     parts = near_sum(grads)
-    parts, *backs[1:] = total_of(parts, FAR, through=backs[1:])
-    for kind in (1, 2, 3):
-        backs[kind] = send(backs[kind], kind, True)
-    ahead = send(jnp.stack([back[1] for back in backs]), 0, True)
-    parts = total_of(lax.all_to_all(parts, "y_hi", 0, 0), FAR)
-    parts = lax.all_to_all(parts, "z_hi", 0, 0)
-    block_out, tokens_grad = pl.pallas_call(
+    home_x = send(back_x, 1, True)
+    parts, back_2 = total_of(parts, FAR, after=(home_x,), through=(back_2,))
+    home_y = send(jnp.stack([back_2, home_x[1]]), 2, True)
+    parts, home_y = total_of(lax.all_to_all(parts, "y_hi", 0, 0), FAR, through=(home_y,))
+    ahead = send(jnp.stack([back_0[1], home_x[0, 1], home_y[0, 1], home_y[1, 1]]), 0, True)
+    parts = total_of(lax.all_to_all(parts, "z_hi", 0, 0), GROUP, after=(ahead,))
+    mine = lax.all_to_all(parts, NEAR, 0, 0).reshape(GRAD_ROWS // 2, LANES)
+    block_out, tokens_grad, token = pl.pallas_call(
         join_kernel,
-        out_shape=(jax.ShapeDtypeStruct((ROWS, D), BF),) * 2,
-        in_specs=[SCALAR] + [WHOLE] * 8,
+        out_shape=(jax.ShapeDtypeStruct((ROWS, D), BF),) * 2 + (jax.ShapeDtypeStruct((8, LANES), F32),),
+        in_specs=[SCALAR] + [WHOLE] * 7,
         compiler_params=SMALL,
-    )(core, token_rows, frozen, cot_rows, *backs, ahead)
-    mine, other = spread_sum(parts, (ahead,))
+        cost_estimate=pl.CostEstimate(flops=300_000_000, bytes_accessed=4_000_000, transcendentals=0),
+    )(core, token_rows, frozen, cot_rows, back_0, home_x, home_y, ahead)
+    mine = hold(mine, token)
+    other = lax.ppermute(mine, "core", [(0, 1), (1, 0)])
     qkv_grad, proj_grad, gain_grad = pl.pallas_call(
         grads_kernel,
         out_shape=(

time: 135 us -> 135 us (level)
  blocking collectives: 51 us -> 17.4 us
  waiting for transfers between devices: 16.8 us -> 39.8 us
  starting transfers between devices: 42.2 us -> 50.3 us
  Pallas kernels: 22.1 us -> 23.7 us
    all_to_all x3 -> x1, blocking collectives: 45.3 us -> 11.7 us  [local(): parts = total_of(lax.all_to_all(parts, 'z_hi', 0, 0), GROUP, after=(ahead,))]
    all_to_all x1 -> x3, waiting for transfers between devices: 0.37 us -> 18.5 us  [the longest x1 11.4 us: local(): lax.all_to_all(parts, 'y_hi', 0, 0)]
    all_to_all x1 -> x3, starting transfers between devices: 3.35 us -> 11.9 us  [the longest x1 4.94 us: near_sum(): parts = lax.all_to_all(parts, NEAR, 0, 0)]
    ppermute x8 -> x7, waiting for transfers between devices: 16.5 us -> 19.7 us  [send(): return lax.ppermute(block, LATTICE, route(kind, back))]
    ppermute x1, starting transfers between devices: 5.14 us -> 3.13 us  [local(): other = lax.ppermute(mine, 'core', [(0, 1), (1, 0)])]
    pallas_call x4, Pallas kernels: 0.95 us -> 2.58 us  [total_of(): pl.pallas_call(functools.partial(total_kernel, copies=copies, out_at=len(...]
    ppermute x1, waiting for transfers between devices: 0.01 us -> 1.61 us  [local(): other = lax.ppermute(mine, 'core', [(0, 1), (1, 0)])]
    ppermute x8 -> x7, starting transfers between devices: 33.8 us -> 35.3 us  [send(): return lax.ppermute(block, LATTICE, route(kind, back))]
  transfers between devices with their start and end apart: 10 -> 11, of which waited for: 5 -> 7; matrix products, arithmetic and copies ran while one was open for 1% -> 1% of each run, Pallas kernels for 2% -> 2%
where the time goes in v7:
time: 135 us; the launch traced here: 134 us
  starting transfers between devices  50.3 us (37%)
  waiting for transfers between devices  39.8 us (29%)
  Pallas kernels  23.7 us (18%)
  blocking collectives  17.4 us (13%)
  local copies, waits for them, and re-layouts  2.19 us (2%)
    ppermute x7, starting transfers between devices, send(): return lax.ppermute(block, LATTICE, route(kind, back))  35.3 us
    ppermute x7, waiting for transfers between devices, send(): return lax.ppermute(block, LATTICE, route(kind, back))  19.7 us
    pallas_call x1, Pallas kernels, window_pass(): pl.pallas_call(window_kernel, out_shape=(jax.ShapeDtypeStruct((2, 2, PIEC...  14.5 us
    all_to_all x1, blocking collectives, local(): parts = total_of(lax.all_to_all(parts, 'z_hi', 0, 0), GROUP, after=(ahead,))  11.7 us
    all_to_all x1, waiting for transfers between devices, local(): lax.all_to_all(parts, 'y_hi', 0, 0)  11.4 us
    all_to_all x1, waiting for transfers between devices, local(): mine = lax.all_to_all(parts, NEAR, 0, 0).reshape(GRAD_ROWS // 2, LANES)  7.05 us
    all_to_all x1, blocking collectives, near_sum(): lax.all_to_all(rows.reshape(2, GRAD_ROWS // 2, LANES), 'core', 0, 0)  5.7 us
    all_to_all x1, starting transfers between devices, near_sum(): parts = lax.all_to_all(parts, NEAR, 0, 0)  4.94 us
  transfers between devices with their start and end apart: 11, of which 7 were waited for; matrix products, arithmetic and copies ran while one was open for 1% of the time, Pallas kernels for 2%

profile of v7, /device:TPU:1, one launch (start us, length us, event | category | flops | bytes accessed | tf_op | source)
XLA Modules:
  0.0 134.5 jit_solution(13357269875192846564)
XLA Ops:
  0.6 2.4 %shard_map.101 = (bf16[4,2,64,384]{3,2,1,0:T(8,128)(2,1)}, bf16[4,2,64,384]{3,2,1,0:T(8,128)(2,1)}) custom-call(s32[1]{0:T(128)} %bitcast.odd.core, bf16[512,384]{1,0:T(8,128)(2,1)} %bitcast.16, s32[8,8,8]{2,1,0:T(8,128)} %frozen.1, bf16[512,384]{1,0:T(8,128)(2,1)} %bitcast.18), custom_call_target="tpu_custom_call" | custom-call | tf_op jit(solution)/shard_map/pallas_call | solution.py:340
  3.1 6.9 %collective-permute-start = (bf16[4,2,64,384]{3,2,1,0:T(8,128)(2,1)}, bf16[4,2,64,384]{3,2,1,0:T(8,128)(2,1)S(1)}, u32[]{:S(2)}, u32[]{:S(2)}) collective-permute-start(bf16[4,2,64,384]{3,2,1,0:T(8,128)(2,1)} %get-tuple-element.22), channel_id=1, source_target_pairs={{0,480},{1,481},{2,482},{3,483},{4,484},{5,485},{6,486},{7,487},{8... | collective-permute-start | bytes 1179656 | tf_op jit(solution)/shard_map/ppermute | solution.py:334
  10.0 1.1 fusion
  12.3 5.1 %collective-permute-start.1 = (bf16[2,2,64,384]{3,2,1,0:T(8,128)(2,1)S(1)}, bf16[2,2,64,384]{3,2,1,0:T(8,128)(2,1)S(1)}, u32[]{:S(2)}, u32[]{:S(2)}) collective-permute-start(bf16[2,2,64,384]{3,2,1,0:T(8,128)(2,1)S(1)} %pad_maximum_fusion.2), channel_id=1, source_target_pairs={{0,31},{1,24},{2,25},{3,26},{4,27},{5,28},{6,29},{7,30},{8,7},{9,0... | collective-permute-start | bytes 589832 | tf_op jit(solution)/shard_map/ppermute | solution.py:334
  17.5 5.4 %collective-permute-start.2 = (bf16[2,2,64,384]{3,2,1,0:T(8,128)(2,1)S(1)}, bf16[2,2,64,384]{3,2,1,0:T(8,128)(2,1)S(1)}, u32[]{:S(2)}, u32[]{:S(2)}) collective-permute-start(bf16[2,2,64,384]{3,2,1,0:T(8,128)(2,1)S(1)} %pad_maximum_fusion.3), channel_id=1, source_target_pairs={{0,24},{1,25},{2,26},{3,27},{4,28},{5,29},{6,30},{7,31},{8,0},{9,1... | collective-permute-start | bytes 589832 | tf_op jit(solution)/shard_map/ppermute | solution.py:334
  22.9 3.1 %collective-permute-start.3 = (bf16[2,2,64,384]{3,2,1,0:T(8,128)(2,1)S(1)}, bf16[2,2,64,384]{3,2,1,0:T(8,128)(2,1)S(1)}, u32[]{:S(2)}, u32[]{:S(2)}) collective-permute-start(bf16[2,2,64,384]{3,2,1,0:T(8,128)(2,1)S(1)} %pad_maximum_fusion.4), channel_id=1, source_target_pairs={{0,7},{1,0},{2,1},{3,2},{4,3},{5,4},{6,5},{7,6},{8,15},{9,8},{10,9... | collective-permute-start | bytes 589832 | tf_op jit(solution)/shard_map/ppermute | solution.py:334
  26.1 3.4 %collective-permute-done.2.side_2 = bf16[2,2,64,384]{3,2,1,0:T(8,128)(2,1)S(1)} collective-permute-done((bf16[2,2,64,384]{3,2,1,0:T(8,128)(2,1)S(1)}, bf16[2,2,64,384]{3,2,1,0:T(8,128)(2,1)S(1)}, u32[]{:S(2)}, u32[]{:S(2)}) %collective-permute-start.2) | collective-permute-done | bytes 196640 | tf_op jit(solution)/shard_map/ppermute | solution.py:334
  29.5 7.1 %collective-permute-done.3.side_1 = bf16[2,2,64,384]{3,2,1,0:T(8,128)(2,1)S(1)} collective-permute-done((bf16[2,2,64,384]{3,2,1,0:T(8,128)(2,1)S(1)}, bf16[2,2,64,384]{3,2,1,0:T(8,128)(2,1)S(1)}, u32[]{:S(2)}, u32[]{:S(2)}) %collective-permute-start.3) | collective-permute-done | bytes 196640 | tf_op jit(solution)/shard_map/ppermute | solution.py:334
  36.6 14.5 %shard_map.102 = (bf16[2,2,64,384]{3,2,1,0:T(8,128)(2,1)S(1)}, bf16[2,2,64,384]{3,2,1,0:T(8,128)(2,1)S(1)}, bf16[2,2,2,64,384]{4,3,2,1,0:T(8,128)(2,1)S(1)}, bf16[4608,128]{1,0:T(8,128)(2,1)S(1)}) custom-call(bf16[4,2,64,384]{3,2,1,0:T(8,128)(2,1)S(1)} %copy-done.5, bf16[4,2,64,384]{3,2,1,0:T(8,128)(2,1)S(1)} %collective-permute-done.behind, ...), custom_call_target="tpu_custom_call" | custom-call | flops 16000000000 | bytes 5000000 | tf_op jit(solution)/shard_map/pallas_call | solution.py:273
  51.2 5.7 %all_to_all.25.parts = bf16[2,2304,128]{2,1,0:T(8,128)(2,1)S(1)} all-to-all(bf16[2,2304,128]{2,1,0:T(8,128)(2,1)S(1)} %bitcast.20), channel_id=1, replica_groups=mesh['z_hi'=4,'z_lo'=2,'core'=2,'y_hi'=4,'y_lo'=2,'x'=4] {'core'}, dimensions={0} | all-to-all | bytes 2359296 | tf_op jit(solution)/shard_map/all_to_all | solution.py:308
  57.8 4.9 %all-to-all-start.1 = ((bf16[16,144,128]{2,1,0:T(8,128)(2,1)}), bf16[16,144,128]{2,1,0:T(8,128)(2,1)S(1)}, u32[]{:S(2)}, u32[]{:S(2)}) async-start(bf16[16,144,128]{2,1,0:T(8,128)(2,1)} %bitcast.4), calls=%async_computation.1 | async-start | bytes 1179648 | tf_op jit(solution)/shard_map/all_to_all | solution.py:310
  62.8 5.4 %collective-permute-start.4 = (bf16[2,2,2,64,384]{4,3,2,1,0:T(8,128)(2,1)S(1)}, bf16[2,2,2,64,384]{4,3,2,1,0:T(8,128)(2,1)S(1)}, u32[]{:S(2)}, u32[]{:S(2)}) collective-permute-start(bf16[2,2,2,64,384]{4,3,2,1,0:T(8,128)(2,1)S(1)} %get-tuple-element.24), channel_id=1, source_target_pairs={{7,0},{0,1},{1,2},{2,3},{3,4},{4,5},{5,6},{6,7},{15,8},{8,9},{9,10... | collective-permute-start | bytes 1179656 | tf_op jit(solution)/shard_map/ppermute | solution.py:334
  68.2 8.1 %collective-permute-done.4.rest_0_.home_x = bf16[2,2,2,64,384]{4,3,2,1,0:T(8,128)(2,1)S(1)} collective-permute-done((bf16[2,2,2,64,384]{4,3,2,1,0:T(8,128)(2,1)S(1)}, bf16[2,2,2,64,384]{4,3,2,1,0:T(8,128)(2,1)S(1)}, u32[]{:S(2)}, u32[]{:S(2)}) %collective-permute-start.4) | collective-permute-done | bytes 393248 | tf_op jit(solution)/shard_map/ppermute | solution.py:334
  77.1 5.3 %collective-permute-start.5 = (bf16[2,2,2,64,384]{4,3,2,1,0:T(8,128)(2,1)S(1)}, bf16[2,2,2,64,384]{4,3,2,1,0:T(8,128)(2,1)S(1)}, u32[]{:S(2)}, u32[]{:S(2)}) collective-permute-start(bf16[2,2,2,64,384]{4,3,2,1,0:T(8,128)(2,1)S(1)} %pad_maximum_fusion), channel_id=1, source_target_pairs={{24,0},{25,1},{26,2},{27,3},{28,4},{29,5},{30,6},{31,7},{0,8},{1,9... | collective-permute-start | bytes 1179656 | tf_op jit(solution)/shard_map/ppermute | solution.py:334
  82.4 3.3 %all-to-all-start.2 = ((bf16[4,144,128]{2,1,0:T(8,128)(2,1)}), bf16[4,144,128]{2,1,0:T(8,128)(2,1)S(1)}, u32[]{:S(2)}, u32[]{:S(2)}) async-start(bf16[4,144,128]{2,1,0:T(8,128)(2,1)} %get-tuple-element.27), calls=%async_computation.2 | async-start | bytes 294912 | tf_op jit(solution)/shard_map/all_to_all | solution.py:361
  85.7 11.4 %all-to-all-done.2.parts = bf16[4,144,128]{2,1,0:T(8,128)(2,1)S(1)} async-done(((bf16[4,144,128]{2,1,0:T(8,128)(2,1)}), bf16[4,144,128]{2,1,0:T(8,128)(2,1)S(1)}, u32[]{:S(2)}, u32[]{:S(2)}) %all-to-all-start.2) | async-done | bytes 147488 | tf_op jit(solution)/shard_map/all_to_all | solution.py:361
  97.3 4.0 %collective-permute-start.6 = (bf16[4,2,64,384]{3,2,1,0:T(8,128)(2,1)S(1)}, bf16[4,2,64,384]{3,2,1,0:T(8,128)(2,1)S(1)}, u32[]{:S(2)}, u32[]{:S(2)}) collective-permute-start(bf16[4,2,64,384]{3,2,1,0:T(8,128)(2,1)S(1)} %pad_maximum_fusion.1), channel_id=1, source_target_pairs={{480,0},{481,1},{482,2},{483,3},{484,4},{485,5},{486,6},{487,7},{4... | collective-permute-start | bytes 1179656 | tf_op jit(solution)/shard_map/ppermute | solution.py:334
  101.3 11.7 %all_to_all.26.parts = bf16[4,144,128]{2,1,0:T(8,128)(2,1)S(1)} all-to-all(bf16[4,144,128]{2,1,0:T(8,128)(2,1)S(1)} %get-tuple-element.32), channel_id=1, replica_groups=mesh['z_hi'=4,'z_lo'=2,'core'=2,'y_hi'=4,'y_lo'=2,'x'=4] {'z_hi'}, dimensions={0} | all-to-all | bytes 294912 | tf_op jit(solution)/shard_map/all_to_all | solution.py:363
  114.0 3.6 %all-to-all-start.4 = ((bf16[16,144,128]{2,1,0:T(8,128)(2,1)}), bf16[16,144,128]{2,1,0:T(8,128)(2,1)S(1)}, u32[]{:S(2)}, u32[]{:S(2)}) async-start(bf16[16,144,128]{2,1,0:T(8,128)(2,1)} %shard_map.107), calls=%async_computation.4 | async-start | bytes 1179648 | tf_op jit(solution)/shard_map/all_to_all | solution.py:364
  118.5 2.4 %shard_map.106 = (bf16[512,384]{1,0:T(8,128)(2,1)}, bf16[512,384]{1,0:T(8,128)(2,1)}, f32[8,128]{1,0:T(8,128)S(1)}) custom-call(s32[1]{0:T(128)} %bitcast.odd.core, bf16[512,384]{1,0:T(8,128)(2,1)S(1)} %bitcast.17, s32[8,8,8]{2,1,0:T(8,128)S(1)} %copy-done.6, bf16[512,384]{1,0:T(8,128)(2,1)S(1)} %bitcast.19, bf16[2,2,64,384]{3,2,1,0:T(8,128)(2,1)S(1)} %copy-done.4, ...), custom_call_target="tpu_custom_call" | custom-call | flops 300000000 | bytes 4000000 | tf_op jit(solution)/shard_map/pallas_call | solution.py:365
  120.9 7.0 %all-to-all-done.4 = bf16[16,144,128]{2,1,0:T(8,128)(2,1)S(1)} async-done(((bf16[16,144,128]{2,1,0:T(8,128)(2,1)}), bf16[16,144,128]{2,1,0:T(8,128)(2,1)S(1)}, u32[]{:S(2)}, u32[]{:S(2)}) %all-to-all-start.4) | async-done | bytes 589856 | tf_op jit(solution)/shard_map/all_to_all | solution.py:364
  128.0 3.1 %collective-permute-start.7 = (bf16[2304,128]{1,0:T(8,128)(2,1)S(1)}, bf16[2304,128]{1,0:T(8,128)(2,1)S(1)}, u32[]{:S(2)}, u32[]{:S(2)}) collective-permute-start(bf16[2304,128]{1,0:T(8,128)(2,1)S(1)} %shard_map.108.mine), channel_id=1, source_target_pairs={{0,32},{32,0},{1,33},{33,1},{2,34},{34,2},{3,35},{35,3},{4,36},{36... | collective-permute-start | bytes 1769480 | tf_op jit(solution)/shard_map/ppermute | solution.py:373
  131.1 1.6 %collective-permute-done.7.other = bf16[2304,128]{1,0:T(8,128)(2,1)S(1)} collective-permute-done((bf16[2304,128]{1,0:T(8,128)(2,1)S(1)}, bf16[2304,128]{1,0:T(8,128)(2,1)S(1)}, u32[]{:S(2)}, u32[]{:S(2)}) %collective-permute-start.7) | collective-permute-done | bytes 589856 | tf_op jit(solution)/shard_map/ppermute | solution.py:373
  132.7 1.8 %shard_map.109 = (f32[384,1152]{1,0:T(8,128)}, f32[384,384]{1,0:T(8,128)}, f32[384]{0:T(512)}) custom-call(s32[1]{0:T(128)} %bitcast.odd.core, bf16[2304,128]{1,0:T(8,128)(2,1)S(1)} %shard_map.108.mine, bf16[2304,128]{1,0:T(8,128)(2,1)S(1)} %collective-permute-done.7.other, bf16[384,1152]{1,0:T(8,128)(2,1)S(1)} %copy-done.2, f32[1,384]{1,0:T(1,128)S(1)} %reshape.41.gain), custom_call_target="tpu_custom_call" | custom-call | tf_op jit(solution)/shard_map/pallas_call | solution.py:374
  (39 shorter events, 5.0 us)
Async XLA Ops:
  3.1 9.2 %collective-permute-start = (bf16[4,2,64,384]{3,2,1,0:T(8,128)(2,1)}, bf16[4,2,64,384]{3,2,1,0:T(8,128)(2,1)S(1)}, u32[]{:S(2)}, u32[]{:S(2)}) collective-permute-start(bf16[4,2,64,384]{3,2,1,0:T(8,128)(2,1)} %get-tuple-element.22), channel_id=1, source_target_pairs={{0,480},{1,481},{2,482},{3,483},{4,484},{5,485},{6,486},{7,487},{8... | collective-permute-start | bytes 1179656 | tf_op jit(solution)/shard_map/ppermute | solution.py:334
  9.9 16.1 %copy-start.8 = (f32[384]{0:T(512)S(1)}, f32[384]{0:T(512)}, u32[]{:S(2)}) copy-start(f32[384]{0:T(512)} %param.11) | copy-start | bytes 4612
  9.9 26.7 %copy-start.2 = (bf16[384,1152]{1,0:T(8,128)(2,1)S(1)}, bf16[384,1152]{1,0:T(8,128)(2,1)}, u32[]{:S(2)}) copy-start(bf16[384,1152]{1,0:T(8,128)(2,1)} %w_qkv.3) | copy-start | bytes 2654212
  10.0 26.7 %copy-start.5 = (bf16[4,2,64,384]{3,2,1,0:T(8,128)(2,1)S(1)}, bf16[4,2,64,384]{3,2,1,0:T(8,128)(2,1)}, u32[]{:S(2)}) copy-start(bf16[4,2,64,384]{3,2,1,0:T(8,128)(2,1)} %get-tuple-element.21.own) | copy-start | bytes 1179652
  10.0 26.7 %copy-start.7 = (bf16[384,384]{1,0:T(8,128)(2,1)S(1)}, bf16[384,384]{1,0:T(8,128)(2,1)}, u32[]{:S(2)}) copy-start(bf16[384,384]{1,0:T(8,128)(2,1)} %w_proj.1) | copy-start | bytes 884740
  12.3 13.8 %collective-permute-start.1 = (bf16[2,2,64,384]{3,2,1,0:T(8,128)(2,1)S(1)}, bf16[2,2,64,384]{3,2,1,0:T(8,128)(2,1)S(1)}, u32[]{:S(2)}, u32[]{:S(2)}) collective-permute-start(bf16[2,2,64,384]{3,2,1,0:T(8,128)(2,1)S(1)} %pad_maximum_fusion.2), channel_id=1, source_target_pairs={{0,31},{1,24},{2,25},{3,26},{4,27},{5,28},{6,29},{7,30},{8,7},{9,0... | collective-permute-start | bytes 589832 | tf_op jit(solution)/shard_map/ppermute | solution.py:334
  17.5 12.0 %collective-permute-start.2 = (bf16[2,2,64,384]{3,2,1,0:T(8,128)(2,1)S(1)}, bf16[2,2,64,384]{3,2,1,0:T(8,128)(2,1)S(1)}, u32[]{:S(2)}, u32[]{:S(2)}) collective-permute-start(bf16[2,2,64,384]{3,2,1,0:T(8,128)(2,1)S(1)} %pad_maximum_fusion.3), channel_id=1, source_target_pairs={{0,24},{1,25},{2,26},{3,27},{4,28},{5,29},{6,30},{7,31},{8,0},{9,1... | collective-permute-start | bytes 589832 | tf_op jit(solution)/shard_map/ppermute | solution.py:334
  22.9 13.7 %collective-permute-start.3 = (bf16[2,2,64,384]{3,2,1,0:T(8,128)(2,1)S(1)}, bf16[2,2,64,384]{3,2,1,0:T(8,128)(2,1)S(1)}, u32[]{:S(2)}, u32[]{:S(2)}) collective-permute-start(bf16[2,2,64,384]{3,2,1,0:T(8,128)(2,1)S(1)} %pad_maximum_fusion.4), channel_id=1, source_target_pairs={{0,7},{1,0},{2,1},{3,2},{4,3},{5,4},{6,5},{7,6},{8,15},{9,8},{10,9... | collective-permute-start | bytes 589832 | tf_op jit(solution)/shard_map/ppermute | solution.py:334
  51.2 31.2 %copy-start.3 = (bf16[2,2,64,384]{3,2,1,0:T(8,128)(2,1)}, bf16[2,2,64,384]{3,2,1,0:T(8,128)(2,1)S(1)}, u32[]{:S(2)}) copy-start(bf16[2,2,64,384]{3,2,1,0:T(8,128)(2,1)S(1)} %get-tuple-element.23.home_0) | copy-start | bytes 589828
  57.8 18.4 %all-to-all-start.1 = ((bf16[16,144,128]{2,1,0:T(8,128)(2,1)}), bf16[16,144,128]{2,1,0:T(8,128)(2,1)S(1)}, u32[]{:S(2)}, u32[]{:S(2)}) async-start(bf16[16,144,128]{2,1,0:T(8,128)(2,1)} %bitcast.4), calls=%async_computation.1 | async-start | bytes 1179648 | tf_op jit(solution)/shard_map/all_to_all | solution.py:310
  62.8 13.5 %collective-permute-start.4 = (bf16[2,2,2,64,384]{4,3,2,1,0:T(8,128)(2,1)S(1)}, bf16[2,2,2,64,384]{4,3,2,1,0:T(8,128)(2,1)S(1)}, u32[]{:S(2)}, u32[]{:S(2)}) collective-permute-start(bf16[2,2,2,64,384]{4,3,2,1,0:T(8,128)(2,1)S(1)} %get-tuple-element.24), channel_id=1, source_target_pairs={{7,0},{0,1},{1,2},{2,3},{3,4},{4,5},{5,6},{6,7},{15,8},{8,9},{9,10... | collective-permute-start | bytes 1179656 | tf_op jit(solution)/shard_map/ppermute | solution.py:334
  77.1 20.1 %collective-permute-start.5 = (bf16[2,2,2,64,384]{4,3,2,1,0:T(8,128)(2,1)S(1)}, bf16[2,2,2,64,384]{4,3,2,1,0:T(8,128)(2,1)S(1)}, u32[]{:S(2)}, u32[]{:S(2)}) collective-permute-start(bf16[2,2,2,64,384]{4,3,2,1,0:T(8,128)(2,1)S(1)} %pad_maximum_fusion), channel_id=1, source_target_pairs={{24,0},{25,1},{26,2},{27,3},{28,4},{29,5},{30,6},{31,7},{0,8},{1,9... | collective-permute-start | bytes 1179656 | tf_op jit(solution)/shard_map/ppermute | solution.py:334
  82.4 14.8 %all-to-all-start.2 = ((bf16[4,144,128]{2,1,0:T(8,128)(2,1)}), bf16[4,144,128]{2,1,0:T(8,128)(2,1)S(1)}, u32[]{:S(2)}, u32[]{:S(2)}) async-start(bf16[4,144,128]{2,1,0:T(8,128)(2,1)} %get-tuple-element.27), calls=%async_computation.2 | async-start | bytes 294912 | tf_op jit(solution)/shard_map/all_to_all | solution.py:361
  97.3 15.8 %collective-permute-start.6 = (bf16[4,2,64,384]{3,2,1,0:T(8,128)(2,1)S(1)}, bf16[4,2,64,384]{3,2,1,0:T(8,128)(2,1)S(1)}, u32[]{:S(2)}, u32[]{:S(2)}) collective-permute-start(bf16[4,2,64,384]{3,2,1,0:T(8,128)(2,1)S(1)} %pad_maximum_fusion.1), channel_id=1, source_target_pairs={{480,0},{481,1},{482,2},{483,3},{484,4},{485,5},{486,6},{487,7},{4... | collective-permute-start | bytes 1179656 | tf_op jit(solution)/shard_map/ppermute | solution.py:334
  113.1 4.5 %copy-start = (bf16[8,8,8,384]{3,2,1,0:T(8,128)(2,1)S(1)}, bf16[8,8,8,384]{3,2,1,0:T(8,128)(2,1)}, u32[]{:S(2)}) copy-start(bf16[8,8,8,384]{3,2,1,0:T(8,128)(2,1)} %param.6) | copy-start | bytes 1179652
  113.1 4.5 %copy-start.1 = (bf16[8,8,8,384]{3,2,1,0:T(8,128)(2,1)S(1)}, bf16[8,8,8,384]{3,2,1,0:T(8,128)(2,1)}, u32[]{:S(2)}) copy-start(bf16[8,8,8,384]{3,2,1,0:T(8,128)(2,1)} %param.8) | copy-start | bytes 1179652
  113.1 4.5 %copy-start.6 = (s32[8,8,8]{2,1,0:T(8,128)S(1)}, s32[8,8,8]{2,1,0:T(8,128)}, u32[]{:S(2)}) copy-start(s32[8,8,8]{2,1,0:T(8,128)} %frozen.1) | copy-start | bytes 6148
  114.0 14.0 %all-to-all-start.4 = ((bf16[16,144,128]{2,1,0:T(8,128)(2,1)}), bf16[16,144,128]{2,1,0:T(8,128)(2,1)S(1)}, u32[]{:S(2)}, u32[]{:S(2)}) async-start(bf16[16,144,128]{2,1,0:T(8,128)(2,1)} %shard_map.107), calls=%async_computation.4 | async-start | bytes 1179648 | tf_op jit(solution)/shard_map/all_to_all | solution.py:364
  117.6 0.9 copy-start.4
  128.0 4.7 %collective-permute-start.7 = (bf16[2304,128]{1,0:T(8,128)(2,1)S(1)}, bf16[2304,128]{1,0:T(8,128)(2,1)S(1)}, u32[]{:S(2)}, u32[]{:S(2)}) collective-permute-start(bf16[2304,128]{1,0:T(8,128)(2,1)S(1)} %shard_map.108.mine), channel_id=1, source_target_pairs={{0,32},{32,0},{1,33},{33,1},{2,34},{34,2},{3,35},{35,3},{4,36},{36... | collective-permute-start | bytes 1769480 | tf_op jit(solution)/shard_map/ppermute | solution.py:373

commit v8 on v6

--- a/solution.py
+++ b/solution.py
@@ -179,9 +179,8 @@
                 target[group, 1, pl.ds(plane * 16, 16), :] = cot[rows]
 
 
-def join_kernel(odd, tokens, frozen, cotangent, home_0, home_x, home_2, ahead, block_out, tokens_grad, token):
+def join_kernel(odd, tokens, frozen, cotangent, home_0, home_x, home_2, ahead, block_out, tokens_grad):
     homes = (home_0, home_x.at[0], home_2.at[0], home_x.at[1])
-    token[...] = jnp.zeros_like(token)
     keeps = keep_rows(frozen)
     shape = (WIN * WIN, WIN * WIN)
     diagonal = ones_where(lax.broadcasted_iota(jnp.int32, shape, 0) == lax.broadcasted_iota(jnp.int32, shape, 1))
@@ -369,19 +368,19 @@
     parts = near_sum(grads)
     parts, back_y = total_of(parts, FAR, through=(back_y,))
     home_y = send(back_y, 2, True)
-    parts = total_of(lax.all_to_all(parts, "y_hi", 0, 0), FAR)
+    parts = total_of(lax.all_to_all(parts, "z_hi", 0, 0), FAR)
     home_x = send(jnp.stack([back_1, home_y[1]]), 1, True)
-    parts = total_of(lax.all_to_all(parts, "z_hi", 0, 0), GROUP, after=(home_x,))
+    parts = total_of(lax.all_to_all(parts, "y_hi", 0, 0), GROUP, after=(home_x,))
     mine = lax.all_to_all(parts, NEAR, 0, 0).reshape(GRAD_ROWS // 2, LANES)
     ahead = send(jnp.stack([back_0[1], home_x[0, 1], home_y[0, 1], home_x[1, 1]]), 0, True)
-    block_out, tokens_grad, token = pl.pallas_call(
+    block_out, tokens_grad = pl.pallas_call(
         join_kernel,
-        out_shape=(jax.ShapeDtypeStruct((ROWS, D), BF),) * 2 + (jax.ShapeDtypeStruct((8, LANES), F32),),
+        out_shape=(jax.ShapeDtypeStruct((ROWS, D), BF),) * 2,
         in_specs=[SCALAR] + [WHOLE] * 7,
         compiler_params=SMALL,
         cost_estimate=pl.CostEstimate(flops=300_000_000, bytes_accessed=4_000_000, transcendentals=0),
     )(core, token_rows, frozen, cot_rows, back_0, home_x, home_y, ahead)
-    mine = hold(mine, token)
+    mine = hold(mine, ahead)
     other = lax.ppermute(mine, "core", [(0, 1), (1, 0)])
     qkv_grad, proj_grad, gain_grad = pl.pallas_call(
         grads_kernel,

time: 131 us -> 128 us (0.977)
  waiting for transfers between devices: 33.6 us -> 28.8 us
    ppermute x1, waiting for transfers between devices: 1.61 us -> 0.01 us  [local(): other = lax.ppermute(mine, 'core', [(0, 1), (1, 0)])]
    all_to_all x1, waiting for transfers between devices: 1.55 us -> 0.01 us  [local(): parts = total_of(lax.all_to_all(parts, 'z_hi', 0, 0), FAR)]
    all_to_all x1, blocking collectives: 11.3 us -> 12.6 us  [local(): lax.all_to_all(parts, 'y_hi', 0, 0)]
    unnamed x22 -> x30, local copies, waits for them, and re-layouts: 2.43 us -> 3.27 us
  transfers between devices with their start and end apart: 11 -> 11, of which waited for: 8 -> 6; matrix products, arithmetic and copies ran while one was open for 1% -> 1% of each run, Pallas kernels for 3% -> 3%
where the time goes in v8:
time: 128 us
  starting transfers between devices  50.8 us (40%)
  waiting for transfers between devices  28.8 us (22%)
  Pallas kernels  24.1 us (19%)
  blocking collectives  18.3 us (14%)
  local copies, waits for them, and re-layouts  4.51 us (4%)
    ppermute x7, starting transfers between devices, send(): return lax.ppermute(block, LATTICE, route(kind, back))  35.3 us
    ppermute x7, waiting for transfers between devices, send(): return lax.ppermute(block, LATTICE, route(kind, back))  23.5 us
    pallas_call x1, Pallas kernels, window_pass(): pl.pallas_call(window_kernel, out_shape=(jax.ShapeDtypeStruct((GRAD_ROWS,...  13.4 us
    all_to_all x1, blocking collectives, local(): lax.all_to_all(parts, 'y_hi', 0, 0)  12.6 us
    all_to_all x1, blocking collectives, near_sum(): lax.all_to_all(rows.reshape(2, GRAD_ROWS // 2, LANES), 'core', 0, 0)  5.69 us
    all_to_all x1, waiting for transfers between devices, near_sum(): parts = lax.all_to_all(parts, NEAR, 0, 0)  5.32 us
    all_to_all x1, starting transfers between devices, near_sum(): parts = lax.all_to_all(parts, NEAR, 0, 0)  4.94 us
    all_to_all x1, starting transfers between devices, local(): mine = lax.all_to_all(parts, NEAR, 0, 0).reshape(GRAD_ROWS // 2, LANES)  4.03 us
  transfers between devices with their start and end apart: 11, of which 6 were waited for; matrix products, arithmetic and copies ran while one was open for 1% of the time, Pallas kernels for 3%

profile of v8, /device:TPU:1, one launch (start us, length us, event | category | flops | bytes accessed | tf_op | source)
XLA Modules:
  0.0 127.6 jit_solution(14766482514971181764)
XLA Ops:
  0.6 2.4 %shard_map.101 = (bf16[4,2,64,384]{3,2,1,0:T(8,128)(2,1)}, bf16[4,2,64,384]{3,2,1,0:T(8,128)(2,1)}) custom-call(s32[1]{0:T(128)} %bitcast.odd.core, bf16[512,384]{1,0:T(8,128)(2,1)} %bitcast.16, s32[8,8,8]{2,1,0:T(8,128)} %frozen.1, bf16[512,384]{1,0:T(8,128)(2,1)} %bitcast.18), custom_call_target="tpu_custom_call" | custom-call | tf_op jit(solution)/shard_map/pallas_call | solution.py:351
  3.1 6.9 %collective-permute-start = (bf16[4,2,64,384]{3,2,1,0:T(8,128)(2,1)}, bf16[4,2,64,384]{3,2,1,0:T(8,128)(2,1)S(1)}, u32[]{:S(2)}, u32[]{:S(2)}) collective-permute-start(bf16[4,2,64,384]{3,2,1,0:T(8,128)(2,1)} %get-tuple-element.23), channel_id=1, source_target_pairs={{0,480},{1,481},{2,482},{3,483},{4,484},{5,485},{6,486},{7,487},{8... | collective-permute-start | bytes 1179656 | tf_op jit(solution)/shard_map/ppermute | solution.py:345
  12.3 5.1 %collective-permute-start.1 = (bf16[2,2,64,384]{3,2,1,0:T(8,128)(2,1)S(1)}, bf16[2,2,64,384]{3,2,1,0:T(8,128)(2,1)S(1)}, u32[]{:S(2)}, u32[]{:S(2)}) collective-permute-start(bf16[2,2,64,384]{3,2,1,0:T(8,128)(2,1)S(1)} %pad_maximum_fusion.2), channel_id=1, source_target_pairs={{0,31},{1,24},{2,25},{3,26},{4,27},{5,28},{6,29},{7,30},{8,7},{9,0... | collective-permute-start | bytes 589832 | tf_op jit(solution)/shard_map/ppermute | solution.py:345
  17.5 5.4 %collective-permute-start.2 = (bf16[2,2,64,384]{3,2,1,0:T(8,128)(2,1)S(1)}, bf16[2,2,64,384]{3,2,1,0:T(8,128)(2,1)S(1)}, u32[]{:S(2)}, u32[]{:S(2)}) collective-permute-start(bf16[2,2,64,384]{3,2,1,0:T(8,128)(2,1)S(1)} %pad_maximum_fusion.3), channel_id=1, source_target_pairs={{0,24},{1,25},{2,26},{3,27},{4,28},{5,29},{6,30},{7,31},{8,0},{9,1... | collective-permute-start | bytes 589832 | tf_op jit(solution)/shard_map/ppermute | solution.py:345
  23.0 3.1 %collective-permute-start.3 = (bf16[2,2,64,384]{3,2,1,0:T(8,128)(2,1)S(1)}, bf16[2,2,64,384]{3,2,1,0:T(8,128)(2,1)S(1)}, u32[]{:S(2)}, u32[]{:S(2)}) collective-permute-start(bf16[2,2,64,384]{3,2,1,0:T(8,128)(2,1)S(1)} %pad_maximum_fusion.4), channel_id=1, source_target_pairs={{0,7},{1,0},{2,1},{3,2},{4,3},{5,4},{6,5},{7,6},{8,15},{9,8},{10,9... | collective-permute-start | bytes 589832 | tf_op jit(solution)/shard_map/ppermute | solution.py:345
  26.1 3.4 %collective-permute-done.2.side_2 = bf16[2,2,64,384]{3,2,1,0:T(8,128)(2,1)S(1)} collective-permute-done((bf16[2,2,64,384]{3,2,1,0:T(8,128)(2,1)S(1)}, bf16[2,2,64,384]{3,2,1,0:T(8,128)(2,1)S(1)}, u32[]{:S(2)}, u32[]{:S(2)}) %collective-permute-start.2) | collective-permute-done | bytes 196640 | tf_op jit(solution)/shard_map/ppermute | solution.py:345
  29.5 7.1 %collective-permute-done.3.side_1 = bf16[2,2,64,384]{3,2,1,0:T(8,128)(2,1)S(1)} collective-permute-done((bf16[2,2,64,384]{3,2,1,0:T(8,128)(2,1)S(1)}, bf16[2,2,64,384]{3,2,1,0:T(8,128)(2,1)S(1)}, u32[]{:S(2)}, u32[]{:S(2)}) %collective-permute-start.3) | collective-permute-done | bytes 196640 | tf_op jit(solution)/shard_map/ppermute | solution.py:345
  36.6 13.4 %shard_map.102 = (bf16[4608,128]{1,0:T(8,128)(2,1)S(1)}, bf16[384,512]{1,0:T(8,128)(2,1)S(1)}, bf16[512,1152]{1,0:T(8,128)(2,1)S(1)}, f32[512,384]{1,0:T(8,128)S(1)}, f32[512,128]{1,0:T(8,128)S(1)}) custom-call(bf16[4,2,64,384]{3,2,1,0:T(8,128)(2,1)S(1)} %copy-done.5, bf16[4,2,64,384]{3,2,1,0:T(8,128)(2,1)S(1)} %collective-permute-done.behind, ...), custom_call_target="tpu_custom_call" | custom-call | flops 12000000000 | bytes 5000000 | tf_op jit(solution)/shard_map/pallas_call | solution.py:275
  50.0 5.7 %all_to_all.25.parts = bf16[2,2304,128]{2,1,0:T(8,128)(2,1)S(1)} all-to-all(bf16[2,2304,128]{2,1,0:T(8,128)(2,1)S(1)} %bitcast.20), channel_id=1, replica_groups=mesh['z_hi'=4,'z_lo'=2,'core'=2,'y_hi'=4,'y_lo'=2,'x'=4] {'core'}, dimensions={0} | all-to-all | bytes 2359296 | tf_op jit(solution)/shard_map/all_to_all | solution.py:319
  56.7 4.9 %all-to-all-start.1 = ((bf16[16,144,128]{2,1,0:T(8,128)(2,1)}), bf16[16,144,128]{2,1,0:T(8,128)(2,1)S(1)}, u32[]{:S(2)}, u32[]{:S(2)}) async-start(bf16[16,144,128]{2,1,0:T(8,128)(2,1)} %bitcast.5), calls=%async_computation.1 | async-start | bytes 1179648 | tf_op jit(solution)/shard_map/all_to_all | solution.py:321
  61.6 1.3 copy-done.9
  64.8 1.5 %shard_map.103 = (bf16[2,2,64,384]{3,2,1,0:T(8,128)(2,1)S(1)}, bf16[2,2,64,384]{3,2,1,0:T(8,128)(2,1)S(1)}, bf16[2,2,2,64,384]{4,3,2,1,0:T(8,128)(2,1)S(1)}) custom-call(bf16[384,512]{1,0:T(8,128)(2,1)S(1)} %copy-done.11, bf16[512,1152]{1,0:T(8,128)(2,1)S(1)} %copy-done.9, f32[512,384]{1,0:T(8,128)S(1)} %get-tuple-element.26.unit, ...), custom_call_target="tpu_custom_call" | custom-call | flops 2000000000 | bytes 4000000 | tf_op jit(solution)/shard_map/pallas_call | solution.py:298
  66.4 5.3 %all-to-all-done.1.parts = bf16[16,144,128]{2,1,0:T(8,128)(2,1)S(1)} async-done(((bf16[16,144,128]{2,1,0:T(8,128)(2,1)}), bf16[16,144,128]{2,1,0:T(8,128)(2,1)S(1)}, u32[]{:S(2)}, u32[]{:S(2)}) %all-to-all-start.1) | async-done | bytes 589856 | tf_op jit(solution)/shard_map/all_to_all | solution.py:321
  72.5 5.2 %collective-permute-start.4 = (bf16[2,2,2,64,384]{4,3,2,1,0:T(8,128)(2,1)S(1)}, bf16[2,2,2,64,384]{4,3,2,1,0:T(8,128)(2,1)S(1)}, u32[]{:S(2)}, u32[]{:S(2)}) collective-permute-start(bf16[2,2,2,64,384]{4,3,2,1,0:T(8,128)(2,1)S(1)} %get-tuple-element.32), channel_id=1, source_target_pairs={{24,0},{25,1},{26,2},{27,3},{28,4},{29,5},{30,6},{31,7},{0,8},{1,9... | collective-permute-start | bytes 1179656 | tf_op jit(solution)/shard_map/ppermute | solution.py:345
  77.7 3.3 %all-to-all-start.2 = ((bf16[4,144,128]{2,1,0:T(8,128)(2,1)}), bf16[4,144,128]{2,1,0:T(8,128)(2,1)S(1)}, u32[]{:S(2)}, u32[]{:S(2)}) async-start(bf16[4,144,128]{2,1,0:T(8,128)(2,1)} %get-tuple-element.35), calls=%async_computation.2 | async-start | bytes 294912 | tf_op jit(solution)/shard_map/all_to_all | solution.py:371
  81.1 5.4 %collective-permute-done.4.home_2 = bf16[2,2,2,64,384]{4,3,2,1,0:T(8,128)(2,1)S(1)} collective-permute-done((bf16[2,2,2,64,384]{4,3,2,1,0:T(8,128)(2,1)S(1)}, bf16[2,2,2,64,384]{4,3,2,1,0:T(8,128)(2,1)S(1)}, u32[]{:S(2)}, u32[]{:S(2)}) %collective-permute-start.4) | collective-permute-done | bytes 393248 | tf_op jit(solution)/shard_map/ppermute | solution.py:345
  86.5 2.6 %collective-permute-start.5 = (bf16[2,2,2,64,384]{4,3,2,1,0:T(8,128)(2,1)S(1)}, bf16[2,2,2,64,384]{4,3,2,1,0:T(8,128)(2,1)S(1)}, u32[]{:S(2)}, u32[]{:S(2)}) collective-permute-start(bf16[2,2,2,64,384]{4,3,2,1,0:T(8,128)(2,1)S(1)} %pad_maximum_fusion), channel_id=1, source_target_pairs={{7,0},{0,1},{1,2},{2,3},{3,4},{4,5},{5,6},{6,7},{15,8},{8,9},{9,10... | collective-permute-start | bytes 1179656 | tf_op jit(solution)/shard_map/ppermute | solution.py:345
  89.2 12.6 %all_to_all.26.parts = bf16[4,144,128]{2,1,0:T(8,128)(2,1)S(1)} all-to-all(bf16[4,144,128]{2,1,0:T(8,128)(2,1)S(1)} %shard_map.107), channel_id=1, replica_groups=mesh['z_hi'=4,'z_lo'=2,'core'=2,'y_hi'=4,'y_lo'=2,'x'=4] {'y_hi'}, dimensions={0} | all-to-all | bytes 294912 | tf_op jit(solution)/shard_map/all_to_all | solution.py:373
  102.6 4.0 %all-to-all-start.4 = ((bf16[16,144,128]{2,1,0:T(8,128)(2,1)}), bf16[16,144,128]{2,1,0:T(8,128)(2,1)S(1)}, u32[]{:S(2)}, u32[]{:S(2)}) async-start(bf16[16,144,128]{2,1,0:T(8,128)(2,1)} %shard_map.108), calls=%async_computation.4 | async-start | bytes 1179648 | tf_op jit(solution)/shard_map/all_to_all | solution.py:374
  106.9 6.8 %collective-permute-start.6 = (bf16[4,2,64,384]{3,2,1,0:T(8,128)(2,1)S(1)}, bf16[4,2,64,384]{3,2,1,0:T(8,128)(2,1)S(1)}, u32[]{:S(2)}, u32[]{:S(2)}) collective-permute-start(bf16[4,2,64,384]{3,2,1,0:T(8,128)(2,1)S(1)} %pad_maximum_fusion.1), channel_id=1, source_target_pairs={{480,0},{481,1},{482,2},{483,3},{484,4},{485,5},{486,6},{487,7},{4... | collective-permute-start | bytes 1179656 | tf_op jit(solution)/shard_map/ppermute | solution.py:345
  113.7 6.5 %collective-permute-done.6.ahead.refs_1_ = bf16[4,2,64,384]{3,2,1,0:T(8,128)(2,1)S(1)} collective-permute-done((bf16[4,2,64,384]{3,2,1,0:T(8,128)(2,1)S(1)}, bf16[4,2,64,384]{3,2,1,0:T(8,128)(2,1)S(1)}, u32[]{:S(2)}, u32[]{:S(2)}) %collective-permute-start.6) | collective-permute-done | bytes 393248 | tf_op jit(solution)/shard_map/ppermute | solution.py:345
  120.2 3.2 %collective-permute-start.7 = (bf16[2304,128]{1,0:T(8,128)(2,1)S(1)}, bf16[2304,128]{1,0:T(8,128)(2,1)S(1)}, u32[]{:S(2)}, u32[]{:S(2)}) collective-permute-start(bf16[2304,128]{1,0:T(8,128)(2,1)S(1)} %shard_map.109.mine), channel_id=1, source_target_pairs={{0,32},{32,0},{1,33},{33,1},{2,34},{34,2},{3,35},{35,3},{4,36},{36... | collective-permute-start | bytes 1769480 | tf_op jit(solution)/shard_map/ppermute | solution.py:384
  123.4 2.4 %shard_map.106 = (bf16[512,384]{1,0:T(8,128)(2,1)}, bf16[512,384]{1,0:T(8,128)(2,1)}) custom-call(s32[1]{0:T(128)} %bitcast.odd.core, bf16[512,384]{1,0:T(8,128)(2,1)S(1)} %bitcast.17, s32[8,8,8]{2,1,0:T(8,128)S(1)} %copy-done.6, bf16[512,384]{1,0:T(8,128)(2,1)S(1)} %bitcast.19, bf16[2,2,64,384]{3,2,1,0:T(8,128)(2,1)S(1)} %copy-done.4, ...), custom_call_target="tpu_custom_call" | custom-call | flops 300000000 | bytes 4000000 | tf_op jit(solution)/shard_map/pallas_call | solution.py:376
  125.9 1.8 %shard_map.110 = (f32[384,1152]{1,0:T(8,128)}, f32[384,384]{1,0:T(8,128)}, f32[384]{0:T(512)}) custom-call(s32[1]{0:T(128)} %bitcast.odd.core, bf16[2304,128]{1,0:T(8,128)(2,1)S(1)} %shard_map.109.mine, bf16[2304,128]{1,0:T(8,128)(2,1)S(1)} %collective-permute-done.7.other, bf16[384,1152]{1,0:T(8,128)(2,1)S(1)} %copy-done.2, f32[1,384]{1,0:T(1,128)S(1)} %reshape.41.gain), custom_call_target="tpu_custom_call" | custom-call | tf_op jit(solution)/shard_map/pallas_call | solution.py:385
  (52 shorter events, 7.2 us)
Async XLA Ops:
  3.1 9.2 %collective-permute-start = (bf16[4,2,64,384]{3,2,1,0:T(8,128)(2,1)}, bf16[4,2,64,384]{3,2,1,0:T(8,128)(2,1)S(1)}, u32[]{:S(2)}, u32[]{:S(2)}) collective-permute-start(bf16[4,2,64,384]{3,2,1,0:T(8,128)(2,1)} %get-tuple-element.23), channel_id=1, source_target_pairs={{0,480},{1,481},{2,482},{3,483},{4,484},{5,485},{6,486},{7,487},{8... | collective-permute-start | bytes 1179656 | tf_op jit(solution)/shard_map/ppermute | solution.py:345
  9.9 16.1 %copy-start.14 = (f32[384]{0:T(512)S(1)}, f32[384]{0:T(512)}, u32[]{:S(2)}) copy-start(f32[384]{0:T(512)} %param.11) | copy-start | bytes 4612
  9.9 26.7 %copy-start.2 = (bf16[384,1152]{1,0:T(8,128)(2,1)S(1)}, bf16[384,1152]{1,0:T(8,128)(2,1)}, u32[]{:S(2)}) copy-start(bf16[384,1152]{1,0:T(8,128)(2,1)} %w_qkv.5) | copy-start | bytes 2654212
  10.0 26.7 %copy-start.5 = (bf16[4,2,64,384]{3,2,1,0:T(8,128)(2,1)S(1)}, bf16[4,2,64,384]{3,2,1,0:T(8,128)(2,1)}, u32[]{:S(2)}) copy-start(bf16[4,2,64,384]{3,2,1,0:T(8,128)(2,1)} %get-tuple-element.22.own) | copy-start | bytes 1179652
  10.0 26.7 %copy-start.7 = (bf16[384,384]{1,0:T(8,128)(2,1)S(1)}, bf16[384,384]{1,0:T(8,128)(2,1)}, u32[]{:S(2)}) copy-start(bf16[384,384]{1,0:T(8,128)(2,1)} %w_proj.3) | copy-start | bytes 884740
  12.3 13.8 %collective-permute-start.1 = (bf16[2,2,64,384]{3,2,1,0:T(8,128)(2,1)S(1)}, bf16[2,2,64,384]{3,2,1,0:T(8,128)(2,1)S(1)}, u32[]{:S(2)}, u32[]{:S(2)}) collective-permute-start(bf16[2,2,64,384]{3,2,1,0:T(8,128)(2,1)S(1)} %pad_maximum_fusion.2), channel_id=1, source_target_pairs={{0,31},{1,24},{2,25},{3,26},{4,27},{5,28},{6,29},{7,30},{8,7},{9,0... | collective-permute-start | bytes 589832 | tf_op jit(solution)/shard_map/ppermute | solution.py:345
  17.5 12.0 %collective-permute-start.2 = (bf16[2,2,64,384]{3,2,1,0:T(8,128)(2,1)S(1)}, bf16[2,2,64,384]{3,2,1,0:T(8,128)(2,1)S(1)}, u32[]{:S(2)}, u32[]{:S(2)}) collective-permute-start(bf16[2,2,64,384]{3,2,1,0:T(8,128)(2,1)S(1)} %pad_maximum_fusion.3), channel_id=1, source_target_pairs={{0,24},{1,25},{2,26},{3,27},{4,28},{5,29},{6,30},{7,31},{8,0},{9,1... | collective-permute-start | bytes 589832 | tf_op jit(solution)/shard_map/ppermute | solution.py:345
  23.0 13.7 %collective-permute-start.3 = (bf16[2,2,64,384]{3,2,1,0:T(8,128)(2,1)S(1)}, bf16[2,2,64,384]{3,2,1,0:T(8,128)(2,1)S(1)}, u32[]{:S(2)}, u32[]{:S(2)}) collective-permute-start(bf16[2,2,64,384]{3,2,1,0:T(8,128)(2,1)S(1)} %pad_maximum_fusion.4), channel_id=1, source_target_pairs={{0,7},{1,0},{2,1},{3,2},{4,3},{5,4},{6,5},{7,6},{8,15},{9,8},{10,9... | collective-permute-start | bytes 589832 | tf_op jit(solution)/shard_map/ppermute | solution.py:345
  50.0 5.7 %copy-start.8 = (bf16[512,1152]{1,0:T(8,128)(2,1)}, bf16[512,1152]{1,0:T(8,128)(2,1)S(1)}, u32[]{:S(2)}) copy-start(bf16[512,1152]{1,0:T(8,128)(2,1)S(1)} %get-tuple-element.25.d_qkv) | copy-start | bytes 3538948
  50.0 5.7 %copy-start.10 = (bf16[384,512]{1,0:T(8,128)(2,1)}, bf16[384,512]{1,0:T(8,128)(2,1)S(1)}, u32[]{:S(2)}) copy-start(bf16[384,512]{1,0:T(8,128)(2,1)S(1)} %get-tuple-element.24.mixed_t) | copy-start | bytes 1179652
  50.0 5.7 %copy-start.12 = (f32[512,128]{1,0:T(8,128)}, f32[512,128]{1,0:T(8,128)S(1)}, u32[]{:S(2)}) copy-start(f32[512,128]{1,0:T(8,128)S(1)} %get-tuple-element.27.inv_std) | copy-start | bytes 786436
  56.7 15.1 %all-to-all-start.1 = ((bf16[16,144,128]{2,1,0:T(8,128)(2,1)}), bf16[16,144,128]{2,1,0:T(8,128)(2,1)S(1)}, u32[]{:S(2)}, u32[]{:S(2)}) async-start(bf16[16,144,128]{2,1,0:T(8,128)(2,1)} %bitcast.5), calls=%async_computation.1 | async-start | bytes 1179648 | tf_op jit(solution)/shard_map/all_to_all | solution.py:321
  61.6 1.3 copy-start.9
  66.4 40.3 %copy-start.3 = (bf16[2,2,64,384]{3,2,1,0:T(8,128)(2,1)}, bf16[2,2,64,384]{3,2,1,0:T(8,128)(2,1)S(1)}, u32[]{:S(2)}) copy-start(bf16[2,2,64,384]{3,2,1,0:T(8,128)(2,1)S(1)} %get-tuple-element.28.home_0) | copy-start | bytes 589828
  72.5 14.0 %collective-permute-start.4 = (bf16[2,2,2,64,384]{4,3,2,1,0:T(8,128)(2,1)S(1)}, bf16[2,2,2,64,384]{4,3,2,1,0:T(8,128)(2,1)S(1)}, u32[]{:S(2)}, u32[]{:S(2)}) collective-permute-start(bf16[2,2,2,64,384]{4,3,2,1,0:T(8,128)(2,1)S(1)} %get-tuple-element.32), channel_id=1, source_target_pairs={{24,0},{25,1},{26,2},{27,3},{28,4},{29,5},{30,6},{31,7},{0,8},{1,9... | collective-permute-start | bytes 1179656 | tf_op jit(solution)/shard_map/ppermute | solution.py:345
  77.7 11.4 %all-to-all-start.2 = ((bf16[4,144,128]{2,1,0:T(8,128)(2,1)}), bf16[4,144,128]{2,1,0:T(8,128)(2,1)S(1)}, u32[]{:S(2)}, u32[]{:S(2)}) async-start(bf16[4,144,128]{2,1,0:T(8,128)(2,1)} %get-tuple-element.35), calls=%async_computation.2 | async-start | bytes 294912 | tf_op jit(solution)/shard_map/all_to_all | solution.py:371
  86.5 15.3 %collective-permute-start.5 = (bf16[2,2,2,64,384]{4,3,2,1,0:T(8,128)(2,1)S(1)}, bf16[2,2,2,64,384]{4,3,2,1,0:T(8,128)(2,1)S(1)}, u32[]{:S(2)}, u32[]{:S(2)}) collective-permute-start(bf16[2,2,2,64,384]{4,3,2,1,0:T(8,128)(2,1)S(1)} %pad_maximum_fusion), channel_id=1, source_target_pairs={{7,0},{0,1},{1,2},{2,3},{3,4},{4,5},{5,6},{6,7},{15,8},{8,9},{9,10... | collective-permute-start | bytes 1179656 | tf_op jit(solution)/shard_map/ppermute | solution.py:345
  102.6 17.6 %all-to-all-start.4 = ((bf16[16,144,128]{2,1,0:T(8,128)(2,1)}), bf16[16,144,128]{2,1,0:T(8,128)(2,1)S(1)}, u32[]{:S(2)}, u32[]{:S(2)}) async-start(bf16[16,144,128]{2,1,0:T(8,128)(2,1)} %shard_map.108), calls=%async_computation.4 | async-start | bytes 1179648 | tf_op jit(solution)/shard_map/all_to_all | solution.py:374
  106.8 16.6 %copy-start = (bf16[8,8,8,384]{3,2,1,0:T(8,128)(2,1)S(1)}, bf16[8,8,8,384]{3,2,1,0:T(8,128)(2,1)}, u32[]{:S(2)}) copy-start(bf16[8,8,8,384]{3,2,1,0:T(8,128)(2,1)} %param.6) | copy-start | bytes 1179652
  106.8 16.6 %copy-start.1 = (bf16[8,8,8,384]{3,2,1,0:T(8,128)(2,1)S(1)}, bf16[8,8,8,384]{3,2,1,0:T(8,128)(2,1)}, u32[]{:S(2)}) copy-start(bf16[8,8,8,384]{3,2,1,0:T(8,128)(2,1)} %param.8) | copy-start | bytes 1179652
  106.8 16.6 %copy-start.6 = (s32[8,8,8]{2,1,0:T(8,128)S(1)}, s32[8,8,8]{2,1,0:T(8,128)}, u32[]{:S(2)}) copy-start(s32[8,8,8]{2,1,0:T(8,128)} %frozen.1) | copy-start | bytes 6148
  106.9 13.3 %collective-permute-start.6 = (bf16[4,2,64,384]{3,2,1,0:T(8,128)(2,1)S(1)}, bf16[4,2,64,384]{3,2,1,0:T(8,128)(2,1)S(1)}, u32[]{:S(2)}, u32[]{:S(2)}) collective-permute-start(bf16[4,2,64,384]{3,2,1,0:T(8,128)(2,1)S(1)} %pad_maximum_fusion.1), channel_id=1, source_target_pairs={{480,0},{481,1},{482,2},{483,3},{484,4},{485,5},{486,6},{487,7},{4... | collective-permute-start | bytes 1179656 | tf_op jit(solution)/shard_map/ppermute | solution.py:345
  120.2 3.2 %copy-start.4 = (bf16[2,2,64,384]{3,2,1,0:T(8,128)(2,1)S(1)}, bf16[2,2,64,384]{3,2,1,0:T(8,128)(2,1)}, u32[]{:S(2)}) copy-start(bf16[2,2,64,384]{3,2,1,0:T(8,128)(2,1)} %copy-done.3) | copy-start | bytes 589828
  120.2 5.7 %collective-permute-start.7 = (bf16[2304,128]{1,0:T(8,128)(2,1)S(1)}, bf16[2304,128]{1,0:T(8,128)(2,1)S(1)}, u32[]{:S(2)}, u32[]{:S(2)}) collective-permute-start(bf16[2304,128]{1,0:T(8,128)(2,1)S(1)} %shard_map.109.mine), channel_id=1, source_target_pairs={{0,32},{32,0},{1,33},{33,1},{2,34},{34,2},{3,35},{35,3},{4,36},{36... | collective-permute-start | bytes 1769480 | tf_op jit(solution)/shard_map/ppermute | solution.py:384
  (2 other events, 1.9 us)

commit v9 on v8

--- a/solution.py
+++ b/solution.py
@@ -366,11 +366,11 @@
         sides[kind] = send(jnp.stack([own[kind], behind[kind]]), kind)
     back_0, back_1, back_y, grads = window_pass(own, behind, sides[1:], w_qkv, w_proj, norm_gain)
     parts = near_sum(grads)
-    parts, back_y = total_of(parts, FAR, through=(back_y,))
+    parts = total_of(parts, FAR)
     home_y = send(back_y, 2, True)
-    parts = total_of(lax.all_to_all(parts, "z_hi", 0, 0), FAR)
+    parts, home_y = total_of(lax.all_to_all(parts, "z_hi", 0, 0), FAR, through=(home_y,))
     home_x = send(jnp.stack([back_1, home_y[1]]), 1, True)
-    parts = total_of(lax.all_to_all(parts, "y_hi", 0, 0), GROUP, after=(home_x,))
+    parts = total_of(lax.all_to_all(parts, "y_hi", 0, 0), GROUP)
     mine = lax.all_to_all(parts, NEAR, 0, 0).reshape(GRAD_ROWS // 2, LANES)
     ahead = send(jnp.stack([back_0[1], home_x[0, 1], home_y[0, 1], home_x[1, 1]]), 0, True)
     block_out, tokens_grad = pl.pallas_call(

time: 128 us -> 123 us (0.961)
  blocking collectives: 18.3 us -> 5.69 us
  starting transfers between devices: 50.8 us -> 56.9 us
    all_to_all x1 -> x0, blocking collectives: 12.6 us -> none  [local(): lax.all_to_all(parts, 'y_hi', 0, 0)]
    all_to_all x1 -> x2, waiting for transfers between devices: 0.01 us -> 7.34 us  [the longest x1 4.18 us: local(): lax.all_to_all(parts, 'z_hi', 0, 0)]
    all_to_all x1, waiting for transfers between devices: 5.32 us -> 0.06 us  [near_sum(): parts = lax.all_to_all(parts, NEAR, 0, 0)]
    all_to_all x1 -> x2, starting transfers between devices: 3.35 us -> 7.97 us  [the longest x1 4.1 us: local(): lax.all_to_all(parts, 'z_hi', 0, 0)]
    ppermute x7, waiting for transfers between devices: 23.5 us -> 21.8 us  [send(): return lax.ppermute(block, LATTICE, route(kind, back))]
  transfers between devices with their start and end apart: 11 -> 12, of which waited for: 6 -> 8; matrix products, arithmetic and copies ran while one was open for 1% -> 1% of each run, Pallas kernels for 3% -> 5%
where the time goes in v9:
time: 123 us; the launch traced here: 122 us
  starting transfers between devices  56.9 us (46%)
  waiting for transfers between devices  29.2 us (24%)
  Pallas kernels  24.7 us (20%)
  blocking collectives  5.69 us (5%)
  local copies, waits for them, and re-layouts  4.51 us (4%)
    ppermute x7, starting transfers between devices, send(): return lax.ppermute(block, LATTICE, route(kind, back))  35.8 us
    ppermute x7, waiting for transfers between devices, send(): return lax.ppermute(block, LATTICE, route(kind, back))  21.8 us
    pallas_call x1, Pallas kernels, window_pass(): pl.pallas_call(window_kernel, out_shape=(jax.ShapeDtypeStruct((GRAD_ROWS,...  13.4 us
    all_to_all x1, blocking collectives, near_sum(): lax.all_to_all(rows.reshape(2, GRAD_ROWS // 2, LANES), 'core', 0, 0)  5.69 us
    all_to_all x1, starting transfers between devices, local(): mine = lax.all_to_all(parts, NEAR, 0, 0).reshape(GRAD_ROWS // 2, LANES)  5.01 us
    all_to_all x1, starting transfers between devices, near_sum(): parts = lax.all_to_all(parts, NEAR, 0, 0)  4.94 us
    all_to_all x1, waiting for transfers between devices, local(): lax.all_to_all(parts, 'z_hi', 0, 0)  4.18 us
    all_to_all x1, starting transfers between devices, local(): lax.all_to_all(parts, 'z_hi', 0, 0)  4.1 us
  transfers between devices with their start and end apart: 12, of which 8 were waited for; matrix products, arithmetic and copies ran while one was open for 1% of the time, Pallas kernels for 5%

profile of v9, /device:TPU:1, one launch (start us, length us, event | category | flops | bytes accessed | tf_op | source)
XLA Modules:
  0.0 122.1 jit_solution(9384016664788543714)
XLA Ops:
  0.6 2.4 %shard_map.101 = (bf16[4,2,64,384]{3,2,1,0:T(8,128)(2,1)}, bf16[4,2,64,384]{3,2,1,0:T(8,128)(2,1)}) custom-call(s32[1]{0:T(128)} %bitcast.odd.core, bf16[512,384]{1,0:T(8,128)(2,1)} %bitcast.16, s32[8,8,8]{2,1,0:T(8,128)} %frozen.1, bf16[512,384]{1,0:T(8,128)(2,1)} %bitcast.18), custom_call_target="tpu_custom_call" | custom-call | tf_op jit(solution)/shard_map/pallas_call | solution.py:351
  3.1 6.9 %collective-permute-start = (bf16[4,2,64,384]{3,2,1,0:T(8,128)(2,1)}, bf16[4,2,64,384]{3,2,1,0:T(8,128)(2,1)S(1)}, u32[]{:S(2)}, u32[]{:S(2)}) collective-permute-start(bf16[4,2,64,384]{3,2,1,0:T(8,128)(2,1)} %get-tuple-element.23), channel_id=1, source_target_pairs={{0,480},{1,481},{2,482},{3,483},{4,484},{5,485},{6,486},{7,487},{8... | collective-permute-start | bytes 1179656 | tf_op jit(solution)/shard_map/ppermute | solution.py:345
  12.3 5.1 %collective-permute-start.1 = (bf16[2,2,64,384]{3,2,1,0:T(8,128)(2,1)S(1)}, bf16[2,2,64,384]{3,2,1,0:T(8,128)(2,1)S(1)}, u32[]{:S(2)}, u32[]{:S(2)}) collective-permute-start(bf16[2,2,64,384]{3,2,1,0:T(8,128)(2,1)S(1)} %pad_maximum_fusion.2), channel_id=1, source_target_pairs={{0,31},{1,24},{2,25},{3,26},{4,27},{5,28},{6,29},{7,30},{8,7},{9,0... | collective-permute-start | bytes 589832 | tf_op jit(solution)/shard_map/ppermute | solution.py:345
  17.5 5.4 %collective-permute-start.2 = (bf16[2,2,64,384]{3,2,1,0:T(8,128)(2,1)S(1)}, bf16[2,2,64,384]{3,2,1,0:T(8,128)(2,1)S(1)}, u32[]{:S(2)}, u32[]{:S(2)}) collective-permute-start(bf16[2,2,64,384]{3,2,1,0:T(8,128)(2,1)S(1)} %pad_maximum_fusion.3), channel_id=1, source_target_pairs={{0,24},{1,25},{2,26},{3,27},{4,28},{5,29},{6,30},{7,31},{8,0},{9,1... | collective-permute-start | bytes 589832 | tf_op jit(solution)/shard_map/ppermute | solution.py:345
  23.0 3.1 %collective-permute-start.3 = (bf16[2,2,64,384]{3,2,1,0:T(8,128)(2,1)S(1)}, bf16[2,2,64,384]{3,2,1,0:T(8,128)(2,1)S(1)}, u32[]{:S(2)}, u32[]{:S(2)}) collective-permute-start(bf16[2,2,64,384]{3,2,1,0:T(8,128)(2,1)S(1)} %pad_maximum_fusion.4), channel_id=1, source_target_pairs={{0,7},{1,0},{2,1},{3,2},{4,3},{5,4},{6,5},{7,6},{8,15},{9,8},{10,9... | collective-permute-start | bytes 589832 | tf_op jit(solution)/shard_map/ppermute | solution.py:345
  26.1 3.4 %collective-permute-done.2.side_2 = bf16[2,2,64,384]{3,2,1,0:T(8,128)(2,1)S(1)} collective-permute-done((bf16[2,2,64,384]{3,2,1,0:T(8,128)(2,1)S(1)}, bf16[2,2,64,384]{3,2,1,0:T(8,128)(2,1)S(1)}, u32[]{:S(2)}, u32[]{:S(2)}) %collective-permute-start.2) | collective-permute-done | bytes 196640 | tf_op jit(solution)/shard_map/ppermute | solution.py:345
  29.5 7.1 %collective-permute-done.3.side_1 = bf16[2,2,64,384]{3,2,1,0:T(8,128)(2,1)S(1)} collective-permute-done((bf16[2,2,64,384]{3,2,1,0:T(8,128)(2,1)S(1)}, bf16[2,2,64,384]{3,2,1,0:T(8,128)(2,1)S(1)}, u32[]{:S(2)}, u32[]{:S(2)}) %collective-permute-start.3) | collective-permute-done | bytes 196640 | tf_op jit(solution)/shard_map/ppermute | solution.py:345
  36.6 13.4 %shard_map.102 = (bf16[4608,128]{1,0:T(8,128)(2,1)S(1)}, bf16[384,512]{1,0:T(8,128)(2,1)S(1)}, bf16[512,1152]{1,0:T(8,128)(2,1)S(1)}, f32[512,384]{1,0:T(8,128)S(1)}, f32[512,128]{1,0:T(8,128)S(1)}) custom-call(bf16[4,2,64,384]{3,2,1,0:T(8,128)(2,1)S(1)} %copy-done.5, bf16[4,2,64,384]{3,2,1,0:T(8,128)(2,1)S(1)} %collective-permute-done.behind, ...), custom_call_target="tpu_custom_call" | custom-call | flops 12000000000 | bytes 5000000 | tf_op jit(solution)/shard_map/pallas_call | solution.py:275
  50.0 5.7 %all_to_all.25.parts = bf16[2,2304,128]{2,1,0:T(8,128)(2,1)S(1)} all-to-all(bf16[2,2304,128]{2,1,0:T(8,128)(2,1)S(1)} %bitcast.20), channel_id=1, replica_groups=mesh['z_hi'=4,'z_lo'=2,'core'=2,'y_hi'=4,'y_lo'=2,'x'=4] {'core'}, dimensions={0} | all-to-all | bytes 2359296 | tf_op jit(solution)/shard_map/all_to_all | solution.py:319
  56.7 4.9 %all-to-all-start.1 = ((bf16[16,144,128]{2,1,0:T(8,128)(2,1)}), bf16[16,144,128]{2,1,0:T(8,128)(2,1)S(1)}, u32[]{:S(2)}, u32[]{:S(2)}) async-start(bf16[16,144,128]{2,1,0:T(8,128)(2,1)} %bitcast.5), calls=%async_computation.1 | async-start | bytes 1179648 | tf_op jit(solution)/shard_map/all_to_all | solution.py:321
  64.8 1.5 %shard_map.103 = (bf16[2,2,64,384]{3,2,1,0:T(8,128)(2,1)S(1)}, bf16[2,2,64,384]{3,2,1,0:T(8,128)(2,1)S(1)}, bf16[2,2,2,64,384]{4,3,2,1,0:T(8,128)(2,1)S(1)}) custom-call(bf16[384,512]{1,0:T(8,128)(2,1)S(1)} %copy-done.11, bf16[512,1152]{1,0:T(8,128)(2,1)S(1)} %copy-done.9, f32[512,384]{1,0:T(8,128)S(1)} %get-tuple-element.26.unit, ...), custom_call_target="tpu_custom_call" | custom-call | flops 2000000000 | bytes 4000000 | tf_op jit(solution)/shard_map/pallas_call | solution.py:298
  66.4 5.3 %collective-permute-start.4 = (bf16[2,2,2,64,384]{4,3,2,1,0:T(8,128)(2,1)S(1)}, bf16[2,2,2,64,384]{4,3,2,1,0:T(8,128)(2,1)S(1)}, u32[]{:S(2)}, u32[]{:S(2)}) collective-permute-start(bf16[2,2,2,64,384]{4,3,2,1,0:T(8,128)(2,1)S(1)} %get-tuple-element.31), channel_id=1, source_target_pairs={{24,0},{25,1},{26,2},{27,3},{28,4},{29,5},{30,6},{31,7},{0,8},{1,9... | collective-permute-start | bytes 1179656 | tf_op jit(solution)/shard_map/ppermute | solution.py:345
  72.5 4.1 %all-to-all-start.2 = ((bf16[4,144,128]{2,1,0:T(8,128)(2,1)}), bf16[4,144,128]{2,1,0:T(8,128)(2,1)S(1)}, u32[]{:S(2)}, u32[]{:S(2)}) async-start(bf16[4,144,128]{2,1,0:T(8,128)(2,1)} %shard_map.105), calls=%async_computation.2 | async-start | bytes 294912 | tf_op jit(solution)/shard_map/all_to_all | solution.py:371
  76.6 3.6 %collective-permute-done.4.rest_0_ = bf16[2,2,2,64,384]{4,3,2,1,0:T(8,128)(2,1)S(1)} collective-permute-done((bf16[2,2,2,64,384]{4,3,2,1,0:T(8,128)(2,1)S(1)}, bf16[2,2,2,64,384]{4,3,2,1,0:T(8,128)(2,1)S(1)}, u32[]{:S(2)}, u32[]{:S(2)}) %collective-permute-start.4) | collective-permute-done | bytes 393248 | tf_op jit(solution)/shard_map/ppermute | solution.py:345
  80.1 4.2 %all-to-all-done.2.parts = bf16[4,144,128]{2,1,0:T(8,128)(2,1)S(1)} async-done(((bf16[4,144,128]{2,1,0:T(8,128)(2,1)}), bf16[4,144,128]{2,1,0:T(8,128)(2,1)S(1)}, u32[]{:S(2)}, u32[]{:S(2)}) %all-to-all-start.2) | async-done | bytes 147488 | tf_op jit(solution)/shard_map/all_to_all | solution.py:371
  85.0 3.9 %all-to-all-start.3 = ((bf16[4,144,128]{2,1,0:T(8,128)(2,1)}), bf16[4,144,128]{2,1,0:T(8,128)(2,1)S(1)}, u32[]{:S(2)}, u32[]{:S(2)}) async-start(bf16[4,144,128]{2,1,0:T(8,128)(2,1)} %get-tuple-element.35), calls=%async_computation.3 | async-start | bytes 294912 | tf_op jit(solution)/shard_map/all_to_all | solution.py:373
  88.9 4.1 %collective-permute-start.5 = (bf16[2,2,2,64,384]{4,3,2,1,0:T(8,128)(2,1)S(1)}, bf16[2,2,2,64,384]{4,3,2,1,0:T(8,128)(2,1)S(1)}, u32[]{:S(2)}, u32[]{:S(2)}) collective-permute-start(bf16[2,2,2,64,384]{4,3,2,1,0:T(8,128)(2,1)S(1)} %pad_maximum_fusion), channel_id=1, source_target_pairs={{7,0},{0,1},{1,2},{2,3},{3,4},{4,5},{5,6},{6,7},{15,8},{8,9},{9,10... | collective-permute-start | bytes 1179656 | tf_op jit(solution)/shard_map/ppermute | solution.py:345
  93.0 3.2 %all-to-all-done.3.parts = bf16[4,144,128]{2,1,0:T(8,128)(2,1)S(1)} async-done(((bf16[4,144,128]{2,1,0:T(8,128)(2,1)}), bf16[4,144,128]{2,1,0:T(8,128)(2,1)S(1)}, u32[]{:S(2)}, u32[]{:S(2)}) %all-to-all-start.3) | async-done | bytes 147488 | tf_op jit(solution)/shard_map/all_to_all | solution.py:373
  97.0 5.0 %all-to-all-start.4 = ((bf16[16,144,128]{2,1,0:T(8,128)(2,1)}), bf16[16,144,128]{2,1,0:T(8,128)(2,1)S(1)}, u32[]{:S(2)}, u32[]{:S(2)}) async-start(bf16[16,144,128]{2,1,0:T(8,128)(2,1)} %shard_map.108), calls=%async_computation.4 | async-start | bytes 1179648 | tf_op jit(solution)/shard_map/all_to_all | solution.py:374
  102.3 5.9 %collective-permute-start.6 = (bf16[4,2,64,384]{3,2,1,0:T(8,128)(2,1)S(1)}, bf16[4,2,64,384]{3,2,1,0:T(8,128)(2,1)S(1)}, u32[]{:S(2)}, u32[]{:S(2)}) collective-permute-start(bf16[4,2,64,384]{3,2,1,0:T(8,128)(2,1)S(1)} %pad_maximum_fusion.1), channel_id=1, source_target_pairs={{480,0},{481,1},{482,2},{483,3},{484,4},{485,5},{486,6},{487,7},{4... | collective-permute-start | bytes 1179656 | tf_op jit(solution)/shard_map/ppermute | solution.py:345
  108.2 6.6 %collective-permute-done.6.ahead.refs_1_ = bf16[4,2,64,384]{3,2,1,0:T(8,128)(2,1)S(1)} collective-permute-done((bf16[4,2,64,384]{3,2,1,0:T(8,128)(2,1)S(1)}, bf16[4,2,64,384]{3,2,1,0:T(8,128)(2,1)S(1)}, u32[]{:S(2)}, u32[]{:S(2)}) %collective-permute-start.6) | collective-permute-done | bytes 393248 | tf_op jit(solution)/shard_map/ppermute | solution.py:345
  114.8 3.1 %collective-permute-start.7 = (bf16[2304,128]{1,0:T(8,128)(2,1)S(1)}, bf16[2304,128]{1,0:T(8,128)(2,1)S(1)}, u32[]{:S(2)}, u32[]{:S(2)}) collective-permute-start(bf16[2304,128]{1,0:T(8,128)(2,1)S(1)} %shard_map.109.mine), channel_id=1, source_target_pairs={{0,32},{32,0},{1,33},{33,1},{2,34},{34,2},{3,35},{35,3},{4,36},{36... | collective-permute-start | bytes 1769480 | tf_op jit(solution)/shard_map/ppermute | solution.py:384
  117.9 2.4 %shard_map.107 = (bf16[512,384]{1,0:T(8,128)(2,1)}, bf16[512,384]{1,0:T(8,128)(2,1)}) custom-call(s32[1]{0:T(128)} %bitcast.odd.core, bf16[512,384]{1,0:T(8,128)(2,1)S(1)} %bitcast.17, s32[8,8,8]{2,1,0:T(8,128)S(1)} %copy-done.6, bf16[512,384]{1,0:T(8,128)(2,1)S(1)} %bitcast.19, bf16[2,2,64,384]{3,2,1,0:T(8,128)(2,1)S(1)} %copy-done.4, ...), custom_call_target="tpu_custom_call" | custom-call | flops 300000000 | bytes 4000000 | tf_op jit(solution)/shard_map/pallas_call | solution.py:376
  120.4 1.8 %shard_map.110 = (f32[384,1152]{1,0:T(8,128)}, f32[384,384]{1,0:T(8,128)}, f32[384]{0:T(512)}) custom-call(s32[1]{0:T(128)} %bitcast.odd.core, bf16[2304,128]{1,0:T(8,128)(2,1)S(1)} %shard_map.109.mine, bf16[2304,128]{1,0:T(8,128)(2,1)S(1)} %collective-permute-done.7.other, bf16[384,1152]{1,0:T(8,128)(2,1)S(1)} %copy-done.2, f32[1,384]{1,0:T(1,128)S(1)} %reshape.41.gain), custom_call_target="tpu_custom_call" | custom-call | tf_op jit(solution)/shard_map/pallas_call | solution.py:385
  (53 shorter events, 9.1 us)
Async XLA Ops:
  3.1 9.2 %collective-permute-start = (bf16[4,2,64,384]{3,2,1,0:T(8,128)(2,1)}, bf16[4,2,64,384]{3,2,1,0:T(8,128)(2,1)S(1)}, u32[]{:S(2)}, u32[]{:S(2)}) collective-permute-start(bf16[4,2,64,384]{3,2,1,0:T(8,128)(2,1)} %get-tuple-element.23), channel_id=1, source_target_pairs={{0,480},{1,481},{2,482},{3,483},{4,484},{5,485},{6,486},{7,487},{8... | collective-permute-start | bytes 1179656 | tf_op jit(solution)/shard_map/ppermute | solution.py:345
  9.9 16.1 %copy-start.14 = (f32[384]{0:T(512)S(1)}, f32[384]{0:T(512)}, u32[]{:S(2)}) copy-start(f32[384]{0:T(512)} %param.11) | copy-start | bytes 4612
  9.9 26.7 %copy-start.2 = (bf16[384,1152]{1,0:T(8,128)(2,1)S(1)}, bf16[384,1152]{1,0:T(8,128)(2,1)}, u32[]{:S(2)}) copy-start(bf16[384,1152]{1,0:T(8,128)(2,1)} %w_qkv.5) | copy-start | bytes 2654212
  10.0 26.7 %copy-start.5 = (bf16[4,2,64,384]{3,2,1,0:T(8,128)(2,1)S(1)}, bf16[4,2,64,384]{3,2,1,0:T(8,128)(2,1)}, u32[]{:S(2)}) copy-start(bf16[4,2,64,384]{3,2,1,0:T(8,128)(2,1)} %get-tuple-element.22.own) | copy-start | bytes 1179652
  10.0 26.7 %copy-start.7 = (bf16[384,384]{1,0:T(8,128)(2,1)S(1)}, bf16[384,384]{1,0:T(8,128)(2,1)}, u32[]{:S(2)}) copy-start(bf16[384,384]{1,0:T(8,128)(2,1)} %w_proj.3) | copy-start | bytes 884740
  12.3 13.8 %collective-permute-start.1 = (bf16[2,2,64,384]{3,2,1,0:T(8,128)(2,1)S(1)}, bf16[2,2,64,384]{3,2,1,0:T(8,128)(2,1)S(1)}, u32[]{:S(2)}, u32[]{:S(2)}) collective-permute-start(bf16[2,2,64,384]{3,2,1,0:T(8,128)(2,1)S(1)} %pad_maximum_fusion.2), channel_id=1, source_target_pairs={{0,31},{1,24},{2,25},{3,26},{4,27},{5,28},{6,29},{7,30},{8,7},{9,0... | collective-permute-start | bytes 589832 | tf_op jit(solution)/shard_map/ppermute | solution.py:345
  17.5 12.0 %collective-permute-start.2 = (bf16[2,2,64,384]{3,2,1,0:T(8,128)(2,1)S(1)}, bf16[2,2,64,384]{3,2,1,0:T(8,128)(2,1)S(1)}, u32[]{:S(2)}, u32[]{:S(2)}) collective-permute-start(bf16[2,2,64,384]{3,2,1,0:T(8,128)(2,1)S(1)} %pad_maximum_fusion.3), channel_id=1, source_target_pairs={{0,24},{1,25},{2,26},{3,27},{4,28},{5,29},{6,30},{7,31},{8,0},{9,1... | collective-permute-start | bytes 589832 | tf_op jit(solution)/shard_map/ppermute | solution.py:345
  23.0 13.7 %collective-permute-start.3 = (bf16[2,2,64,384]{3,2,1,0:T(8,128)(2,1)S(1)}, bf16[2,2,64,384]{3,2,1,0:T(8,128)(2,1)S(1)}, u32[]{:S(2)}, u32[]{:S(2)}) collective-permute-start(bf16[2,2,64,384]{3,2,1,0:T(8,128)(2,1)S(1)} %pad_maximum_fusion.4), channel_id=1, source_target_pairs={{0,7},{1,0},{2,1},{3,2},{4,3},{5,4},{6,5},{7,6},{8,15},{9,8},{10,9... | collective-permute-start | bytes 589832 | tf_op jit(solution)/shard_map/ppermute | solution.py:345
  50.0 5.7 %copy-start.8 = (bf16[512,1152]{1,0:T(8,128)(2,1)}, bf16[512,1152]{1,0:T(8,128)(2,1)S(1)}, u32[]{:S(2)}) copy-start(bf16[512,1152]{1,0:T(8,128)(2,1)S(1)} %get-tuple-element.25.d_qkv) | copy-start | bytes 3538948
  50.0 5.7 %copy-start.10 = (bf16[384,512]{1,0:T(8,128)(2,1)}, bf16[384,512]{1,0:T(8,128)(2,1)S(1)}, u32[]{:S(2)}) copy-start(bf16[384,512]{1,0:T(8,128)(2,1)S(1)} %get-tuple-element.24.mixed_t) | copy-start | bytes 1179652
  50.0 5.7 %copy-start.12 = (f32[512,128]{1,0:T(8,128)}, f32[512,128]{1,0:T(8,128)S(1)}, u32[]{:S(2)}) copy-start(f32[512,128]{1,0:T(8,128)S(1)} %get-tuple-element.27.inv_std) | copy-start | bytes 786436
  56.7 15.1 %all-to-all-start.1 = ((bf16[16,144,128]{2,1,0:T(8,128)(2,1)}), bf16[16,144,128]{2,1,0:T(8,128)(2,1)S(1)}, u32[]{:S(2)}, u32[]{:S(2)}) async-start(bf16[16,144,128]{2,1,0:T(8,128)(2,1)} %bitcast.5), calls=%async_computation.1 | async-start | bytes 1179648 | tf_op jit(solution)/shard_map/all_to_all | solution.py:321
  66.4 35.7 %copy-start.3 = (bf16[2,2,64,384]{3,2,1,0:T(8,128)(2,1)}, bf16[2,2,64,384]{3,2,1,0:T(8,128)(2,1)S(1)}, u32[]{:S(2)}) copy-start(bf16[2,2,64,384]{3,2,1,0:T(8,128)(2,1)S(1)} %get-tuple-element.28.home_0) | copy-start | bytes 589828
  66.4 13.7 %collective-permute-start.4 = (bf16[2,2,2,64,384]{4,3,2,1,0:T(8,128)(2,1)S(1)}, bf16[2,2,2,64,384]{4,3,2,1,0:T(8,128)(2,1)S(1)}, u32[]{:S(2)}, u32[]{:S(2)}) collective-permute-start(bf16[2,2,2,64,384]{4,3,2,1,0:T(8,128)(2,1)S(1)} %get-tuple-element.31), channel_id=1, source_target_pairs={{24,0},{25,1},{26,2},{27,3},{28,4},{29,5},{30,6},{31,7},{0,8},{1,9... | collective-permute-start | bytes 1179656 | tf_op jit(solution)/shard_map/ppermute | solution.py:345
  72.5 11.8 %all-to-all-start.2 = ((bf16[4,144,128]{2,1,0:T(8,128)(2,1)}), bf16[4,144,128]{2,1,0:T(8,128)(2,1)S(1)}, u32[]{:S(2)}, u32[]{:S(2)}) async-start(bf16[4,144,128]{2,1,0:T(8,128)(2,1)} %shard_map.105), calls=%async_computation.2 | async-start | bytes 294912 | tf_op jit(solution)/shard_map/all_to_all | solution.py:371
  85.0 11.2 %all-to-all-start.3 = ((bf16[4,144,128]{2,1,0:T(8,128)(2,1)}), bf16[4,144,128]{2,1,0:T(8,128)(2,1)S(1)}, u32[]{:S(2)}, u32[]{:S(2)}) async-start(bf16[4,144,128]{2,1,0:T(8,128)(2,1)} %get-tuple-element.35), calls=%async_computation.3 | async-start | bytes 294912 | tf_op jit(solution)/shard_map/all_to_all | solution.py:373
  88.9 13.2 %collective-permute-start.5 = (bf16[2,2,2,64,384]{4,3,2,1,0:T(8,128)(2,1)S(1)}, bf16[2,2,2,64,384]{4,3,2,1,0:T(8,128)(2,1)S(1)}, u32[]{:S(2)}, u32[]{:S(2)}) collective-permute-start(bf16[2,2,2,64,384]{4,3,2,1,0:T(8,128)(2,1)S(1)} %pad_maximum_fusion), channel_id=1, source_target_pairs={{7,0},{0,1},{1,2},{2,3},{3,4},{4,5},{5,6},{6,7},{15,8},{8,9},{9,10... | collective-permute-start | bytes 1179656 | tf_op jit(solution)/shard_map/ppermute | solution.py:345
  97.0 17.7 %all-to-all-start.4 = ((bf16[16,144,128]{2,1,0:T(8,128)(2,1)}), bf16[16,144,128]{2,1,0:T(8,128)(2,1)S(1)}, u32[]{:S(2)}, u32[]{:S(2)}) async-start(bf16[16,144,128]{2,1,0:T(8,128)(2,1)} %shard_map.108), calls=%async_computation.4 | async-start | bytes 1179648 | tf_op jit(solution)/shard_map/all_to_all | solution.py:374
  102.2 15.7 %copy-start = (bf16[8,8,8,384]{3,2,1,0:T(8,128)(2,1)S(1)}, bf16[8,8,8,384]{3,2,1,0:T(8,128)(2,1)}, u32[]{:S(2)}) copy-start(bf16[8,8,8,384]{3,2,1,0:T(8,128)(2,1)} %param.6) | copy-start | bytes 1179652
  102.2 15.7 %copy-start.1 = (bf16[8,8,8,384]{3,2,1,0:T(8,128)(2,1)S(1)}, bf16[8,8,8,384]{3,2,1,0:T(8,128)(2,1)}, u32[]{:S(2)}) copy-start(bf16[8,8,8,384]{3,2,1,0:T(8,128)(2,1)} %param.8) | copy-start | bytes 1179652
  102.2 15.7 %copy-start.6 = (s32[8,8,8]{2,1,0:T(8,128)S(1)}, s32[8,8,8]{2,1,0:T(8,128)}, u32[]{:S(2)}) copy-start(s32[8,8,8]{2,1,0:T(8,128)} %frozen.1) | copy-start | bytes 6148
  102.3 12.5 %collective-permute-start.6 = (bf16[4,2,64,384]{3,2,1,0:T(8,128)(2,1)S(1)}, bf16[4,2,64,384]{3,2,1,0:T(8,128)(2,1)S(1)}, u32[]{:S(2)}, u32[]{:S(2)}) collective-permute-start(bf16[4,2,64,384]{3,2,1,0:T(8,128)(2,1)S(1)} %pad_maximum_fusion.1), channel_id=1, source_target_pairs={{480,0},{481,1},{482,2},{483,3},{484,4},{485,5},{486,6},{487,7},{4... | collective-permute-start | bytes 1179656 | tf_op jit(solution)/shard_map/ppermute | solution.py:345
  114.8 3.2 %copy-start.4 = (bf16[2,2,64,384]{3,2,1,0:T(8,128)(2,1)S(1)}, bf16[2,2,64,384]{3,2,1,0:T(8,128)(2,1)}, u32[]{:S(2)}) copy-start(bf16[2,2,64,384]{3,2,1,0:T(8,128)(2,1)} %copy-done.3) | copy-start | bytes 589828
  114.8 5.6 %collective-permute-start.7 = (bf16[2304,128]{1,0:T(8,128)(2,1)S(1)}, bf16[2304,128]{1,0:T(8,128)(2,1)S(1)}, u32[]{:S(2)}, u32[]{:S(2)}) collective-permute-start(bf16[2304,128]{1,0:T(8,128)(2,1)S(1)} %shard_map.109.mine), channel_id=1, source_target_pairs={{0,32},{32,0},{1,33},{33,1},{2,34},{34,2},{3,35},{35,3},{4,36},{36... | collective-permute-start | bytes 1769480 | tf_op jit(solution)/shard_map/ppermute | solution.py:384
  (3 other events, 3.2 us)

commit v10 on v9

--- a/solution.py
+++ b/solution.py
@@ -15,6 +15,7 @@
 HALF = WIN // 2
 ROWS = WIN**3
 PIECE = HALF**3
+HALF_ROWS = ROWS // 2
 EPSILON = 1e-05
 BF = jnp.bfloat16
 F32 = jnp.float32
@@ -143,22 +144,28 @@
 
 
 def keep_rows(frozen):
-    table = ones_where(frozen[...].reshape(WIN * WIN, WIN) == 1).astype(BF)
+    planes = frozen.shape[0]
+    table = ones_where(frozen[...].reshape(planes * WIN, WIN) == 1).astype(BF)
     column = lax.broadcasted_iota(jnp.int32, (WIN, WIN * WIN), 1)
     row = lax.broadcasted_iota(jnp.int32, (WIN, WIN * WIN), 0)
     spread = dot(table, ones_where((column & 7) == row).astype(BF))
     chosen = ones_where((column >> 3) == row)
     return [
         jnp.sum(spread[plane * WIN : (plane + 1) * WIN] * chosen, axis=0, keepdims=True)
-        for plane in range(WIN)
+        for plane in range(planes)
     ]
 
 
-def cut_kernel(odd, tokens_in, frozen_in, cotangent_in, own, ahead, tokens, frozen, cotangent, arrivals):
+def cut_kernel(odd, tokens_in, frozen_in, cotangent_in, target, tokens, frozen, cotangent, arrivals, *, upper):
+    rows = pl.ds(upper * HALF_ROWS, HALF_ROWS)
     moves = [
         pltpu.make_async_copy(source, target, arrivals.at[index])
         for index, (source, target) in enumerate(
-            ((frozen_in, frozen), (tokens_in, tokens), (cotangent_in, cotangent))
+            (
+                (frozen_in.at[pl.ds(upper * HALF, HALF)], frozen),
+                (tokens_in.at[rows], tokens),
+                (cotangent_in.at[rows], cotangent),
+            )
         )
     ]
     for move in moves:
@@ -166,42 +173,77 @@
     for move in moves:
         move.wait()
     keeps = keep_rows(frozen)
-    for upper, target in ((0, ahead), (1, own)):
-        matrix = ones_where(order(odd[0], upper, False))
-        for plane in range(HALF):
-            index = upper * HALF + plane
-            part = pl.ds(index * WIN * WIN, WIN * WIN)
-            kept = dot((matrix * keeps[index]).astype(BF), tokens[part, :]).astype(BF)
-            cot = dot(matrix.astype(BF), cotangent[part, :]).astype(BF)
-            for group in range(4):
-                rows = slice(group * 16, group * 16 + 16)
-                target[group, 0, pl.ds(plane * 16, 16), :] = kept[rows]
-                target[group, 1, pl.ds(plane * 16, 16), :] = cot[rows]
-
-
-def join_kernel(odd, tokens, frozen, cotangent, home_0, home_x, home_2, ahead, block_out, tokens_grad):
-    homes = (home_0, home_x.at[0], home_2.at[0], home_x.at[1])
+    matrix = ones_where(order(odd[0], upper, False))
+    for plane in range(HALF):
+        part = pl.ds(plane * WIN * WIN, WIN * WIN)
+        kept = dot((matrix * keeps[plane]).astype(BF), tokens[part, :]).astype(BF)
+        cot = dot(matrix.astype(BF), cotangent[part, :]).astype(BF)
+        for group in range(4):
+            rows = slice(group * 16, group * 16 + 16)
+            target[group, 0, pl.ds(plane * 16, 16), :] = kept[rows]
+            target[group, 1, pl.ds(plane * 16, 16), :] = cot[rows]
+
+
+def cut(core, tokens, frozen, cotangent, upper):
+    return pl.pallas_call(
+        functools.partial(cut_kernel, upper=upper),
+        out_shape=jax.ShapeDtypeStruct((4, 2, PIECE, D), BF),
+        in_specs=[SCALAR] + [pl.BlockSpec(memory_space=pltpu.HBM)] * 3,
+        scratch_shapes=[
+            pltpu.VMEM((HALF_ROWS, D), BF),
+            pltpu.VMEM((HALF, WIN, WIN), jnp.int32),
+            pltpu.VMEM((HALF_ROWS, D), BF),
+            pltpu.SemaphoreType.DMA((3,)),
+        ],
+        compiler_params=pltpu.CompilerParams(vmem_limit_bytes=56 * 1024 * 1024),
+    )(core, tokens, frozen, cotangent)
+
+
+def join_kernel(odd, tokens, frozen, cotangent, *rest, upper):
+    if upper:
+        pieces, (block_out, tokens_grad, token) = rest[:3], rest[-3:]
+        token[...] = jnp.zeros_like(token)
+    else:
+        pieces, (block_out, tokens_grad) = rest[:1], rest[-2:]
     keeps = keep_rows(frozen)
     shape = (WIN * WIN, WIN * WIN)
     diagonal = ones_where(lax.broadcasted_iota(jnp.int32, shape, 0) == lax.broadcasted_iota(jnp.int32, shape, 1))
-    for upper in range(2):
-        matrix = ones_where(order(odd[0], upper, True)).astype(BF)
-        for plane in range(HALF):
-            index = upper * HALF + plane
-            part = pl.ds(index * WIN * WIN, WIN * WIN)
-            keep = (diagonal * keeps[index]).astype(BF)
-            rows = pl.ds(plane * 16, 16)
-
-            def pieces(array):
-                if upper:
-                    found = [homes[group][0, array, rows, :] for group in range(4)]
-                else:
-                    found = [ahead[group, array, rows, :] for group in range(4)]
-                return dot(matrix, jnp.concatenate(found, axis=0))
-
-            block_out[part, :] = (dot(keep, tokens[part, :]) + pieces(0)).astype(BF)
-            grown = (cotangent[part, :].astype(F32) + pieces(1)).astype(BF)
-            tokens_grad[part, :] = dot(keep, grown).astype(BF)
+    matrix = ones_where(order(odd[0], upper, True)).astype(BF)
+    for plane in range(HALF):
+        part = pl.ds(plane * WIN * WIN, WIN * WIN)
+        keep = (diagonal * keeps[plane]).astype(BF)
+        rows = pl.ds(plane * 16, 16)
+
+        def piece(group, array):
+            if not upper:
+                return pieces[0][group, array, rows, :]
+            home_0, home_x, home_y = pieces
+            home = (home_0, home_x.at[0], home_y.at[0], home_x.at[1])[group]
+            return home[0, array, rows, :]
+
+        def ordered(array):
+            return dot(matrix, jnp.concatenate([piece(group, array) for group in range(4)], axis=0))
+
+        block_out[part, :] = (dot(keep, tokens[part, :]) + ordered(0)).astype(BF)
+        grown = (cotangent[part, :].astype(F32) + ordered(1)).astype(BF)
+        tokens_grad[part, :] = dot(keep, grown).astype(BF)
+
+
+def join(core, tokens, frozen, cotangent, pieces, upper, begun=()):
+    half = pl.BlockSpec((HALF_ROWS, D), lambda step: (upper, 0))
+    return pl.pallas_call(
+        functools.partial(join_kernel, upper=upper),
+        grid=(1,),
+        out_shape=(jax.ShapeDtypeStruct((ROWS, D), BF),) * 2
+        + (jax.ShapeDtypeStruct((8, LANES), F32),) * upper,
+        in_specs=[SCALAR, half, pl.BlockSpec((HALF, WIN, WIN), lambda step: (upper, 0, 0)), half]
+        + [WHOLE] * len(pieces)
+        + [pl.BlockSpec(memory_space=pl.ANY)] * len(begun),
+        out_specs=(half, half) + (WHOLE,) * upper,
+        input_output_aliases={4 + len(pieces) + at: at for at in range(len(begun))},
+        compiler_params=SMALL,
+        cost_estimate=pl.CostEstimate(flops=150_000_000, bytes_accessed=2_000_000, transcendentals=0),
+    )(core, tokens, frozen, cotangent, *pieces, *begun)
 
 
 SCALAR = pl.BlockSpec(memory_space=pltpu.SMEM)
@@ -233,16 +275,16 @@
     return (total, *passed) if through else total
 
 
-def hold(array, until):
+def hold(array, *until):
     anywhere = pl.BlockSpec(memory_space=pl.ANY)
     return pl.pallas_call(
         lambda *refs: None,
         out_shape=jax.ShapeDtypeStruct(array.shape, array.dtype),
-        in_specs=[anywhere] * 2,
+        in_specs=[anywhere] * (1 + len(until)),
         out_specs=anywhere,
         input_output_aliases={0: 0},
         compiler_params=SMALL,
-    )(array, until)
+    )(array, *until)
 
 
 def grads_kernel(core, mine, other, w_qkv, gain, qkv_grad, proj_grad, gain_grad):
@@ -294,7 +336,7 @@
         cost_estimate=pl.CostEstimate(
             flops=12_000_000_000, bytes_accessed=5_000_000, transcendentals=3_200_000
         ),
-    )(own, behind, *sides[::-1], w_qkv, w_proj, gain)
+    )(own, behind, *sides, w_qkv, w_proj, gain)
     backs = pl.pallas_call(
         rows_kernel,
         out_shape=(jax.ShapeDtypeStruct((2, 2, PIECE, D), BF),) * 2
@@ -348,23 +390,10 @@
 def local(tokens, frozen, cotangent, w_qkv, w_proj, norm_gain):
     core = lax.axis_index("core").reshape(1)
     token_rows, cot_rows = tokens.reshape(ROWS, D), cotangent.reshape(ROWS, D)
-    own, ahead = pl.pallas_call(
-        cut_kernel,
-        out_shape=(jax.ShapeDtypeStruct((4, 2, PIECE, D), BF),) * 2,
-        in_specs=[SCALAR] + [pl.BlockSpec(memory_space=pltpu.HBM)] * 3,
-        scratch_shapes=[
-            pltpu.VMEM((ROWS, D), BF),
-            pltpu.VMEM((WIN, WIN, WIN), jnp.int32),
-            pltpu.VMEM((ROWS, D), BF),
-            pltpu.SemaphoreType.DMA((3,)),
-        ],
-        compiler_params=pltpu.CompilerParams(vmem_limit_bytes=56 * 1024 * 1024),
-    )(core, token_rows, frozen, cot_rows)
-    behind = send(ahead, 0)
-    sides = [None] * 4
-    for kind in (1, 2, 3):
-        sides[kind] = send(jnp.stack([own[kind], behind[kind]]), kind)
-    back_0, back_1, back_y, grads = window_pass(own, behind, sides[1:], w_qkv, w_proj, norm_gain)
+    behind = send(cut(core, token_rows, frozen, cot_rows, 0), 0)
+    own = cut(core, token_rows, frozen, cot_rows, 1)
+    sides = [send(jnp.stack([own[kind], behind[kind]]), kind) for kind in (3, 2, 1)]
+    back_0, back_1, back_y, grads = window_pass(own, behind, sides, w_qkv, w_proj, norm_gain)
     parts = near_sum(grads)
     parts = total_of(parts, FAR)
     home_y = send(back_y, 2, True)
@@ -373,14 +402,9 @@
     parts = total_of(lax.all_to_all(parts, "y_hi", 0, 0), GROUP)
     mine = lax.all_to_all(parts, NEAR, 0, 0).reshape(GRAD_ROWS // 2, LANES)
     ahead = send(jnp.stack([back_0[1], home_x[0, 1], home_y[0, 1], home_x[1, 1]]), 0, True)
-    block_out, tokens_grad = pl.pallas_call(
-        join_kernel,
-        out_shape=(jax.ShapeDtypeStruct((ROWS, D), BF),) * 2,
-        in_specs=[SCALAR] + [WHOLE] * 7,
-        compiler_params=SMALL,
-        cost_estimate=pl.CostEstimate(flops=300_000_000, bytes_accessed=4_000_000, transcendentals=0),
-    )(core, token_rows, frozen, cot_rows, back_0, home_x, home_y, ahead)
-    mine = hold(mine, ahead)
+    *begun, token = join(core, token_rows, frozen, cot_rows, (back_0, home_x, home_y), 1)
+    mine = hold(mine, ahead, token)
+    block_out, tokens_grad = join(core, token_rows, frozen, cot_rows, (ahead,), 0, begun)
     other = lax.ppermute(mine, "core", [(0, 1), (1, 0)])
     qkv_grad, proj_grad, gain_grad = pl.pallas_call(
         grads_kernel,

time: 123 us -> 122 us (level)
  waiting for transfers between devices: 29.2 us -> 25.5 us
  Pallas kernels: 24.7 us -> 27.5 us
  starting transfers between devices: 56.9 us -> 55.6 us
    ppermute x7, waiting for transfers between devices: 21.8 us -> 18.9 us  [send(): return lax.ppermute(block, LATTICE, route(kind, back))]
    pallas_call x2 -> x4, Pallas kernels: 4.85 us -> 7.65 us  [the longest x2 4.37 us: cut(): pl.pallas_call(functools.partial(cut_kernel, upper=upper), out_shape=jax....]
    ppermute x7, starting transfers between devices: 35.8 us -> 34.4 us  [send(): return lax.ppermute(block, LATTICE, route(kind, back))]
    unnamed x30 -> x34, local copies, waits for them, and re-layouts: 3.27 us -> 3.97 us
  transfers between devices with their start and end apart: 12 -> 12, of which waited for: 8 -> 7; matrix products, arithmetic and copies ran while one was open for 1% -> 2% of each run, Pallas kernels for 5% -> 7%
where the time goes in v10:
time: 122 us; the launch traced here: 121 us
  starting transfers between devices  55.6 us (46%)
  Pallas kernels  27.5 us (23%)
  waiting for transfers between devices  25.5 us (21%)
  blocking collectives  5.68 us (5%)
  local copies, waits for them, and re-layouts  5.21 us (4%)
    ppermute x7, starting transfers between devices, send(): return lax.ppermute(block, LATTICE, route(kind, back))  34.4 us
    ppermute x7, waiting for transfers between devices, send(): return lax.ppermute(block, LATTICE, route(kind, back))  18.9 us
    pallas_call x1, Pallas kernels, window_pass(): pl.pallas_call(window_kernel, out_shape=(jax.ShapeDtypeStruct((GRAD_ROWS,...  13.3 us
    all_to_all x1, blocking collectives, near_sum(): lax.all_to_all(rows.reshape(2, GRAD_ROWS // 2, LANES), 'core', 0, 0)  5.68 us
    all_to_all x1, starting transfers between devices, local(): mine = lax.all_to_all(parts, NEAR, 0, 0).reshape(GRAD_ROWS // 2, LANES)  5.11 us
    all_to_all x1, starting transfers between devices, near_sum(): parts = lax.all_to_all(parts, NEAR, 0, 0)  5.07 us
    pallas_call x2, Pallas kernels, cut(): pl.pallas_call(functools.partial(cut_kernel, upper=upper), out_shape=jax....  4.37 us
    all_to_all x1, waiting for transfers between devices, local(): lax.all_to_all(parts, 'z_hi', 0, 0)  4.22 us
  transfers between devices with their start and end apart: 12, of which 7 were waited for; matrix products, arithmetic and copies ran while one was open for 2% of the time, Pallas kernels for 7%

profile of v10, /device:TPU:1, one launch (start us, length us, event | category | flops | bytes accessed | tf_op | source)
XLA Modules:
  0.0 121.4 jit_solution(6086206586761944715)
XLA Ops:
  0.6 2.2 %shard_map.102 = bf16[4,2,64,384]{3,2,1,0:T(8,128)(2,1)} custom-call(s32[1]{0:T(128)} %bitcast.odd.core, bf16[512,384]{1,0:T(8,128)(2,1)} %bitcast.15, s32[8,8,8]{2,1,0:T(8,128)} %frozen.3, bf16[512,384]{1,0:T(8,128)(2,1)} %bitcast.19), custom_call_target="tpu_custom_call" | custom-call | tf_op jit(solution)/shard_map/pallas_call | solution.py:188
  2.8 6.9 %collective-permute-start = (bf16[4,2,64,384]{3,2,1,0:T(8,128)(2,1)}, bf16[4,2,64,384]{3,2,1,0:T(8,128)(2,1)S(1)}, u32[]{:S(2)}, u32[]{:S(2)}) collective-permute-start(bf16[4,2,64,384]{3,2,1,0:T(8,128)(2,1)} %shard_map.102), channel_id=1, source_target_pairs={{0,480},{1,481},{2,482},{3,483},{4,484},{5,485},{6,486},{7,487},{8... | collective-permute-start | bytes 1179656 | tf_op jit(solution)/shard_map/ppermute | solution.py:387
  9.7 2.2 %shard_map.101.own = bf16[4,2,64,384]{3,2,1,0:T(8,128)(2,1)} custom-call(s32[1]{0:T(128)} %bitcast.odd.core, bf16[512,384]{1,0:T(8,128)(2,1)} %bitcast.16, s32[8,8,8]{2,1,0:T(8,128)} %frozen.3, bf16[512,384]{1,0:T(8,128)(2,1)} %bitcast.20), custom_call_target="tpu_custom_call" | custom-call | tf_op jit(solution)/shard_map/pallas_call | solution.py:188
  13.2 4.0 %collective-permute-start.1 = (bf16[2,2,64,384]{3,2,1,0:T(8,128)(2,1)S(1)}, bf16[2,2,64,384]{3,2,1,0:T(8,128)(2,1)S(1)}, u32[]{:S(2)}, u32[]{:S(2)}) collective-permute-start(bf16[2,2,64,384]{3,2,1,0:T(8,128)(2,1)S(1)} %pad_maximum_fusion.2), channel_id=1, source_target_pairs={{0,31},{1,24},{2,25},{3,26},{4,27},{5,28},{6,29},{7,30},{8,7},{9,0... | collective-permute-start | bytes 589832 | tf_op jit(solution)/shard_map/ppermute | solution.py:387
  17.3 5.4 %collective-permute-start.2 = (bf16[2,2,64,384]{3,2,1,0:T(8,128)(2,1)S(1)}, bf16[2,2,64,384]{3,2,1,0:T(8,128)(2,1)S(1)}, u32[]{:S(2)}, u32[]{:S(2)}) collective-permute-start(bf16[2,2,64,384]{3,2,1,0:T(8,128)(2,1)S(1)} %pad_maximum_fusion.3), channel_id=1, source_target_pairs={{0,24},{1,25},{2,26},{3,27},{4,28},{5,29},{6,30},{7,31},{8,0},{9,1... | collective-permute-start | bytes 589832 | tf_op jit(solution)/shard_map/ppermute | solution.py:387
  22.7 3.1 %collective-permute-start.3 = (bf16[2,2,64,384]{3,2,1,0:T(8,128)(2,1)S(1)}, bf16[2,2,64,384]{3,2,1,0:T(8,128)(2,1)S(1)}, u32[]{:S(2)}, u32[]{:S(2)}) collective-permute-start(bf16[2,2,64,384]{3,2,1,0:T(8,128)(2,1)S(1)} %pad_maximum_fusion.4), channel_id=1, source_target_pairs={{0,7},{1,0},{2,1},{3,2},{4,3},{5,4},{6,5},{7,6},{8,15},{9,8},{10,9... | collective-permute-start | bytes 589832 | tf_op jit(solution)/shard_map/ppermute | solution.py:387
  25.9 3.4 %collective-permute-done.2.side_2 = bf16[2,2,64,384]{3,2,1,0:T(8,128)(2,1)S(1)} collective-permute-done((bf16[2,2,64,384]{3,2,1,0:T(8,128)(2,1)S(1)}, bf16[2,2,64,384]{3,2,1,0:T(8,128)(2,1)S(1)}, u32[]{:S(2)}, u32[]{:S(2)}) %collective-permute-start.2) | collective-permute-done | bytes 196640 | tf_op jit(solution)/shard_map/ppermute | solution.py:387
  29.2 7.1 %collective-permute-done.3.side_1 = bf16[2,2,64,384]{3,2,1,0:T(8,128)(2,1)S(1)} collective-permute-done((bf16[2,2,64,384]{3,2,1,0:T(8,128)(2,1)S(1)}, bf16[2,2,64,384]{3,2,1,0:T(8,128)(2,1)S(1)}, u32[]{:S(2)}, u32[]{:S(2)}) %collective-permute-start.3) | collective-permute-done | bytes 196640 | tf_op jit(solution)/shard_map/ppermute | solution.py:387
  36.4 13.3 %shard_map.103 = (bf16[4608,128]{1,0:T(8,128)(2,1)S(1)}, bf16[384,512]{1,0:T(8,128)(2,1)S(1)}, bf16[512,1152]{1,0:T(8,128)(2,1)S(1)}, f32[512,384]{1,0:T(8,128)S(1)}, f32[512,128]{1,0:T(8,128)S(1)}) custom-call(bf16[4,2,64,384]{3,2,1,0:T(8,128)(2,1)S(1)} %copy-done.2, bf16[4,2,64,384]{3,2,1,0:T(8,128)(2,1)S(1)} %collective-permute-done.behind, ...), custom_call_target="tpu_custom_call" | custom-call | flops 12000000000 | bytes 5000000 | tf_op jit(solution)/shard_map/pallas_call | solution.py:317
  50.5 5.7 %all_to_all.25.parts = bf16[2,2304,128]{2,1,0:T(8,128)(2,1)S(1)} all-to-all(bf16[2,2304,128]{2,1,0:T(8,128)(2,1)S(1)} %bitcast.24), channel_id=1, replica_groups=mesh['z_hi'=4,'z_lo'=2,'core'=2,'y_hi'=4,'y_lo'=2,'x'=4] {'core'}, dimensions={0} | all-to-all | bytes 2359296 | tf_op jit(solution)/shard_map/all_to_all | solution.py:361
  57.1 5.1 %all-to-all-start.1 = ((bf16[16,144,128]{2,1,0:T(8,128)(2,1)}), bf16[16,144,128]{2,1,0:T(8,128)(2,1)S(1)}, u32[]{:S(2)}, u32[]{:S(2)}) async-start(bf16[16,144,128]{2,1,0:T(8,128)(2,1)} %bitcast.5), calls=%async_computation.1 | async-start | bytes 1179648 | tf_op jit(solution)/shard_map/all_to_all | solution.py:363
  66.9 5.2 %collective-permute-start.4 = (bf16[2,2,2,64,384]{4,3,2,1,0:T(8,128)(2,1)S(1)}, bf16[2,2,2,64,384]{4,3,2,1,0:T(8,128)(2,1)S(1)}, u32[]{:S(2)}, u32[]{:S(2)}) collective-permute-start(bf16[2,2,2,64,384]{4,3,2,1,0:T(8,128)(2,1)S(1)} %get-tuple-element.30), channel_id=1, source_target_pairs={{24,0},{25,1},{26,2},{27,3},{28,4},{29,5},{30,6},{31,7},{0,8},{1,9... | collective-permute-start | bytes 1179656 | tf_op jit(solution)/shard_map/ppermute | solution.py:387
  73.0 4.1 %all-to-all-start.2 = ((bf16[4,144,128]{2,1,0:T(8,128)(2,1)}), bf16[4,144,128]{2,1,0:T(8,128)(2,1)S(1)}, u32[]{:S(2)}, u32[]{:S(2)}) async-start(bf16[4,144,128]{2,1,0:T(8,128)(2,1)} %shard_map.106), calls=%async_computation.2 | async-start | bytes 294912 | tf_op jit(solution)/shard_map/all_to_all | solution.py:400
  77.1 3.5 %collective-permute-done.4.rest_0_ = bf16[2,2,2,64,384]{4,3,2,1,0:T(8,128)(2,1)S(1)} collective-permute-done((bf16[2,2,2,64,384]{4,3,2,1,0:T(8,128)(2,1)S(1)}, bf16[2,2,2,64,384]{4,3,2,1,0:T(8,128)(2,1)S(1)}, u32[]{:S(2)}, u32[]{:S(2)}) %collective-permute-start.4) | collective-permute-done | bytes 393248 | tf_op jit(solution)/shard_map/ppermute | solution.py:387
  80.7 4.2 %all-to-all-done.2.parts = bf16[4,144,128]{2,1,0:T(8,128)(2,1)S(1)} async-done(((bf16[4,144,128]{2,1,0:T(8,128)(2,1)}), bf16[4,144,128]{2,1,0:T(8,128)(2,1)S(1)}, u32[]{:S(2)}, u32[]{:S(2)}) %all-to-all-start.2) | async-done | bytes 147488 | tf_op jit(solution)/shard_map/all_to_all | solution.py:400
  85.6 3.9 %all-to-all-start.3 = ((bf16[4,144,128]{2,1,0:T(8,128)(2,1)}), bf16[4,144,128]{2,1,0:T(8,128)(2,1)S(1)}, u32[]{:S(2)}, u32[]{:S(2)}) async-start(bf16[4,144,128]{2,1,0:T(8,128)(2,1)} %get-tuple-element.36), calls=%async_computation.3 | async-start | bytes 294912 | tf_op jit(solution)/shard_map/all_to_all | solution.py:402
  90.2 4.1 %collective-permute-start.5 = (bf16[2,2,2,64,384]{4,3,2,1,0:T(8,128)(2,1)}, bf16[2,2,2,64,384]{4,3,2,1,0:T(8,128)(2,1)S(1)}, u32[]{:S(2)}, u32[]{:S(2)}) collective-permute-start(bf16[2,2,2,64,384]{4,3,2,1,0:T(8,128)(2,1)} %pad_maximum_fusion), channel_id=1, source_target_pairs={{7,0},{0,1},{1,2},{2,3},{3,4},{4,5},{5,6},{6,7},{15,8},{8,9},{9,10... | collective-permute-start | bytes 1179656 | tf_op jit(solution)/shard_map/ppermute | solution.py:387
  94.4 2.3 %all-to-all-done.3.parts = bf16[4,144,128]{2,1,0:T(8,128)(2,1)S(1)} async-done(((bf16[4,144,128]{2,1,0:T(8,128)(2,1)}), bf16[4,144,128]{2,1,0:T(8,128)(2,1)S(1)}, u32[]{:S(2)}, u32[]{:S(2)}) %all-to-all-start.3) | async-done | bytes 147488 | tf_op jit(solution)/shard_map/all_to_all | solution.py:402
  97.6 5.1 %all-to-all-start.4 = ((bf16[16,144,128]{2,1,0:T(8,128)(2,1)}), bf16[16,144,128]{2,1,0:T(8,128)(2,1)S(1)}, u32[]{:S(2)}, u32[]{:S(2)}) async-start(bf16[16,144,128]{2,1,0:T(8,128)(2,1)} %shard_map.110), calls=%async_computation.4 | async-start | bytes 1179648 | tf_op jit(solution)/shard_map/all_to_all | solution.py:403
  102.9 5.6 %collective-permute-start.6 = (bf16[4,2,64,384]{3,2,1,0:T(8,128)(2,1)S(1)}, bf16[4,2,64,384]{3,2,1,0:T(8,128)(2,1)S(1)}, u32[]{:S(2)}, u32[]{:S(2)}) collective-permute-start(bf16[4,2,64,384]{3,2,1,0:T(8,128)(2,1)S(1)} %pad_maximum_fusion.1), channel_id=1, source_target_pairs={{480,0},{481,1},{482,2},{483,3},{484,4},{485,5},{486,6},{487,7},{4... | collective-permute-start | bytes 1179656 | tf_op jit(solution)/shard_map/ppermute | solution.py:387
  108.5 1.6 %shard_map.108 = (bf16[512,384]{1,0:T(8,128)(2,1)}, bf16[512,384]{1,0:T(8,128)(2,1)}, f32[8,128]{1,0:T(8,128)S(1)}) custom-call(s32[1]{0:T(128)} %bitcast.odd.core, bf16[512,384]{1,0:T(8,128)(2,1)S(1)} %bitcast.17, s32[8,8,8]{2,1,0:T(8,128)S(1)} %copy-done.4, bf16[512,384]{1,0:T(8,128)(2,1)S(1)} %bitcast.21, bf16[2,2,64,384]{3,2,1,0:T(8,128)(2,1)S(1)} %copy-done.6, ...), custom_call_target="tpu_custom_call" | custom-call | flops 150000000 | bytes 2000000 | tf_op jit(solution)/shard_map/pallas_call | solution.py:234
  110.1 4.8 %collective-permute-done.6.rest_0_.refs_1_ = bf16[4,2,64,384]{3,2,1,0:T(8,128)(2,1)S(1)} collective-permute-done((bf16[4,2,64,384]{3,2,1,0:T(8,128)(2,1)S(1)}, bf16[4,2,64,384]{3,2,1,0:T(8,128)(2,1)S(1)}, u32[]{:S(2)}, u32[]{:S(2)}) %collective-permute-start.6) | collective-permute-done | bytes 393248 | tf_op jit(solution)/shard_map/ppermute | solution.py:387
  115.0 3.0 %collective-permute-start.7 = (bf16[2304,128]{1,0:T(8,128)(2,1)S(1)}, bf16[2304,128]{1,0:T(8,128)(2,1)S(1)}, u32[]{:S(2)}, u32[]{:S(2)}) collective-permute-start(bf16[2304,128]{1,0:T(8,128)(2,1)S(1)} %shard_map.111.mine), channel_id=1, source_target_pairs={{0,32},{32,0},{1,33},{33,1},{2,34},{34,2},{3,35},{35,3},{4,36},{36... | collective-permute-start | bytes 1769480 | tf_op jit(solution)/shard_map/ppermute | solution.py:408
  119.6 1.8 %shard_map.112 = (f32[384,1152]{1,0:T(8,128)}, f32[384,384]{1,0:T(8,128)}, f32[384]{0:T(512)}) custom-call(s32[1]{0:T(128)} %bitcast.odd.core, bf16[2304,128]{1,0:T(8,128)(2,1)S(1)} %shard_map.111.mine, bf16[2304,128]{1,0:T(8,128)(2,1)S(1)} %collective-permute-done.7.other, bf16[384,1152]{1,0:T(8,128)(2,1)S(1)} %copy-done.3, f32[1,384]{1,0:T(1,128)S(1)} %reshape.41.gain), custom_call_target="tpu_custom_call" | custom-call | tf_op jit(solution)/shard_map/pallas_call | solution.py:409
  (59 shorter events, 12.6 us)
Async XLA Ops:
  2.8 10.3 %collective-permute-start = (bf16[4,2,64,384]{3,2,1,0:T(8,128)(2,1)}, bf16[4,2,64,384]{3,2,1,0:T(8,128)(2,1)S(1)}, u32[]{:S(2)}, u32[]{:S(2)}) collective-permute-start(bf16[4,2,64,384]{3,2,1,0:T(8,128)(2,1)} %shard_map.102), channel_id=1, source_target_pairs={{0,480},{1,481},{2,482},{3,483},{4,484},{5,485},{6,486},{7,487},{8... | collective-permute-start | bytes 1179656 | tf_op jit(solution)/shard_map/ppermute | solution.py:387
  11.9 13.9 %copy-start.16 = (f32[384]{0:T(512)S(1)}, f32[384]{0:T(512)}, u32[]{:S(2)}) copy-start(f32[384]{0:T(512)} %param.11) | copy-start | bytes 4612
  11.9 24.5 %copy-start.2 = (bf16[4,2,64,384]{3,2,1,0:T(8,128)(2,1)S(1)}, bf16[4,2,64,384]{3,2,1,0:T(8,128)(2,1)}, u32[]{:S(2)}) copy-start(bf16[4,2,64,384]{3,2,1,0:T(8,128)(2,1)} %shard_map.101.own) | copy-start | bytes 1179652
  11.9 24.5 %copy-start.3 = (bf16[384,1152]{1,0:T(8,128)(2,1)S(1)}, bf16[384,1152]{1,0:T(8,128)(2,1)}, u32[]{:S(2)}) copy-start(bf16[384,1152]{1,0:T(8,128)(2,1)} %w_qkv.5) | copy-start | bytes 2654212
  11.9 24.4 %copy-start.7 = (bf16[384,384]{1,0:T(8,128)(2,1)S(1)}, bf16[384,384]{1,0:T(8,128)(2,1)}, u32[]{:S(2)}) copy-start(bf16[384,384]{1,0:T(8,128)(2,1)} %w_proj.3) | copy-start | bytes 884740
  13.2 12.7 %collective-permute-start.1 = (bf16[2,2,64,384]{3,2,1,0:T(8,128)(2,1)S(1)}, bf16[2,2,64,384]{3,2,1,0:T(8,128)(2,1)S(1)}, u32[]{:S(2)}, u32[]{:S(2)}) collective-permute-start(bf16[2,2,64,384]{3,2,1,0:T(8,128)(2,1)S(1)} %pad_maximum_fusion.2), channel_id=1, source_target_pairs={{0,31},{1,24},{2,25},{3,26},{4,27},{5,28},{6,29},{7,30},{8,7},{9,0... | collective-permute-start | bytes 589832 | tf_op jit(solution)/shard_map/ppermute | solution.py:387
  17.3 12.0 %collective-permute-start.2 = (bf16[2,2,64,384]{3,2,1,0:T(8,128)(2,1)S(1)}, bf16[2,2,64,384]{3,2,1,0:T(8,128)(2,1)S(1)}, u32[]{:S(2)}, u32[]{:S(2)}) collective-permute-start(bf16[2,2,64,384]{3,2,1,0:T(8,128)(2,1)S(1)} %pad_maximum_fusion.3), channel_id=1, source_target_pairs={{0,24},{1,25},{2,26},{3,27},{4,28},{5,29},{6,30},{7,31},{8,0},{9,1... | collective-permute-start | bytes 589832 | tf_op jit(solution)/shard_map/ppermute | solution.py:387
  22.7 13.7 %collective-permute-start.3 = (bf16[2,2,64,384]{3,2,1,0:T(8,128)(2,1)S(1)}, bf16[2,2,64,384]{3,2,1,0:T(8,128)(2,1)S(1)}, u32[]{:S(2)}, u32[]{:S(2)}) collective-permute-start(bf16[2,2,64,384]{3,2,1,0:T(8,128)(2,1)S(1)} %pad_maximum_fusion.4), channel_id=1, source_target_pairs={{0,7},{1,0},{2,1},{3,2},{4,3},{5,4},{6,5},{7,6},{8,15},{9,8},{10,9... | collective-permute-start | bytes 589832 | tf_op jit(solution)/shard_map/ppermute | solution.py:387
  50.4 5.7 %copy-start.8 = (bf16[512,1152]{1,0:T(8,128)(2,1)}, bf16[512,1152]{1,0:T(8,128)(2,1)S(1)}, u32[]{:S(2)}) copy-start(bf16[512,1152]{1,0:T(8,128)(2,1)S(1)} %get-tuple-element.24.d_qkv) | copy-start | bytes 3538948
  50.4 5.7 %copy-start.10 = (f32[512,384]{1,0:T(8,128)}, f32[512,384]{1,0:T(8,128)S(1)}, u32[]{:S(2)}) copy-start(f32[512,384]{1,0:T(8,128)S(1)} %get-tuple-element.25.unit) | copy-start | bytes 2359300
  50.4 5.7 %copy-start.12 = (bf16[384,512]{1,0:T(8,128)(2,1)}, bf16[384,512]{1,0:T(8,128)(2,1)S(1)}, u32[]{:S(2)}) copy-start(bf16[384,512]{1,0:T(8,128)(2,1)S(1)} %get-tuple-element.23.mixed_t) | copy-start | bytes 1179652
  57.1 15.2 %all-to-all-start.1 = ((bf16[16,144,128]{2,1,0:T(8,128)(2,1)}), bf16[16,144,128]{2,1,0:T(8,128)(2,1)S(1)}, u32[]{:S(2)}, u32[]{:S(2)}) async-start(bf16[16,144,128]{2,1,0:T(8,128)(2,1)} %bitcast.5), calls=%async_computation.1 | async-start | bytes 1179648 | tf_op jit(solution)/shard_map/all_to_all | solution.py:363
  66.9 35.8 %copy-start.5 = (bf16[2,2,64,384]{3,2,1,0:T(8,128)(2,1)}, bf16[2,2,64,384]{3,2,1,0:T(8,128)(2,1)S(1)}, u32[]{:S(2)}) copy-start(bf16[2,2,64,384]{3,2,1,0:T(8,128)(2,1)S(1)} %get-tuple-element.27.rest_0_) | copy-start | bytes 589828
  66.9 13.7 %collective-permute-start.4 = (bf16[2,2,2,64,384]{4,3,2,1,0:T(8,128)(2,1)S(1)}, bf16[2,2,2,64,384]{4,3,2,1,0:T(8,128)(2,1)S(1)}, u32[]{:S(2)}, u32[]{:S(2)}) collective-permute-start(bf16[2,2,2,64,384]{4,3,2,1,0:T(8,128)(2,1)S(1)} %get-tuple-element.30), channel_id=1, source_target_pairs={{24,0},{25,1},{26,2},{27,3},{28,4},{29,5},{30,6},{31,7},{0,8},{1,9... | collective-permute-start | bytes 1179656 | tf_op jit(solution)/shard_map/ppermute | solution.py:387
  73.0 11.8 %all-to-all-start.2 = ((bf16[4,144,128]{2,1,0:T(8,128)(2,1)}), bf16[4,144,128]{2,1,0:T(8,128)(2,1)S(1)}, u32[]{:S(2)}, u32[]{:S(2)}) async-start(bf16[4,144,128]{2,1,0:T(8,128)(2,1)} %shard_map.106), calls=%async_computation.2 | async-start | bytes 294912 | tf_op jit(solution)/shard_map/all_to_all | solution.py:400
  85.6 11.2 %all-to-all-start.3 = ((bf16[4,144,128]{2,1,0:T(8,128)(2,1)}), bf16[4,144,128]{2,1,0:T(8,128)(2,1)S(1)}, u32[]{:S(2)}, u32[]{:S(2)}) async-start(bf16[4,144,128]{2,1,0:T(8,128)(2,1)} %get-tuple-element.36), calls=%async_computation.3 | async-start | bytes 294912 | tf_op jit(solution)/shard_map/all_to_all | solution.py:402
  90.2 12.5 %collective-permute-start.5 = (bf16[2,2,2,64,384]{4,3,2,1,0:T(8,128)(2,1)}, bf16[2,2,2,64,384]{4,3,2,1,0:T(8,128)(2,1)S(1)}, u32[]{:S(2)}, u32[]{:S(2)}) collective-permute-start(bf16[2,2,2,64,384]{4,3,2,1,0:T(8,128)(2,1)} %pad_maximum_fusion), channel_id=1, source_target_pairs={{7,0},{0,1},{1,2},{2,3},{3,4},{4,5},{5,6},{6,7},{15,8},{8,9},{9,10... | collective-permute-start | bytes 1179656 | tf_op jit(solution)/shard_map/ppermute | solution.py:387
  97.6 10.9 %copy-start = (bf16[8,8,8,384]{3,2,1,0:T(8,128)(2,1)S(1)}, bf16[8,8,8,384]{3,2,1,0:T(8,128)(2,1)}, u32[]{:S(2)}) copy-start(bf16[8,8,8,384]{3,2,1,0:T(8,128)(2,1)} %param.6) | copy-start | bytes 1179652
  97.6 10.9 %copy-start.1 = (bf16[8,8,8,384]{3,2,1,0:T(8,128)(2,1)S(1)}, bf16[8,8,8,384]{3,2,1,0:T(8,128)(2,1)}, u32[]{:S(2)}) copy-start(bf16[8,8,8,384]{3,2,1,0:T(8,128)(2,1)} %param.8) | copy-start | bytes 1179652
  97.6 10.9 %copy-start.4 = (s32[8,8,8]{2,1,0:T(8,128)S(1)}, s32[8,8,8]{2,1,0:T(8,128)}, u32[]{:S(2)}) copy-start(s32[8,8,8]{2,1,0:T(8,128)} %frozen.3) | copy-start | bytes 6148
  97.6 17.3 %all-to-all-start.4 = ((bf16[16,144,128]{2,1,0:T(8,128)(2,1)}), bf16[16,144,128]{2,1,0:T(8,128)(2,1)S(1)}, u32[]{:S(2)}, u32[]{:S(2)}) async-start(bf16[16,144,128]{2,1,0:T(8,128)(2,1)} %shard_map.110), calls=%async_computation.4 | async-start | bytes 1179648 | tf_op jit(solution)/shard_map/all_to_all | solution.py:403
  102.8 5.7 %copy-start.6 = (bf16[2,2,64,384]{3,2,1,0:T(8,128)(2,1)S(1)}, bf16[2,2,64,384]{3,2,1,0:T(8,128)(2,1)}, u32[]{:S(2)}) copy-start(bf16[2,2,64,384]{3,2,1,0:T(8,128)(2,1)} %copy-done.5) | copy-start | bytes 589828
  102.9 12.0 %collective-permute-start.6 = (bf16[4,2,64,384]{3,2,1,0:T(8,128)(2,1)S(1)}, bf16[4,2,64,384]{3,2,1,0:T(8,128)(2,1)S(1)}, u32[]{:S(2)}, u32[]{:S(2)}) collective-permute-start(bf16[4,2,64,384]{3,2,1,0:T(8,128)(2,1)S(1)} %pad_maximum_fusion.1), channel_id=1, source_target_pairs={{480,0},{481,1},{482,2},{483,3},{484,4},{485,5},{486,6},{487,7},{4... | collective-permute-start | bytes 1179656 | tf_op jit(solution)/shard_map/ppermute | solution.py:387
  115.0 4.7 %collective-permute-start.7 = (bf16[2304,128]{1,0:T(8,128)(2,1)S(1)}, bf16[2304,128]{1,0:T(8,128)(2,1)S(1)}, u32[]{:S(2)}, u32[]{:S(2)}) collective-permute-start(bf16[2304,128]{1,0:T(8,128)(2,1)S(1)} %shard_map.111.mine), channel_id=1, source_target_pairs={{0,32},{32,0},{1,33},{33,1},{2,34},{34,2},{3,35},{35,3},{4,36},{36... | collective-permute-start | bytes 1769480 | tf_op jit(solution)/shard_map/ppermute | solution.py:408
  (5 other events, 9.0 us)

commit v11 on v10

--- a/solution.py
+++ b/solution.py
@@ -36,7 +36,7 @@
 
 
 def window_kernel(
-    own, behind, side_3, side_2, side_1, w_qkv, w_proj, gain, grads, mixed_t, d_qkv, unit, inv_std,
+    own, behind, side_3, side_2, side_1, w_qkv, w_proj, gain, grads, mixed_t, d_qkv, unit,
     cot, qkv, d_mixed, keys_t, values_t, d_queries_t, normed,
 ):
     step = 2 * PIECE
@@ -55,8 +55,8 @@
         centred = rows - jnp.mean(rows, axis=-1, keepdims=True)
         inverse = lax.rsqrt(jnp.mean(centred * centred, axis=-1, keepdims=True) + EPSILON)
         unit_rows = centred * inverse
-        unit[part, :] = unit_rows
-        inv_std[part, :] = jnp.broadcast_to(inverse, (step, LANES))
+        unit[part, :D] = unit_rows
+        unit[part, D:] = jnp.broadcast_to(inverse, (step, LANES))
         normed[part, :] = (unit_rows * gain_row).astype(BF)
     qkv[...] = dot(normed[...], w_qkv[...]).astype(BF)
     d_mixed[...] = dot_t(cot[...], w_proj[...]).astype(BF)
@@ -111,18 +111,18 @@
         grads[pl.ds((9 + block) * D, D), :] = term.astype(BF)
 
 
-def rows_kernel(mixed_t, d_qkv, unit, inv_std, w_qkv, w_proj, gain, back_0, back_1, back_y):
+def rows_kernel(mixed_t, d_qkv, unit, w_qkv, w_proj, gain, back_0, back_1, back_y):
     step = 2 * PIECE
     backs = (back_0, back_1, back_y.at[0], back_y.at[1])
     branch = dot(mixed_t[...].T, w_proj[...]).astype(BF)
     for group in range(4):
         part = pl.ds(group * step, step)
         d_normed = dot_t(d_qkv[part, :], w_qkv[...])
-        unit_rows = unit[part, :]
+        unit_rows = unit[part, :D]
         scaled = d_normed * gain[...]
         mean_1 = jnp.mean(scaled, axis=-1, keepdims=True)
         mean_2 = jnp.mean(scaled * unit_rows, axis=-1, keepdims=True)
-        d_rows = (inv_std[part, 0:1] * (scaled - mean_1 - unit_rows * mean_2)).astype(BF)
+        d_rows = (unit[part, D : D + 1] * (scaled - mean_1 - unit_rows * mean_2)).astype(BF)
         for place in range(2):
             start = (2 * group + place) * PIECE
             backs[group][place, 0] = branch[start : start + PIECE]
@@ -320,8 +320,7 @@
             jax.ShapeDtypeStruct((GRAD_ROWS, LANES), BF),
             jax.ShapeDtypeStruct((D, ROWS), BF),
             jax.ShapeDtypeStruct((ROWS, 3 * D), BF),
-            jax.ShapeDtypeStruct((ROWS, D), F32),
-            jax.ShapeDtypeStruct((ROWS, LANES), F32),
+            jax.ShapeDtypeStruct((ROWS, D + LANES), F32),
         ),
         scratch_shapes=[
             buffer((ROWS, D), BF),

time: 122 us -> 122 us (level)
  local copies, waits for them, and re-layouts: 5.21 us -> 3.78 us
  waiting for transfers between devices: 25.5 us -> 26.8 us
    all_to_all x1, waiting for transfers between devices: 4.22 us -> 5.87 us  [local(): lax.all_to_all(parts, 'z_hi', 0, 0)]
    ppermute x7, waiting for transfers between devices: 18.9 us -> 17.3 us  [send(): return lax.ppermute(block, LATTICE, route(kind, back))]
    unnamed x34 -> x26, local copies, waits for them, and re-layouts: 3.97 us -> 2.55 us
where the time goes in v11:
time: 122 us; the launch traced here: 121 us
  starting transfers between devices  55.3 us (45%)
  Pallas kernels  27.5 us (23%)
  waiting for transfers between devices  26.8 us (22%)
  blocking collectives  5.71 us (5%)
  local copies, waits for them, and re-layouts  3.78 us (3%)
    ppermute x7, starting transfers between devices, send(): return lax.ppermute(block, LATTICE, route(kind, back))  35 us
    ppermute x7, waiting for transfers between devices, send(): return lax.ppermute(block, LATTICE, route(kind, back))  17.3 us
    pallas_call x1, Pallas kernels, window_pass(): pl.pallas_call(window_kernel, out_shape=(jax.ShapeDtypeStruct((GRAD_ROWS,...  13.3 us
    all_to_all x1, waiting for transfers between devices, local(): lax.all_to_all(parts, 'z_hi', 0, 0)  5.87 us
    all_to_all x1, blocking collectives, near_sum(): lax.all_to_all(rows.reshape(2, GRAD_ROWS // 2, LANES), 'core', 0, 0)  5.71 us
    all_to_all x1, starting transfers between devices, near_sum(): parts = lax.all_to_all(parts, NEAR, 0, 0)  4.92 us
    all_to_all x1, starting transfers between devices, local(): mine = lax.all_to_all(parts, NEAR, 0, 0).reshape(GRAD_ROWS // 2, LANES)  4.41 us
    pallas_call x2, Pallas kernels, cut(): pl.pallas_call(functools.partial(cut_kernel, upper=upper), out_shape=jax....  4.37 us
  transfers between devices with their start and end apart: 12, of which 7 were waited for; matrix products, arithmetic and copies ran while one was open for 2% of the time, Pallas kernels for 7%

profile of v11, /device:TPU:1, one launch (start us, length us, event | category | flops | bytes accessed | tf_op | source)
XLA Modules:
  0.0 121.0 jit_solution(3393578684405800376)
XLA Ops:
  0.6 2.2 %shard_map.102 = bf16[4,2,64,384]{3,2,1,0:T(8,128)(2,1)} custom-call(s32[1]{0:T(128)} %bitcast.odd.core, bf16[512,384]{1,0:T(8,128)(2,1)} %bitcast.15, s32[8,8,8]{2,1,0:T(8,128)} %frozen.3, bf16[512,384]{1,0:T(8,128)(2,1)} %bitcast.19), custom_call_target="tpu_custom_call" | custom-call | tf_op jit(solution)/shard_map/pallas_call | solution.py:188
  2.8 6.9 %collective-permute-start = (bf16[4,2,64,384]{3,2,1,0:T(8,128)(2,1)}, bf16[4,2,64,384]{3,2,1,0:T(8,128)(2,1)S(1)}, u32[]{:S(2)}, u32[]{:S(2)}) collective-permute-start(bf16[4,2,64,384]{3,2,1,0:T(8,128)(2,1)} %shard_map.102), channel_id=1, source_target_pairs={{0,480},{1,481},{2,482},{3,483},{4,484},{5,485},{6,486},{7,487},{8... | collective-permute-start | bytes 1179656 | tf_op jit(solution)/shard_map/ppermute | solution.py:386
  9.7 2.2 %shard_map.101.own = bf16[4,2,64,384]{3,2,1,0:T(8,128)(2,1)} custom-call(s32[1]{0:T(128)} %bitcast.odd.core, bf16[512,384]{1,0:T(8,128)(2,1)} %bitcast.16, s32[8,8,8]{2,1,0:T(8,128)} %frozen.3, bf16[512,384]{1,0:T(8,128)(2,1)} %bitcast.20), custom_call_target="tpu_custom_call" | custom-call | tf_op jit(solution)/shard_map/pallas_call | solution.py:188
  13.2 4.0 %collective-permute-start.1 = (bf16[2,2,64,384]{3,2,1,0:T(8,128)(2,1)S(1)}, bf16[2,2,64,384]{3,2,1,0:T(8,128)(2,1)S(1)}, u32[]{:S(2)}, u32[]{:S(2)}) collective-permute-start(bf16[2,2,64,384]{3,2,1,0:T(8,128)(2,1)S(1)} %pad_maximum_fusion.2), channel_id=1, source_target_pairs={{0,31},{1,24},{2,25},{3,26},{4,27},{5,28},{6,29},{7,30},{8,7},{9,0... | collective-permute-start | bytes 589832 | tf_op jit(solution)/shard_map/ppermute | solution.py:386
  17.3 5.4 %collective-permute-start.2 = (bf16[2,2,64,384]{3,2,1,0:T(8,128)(2,1)S(1)}, bf16[2,2,64,384]{3,2,1,0:T(8,128)(2,1)S(1)}, u32[]{:S(2)}, u32[]{:S(2)}) collective-permute-start(bf16[2,2,64,384]{3,2,1,0:T(8,128)(2,1)S(1)} %pad_maximum_fusion.3), channel_id=1, source_target_pairs={{0,24},{1,25},{2,26},{3,27},{4,28},{5,29},{6,30},{7,31},{8,0},{9,1... | collective-permute-start | bytes 589832 | tf_op jit(solution)/shard_map/ppermute | solution.py:386
  22.7 3.1 %collective-permute-start.3 = (bf16[2,2,64,384]{3,2,1,0:T(8,128)(2,1)S(1)}, bf16[2,2,64,384]{3,2,1,0:T(8,128)(2,1)S(1)}, u32[]{:S(2)}, u32[]{:S(2)}) collective-permute-start(bf16[2,2,64,384]{3,2,1,0:T(8,128)(2,1)S(1)} %pad_maximum_fusion.4), channel_id=1, source_target_pairs={{0,7},{1,0},{2,1},{3,2},{4,3},{5,4},{6,5},{7,6},{8,15},{9,8},{10,9... | collective-permute-start | bytes 589832 | tf_op jit(solution)/shard_map/ppermute | solution.py:386
  25.9 3.4 %collective-permute-done.2.side_2 = bf16[2,2,64,384]{3,2,1,0:T(8,128)(2,1)S(1)} collective-permute-done((bf16[2,2,64,384]{3,2,1,0:T(8,128)(2,1)S(1)}, bf16[2,2,64,384]{3,2,1,0:T(8,128)(2,1)S(1)}, u32[]{:S(2)}, u32[]{:S(2)}) %collective-permute-start.2) | collective-permute-done | bytes 196640 | tf_op jit(solution)/shard_map/ppermute | solution.py:386
  29.2 7.1 %collective-permute-done.3.side_1 = bf16[2,2,64,384]{3,2,1,0:T(8,128)(2,1)S(1)} collective-permute-done((bf16[2,2,64,384]{3,2,1,0:T(8,128)(2,1)S(1)}, bf16[2,2,64,384]{3,2,1,0:T(8,128)(2,1)S(1)}, u32[]{:S(2)}, u32[]{:S(2)}) %collective-permute-start.3) | collective-permute-done | bytes 196640 | tf_op jit(solution)/shard_map/ppermute | solution.py:386
  36.4 13.3 %shard_map.103 = (bf16[4608,128]{1,0:T(8,128)(2,1)S(1)}, bf16[384,512]{1,0:T(8,128)(2,1)S(1)}, bf16[512,1152]{1,0:T(8,128)(2,1)S(1)}, f32[512,512]{1,0:T(8,128)S(1)}) custom-call(bf16[4,2,64,384]{3,2,1,0:T(8,128)(2,1)S(1)} %copy-done.2, bf16[4,2,64,384]{3,2,1,0:T(8,128)(2,1)S(1)} %collective-permute-done.behind, ...), custom_call_target="tpu_custom_call" | custom-call | flops 12000000000 | bytes 5000000 | tf_op jit(solution)/shard_map/pallas_call | solution.py:317
  49.8 5.7 %all_to_all.25.parts = bf16[2,2304,128]{2,1,0:T(8,128)(2,1)S(1)} all-to-all(bf16[2,2304,128]{2,1,0:T(8,128)(2,1)S(1)} %bitcast.24), channel_id=1, replica_groups=mesh['z_hi'=4,'z_lo'=2,'core'=2,'y_hi'=4,'y_lo'=2,'x'=4] {'core'}, dimensions={0} | all-to-all | bytes 2359296 | tf_op jit(solution)/shard_map/all_to_all | solution.py:360
  56.4 4.9 %all-to-all-start.1 = ((bf16[16,144,128]{2,1,0:T(8,128)(2,1)}), bf16[16,144,128]{2,1,0:T(8,128)(2,1)S(1)}, u32[]{:S(2)}, u32[]{:S(2)}) async-start(bf16[16,144,128]{2,1,0:T(8,128)(2,1)} %bitcast.5), calls=%async_computation.1 | async-start | bytes 1179648 | tf_op jit(solution)/shard_map/all_to_all | solution.py:362
  65.4 5.3 %collective-permute-start.4 = (bf16[2,2,2,64,384]{4,3,2,1,0:T(8,128)(2,1)S(1)}, bf16[2,2,2,64,384]{4,3,2,1,0:T(8,128)(2,1)S(1)}, u32[]{:S(2)}, u32[]{:S(2)}) collective-permute-start(bf16[2,2,2,64,384]{4,3,2,1,0:T(8,128)(2,1)S(1)} %get-tuple-element.28), channel_id=1, source_target_pairs={{24,0},{25,1},{26,2},{27,3},{28,4},{29,5},{30,6},{31,7},{0,8},{1,9... | collective-permute-start | bytes 1179656 | tf_op jit(solution)/shard_map/ppermute | solution.py:386
  72.2 4.1 %all-to-all-start.2 = ((bf16[4,144,128]{2,1,0:T(8,128)(2,1)}), bf16[4,144,128]{2,1,0:T(8,128)(2,1)S(1)}, u32[]{:S(2)}, u32[]{:S(2)}) async-start(bf16[4,144,128]{2,1,0:T(8,128)(2,1)} %shard_map.106), calls=%async_computation.2 | async-start | bytes 294912 | tf_op jit(solution)/shard_map/all_to_all | solution.py:399
  76.3 1.9 %collective-permute-done.4.rest_0_ = bf16[2,2,2,64,384]{4,3,2,1,0:T(8,128)(2,1)S(1)} collective-permute-done((bf16[2,2,2,64,384]{4,3,2,1,0:T(8,128)(2,1)S(1)}, bf16[2,2,2,64,384]{4,3,2,1,0:T(8,128)(2,1)S(1)}, u32[]{:S(2)}, u32[]{:S(2)}) %collective-permute-start.4) | collective-permute-done | bytes 393248 | tf_op jit(solution)/shard_map/ppermute | solution.py:386
  78.2 5.9 %all-to-all-done.2.parts = bf16[4,144,128]{2,1,0:T(8,128)(2,1)S(1)} async-done(((bf16[4,144,128]{2,1,0:T(8,128)(2,1)}), bf16[4,144,128]{2,1,0:T(8,128)(2,1)S(1)}, u32[]{:S(2)}, u32[]{:S(2)}) %all-to-all-start.2) | async-done | bytes 147488 | tf_op jit(solution)/shard_map/all_to_all | solution.py:399
  84.7 3.8 %all-to-all-start.3 = ((bf16[4,144,128]{2,1,0:T(8,128)(2,1)}), bf16[4,144,128]{2,1,0:T(8,128)(2,1)S(1)}, u32[]{:S(2)}, u32[]{:S(2)}) async-start(bf16[4,144,128]{2,1,0:T(8,128)(2,1)} %get-tuple-element.34), calls=%async_computation.3 | async-start | bytes 294912 | tf_op jit(solution)/shard_map/all_to_all | solution.py:401
  89.4 3.7 %collective-permute-start.5 = (bf16[2,2,2,64,384]{4,3,2,1,0:T(8,128)(2,1)}, bf16[2,2,2,64,384]{4,3,2,1,0:T(8,128)(2,1)S(1)}, u32[]{:S(2)}, u32[]{:S(2)}) collective-permute-start(bf16[2,2,2,64,384]{4,3,2,1,0:T(8,128)(2,1)} %pad_maximum_fusion), channel_id=1, source_target_pairs={{7,0},{0,1},{1,2},{2,3},{3,4},{4,5},{5,6},{6,7},{15,8},{8,9},{9,10... | collective-permute-start | bytes 1179656 | tf_op jit(solution)/shard_map/ppermute | solution.py:386
  93.1 2.8 %all-to-all-done.3.parts = bf16[4,144,128]{2,1,0:T(8,128)(2,1)S(1)} async-done(((bf16[4,144,128]{2,1,0:T(8,128)(2,1)}), bf16[4,144,128]{2,1,0:T(8,128)(2,1)S(1)}, u32[]{:S(2)}, u32[]{:S(2)}) %all-to-all-start.3) | async-done | bytes 147488 | tf_op jit(solution)/shard_map/all_to_all | solution.py:401
  96.8 4.4 %all-to-all-start.4 = ((bf16[16,144,128]{2,1,0:T(8,128)(2,1)}), bf16[16,144,128]{2,1,0:T(8,128)(2,1)S(1)}, u32[]{:S(2)}, u32[]{:S(2)}) async-start(bf16[16,144,128]{2,1,0:T(8,128)(2,1)} %shard_map.110), calls=%async_computation.4 | async-start | bytes 1179648 | tf_op jit(solution)/shard_map/all_to_all | solution.py:402
  101.3 6.6 %collective-permute-start.6 = (bf16[4,2,64,384]{3,2,1,0:T(8,128)(2,1)S(1)}, bf16[4,2,64,384]{3,2,1,0:T(8,128)(2,1)S(1)}, u32[]{:S(2)}, u32[]{:S(2)}) collective-permute-start(bf16[4,2,64,384]{3,2,1,0:T(8,128)(2,1)S(1)} %pad_maximum_fusion.1), channel_id=1, source_target_pairs={{480,0},{481,1},{482,2},{483,3},{484,4},{485,5},{486,6},{487,7},{4... | collective-permute-start | bytes 1179656 | tf_op jit(solution)/shard_map/ppermute | solution.py:386
  109.6 5.0 %collective-permute-done.6.rest_0_.refs_1_ = bf16[4,2,64,384]{3,2,1,0:T(8,128)(2,1)S(1)} collective-permute-done((bf16[4,2,64,384]{3,2,1,0:T(8,128)(2,1)S(1)}, bf16[4,2,64,384]{3,2,1,0:T(8,128)(2,1)S(1)}, u32[]{:S(2)}, u32[]{:S(2)}) %collective-permute-start.6) | collective-permute-done | bytes 393248 | tf_op jit(solution)/shard_map/ppermute | solution.py:386
  114.6 3.0 %collective-permute-start.7 = (bf16[2304,128]{1,0:T(8,128)(2,1)S(1)}, bf16[2304,128]{1,0:T(8,128)(2,1)S(1)}, u32[]{:S(2)}, u32[]{:S(2)}) collective-permute-start(bf16[2304,128]{1,0:T(8,128)(2,1)S(1)} %shard_map.111.mine), channel_id=1, source_target_pairs={{0,32},{32,0},{1,33},{33,1},{2,34},{34,2},{3,35},{35,3},{4,36},{36... | collective-permute-start | bytes 1769480 | tf_op jit(solution)/shard_map/ppermute | solution.py:407
  117.6 1.6 %shard_map.109 = (bf16[512,384]{1,0:T(8,128)(2,1)}, bf16[512,384]{1,0:T(8,128)(2,1)}) custom-call(s32[1]{0:T(128)} %bitcast.odd.core, bf16[512,384]{1,0:T(8,128)(2,1)S(1)} %bitcast.18, s32[8,8,8]{2,1,0:T(8,128)S(1)} %copy-done.4, bf16[512,384]{1,0:T(8,128)(2,1)S(1)} %bitcast.22, ...), custom_call_target="tpu_custom_call", output_to_operand_aliasing={{0}: (5, {}), {1}: (6, {})} | custom-call | flops 150000000 | bytes 2000000 | tf_op jit(solution)/shard_map/pallas_call | solution.py:234
  119.2 1.8 %shard_map.112 = (f32[384,1152]{1,0:T(8,128)}, f32[384,384]{1,0:T(8,128)}, f32[384]{0:T(512)}) custom-call(s32[1]{0:T(128)} %bitcast.odd.core, bf16[2304,128]{1,0:T(8,128)(2,1)S(1)} %shard_map.111.mine, bf16[2304,128]{1,0:T(8,128)(2,1)S(1)} %collective-permute-done.7.other, bf16[384,1152]{1,0:T(8,128)(2,1)S(1)} %copy-done.3, f32[1,384]{1,0:T(1,128)S(1)} %reshape.41.gain), custom_call_target="tpu_custom_call" | custom-call | tf_op jit(solution)/shard_map/pallas_call | solution.py:408
  (51 shorter events, 11.9 us)
Async XLA Ops:
  2.8 10.3 %collective-permute-start = (bf16[4,2,64,384]{3,2,1,0:T(8,128)(2,1)}, bf16[4,2,64,384]{3,2,1,0:T(8,128)(2,1)S(1)}, u32[]{:S(2)}, u32[]{:S(2)}) collective-permute-start(bf16[4,2,64,384]{3,2,1,0:T(8,128)(2,1)} %shard_map.102), channel_id=1, source_target_pairs={{0,480},{1,481},{2,482},{3,483},{4,484},{5,485},{6,486},{7,487},{8... | collective-permute-start | bytes 1179656 | tf_op jit(solution)/shard_map/ppermute | solution.py:386
  11.9 13.9 %copy-start.12 = (f32[384]{0:T(512)S(1)}, f32[384]{0:T(512)}, u32[]{:S(2)}) copy-start(f32[384]{0:T(512)} %param.11) | copy-start | bytes 4612
  11.9 24.5 %copy-start.2 = (bf16[4,2,64,384]{3,2,1,0:T(8,128)(2,1)S(1)}, bf16[4,2,64,384]{3,2,1,0:T(8,128)(2,1)}, u32[]{:S(2)}) copy-start(bf16[4,2,64,384]{3,2,1,0:T(8,128)(2,1)} %shard_map.101.own) | copy-start | bytes 1179652
  11.9 24.4 %copy-start.3 = (bf16[384,1152]{1,0:T(8,128)(2,1)S(1)}, bf16[384,1152]{1,0:T(8,128)(2,1)}, u32[]{:S(2)}) copy-start(bf16[384,1152]{1,0:T(8,128)(2,1)} %w_qkv.5) | copy-start | bytes 2654212
  11.9 24.4 %copy-start.7 = (bf16[384,384]{1,0:T(8,128)(2,1)S(1)}, bf16[384,384]{1,0:T(8,128)(2,1)}, u32[]{:S(2)}) copy-start(bf16[384,384]{1,0:T(8,128)(2,1)} %w_proj.3) | copy-start | bytes 884740
  13.2 12.7 %collective-permute-start.1 = (bf16[2,2,64,384]{3,2,1,0:T(8,128)(2,1)S(1)}, bf16[2,2,64,384]{3,2,1,0:T(8,128)(2,1)S(1)}, u32[]{:S(2)}, u32[]{:S(2)}) collective-permute-start(bf16[2,2,64,384]{3,2,1,0:T(8,128)(2,1)S(1)} %pad_maximum_fusion.2), channel_id=1, source_target_pairs={{0,31},{1,24},{2,25},{3,26},{4,27},{5,28},{6,29},{7,30},{8,7},{9,0... | collective-permute-start | bytes 589832 | tf_op jit(solution)/shard_map/ppermute | solution.py:386
  17.3 12.0 %collective-permute-start.2 = (bf16[2,2,64,384]{3,2,1,0:T(8,128)(2,1)S(1)}, bf16[2,2,64,384]{3,2,1,0:T(8,128)(2,1)S(1)}, u32[]{:S(2)}, u32[]{:S(2)}) collective-permute-start(bf16[2,2,64,384]{3,2,1,0:T(8,128)(2,1)S(1)} %pad_maximum_fusion.3), channel_id=1, source_target_pairs={{0,24},{1,25},{2,26},{3,27},{4,28},{5,29},{6,30},{7,31},{8,0},{9,1... | collective-permute-start | bytes 589832 | tf_op jit(solution)/shard_map/ppermute | solution.py:386
  22.7 13.7 %collective-permute-start.3 = (bf16[2,2,64,384]{3,2,1,0:T(8,128)(2,1)S(1)}, bf16[2,2,64,384]{3,2,1,0:T(8,128)(2,1)S(1)}, u32[]{:S(2)}, u32[]{:S(2)}) collective-permute-start(bf16[2,2,64,384]{3,2,1,0:T(8,128)(2,1)S(1)} %pad_maximum_fusion.4), channel_id=1, source_target_pairs={{0,7},{1,0},{2,1},{3,2},{4,3},{5,4},{6,5},{7,6},{8,15},{9,8},{10,9... | collective-permute-start | bytes 589832 | tf_op jit(solution)/shard_map/ppermute | solution.py:386
  49.7 5.7 %copy-start.8 = (bf16[512,1152]{1,0:T(8,128)(2,1)}, bf16[512,1152]{1,0:T(8,128)(2,1)S(1)}, u32[]{:S(2)}) copy-start(bf16[512,1152]{1,0:T(8,128)(2,1)S(1)} %get-tuple-element.23.d_qkv) | copy-start | bytes 3538948
  49.8 5.7 %copy-start.10 = (f32[512,512]{1,0:T(8,128)}, f32[512,512]{1,0:T(8,128)S(1)}, u32[]{:S(2)}) copy-start(f32[512,512]{1,0:T(8,128)S(1)} %get-tuple-element.24.unit) | copy-start | bytes 3145732
  56.4 15.0 %all-to-all-start.1 = ((bf16[16,144,128]{2,1,0:T(8,128)(2,1)}), bf16[16,144,128]{2,1,0:T(8,128)(2,1)S(1)}, u32[]{:S(2)}, u32[]{:S(2)}) async-start(bf16[16,144,128]{2,1,0:T(8,128)(2,1)} %bitcast.5), calls=%async_computation.1 | async-start | bytes 1179648 | tf_op jit(solution)/shard_map/all_to_all | solution.py:362
  61.4 1.3 %copy-start.9 = (bf16[512,1152]{1,0:T(8,128)(2,1)S(1)}, bf16[512,1152]{1,0:T(8,128)(2,1)}, u32[]{:S(2)}) copy-start(bf16[512,1152]{1,0:T(8,128)(2,1)} %copy-done.8) | copy-start | bytes 3538948
  65.4 35.8 %copy-start.5 = (bf16[2,2,64,384]{3,2,1,0:T(8,128)(2,1)}, bf16[2,2,64,384]{3,2,1,0:T(8,128)(2,1)S(1)}, u32[]{:S(2)}) copy-start(bf16[2,2,64,384]{3,2,1,0:T(8,128)(2,1)S(1)} %get-tuple-element.25.rest_0_) | copy-start | bytes 589828
  65.4 12.8 %collective-permute-start.4 = (bf16[2,2,2,64,384]{4,3,2,1,0:T(8,128)(2,1)S(1)}, bf16[2,2,2,64,384]{4,3,2,1,0:T(8,128)(2,1)S(1)}, u32[]{:S(2)}, u32[]{:S(2)}) collective-permute-start(bf16[2,2,2,64,384]{4,3,2,1,0:T(8,128)(2,1)S(1)} %get-tuple-element.28), channel_id=1, source_target_pairs={{24,0},{25,1},{26,2},{27,3},{28,4},{29,5},{30,6},{31,7},{0,8},{1,9... | collective-permute-start | bytes 1179656 | tf_op jit(solution)/shard_map/ppermute | solution.py:386
  72.2 11.8 %all-to-all-start.2 = ((bf16[4,144,128]{2,1,0:T(8,128)(2,1)}), bf16[4,144,128]{2,1,0:T(8,128)(2,1)S(1)}, u32[]{:S(2)}, u32[]{:S(2)}) async-start(bf16[4,144,128]{2,1,0:T(8,128)(2,1)} %shard_map.106), calls=%async_computation.2 | async-start | bytes 294912 | tf_op jit(solution)/shard_map/all_to_all | solution.py:399
  84.7 11.2 %all-to-all-start.3 = ((bf16[4,144,128]{2,1,0:T(8,128)(2,1)}), bf16[4,144,128]{2,1,0:T(8,128)(2,1)S(1)}, u32[]{:S(2)}, u32[]{:S(2)}) async-start(bf16[4,144,128]{2,1,0:T(8,128)(2,1)} %get-tuple-element.34), calls=%async_computation.3 | async-start | bytes 294912 | tf_op jit(solution)/shard_map/all_to_all | solution.py:401
  89.4 11.8 %collective-permute-start.5 = (bf16[2,2,2,64,384]{4,3,2,1,0:T(8,128)(2,1)}, bf16[2,2,2,64,384]{4,3,2,1,0:T(8,128)(2,1)S(1)}, u32[]{:S(2)}, u32[]{:S(2)}) collective-permute-start(bf16[2,2,2,64,384]{4,3,2,1,0:T(8,128)(2,1)} %pad_maximum_fusion), channel_id=1, source_target_pairs={{7,0},{0,1},{1,2},{2,3},{3,4},{4,5},{5,6},{6,7},{15,8},{8,9},{9,10... | collective-permute-start | bytes 1179656 | tf_op jit(solution)/shard_map/ppermute | solution.py:386
  96.7 11.2 %copy-start = (bf16[8,8,8,384]{3,2,1,0:T(8,128)(2,1)S(1)}, bf16[8,8,8,384]{3,2,1,0:T(8,128)(2,1)}, u32[]{:S(2)}) copy-start(bf16[8,8,8,384]{3,2,1,0:T(8,128)(2,1)} %param.6) | copy-start | bytes 1179652
  96.8 11.2 %copy-start.1 = (bf16[8,8,8,384]{3,2,1,0:T(8,128)(2,1)S(1)}, bf16[8,8,8,384]{3,2,1,0:T(8,128)(2,1)}, u32[]{:S(2)}) copy-start(bf16[8,8,8,384]{3,2,1,0:T(8,128)(2,1)} %param.8) | copy-start | bytes 1179652
  96.8 11.2 %copy-start.4 = (s32[8,8,8]{2,1,0:T(8,128)S(1)}, s32[8,8,8]{2,1,0:T(8,128)}, u32[]{:S(2)}) copy-start(s32[8,8,8]{2,1,0:T(8,128)} %frozen.3) | copy-start | bytes 6148
  96.8 17.8 %all-to-all-start.4 = ((bf16[16,144,128]{2,1,0:T(8,128)(2,1)}), bf16[16,144,128]{2,1,0:T(8,128)(2,1)S(1)}, u32[]{:S(2)}, u32[]{:S(2)}) async-start(bf16[16,144,128]{2,1,0:T(8,128)(2,1)} %shard_map.110), calls=%async_computation.4 | async-start | bytes 1179648 | tf_op jit(solution)/shard_map/all_to_all | solution.py:402
  101.2 6.8 %copy-start.6 = (bf16[2,2,64,384]{3,2,1,0:T(8,128)(2,1)S(1)}, bf16[2,2,64,384]{3,2,1,0:T(8,128)(2,1)}, u32[]{:S(2)}) copy-start(bf16[2,2,64,384]{3,2,1,0:T(8,128)(2,1)} %copy-done.5) | copy-start | bytes 589828
  101.3 13.2 %collective-permute-start.6 = (bf16[4,2,64,384]{3,2,1,0:T(8,128)(2,1)S(1)}, bf16[4,2,64,384]{3,2,1,0:T(8,128)(2,1)S(1)}, u32[]{:S(2)}, u32[]{:S(2)}) collective-permute-start(bf16[4,2,64,384]{3,2,1,0:T(8,128)(2,1)S(1)} %pad_maximum_fusion.1), channel_id=1, source_target_pairs={{480,0},{481,1},{482,2},{483,3},{484,4},{485,5},{486,6},{487,7},{4... | collective-permute-start | bytes 1179656 | tf_op jit(solution)/shard_map/ppermute | solution.py:386
  114.6 4.6 %collective-permute-start.7 = (bf16[2304,128]{1,0:T(8,128)(2,1)S(1)}, bf16[2304,128]{1,0:T(8,128)(2,1)S(1)}, u32[]{:S(2)}, u32[]{:S(2)}) collective-permute-start(bf16[2304,128]{1,0:T(8,128)(2,1)S(1)} %shard_map.111.mine), channel_id=1, source_target_pairs={{0,32},{32,0},{1,33},{33,1},{2,34},{34,2},{3,35},{35,3},{4,36},{36... | collective-permute-start | bytes 1769480 | tf_op jit(solution)/shard_map/ppermute | solution.py:407
  (1 other events, 1.2 us)
